TPU v7x, 32 devices: a whole 2x2x4 slice. The times are simulated.
32 devices in a mesh: gy: 8 (over y, x, core), gx: 4 (over z).
Axes of the slice: x: 2, y: 2, z: 4, core: 2. Of those that a mesh axis runs over, the one named last changes fastest.
Arguments:
- frames: bfloat16 [384, 256, 512], P('gy', 'gx'), may hold values from -2.390625 to 2.390625
- hidden_state: bfloat16 [384, 256, 128], P('gy', 'gx'), may hold values from -0.8984375 to 0.8984375
- cell_state: float32 [384, 256, 128], P('gy', 'gx'), may hold values from -4 to 4
- w_gates: bfloat16 [3, 3, 384, 512], replicated, may hold values from -0.3125 to 0.3125
- gate_bias: float32 [512], replicated, may hold values from -3 to 3
- w_qkv: bfloat16 [128, 768], replicated, may hold values from -0.5 to 0.5
- w_out: bfloat16 [256, 128], replicated, may hold values from -0.375 to 0.375
- w_up: bfloat16 [128, 512], replicated, may hold values from -0.5 to 0.5
- w_down: bfloat16 [512, 128], replicated, may hold values from -0.25 to 0.25
Outputs:
- block_out: bfloat16 [384, 256, 128], P('gy', 'gx')
- cell_out: float32 [384, 256, 128], P('gy', 'gx')
All inputs are finite; a program needn't handle non-finite values.
Results may differ from a plain program's by a relative error of at most 0.014.
Values may be sent and summed in bfloat16 or wider, within the bound.
No kernel may reach another device: no remote copies, remote signals or barrier semaphores. Data moves between devices by JAX's collectives and lax.ppermute only.
A program may use at most 192 MiB of HBM per device.

v0:
```python
import functools

import jax
import jax.numpy as jnp
from jax import lax
from jax.experimental import pallas as pl
from jax.experimental.pallas import tpu as pltpu
from jax.sharding import PartitionSpec as P

HEADS = 8
HDIM = 32
GRID = 8
STEP = 8
SUB = 4
BF = jnp.bfloat16
F32 = jnp.float32
BF_MAX = 3.3895313892515355e38
VMEM_LIMIT = 40 * 1024 * 1024


def sigmoid(x):
    return 0.5 * jnp.tanh(0.5 * x) + 0.5


def lstm(gates, cell_prev):
    width = cell_prev.shape[-1]
    in_gate = sigmoid(gates[:, 0:width])
    forget_gate = sigmoid(gates[:, width : 2 * width])
    candidate = jnp.tanh(gates[:, 2 * width : 3 * width])
    out_gate = sigmoid(gates[:, 3 * width :])
    cell = forget_gate * cell_prev + in_gate * candidate
    return cell, out_gate * jnp.tanh(cell)


def layer_norm(values):
    center = values - jnp.mean(values, axis=-1, keepdims=True)
    spread = jnp.mean(center * center, axis=-1, keepdims=True)
    return center * lax.rsqrt(spread + 1e-05)


def three_columns(cells, left, right):
    count = cells.shape[1]
    wide = cells.astype(F32)
    place = lax.broadcasted_iota(jnp.int32, wide.shape, 1)
    before = jnp.where(place == 0, left, pltpu.roll(wide, 1, axis=1))
    after = jnp.where(place == count - 1, right, pltpu.roll(wide, count - 1, axis=1))
    return before.astype(BF), cells, after.astype(BF)


def conv_kernel(
    first_block,
    last_block,
    frame, frame_prev, frame_next, frame_top, frame_bot,
    hid, hid_prev, hid_next, hid_top, hid_bot,
    left, right, cell, weights, bias,
    *rest,
    packed,
):
    hid_out, cell_out, spread = rest[-3:]
    block = first_block + pl.program_id(0)
    latent = frame.shape[2]
    chans = latent + hid.shape[2]
    cols = hid.shape[1]

    def place(at, count, lead, x, h):
        low = left[pl.ds(lead, count)]
        high = right[pl.ds(lead, count)]
        for part, start, width in ((x, 0, latent), (h, latent, chans - latent)):
            pieces = three_columns(part, low[:, :, start : start + width], high[:, :, start : start + width])
            for tap in range(3):
                begin = tap * chans + start
                spread[pl.ds(at, count), :, begin : begin + width] = pieces[tap]

    base = block * STEP

    @pl.when(block == 0)
    def _():
        place(0, 1, base, frame_top[...], hid_top[...])

    @pl.when(block != 0)
    def _():
        place(0, 1, base, frame_prev[...], hid_prev[...])

    @pl.when(block == last_block)
    def _():
        place(STEP + 1, 1, base + STEP + 1, frame_bot[...], hid_bot[...])

    @pl.when(block != last_block)
    def _():
        place(STEP + 1, 1, base + STEP + 1, frame_next[...], hid_next[...])

    for at in range(0, STEP, SUB):
        place(1 + at, SUB, base + 1 + at, frame[at : at + SUB], hid[at : at + SUB])

    width = hid.shape[2]
    for at in range(0, STEP, SUB):
        lhs = jnp.concatenate(
            [spread[at + tap : at + tap + SUB].reshape(SUB * cols, 3 * chans) for tap in range(3)], axis=1
        )
        gates = jnp.dot(lhs, weights[...], preferred_element_type=F32) + bias[...]
        new_cell, new_hidden = lstm(gates, cell[at : at + SUB].reshape(SUB * cols, width))
        cell_out[at : at + SUB] = new_cell.reshape(SUB, cols, width)
        new_hidden = new_hidden.reshape(SUB, cols, width)
        if not packed:
            hid_out[at : at + SUB] = new_hidden.astype(BF)
            continue
        owners_x, piece_y = hid_out.shape[1:3]
        local_m, piece_x = packed
        for owner in range(owners_x):
            picked = jnp.concatenate(
                [
                    new_hidden[:, (m * owners_x + owner) * piece_x : (m * owners_x + owner + 1) * piece_x]
                    for m in range(local_m)
                ],
                axis=1,
            ).astype(BF)
            for row in range(SUB):
                line = at + row
                hid_out[line // piece_y, owner, line % piece_y] = picked[row]


def conv_step(
    frames, part, hid, cell, tops, bots, left, right, weights, bias, blocks, out_shapes, out_specs, packed, carry
):
    rows, cols, width = hid.shape
    latent = weights.shape[0] // 9 - width
    first, count = blocks
    last = rows // STEP - 1

    def rowed(depth, channels, channel, index):
        return pl.BlockSpec((depth, cols, channels), lambda i: (index(first + i), 0, channel))

    def whole(array):
        return pl.BlockSpec(array.shape, lambda i: (0,) * array.ndim)

    before = lambda b: jnp.maximum(b * STEP - 1, 0)
    after = lambda b: jnp.minimum(b * STEP + STEP, rows - 1)
    here = lambda b: b
    in_specs = [
        rowed(STEP, latent, part, here), rowed(1, latent, part, before), rowed(1, latent, part, after),
        whole(tops[0]), whole(bots[0]),
        rowed(STEP, width, 0, here), rowed(1, width, 0, before), rowed(1, width, 0, after),
        whole(tops[1]), whole(bots[1]),
        whole(left), whole(right), rowed(STEP, width, 0, here), whole(weights), whole(bias),
    ]
    operands = [
        frames, frames, frames, tops[0], bots[0], hid, hid, hid, tops[1], bots[1], left, right, cell, weights, bias,
    ]
    aliases = {}
    if carry is not None:
        aliases = {len(operands): 1}
        in_specs.append(pl.BlockSpec(memory_space=pl.ANY))
        operands.append(carry)
    cells = count * STEP * cols
    return pl.pallas_call(
        functools.partial(conv_kernel, first, last, packed=packed),
        grid=(count,),
        in_specs=in_specs,
        out_specs=out_specs,
        out_shape=out_shapes,
        scratch_shapes=[pltpu.VMEM((STEP + 2, cols, 3 * (latent + width)), BF)],
        input_output_aliases=aliases,
        compiler_params=pltpu.CompilerParams(vmem_limit_bytes=VMEM_LIMIT),
        cost_estimate=pl.CostEstimate(
            flops=2 * cells * weights.size, bytes_accessed=2 * weights.size + cells * 2048, transcendentals=cells * width * 5
        ),
    )(*operands)


def halo_kernel(lines, strips, left, right, weights, bias, out):
    chans = left.shape[2]
    extent = lines.shape[2]
    rows = left.shape[0] - 4
    parts = []
    for side in range(2):
        lead = side * (rows + 1)
        pieces = three_columns(lines[side, :, :, :chans], left[lead : lead + 3], right[lead : lead + 3])
        parts.append(jnp.concatenate([pieces[tap][row] for row in range(3) for tap in range(3)], axis=1))
    length = strips.shape[2]
    for side in range(2):
        rolled = []
        for col in range(3):
            wide = strips[side, col, :, :chans].astype(F32)
            rolled.append((pltpu.roll(wide, 1, axis=0), wide, pltpu.roll(wide, length - 1, axis=0)))
        parts.append(jnp.concatenate([rolled[col][row].astype(BF) for row in range(3) for col in range(3)], axis=1))
    lhs = jnp.concatenate(parts, axis=0)
    gates = jnp.dot(lhs, weights[...], preferred_element_type=F32) + bias[...]
    cell = jnp.concatenate(
        [lines[0, 1, :, chans:], lines[1, 1, :, chans:], strips[0, 1, :, chans:], strips[1, 1, :, chans:]], axis=0
    ).astype(F32)
    _, hidden = lstm(gates, cell)
    hidden = hidden.astype(BF).astype(F32)
    row, rows_of = lax.axis_index("gy"), lax.axis_size("gy")
    col, cols_of = lax.axis_index("gx"), lax.axis_size("gx")
    above, below = (row > 0).astype(F32), (row < rows_of - 1).astype(F32)
    before, after = (col > 0).astype(F32), (col < cols_of - 1).astype(F32)
    out[0] = hidden[:extent] * above
    out[1] = hidden[extent : 2 * extent] * below
    spot = lax.broadcasted_iota(jnp.int32, (length, hidden.shape[1]), 0)
    inside = jnp.where(spot == 1, above, jnp.where(spot == rows + 2, below, 1.0))
    out[2] = hidden[2 * extent : 2 * extent + length] * (inside * before)
    out[3] = hidden[2 * extent + length :] * (inside * after)


def block_kernel(x, w_qkv, w_out, w_up, w_down, out, flat, back):
    width = x.shape[-1]
    group = GRID * GRID
    flat[...] = x[...].astype(F32).reshape(flat.shape)
    groups = flat.shape[0] // group
    cells = jnp.concatenate([flat[pl.ds(g, group, stride=groups), :] for g in range(groups)], axis=0)
    normed = layer_norm(cells).astype(BF)
    qkv = jnp.dot(normed, w_qkv[...], preferred_element_type=F32).astype(BF)
    embed = w_qkv.shape[1] // 3
    keys = HEADS * group
    own = (
        lax.broadcasted_iota(jnp.int32, (keys, embed), 0) // group
        == lax.broadcasted_iota(jnp.int32, (keys, embed), 1) // HDIM
    )
    ones = (
        lax.broadcasted_iota(jnp.int32, (keys, keys), 0) // group
        == lax.broadcasted_iota(jnp.int32, (keys, keys), 1) // group
    ).astype(F32).astype(BF)
    own = own.astype(F32).astype(BF)
    raised = []
    for g in range(groups):
        part = qkv[g * group : (g + 1) * group]
        spread = jnp.concatenate([part[:, embed : 2 * embed]] * HEADS, axis=0) * own
        scores = lax.dot_general(
            part[:, :embed], spread, (((1,), (1,)), ((), ())), preferred_element_type=F32
        )
        raised.append(jnp.minimum(jnp.exp(scores * HDIM**-0.5), BF_MAX).astype(BF))
    raised = jnp.concatenate(raised, axis=0)
    total = jnp.dot(raised, ones, preferred_element_type=F32)
    attn = (raised.astype(F32) / total).astype(BF)
    heads = []
    for g in range(groups):
        part = qkv[g * group : (g + 1) * group]
        spread = jnp.concatenate([part[:, 2 * embed :]] * HEADS, axis=0) * own
        heads.append(
            jnp.dot(attn[g * group : (g + 1) * group], spread, preferred_element_type=F32).astype(BF)
        )
    heads = jnp.concatenate(heads, axis=0)
    attended = jnp.dot(heads, w_out[...], preferred_element_type=F32).astype(BF)
    mixed = cells + attended.astype(F32)
    normed_two = layer_norm(mixed).astype(BF)
    up = jnp.dot(normed_two, w_up[...], preferred_element_type=F32)
    expanded = (0.5 * up * (1.0 + jnp.tanh(0.7978845608 * (up + 0.044715 * (up * up * up))))).astype(BF)
    result = mixed + jnp.dot(expanded, w_down[...], preferred_element_type=F32)
    for g in range(groups):
        back[pl.ds(g, group, stride=groups), :] = result[g * group : (g + 1) * group]
    out[...] = back[...].reshape(x.shape).astype(BF)


def block_step(moved, devices_y, devices_x, w_qkv, w_out, w_up, w_down):
    _, piece_y, piece_cols, width = moved.shape
    lanes = devices_y // GRID
    view = moved.reshape(GRID, lanes, devices_x, piece_y, piece_cols, width)
    tokens = GRID * devices_x * piece_cols
    spec = pl.BlockSpec(
        (GRID, None, devices_x, None, piece_cols, width), lambda i, j: (0, i, 0, j, 0, 0)
    )

    def whole(array):
        return pl.BlockSpec(array.shape, lambda i, j: (0,) * array.ndim)

    total = lanes * piece_y * tokens
    out = pl.pallas_call(
        block_kernel,
        grid=(lanes, piece_y),
        in_specs=[spec, whole(w_qkv), whole(w_out), whole(w_up), whole(w_down)],
        out_specs=spec,
        out_shape=jax.ShapeDtypeStruct(view.shape, BF),
        scratch_shapes=[pltpu.VMEM((tokens, width), F32), pltpu.VMEM((tokens, width), F32)],
        compiler_params=pltpu.CompilerParams(vmem_limit_bytes=VMEM_LIMIT),
        cost_estimate=pl.CostEstimate(
            flops=total * 3_000_000, bytes_accessed=total * width * 4 + 800_000, transcendentals=total * 1100
        ),
    )(view, w_qkv, w_out, w_up, w_down)
    return out.reshape(moved.shape)


def unpack_kernel(local_m, piece_x, *refs):
    src, out = refs[0], refs[-1]
    owners_y, owners_x, piece_y, _, width = src.shape
    for owner_y in range(owners_y):
        for row in range(piece_y):
            wide = src[owner_y, :, row].astype(F32)
            out[owner_y * piece_y + row] = jnp.concatenate(
                [wide[owner, m * piece_x : (m + 1) * piece_x] for m in range(local_m) for owner in range(owners_x)],
                axis=0,
            ).astype(BF)


def unpack_step(landed, carry, chunk, rows, cols, local_m, piece_x):
    owners_y, owners_x, piece_y, _, width = landed.shape
    depth = owners_y * piece_y
    specs = [pl.BlockSpec(landed.shape, lambda i: (0,) * landed.ndim)]
    operands = [landed]
    aliases = {}
    if carry is not None:
        specs.append(pl.BlockSpec(memory_space=pl.ANY))
        operands.append(carry)
        aliases = {1: 0}
    return pl.pallas_call(
        functools.partial(unpack_kernel, local_m, piece_x),
        grid=(1,),
        in_specs=specs,
        out_specs=pl.BlockSpec((depth, cols, width), lambda i: (chunk, 0, 0)),
        out_shape=jax.ShapeDtypeStruct((rows, cols, width), BF),
        input_output_aliases=aliases,
        compiler_params=pltpu.CompilerParams(vmem_limit_bytes=VMEM_LIMIT),
        cost_estimate=pl.CostEstimate(flops=0, bytes_accessed=depth * cols * width * 4, transcendentals=0),
    )(*operands)


def body(frames, hidden_state, cell_state, w_gates, gate_bias, w_qkv, w_out, w_up, w_down):
    rows, cols, width = hidden_state.shape
    latent = frames.shape[2] // 2
    chans = latent + width
    devices_y, devices_x = lax.axis_size("gy"), lax.axis_size("gx")
    local_m = GRID // devices_x
    piece_x = cols // local_m // devices_x
    weights = w_gates.reshape(-1, w_gates.shape[3])
    bias = gate_bias.reshape(1, -1)

    def pack(row, col):
        return jnp.concatenate(
            [
                frames[row, col, :latent],
                hidden_state[row, col],
                cell_state[row, col].astype(BF),
                frames[row, col, latent:],
            ],
            axis=-1,
        )

    def shifted(value, axis, step):
        count = lax.axis_size(axis)
        pairs = [(i, i + step) for i in range(count) if 0 <= i + step < count]
        return lax.ppermute(value, axis, pairs)

    every = slice(None)
    from_left = shifted(pack(every, slice(cols - 2, cols)), "gx", 1)
    from_right = shifted(pack(every, slice(0, 2)), "gx", -1)
    line_top = pack(slice(0, 2), every)
    line_bot = pack(slice(rows - 2, rows), every)
    from_up = shifted(jnp.concatenate([line_bot, from_left[-2:], from_right[-2:]], axis=1), "gy", 1)
    from_down = shifted(jnp.concatenate([line_top, from_left[:2], from_right[:2]], axis=1), "gy", -1)

    def column(at, middle):
        return jnp.concatenate([from_up[:, at], middle, from_down[:, at]], axis=0)

    columns = [
        column(cols, from_left[:, 0]),
        column(cols + 1, from_left[:, 1]),
        column(0, pack(every, 0)),
        column(cols - 1, pack(every, cols - 1)),
        column(cols + 2, from_right[:, 0]),
        column(cols + 3, from_right[:, 1]),
    ]
    held = chans + width
    length = -(-(rows + 4) // 16) * 16
    strips = jnp.stack(columns)[:, :, :held].reshape(2, 3, rows + 4, held)
    strips = jnp.pad(strips, ((0, 0), (0, 0), (0, length - rows - 4), (0, 0)))
    low = columns[1].astype(F32)[:, None]
    high = columns[4].astype(F32)[:, None]
    lines = jnp.stack(
        [
            jnp.concatenate([from_up[:, :cols, :held], line_top[:1, :, :held]], axis=0),
            jnp.concatenate([line_bot[1:, :, :held], from_down[:, :cols, :held]], axis=0),
        ]
    )
    cell_one_shape = jax.ShapeDtypeStruct((rows, cols, width), F32)
    row_spec = pl.BlockSpec((STEP, cols, width), lambda i: (i, 0, 0))
    hidden_one, cell_one = conv_step(
        frames, 0, hidden_state, cell_state,
        (from_up[1:, :cols, :latent], from_up[1:, :cols, latent:chans]),
        (from_down[:1, :cols, :latent], from_down[:1, :cols, latent:chans]),
        low[1:-1, :, :chans], high[1:-1, :, :chans], weights, bias, (0, rows // STEP),
        (jax.ShapeDtypeStruct((rows, cols, width), BF), cell_one_shape), (row_spec, row_spec), None, None,
    )
    halo = pl.pallas_call(
        halo_kernel,
        out_shape=jax.ShapeDtypeStruct((4, length, width), F32),
        compiler_params=pltpu.CompilerParams(vmem_limit_bytes=VMEM_LIMIT),
        cost_estimate=pl.CostEstimate(flops=2 * 4 * length * weights.size, bytes_accessed=2 * weights.size, transcendentals=0),
    )(lines, strips, low[:, :, :chans], high[:, :, :chans], weights, bias)
    second_low = jnp.concatenate([low[1:-1, :, held:], halo[2, 1 : rows + 3][:, None]], axis=2)
    second_high = jnp.concatenate([high[1:-1, :, held:], halo[3, 1 : rows + 3][:, None]], axis=2)
    tops = (from_up[1:, :cols, held:], halo[0:1].astype(BF))
    bots = (from_down[:1, :cols, held:], halo[1:2].astype(BF))

    depth = 2 * devices_y if devices_y == GRID else devices_y
    chunks = rows // depth
    piece_y = depth // devices_y
    piece_cols = local_m * piece_x
    per_chunk = depth // STEP
    cell_out, moved = None, []
    for chunk in range(chunks):
        first = chunk * per_chunk
        sent, cell_out = conv_step(
            frames, 1, hidden_one, cell_one, tops, bots, second_low, second_high, weights, bias, (first, per_chunk),
            (jax.ShapeDtypeStruct((devices_y, devices_x, piece_y, piece_cols, width), BF), cell_one_shape),
            (
                pl.BlockSpec((STEP // piece_y, devices_x, piece_y, piece_cols, width), lambda i: (i, 0, 0, 0, 0)),
                pl.BlockSpec((STEP, cols, width), lambda i, first=first: (first + i, 0, 0)),
            ),
            (local_m, piece_x), cell_out,
        )
        sent = sent.reshape(devices_y * devices_x, piece_y, piece_cols, width)
        moved.append(lax.all_to_all(sent, ("gy", "gx"), split_axis=0, concat_axis=0, tiled=True))
    landed = []
    for chunk in range(chunks):
        done = block_step(moved[chunk], devices_y, devices_x, w_qkv, w_out, w_up, w_down)
        landed.append(lax.all_to_all(done, ("gy", "gx"), split_axis=0, concat_axis=0, tiled=True))
    result = None
    for chunk in range(chunks):
        view = landed[chunk].reshape(devices_y, devices_x, piece_y, piece_cols, width)
        result = unpack_step(view, result, chunk, rows, cols, local_m, piece_x)
    return result, cell_out


def solution(mesh):
    tiled = P("gy", "gx", None)
    in_specs = (tiled, tiled, tiled, P(), P(), P(), P(), P(), P())
    return jax.shard_map(body, mesh=mesh, in_specs=in_specs, out_specs=(tiled, tiled), check_vma=False)
```

profile of v0, /device:TPU:1, one launch (start us, length us, event | category | flops | bytes accessed | tf_op | source)
XLA Modules:
  0.0 142.4 jit_solution(3102291697460502114)
XLA Ops:
  0.7 1.5 %fusion.12 = (bf16[48,2,256]{2,1,0:T(2,128)(2,1)S(1)}, bf16[48,2,256]{2,1,0:T(2,128)(2,1)S(1)}, bf16[48,2,256]{2,1,0:T(2,128)(2,1)S(1)}, bf16[48,2,256]{2,1,0:T(2,128)(2,1)S(1)}) fusion(bf16[48,64,512]{2,1,0:T(8,128)(2,1)} %frame_next.7), kind=kLoop, calls=%fused_computation.59 | loop fusion | bytes 393216 | tf_op jit(solution)/shard_map/slice | solution.py:329
  2.2 1.5 %convert.12 = bf16[48,64,128]{2,1,0:T(8,128)(2,1)S(1)} convert(f32[48,64,128]{2,1,0:T(8,128)} %cell.1) | non-fusion elementwise | flops 393216 | bytes 2359296 | tf_op jit(solution)/shard_map/convert.7
  6.4 4.7 %collective-permute-start = (bf16[48,2,768]{2,1,0:T(2,128)(2,1)S(1)}, bf16[48,2,768]{2,1,0:T(2,128)(2,1)S(1)}, u32[]{:S(2)}, u32[]{:S(2)}) collective-permute-start(bf16[48,2,768]{2,1,0:T(2,128)(2,1)S(1)} %pad_maximum_fusion.7), channel_id=1, source_target_pairs={{0,1},{1,2},{2,3},{4,5},{5,6},{6,7},{8,9},{9,10},{10,11},{12,13},{... | collective-permute-start | bytes 442376 | tf_op jit(solution)/shard_map/ppermute | solution.py:340
  13.6 4.7 %collective-permute-start.2 = (bf16[2,68,768]{2,1,0:T(8,128)(2,1)S(1)}, bf16[2,68,768]{2,1,0:T(8,128)(2,1)S(1)}, u32[]{:S(2)}, u32[]{:S(2)}) collective-permute-start(bf16[2,68,768]{2,1,0:T(8,128)(2,1)S(1)} %pad_maximum_fusion.1), channel_id=1, source_target_pairs={{0,4},{4,8},{8,12},{12,16},{16,20},{20,24},{24,28},{1,5},{5,9},{9,... | collective-permute-start | bytes 626696 | tf_op jit(solution)/shard_map/ppermute | solution.py:340
  18.9 1.9 %collective-permute-start.3 = (bf16[2,68,768]{2,1,0:T(8,128)(2,1)S(1)}, bf16[2,68,768]{2,1,0:T(8,128)(2,1)S(1)}, u32[]{:S(2)}, u32[]{:S(2)}) collective-permute-start(bf16[2,68,768]{2,1,0:T(8,128)(2,1)S(1)} %pad_maximum_fusion.2), channel_id=1, source_target_pairs={{4,0},{8,4},{12,8},{16,12},{20,16},{24,20},{28,24},{5,1},{9,5},{13... | collective-permute-start | bytes 626696 | tf_op jit(solution)/shard_map/ppermute | solution.py:340
  21.2 4.9 %collective-permute-done.3 = bf16[2,68,768]{2,1,0:T(8,128)(2,1)S(1)} collective-permute-done((bf16[2,68,768]{2,1,0:T(8,128)(2,1)S(1)}, bf16[2,68,768]{2,1,0:T(8,128)(2,1)S(1)}, u32[]{:S(2)}, u32[]{:S(2)}) %collective-permute-start.3) | collective-permute-done | bytes 208928 | tf_op jit(solution)/shard_map/ppermute | solution.py:340
  29.7 13.9 %shard_map.104 = (bf16[48,64,128]{2,1,0:T(8,128)(2,1)S(1)}, f32[48,64,128]{2,1,0:T(8,128)S(1)}) custom-call(bf16[48,64,512]{2,1,0:T(8,128)(2,1)S(1)} %copy-done, bf16[48,64,512]{2,1,0:T(8,128)(2,1)S(1)} %copy-done, bf16[48,64,512]{2,1,0:T(8,128)(2,1)S(1)} %copy-done, bf16[1,64,256]{2,1,0:T(8,128)(2,1)S(1)} %get-tuple-element.56.frame_top, ...), custom_call_target="tpu_custom_call" | custom-call | flops 10871635968 | bytes 9830400 | tf_op jit(solution)/shard_map/pallas_call | solution.py:155
  43.6 5.4 %shard_map.106 = (bf16[8,4,2,16,128]{4,3,2,1,0:T(8,128)(2,1)S(1)}, f32[48,64,128]{2,1,0:T(8,128)}) custom-call(bf16[48,64,512]{2,1,0:T(8,128)(2,1)S(1)} %copy-done, bf16[48,64,512]{2,1,0:T(8,128)(2,1)S(1)} %copy-done, bf16[48,64,512]{2,1,0:T(8,128)(2,1)S(1)} %copy-done, bf16[1,64,256]{2,1,0:T(8,128)(2,1)S(1)} %get-tuple-element.57.frame_top, ...), custom_call_target="tpu_custom_call" | custom-call | flops 3623878656 | bytes 5636096 | tf_op jit(solution)/shard_map/pallas_call | solution.py:155
  49.7 6.6 %all-to-all-start.4 = ((bf16[32,2,16,128]{3,2,1,0:T(8,128)(2,1)}), bf16[32,2,16,128]{3,2,1,0:T(8,128)(2,1)}, u32[]{:S(2)}, u32[]{:S(2)}) async-start(bf16[32,2,16,128]{3,2,1,0:T(8,128)(2,1)} %bitcast.124), calls=%async_computation.4 | async-start | bytes 524288 | tf_op jit(solution)/shard_map/all_to_all | solution.py:411
  57.5 2.0 %copy-done.5 = bf16[3,3,384,512]{3,2,1,0:T(8,128)(2,1)S(1)} copy-done((bf16[3,3,384,512]{3,2,1,0:T(8,128)(2,1)S(1)}, bf16[3,3,384,512]{3,2,1,0:T(8,128)(2,1)}, u32[]{:S(2)}) %copy-start.5) | copy-done | bytes 3538968
  60.9 5.3 %shard_map.107 = (bf16[8,4,2,16,128]{4,3,2,1,0:T(8,128)(2,1)S(1)}, f32[48,64,128]{2,1,0:T(8,128)}) custom-call(bf16[48,64,512]{2,1,0:T(8,128)(2,1)S(1)} %copy-done, bf16[48,64,512]{2,1,0:T(8,128)(2,1)S(1)} %copy-done, bf16[48,64,512]{2,1,0:T(8,128)(2,1)S(1)} %copy-done, ...), custom_call_target="tpu_custom_call", output_to_operand_aliasing={{1}: (15, {})} | custom-call | flops 3623878656 | bytes 5636096 | tf_op jit(solution)/shard_map/pallas_call | solution.py:155
  66.9 5.9 %all-to-all-start.2 = ((bf16[32,2,16,128]{3,2,1,0:T(8,128)(2,1)}), bf16[32,2,16,128]{3,2,1,0:T(8,128)(2,1)}, u32[]{:S(2)}, u32[]{:S(2)}) async-start(bf16[32,2,16,128]{3,2,1,0:T(8,128)(2,1)} %bitcast.122), calls=%async_computation.2 | async-start | bytes 524288 | tf_op jit(solution)/shard_map/all_to_all | solution.py:411
  74.0 2.0 %copy-done.6 = bf16[3,3,384,512]{3,2,1,0:T(8,128)(2,1)S(1)} copy-done((bf16[3,3,384,512]{3,2,1,0:T(8,128)(2,1)S(1)}, bf16[3,3,384,512]{3,2,1,0:T(8,128)(2,1)}, u32[]{:S(2)}) %copy-start.6) | copy-done | bytes 3538968
  77.4 5.3 %shard_map.108 = (bf16[8,4,2,16,128]{4,3,2,1,0:T(8,128)(2,1)S(1)}, f32[48,64,128]{2,1,0:T(8,128)}) custom-call(bf16[48,64,512]{2,1,0:T(8,128)(2,1)S(1)} %copy-done, bf16[48,64,512]{2,1,0:T(8,128)(2,1)S(1)} %copy-done, bf16[48,64,512]{2,1,0:T(8,128)(2,1)S(1)} %copy-done, ...), custom_call_target="tpu_custom_call", output_to_operand_aliasing={{1}: (15, {})} | custom-call | flops 3623878656 | bytes 5636096 | tf_op jit(solution)/shard_map/pallas_call | solution.py:155
  83.4 5.8 %all-to-all-start = ((bf16[32,2,16,128]{3,2,1,0:T(8,128)(2,1)}), bf16[32,2,16,128]{3,2,1,0:T(8,128)(2,1)S(1)}, u32[]{:S(2)}, u32[]{:S(2)}) async-start(bf16[32,2,16,128]{3,2,1,0:T(8,128)(2,1)} %bitcast.123), calls=%async_computation | async-start | bytes 524288 | tf_op jit(solution)/shard_map/all_to_all | solution.py:411
  92.0 7.3 %shard_map.111 = bf16[8,1,4,2,16,128]{5,4,3,2,1,0:T(8,128)(2,1)} custom-call(bf16[8,1,4,2,16,128]{5,4,3,2,1,0:T(8,128)(2,1)} %bitcast.28.x, bf16[128,768]{1,0:T(8,128)(2,1)S(1)} %copy-done.16, bf16[256,128]{1,0:T(8,128)(2,1)S(1)} %copy-done.21, bf16[128,512]{1,0:T(8,128)(2,1)S(1)} %copy-done.18, bf16[512,128]{1,0:T(8,128)(2,1)S(1)} %copy-done.19), custom_call_target="tpu_custom_call" | custom-call | flops 3072000000 | bytes 1324288 | tf_op jit(solution)/shard_map/pallas_call | solution.py:267
  99.6 5.5 %all-to-all-start.5 = ((bf16[32,2,16,128]{3,2,1,0:T(8,128)(2,1)}), bf16[32,2,16,128]{3,2,1,0:T(8,128)(2,1)S(1)}, u32[]{:S(2)}, u32[]{:S(2)}) async-start(bf16[32,2,16,128]{3,2,1,0:T(8,128)(2,1)} %bitcast.29), calls=%async_computation.5 | async-start | bytes 524288 | tf_op jit(solution)/shard_map/all_to_all | solution.py:415
  105.2 7.3 %shard_map.110 = bf16[8,1,4,2,16,128]{5,4,3,2,1,0:T(8,128)(2,1)} custom-call(bf16[8,1,4,2,16,128]{5,4,3,2,1,0:T(8,128)(2,1)} %bitcast.24.x, bf16[128,768]{1,0:T(8,128)(2,1)S(1)} %copy-done.17, bf16[256,128]{1,0:T(8,128)(2,1)S(1)} %copy-done.21, bf16[128,512]{1,0:T(8,128)(2,1)S(1)} %copy-done.18, bf16[512,128]{1,0:T(8,128)(2,1)S(1)} %copy-done.20), custom_call_target="tpu_custom_call" | custom-call | flops 3072000000 | bytes 1324288 | tf_op jit(solution)/shard_map/pallas_call | solution.py:267
  112.5 3.0 %all-to-all-done.5 = bf16[32,2,16,128]{3,2,1,0:T(8,128)(2,1)S(1)} async-done(((bf16[32,2,16,128]{3,2,1,0:T(8,128)(2,1)}), bf16[32,2,16,128]{3,2,1,0:T(8,128)(2,1)S(1)}, u32[]{:S(2)}, u32[]{:S(2)}) %all-to-all-start.5) | async-done | bytes 262176 | tf_op jit(solution)/shard_map/all_to_all | solution.py:415
  115.5 2.8 %all-to-all-start.3 = ((bf16[32,2,16,128]{3,2,1,0:T(8,128)(2,1)}), bf16[32,2,16,128]{3,2,1,0:T(8,128)(2,1)S(1)}, u32[]{:S(2)}, u32[]{:S(2)}) async-start(bf16[32,2,16,128]{3,2,1,0:T(8,128)(2,1)} %bitcast.25), calls=%async_computation.3 | async-start | bytes 524288 | tf_op jit(solution)/shard_map/all_to_all | solution.py:415
  118.4 6.4 %shard_map.109 = bf16[8,1,4,2,16,128]{5,4,3,2,1,0:T(8,128)(2,1)} custom-call(bf16[8,1,4,2,16,128]{5,4,3,2,1,0:T(8,128)(2,1)S(1)} %bitcast.121, bf16[128,768]{1,0:T(8,128)(2,1)S(1)} %copy-done.17, bf16[256,128]{1,0:T(8,128)(2,1)S(1)} %copy-done.22, bf16[128,512]{1,0:T(8,128)(2,1)S(1)} %copy-done.18, bf16[512,128]{1,0:T(8,128)(2,1)S(1)} %copy-done.20), custom_call_target="tpu_custom_call" | custom-call | flops 3072000000 | bytes 1324288 | tf_op jit(solution)/shard_map/pallas_call | solution.py:267
  124.8 3.9 %all-to-all-done.3 = bf16[32,2,16,128]{3,2,1,0:T(8,128)(2,1)S(1)} async-done(((bf16[32,2,16,128]{3,2,1,0:T(8,128)(2,1)}), bf16[32,2,16,128]{3,2,1,0:T(8,128)(2,1)S(1)}, u32[]{:S(2)}, u32[]{:S(2)}) %all-to-all-start.3) | async-done | bytes 262176 | tf_op jit(solution)/shard_map/all_to_all | solution.py:415
  128.7 2.6 %all-to-all-start.1 = ((bf16[32,2,16,128]{3,2,1,0:T(8,128)(2,1)}), bf16[32,2,16,128]{3,2,1,0:T(8,128)(2,1)S(1)}, u32[]{:S(2)}, u32[]{:S(2)}) async-start(bf16[32,2,16,128]{3,2,1,0:T(8,128)(2,1)} %bitcast.21), calls=%async_computation.1 | async-start | bytes 524288 | tf_op jit(solution)/shard_map/all_to_all | solution.py:415
  132.8 8.8 %all-to-all-done.1 = bf16[32,2,16,128]{3,2,1,0:T(8,128)(2,1)S(1)} async-done(((bf16[32,2,16,128]{3,2,1,0:T(8,128)(2,1)}), bf16[32,2,16,128]{3,2,1,0:T(8,128)(2,1)S(1)}, u32[]{:S(2)}, u32[]{:S(2)}) %all-to-all-start.1) | async-done | bytes 262176 | tf_op jit(solution)/shard_map/all_to_all | solution.py:415
  (123 shorter events, 21.7 us)
Async XLA Ops:
  0.6 11.4 %copy-start = (bf16[48,64,512]{2,1,0:T(8,128)(2,1)S(1)}, bf16[48,64,512]{2,1,0:T(8,128)(2,1)}, u32[]{:S(2)}) copy-start(bf16[48,64,512]{2,1,0:T(8,128)(2,1)} %frame_next.7) | copy-start | bytes 9437188
  0.6 11.7 %copy-start.14 = (bf16[48,64,128]{2,1,0:T(8,128)(2,1)S(1)}, bf16[48,64,128]{2,1,0:T(8,128)(2,1)}, u32[]{:S(2)}) copy-start(bf16[48,64,128]{2,1,0:T(8,128)(2,1)} %hid_next.1) | copy-start | bytes 2359300
  4.9 7.6 %collective-permute-start.1 = (bf16[48,2,768]{2,1,0:T(2,128)(2,1)S(1)}, bf16[48,2,768]{2,1,0:T(2,128)(2,1)S(1)}, u32[]{:S(2)}, u32[]{:S(2)}) collective-permute-start(bf16[48,2,768]{2,1,0:T(2,128)(2,1)S(1)} %pad_maximum_fusion.8), channel_id=1, source_target_pairs={{1,0},{2,1},{3,2},{5,4},{6,5},{7,6},{9,8},{10,9},{11,10},{13,12},{... | collective-permute-start | bytes 442376 | tf_op jit(solution)/shard_map/ppermute | solution.py:340
  6.4 7.2 %collective-permute-start = (bf16[48,2,768]{2,1,0:T(2,128)(2,1)S(1)}, bf16[48,2,768]{2,1,0:T(2,128)(2,1)S(1)}, u32[]{:S(2)}, u32[]{:S(2)}) collective-permute-start(bf16[48,2,768]{2,1,0:T(2,128)(2,1)S(1)} %pad_maximum_fusion.7), channel_id=1, source_target_pairs={{0,1},{1,2},{2,3},{4,5},{5,6},{6,7},{8,9},{9,10},{10,11},{12,13},{... | collective-permute-start | bytes 442376 | tf_op jit(solution)/shard_map/ppermute | solution.py:340
  13.6 7.6 %collective-permute-start.2 = (bf16[2,68,768]{2,1,0:T(8,128)(2,1)S(1)}, bf16[2,68,768]{2,1,0:T(8,128)(2,1)S(1)}, u32[]{:S(2)}, u32[]{:S(2)}) collective-permute-start(bf16[2,68,768]{2,1,0:T(8,128)(2,1)S(1)} %pad_maximum_fusion.1), channel_id=1, source_target_pairs={{0,4},{4,8},{8,12},{12,16},{16,20},{20,24},{24,28},{1,5},{5,9},{9,... | collective-permute-start | bytes 626696 | tf_op jit(solution)/shard_map/ppermute | solution.py:340
  18.9 7.3 %collective-permute-start.3 = (bf16[2,68,768]{2,1,0:T(8,128)(2,1)S(1)}, bf16[2,68,768]{2,1,0:T(8,128)(2,1)S(1)}, u32[]{:S(2)}, u32[]{:S(2)}) collective-permute-start(bf16[2,68,768]{2,1,0:T(8,128)(2,1)S(1)} %pad_maximum_fusion.2), channel_id=1, source_target_pairs={{4,0},{8,4},{12,8},{16,12},{20,16},{24,20},{28,24},{5,1},{9,5},{13... | collective-permute-start | bytes 626696 | tf_op jit(solution)/shard_map/ppermute | solution.py:340
  26.2 2.0 %copy-start.4 = (bf16[3,3,384,512]{3,2,1,0:T(8,128)(2,1)S(1)}, bf16[3,3,384,512]{3,2,1,0:T(8,128)(2,1)}, u32[]{:S(2)}) copy-start(bf16[3,3,384,512]{3,2,1,0:T(8,128)(2,1)} %param.12) | copy-start | bytes 10616836
  26.2 2.0 %copy-start.15 = (f32[512]{0:T(512)S(1)}, f32[512]{0:T(512)}, u32[]{:S(2)}) copy-start(f32[512]{0:T(512)} %param.13) | copy-start | bytes 6148
  27.5 2.2 %copy-start.10 = (f32[48,64,128]{2,1,0:T(8,128)S(1)}, f32[48,64,128]{2,1,0:T(8,128)}, u32[]{:S(2)}) copy-start(f32[48,64,128]{2,1,0:T(8,128)} %cell.1) | copy-start | bytes 4718596
  43.6 5.4 %copy-start.1 = (bf16[48,64,128]{2,1,0:T(8,128)(2,1)}, bf16[48,64,128]{2,1,0:T(8,128)(2,1)S(1)}, u32[]{:S(2)}) copy-start(bf16[48,64,128]{2,1,0:T(8,128)(2,1)S(1)} %get-tuple-element.10.hid.hid_prev.hid_next) | copy-start | bytes 2359300
  43.6 5.4 %copy-start.7 = (f32[48,64,128]{2,1,0:T(8,128)}, f32[48,64,128]{2,1,0:T(8,128)S(1)}, u32[]{:S(2)}) copy-start(f32[48,64,128]{2,1,0:T(8,128)S(1)} %get-tuple-element.11.cell) | copy-start | bytes 4718596
  49.7 17.2 %all-to-all-start.4 = ((bf16[32,2,16,128]{3,2,1,0:T(8,128)(2,1)}), bf16[32,2,16,128]{3,2,1,0:T(8,128)(2,1)}, u32[]{:S(2)}, u32[]{:S(2)}) async-start(bf16[32,2,16,128]{3,2,1,0:T(8,128)(2,1)} %bitcast.124), calls=%async_computation.4 | async-start | bytes 524288 | tf_op jit(solution)/shard_map/all_to_all | solution.py:411
  57.5 2.0 %copy-start.5 = (bf16[3,3,384,512]{3,2,1,0:T(8,128)(2,1)S(1)}, bf16[3,3,384,512]{3,2,1,0:T(8,128)(2,1)}, u32[]{:S(2)}) copy-start(bf16[3,3,384,512]{3,2,1,0:T(8,128)(2,1)} %param.12) | copy-start | bytes 10616836
  59.5 1.4 copy-start.8
  66.9 16.5 %all-to-all-start.2 = ((bf16[32,2,16,128]{3,2,1,0:T(8,128)(2,1)}), bf16[32,2,16,128]{3,2,1,0:T(8,128)(2,1)}, u32[]{:S(2)}, u32[]{:S(2)}) async-start(bf16[32,2,16,128]{3,2,1,0:T(8,128)(2,1)} %bitcast.122), calls=%async_computation.2 | async-start | bytes 524288 | tf_op jit(solution)/shard_map/all_to_all | solution.py:411
  74.0 2.0 %copy-start.6 = (bf16[3,3,384,512]{3,2,1,0:T(8,128)(2,1)S(1)}, bf16[3,3,384,512]{3,2,1,0:T(8,128)(2,1)}, u32[]{:S(2)}) copy-start(bf16[3,3,384,512]{3,2,1,0:T(8,128)(2,1)} %param.12) | copy-start | bytes 10616836
  77.4 11.9 %copy-start.18 = (bf16[128,512]{1,0:T(8,128)(2,1)S(1)}, bf16[128,512]{1,0:T(8,128)(2,1)}, u32[]{:S(2)}) copy-start(bf16[128,512]{1,0:T(8,128)(2,1)} %w_up.5) | copy-start | bytes 393220
  83.4 16.2 %all-to-all-start = ((bf16[32,2,16,128]{3,2,1,0:T(8,128)(2,1)}), bf16[32,2,16,128]{3,2,1,0:T(8,128)(2,1)S(1)}, u32[]{:S(2)}, u32[]{:S(2)}) async-start(bf16[32,2,16,128]{3,2,1,0:T(8,128)(2,1)} %bitcast.123), calls=%async_computation | async-start | bytes 524288 | tf_op jit(solution)/shard_map/all_to_all | solution.py:411
  92.0 13.2 %copy-start.17 = (bf16[128,768]{1,0:T(8,128)(2,1)S(1)}, bf16[128,768]{1,0:T(8,128)(2,1)}, u32[]{:S(2)}) copy-start(bf16[128,768]{1,0:T(8,128)(2,1)} %w_qkv.5) | copy-start | bytes 589828
  92.0 13.2 %copy-start.20 = (bf16[512,128]{1,0:T(8,128)(2,1)S(1)}, bf16[512,128]{1,0:T(8,128)(2,1)}, u32[]{:S(2)}) copy-start(bf16[512,128]{1,0:T(8,128)(2,1)} %w_down.5) | copy-start | bytes 393220
  99.6 15.9 %all-to-all-start.5 = ((bf16[32,2,16,128]{3,2,1,0:T(8,128)(2,1)}), bf16[32,2,16,128]{3,2,1,0:T(8,128)(2,1)S(1)}, u32[]{:S(2)}, u32[]{:S(2)}) async-start(bf16[32,2,16,128]{3,2,1,0:T(8,128)(2,1)} %bitcast.29), calls=%async_computation.5 | async-start | bytes 524288 | tf_op jit(solution)/shard_map/all_to_all | solution.py:415
  105.2 13.2 %copy-start.22 = (bf16[256,128]{1,0:T(8,128)(2,1)S(1)}, bf16[256,128]{1,0:T(8,128)(2,1)}, u32[]{:S(2)}) copy-start(bf16[256,128]{1,0:T(8,128)(2,1)} %w_out.5) | copy-start | bytes 196612
  115.5 13.2 %all-to-all-start.3 = ((bf16[32,2,16,128]{3,2,1,0:T(8,128)(2,1)}), bf16[32,2,16,128]{3,2,1,0:T(8,128)(2,1)S(1)}, u32[]{:S(2)}, u32[]{:S(2)}) async-start(bf16[32,2,16,128]{3,2,1,0:T(8,128)(2,1)} %bitcast.25), calls=%async_computation.3 | async-start | bytes 524288 | tf_op jit(solution)/shard_map/all_to_all | solution.py:415
  128.7 12.9 %all-to-all-start.1 = ((bf16[32,2,16,128]{3,2,1,0:T(8,128)(2,1)}), bf16[32,2,16,128]{3,2,1,0:T(8,128)(2,1)S(1)}, u32[]{:S(2)}, u32[]{:S(2)}) async-start(bf16[32,2,16,128]{3,2,1,0:T(8,128)(2,1)} %bitcast.21), calls=%async_computation.1 | async-start | bytes 524288 | tf_op jit(solution)/shard_map/all_to_all | solution.py:415
  (9 other events, 8.5 us)
where the time goes:
time: 143 us; the launch traced here: 142 us
  Pallas kernels  54.4 us (38%)
  starting transfers between devices  41.9 us (29%)
  waiting for transfers between devices  22.5 us (16%)
  local copies, waits for them, and re-layouts  19.3 us (13%)
  other arithmetic  2.92 us (2%)
    pallas_call x4, Pallas kernels, conv_step(): pl.pallas_call(functools.partial(conv_kernel, first, last, packed=packed)...  29.9 us
    pallas_call x3, Pallas kernels, block_step(): pl.pallas_call(block_kernel, grid=(lanes, piece_y), in_specs=[spec, whole...  21.1 us
    all_to_all x3, starting transfers between devices, body(): lax.all_to_all(sent, ('gy', 'gx'), split_axis=0, concat_axis=0, tiled=True)  18.4 us
    all_to_all x3, waiting for transfers between devices, body(): lax.all_to_all(done, ('gy', 'gx'), split_axis=0, concat_axis=0, tiled=True)  15.7 us
    unnamed x64, local copies, waits for them, and re-layouts  14.7 us
    ppermute x4, starting transfers between devices, shifted(): return lax.ppermute(value, axis, pairs)  12.6 us
    all_to_all x3, starting transfers between devices, body(): lax.all_to_all(done, ('gy', 'gx'), split_axis=0, concat_axis=0, tiled=True)  10.9 us
    ppermute x4, waiting for transfers between devices, shifted(): return lax.ppermute(value, axis, pairs)  6.41 us
  transfers between devices with their start and end apart: 10, of which 8 were waited for; matrix products, arithmetic and copies ran while one was open for 1% of the time, Pallas kernels for 23%

commit v1 on v0

v1 whole, which is shorter than its diff:
```python
import functools

import jax
import jax.numpy as jnp
from jax import lax
from jax.experimental import pallas as pl
from jax.experimental.pallas import tpu as pltpu
from jax.sharding import PartitionSpec as P

HEADS = 8
HDIM = 32
GRID = 8
STEP = 8
SUB = 4
BF = jnp.bfloat16
F32 = jnp.float32
BF_MAX = 3.3895313892515355e38
VMEM_LIMIT = 60 * 1024 * 1024


def sigmoid(x):
    return 0.5 * jnp.tanh(0.5 * x) + 0.5


def lstm(gates, cell_prev):
    width = cell_prev.shape[-1]
    in_gate = sigmoid(gates[:, 0:width])
    forget_gate = sigmoid(gates[:, width : 2 * width])
    candidate = jnp.tanh(gates[:, 2 * width : 3 * width])
    out_gate = sigmoid(gates[:, 3 * width :])
    cell = forget_gate * cell_prev + in_gate * candidate
    return cell, out_gate * jnp.tanh(cell)


def layer_norm(values):
    center = values - jnp.mean(values, axis=-1, keepdims=True)
    spread = jnp.mean(center * center, axis=-1, keepdims=True)
    return center * lax.rsqrt(spread + 1e-05)


def three_columns(wide, left, right):
    count = wide.shape[0]
    place = lax.broadcasted_iota(jnp.int32, wide.shape, 0)
    before = jnp.where(place == 0, left, pltpu.roll(wide, 1, axis=0))
    after = jnp.where(place == count - 1, right, pltpu.roll(wide, count - 1, axis=0))
    return before.astype(BF), wide.astype(BF), after.astype(BF)


def conv_kernel(first, count, last, refs, packed, *args):
    ref = dict(zip(refs, args))
    frame, hid, bias = ref["frame"], ref["hid"], ref["bias"]
    hid_out, cell_out = ref["hid_out"], ref["cell_out"]
    ring = "left" in ref
    step = pl.program_id(0)
    latent, width = frame.shape[2], hid.shape[2]
    chans = latent + width
    cols = hid.shape[1]
    load = pltpu.make_async_copy(ref["weights"], ref["held"], ref["sem"])

    def build(spread):
        block = first + step
        base = block * STEP
        top, bot = block == 0, block == last
        for pos in range(STEP + 2):
            if pos == 0:
                x, h = ref["frame_prev"][0].astype(F32), ref["hid_prev"][0].astype(F32)
            elif pos == STEP + 1:
                x, h = ref["frame_next"][0].astype(F32), ref["hid_next"][0].astype(F32)
            else:
                x, h = frame[pos - 1].astype(F32), hid[pos - 1].astype(F32)
            low = high = jnp.zeros((1, chans), F32)
            if ring:
                low, high = ref["left"][base + pos], ref["right"][base + pos]
                place = lax.broadcasted_iota(jnp.int32, h.shape, 0)
                h = jnp.where(place == 0, ref["first_col"][base + pos], h)
                h = jnp.where(place == cols - 1, ref["last_col"][base + pos], h)
                for spot, edge, line in ((0, top, 0), (1, top, 1), (STEP, bot, 2), (STEP + 1, bot, 3)):
                    if pos == spot:
                        h = jnp.where(edge, ref["lines"][line], h)
                if pos == 0:
                    x = jnp.where(top, ref["frame_top"][0].astype(F32), x)
                if pos == STEP + 1:
                    x = jnp.where(bot, ref["frame_bot"][0].astype(F32), x)
            elif pos == 0:
                x, h = jnp.where(top, 0.0, x), jnp.where(top, 0.0, h)
            elif pos == STEP + 1:
                x, h = jnp.where(bot, 0.0, x), jnp.where(bot, 0.0, h)
            for part, start in ((x, 0), (h, latent)):
                size = part.shape[1]
                pieces = three_columns(part, low[:, start : start + size], high[:, start : start + size])
                for tap in range(3):
                    spread[pos, :, tap * chans + start : tap * chans + start + size] = pieces[tap]

    def multiply(spread):
        block = first + step - 1
        base = block * STEP
        for at in range(0, STEP, SUB):
            lhs = jnp.concatenate(
                [spread[at + tap : at + tap + SUB].reshape(SUB * cols, 3 * chans) for tap in range(3)], axis=1
            )
            gates = jnp.dot(lhs, ref["held"][...], preferred_element_type=F32) + bias[...]
            cell_prev = ref["cell"][at : at + SUB]
            if ring:
                place = lax.broadcasted_iota(jnp.int32, cell_prev.shape, 1)
                cell_prev = jnp.where(place == 0, ref["first_cell"][pl.ds(base + at + 1, SUB)], cell_prev)
                cell_prev = jnp.where(place == cols - 1, ref["last_cell"][pl.ds(base + at + 1, SUB)], cell_prev)
                if at == 0:
                    edge = jnp.where(block == 0, ref["cell_lines"][1:2], cell_prev[:1])
                    cell_prev = jnp.concatenate([edge, cell_prev[1:]], axis=0)
                if at == STEP - SUB:
                    edge = jnp.where(block == last, ref["cell_lines"][2:3], cell_prev[-1:])
                    cell_prev = jnp.concatenate([cell_prev[:-1], edge], axis=0)
            new_cell, new_hidden = lstm(gates, cell_prev.reshape(SUB * cols, width))
            cell_out[at : at + SUB] = new_cell.reshape(SUB, cols, width)
            new_hidden = new_hidden.reshape(SUB, cols, width)
            if not packed:
                hid_out[at : at + SUB] = new_hidden.astype(BF)
                continue
            owners_x, piece_y = hid_out.shape[1:3]
            local_m, piece_x = packed
            for owner in range(owners_x):
                picked = jnp.concatenate(
                    [
                        new_hidden[:, (m * owners_x + owner) * piece_x : (m * owners_x + owner + 1) * piece_x]
                        for m in range(local_m)
                    ],
                    axis=1,
                ).astype(BF)
                for row in range(SUB):
                    line = (step - 1) * STEP + at + row
                    hid_out[lax.div(line, piece_y), owner, lax.rem(line, piece_y)] = picked[row]

    slots = ref["even"], ref["odd"]

    @pl.when(step == 0)
    def _():
        load.start()
        build(slots[0])

    @pl.when(step == 1)
    def _():
        load.wait()

    for parity in range(2):

        @pl.when((step > 0) & (step < count) & (lax.rem(step, 2) == parity))
        def _():
            build(slots[parity])
            multiply(slots[1 - parity])

    @pl.when(step == count)
    def _():
        multiply(slots[(count - 1) % 2])


def conv_step(frames, part, hid, cell, ring, weights, bias, blocks, out_shapes, out_specs, packed, carry):
    rows, cols, width = hid.shape
    latent = weights.shape[0] // 9 - width
    first, count = blocks
    last = rows // STEP - 1

    def rowed(depth, channels, channel, index):
        def place(step):
            return index(first + jnp.minimum(step, count - 1)), 0, channel

        return pl.BlockSpec((depth, cols, channels), place)

    def whole(array):
        return pl.BlockSpec(array.shape, lambda step: (0,) * array.ndim)

    def before(block):
        return jnp.maximum(block * STEP - 1, 0)

    def after(block):
        return jnp.minimum(block * STEP + STEP, rows - 1)

    inputs = {
        "frame": (frames, rowed(STEP, latent, part, lambda block: block)),
        "frame_prev": (frames, rowed(1, latent, part, before)),
        "frame_next": (frames, rowed(1, latent, part, after)),
        "hid": (hid, rowed(STEP, width, 0, lambda block: block)),
        "hid_prev": (hid, rowed(1, width, 0, before)),
        "hid_next": (hid, rowed(1, width, 0, after)),
        "cell": (cell, pl.BlockSpec((STEP, cols, width), lambda step: (first + jnp.maximum(step - 1, 0), 0, 0))),
        "weights": (weights, pl.BlockSpec(memory_space=pl.ANY)),
        "bias": (bias, whole(bias)),
    }
    inputs |= {name: (array, whole(array)) for name, array in ring.items()}
    aliases = {}
    for place, array in enumerate(carry):
        if array is not None:
            aliases[len(inputs)] = place
            inputs[f"carry{place}"] = (array, pl.BlockSpec(memory_space=pl.ANY))
    refs = (*inputs, "hid_out", "cell_out", "even", "odd", "held", "sem")
    cells = count * STEP * cols
    slot = pltpu.VMEM((STEP + 2, cols, 3 * (latent + width)), BF)
    return pl.pallas_call(
        functools.partial(conv_kernel, first, count, last, refs, packed),
        grid=(count + 1,),
        in_specs=[spec for _, spec in inputs.values()],
        out_specs=out_specs,
        out_shape=out_shapes,
        scratch_shapes=[slot, slot, pltpu.VMEM(weights.shape, BF), pltpu.SemaphoreType.DMA(())],
        input_output_aliases=aliases,
        compiler_params=pltpu.CompilerParams(vmem_limit_bytes=VMEM_LIMIT),
        cost_estimate=pl.CostEstimate(
            flops=2 * cells * weights.size, bytes_accessed=2 * weights.size + cells * 2048, transcendentals=cells * width * 5
        ),
    )(*(array for array, _ in inputs.values()))


def ring_kernel(lines, strips, left, right, weights, bias, line_hid, line_cell, strip_hid, strip_cell):
    chans = left.shape[2]
    cols, length = lines.shape[2], strips.shape[2]
    rows = left.shape[0] - 4
    parts = []
    for side in range(2):
        pieces = [
            three_columns(lines[side, row, :, :chans].astype(F32), left[side * rows + row], right[side * rows + row])
            for row in range(4)
        ]
        for row in range(2):
            parts.append(jnp.concatenate([pieces[row + tap][col] for tap in range(3) for col in range(3)], axis=1))
    for side in range(2):
        rolled = []
        for col in range(4):
            wide = strips[side, col, :, :chans].astype(F32)
            rolled.append((pltpu.roll(wide, 1, axis=0), wide, pltpu.roll(wide, length - 1, axis=0)))
        for col in range(2):
            parts.append(
                jnp.concatenate([rolled[col + tap][row].astype(BF) for row in range(3) for tap in range(3)], axis=1)
            )
    row_at, col_at = lax.axis_index("gy"), lax.axis_index("gx")
    above = (row_at > 0).astype(F32)
    below = (row_at < lax.axis_size("gy") - 1).astype(F32)
    before = (col_at > 0).astype(F32)
    after = (col_at < lax.axis_size("gx") - 1).astype(F32)
    width = line_hid.shape[2]
    spot = lax.broadcasted_iota(jnp.int32, (length, width), 0)
    inside = jnp.where(spot == 1, above, jnp.where(spot == rows + 2, below, 1.0))
    keep = [above, 1.0, 1.0, below, inside * before, inside, inside, inside * after]
    for half, (hid, cell) in enumerate(((line_hid, line_cell), (strip_hid, strip_cell))):
        lhs = jnp.concatenate(parts[4 * half : 4 * half + 4], axis=0)
        gates = jnp.dot(lhs, weights[...], preferred_element_type=F32) + bias[...]
        if half == 0:
            held = [lines[side, row, :, chans:] for side in range(2) for row in (1, 2)]
        else:
            held = [strips[side, col, :, chans:] for side in range(2) for col in (1, 2)]
        new_cell, hidden = lstm(gates, jnp.concatenate(held, axis=0).astype(F32))
        hidden = hidden.astype(BF).astype(F32)
        size = hid.shape[1]
        for place in range(4):
            hid[place] = hidden[place * size : (place + 1) * size] * keep[4 * half + place]
            cell[place] = new_cell[place * size : (place + 1) * size]


def block_kernel(x, w_qkv, w_out, w_up, w_down, out, flat, back, own, ones):
    width = x.shape[-1]
    group = GRID * GRID
    flat[...] = x[...].astype(F32).reshape(flat.shape)
    groups = flat.shape[0] // group
    cells = jnp.concatenate([flat[pl.ds(g, group, stride=groups), :] for g in range(groups)], axis=0)
    normed = layer_norm(cells).astype(BF)
    qkv = jnp.dot(normed, w_qkv[...], preferred_element_type=F32).astype(BF)
    embed = w_qkv.shape[1] // 3

    @pl.when((pl.program_id(0) == 0) & (pl.program_id(1) == 0))
    def _():
        def fill(target, size):
            down = lax.broadcasted_iota(jnp.int32, target.shape, 0) // group
            across = lax.broadcasted_iota(jnp.int32, target.shape, 1) // size
            target[...] = (down == across).astype(F32).astype(BF)

        fill(own, HDIM)
        fill(ones, group)

    raised = []
    for g in range(groups):
        part = qkv[g * group : (g + 1) * group]
        spread = jnp.concatenate([part[:, embed : 2 * embed]] * HEADS, axis=0) * own[...]
        scores = lax.dot_general(
            part[:, :embed], spread, (((1,), (1,)), ((), ())), preferred_element_type=F32
        )
        raised.append(jnp.minimum(jnp.exp(scores * HDIM**-0.5), BF_MAX).astype(BF))
    raised = jnp.concatenate(raised, axis=0)
    total = jnp.dot(raised, ones[...], preferred_element_type=F32)
    attn = (raised.astype(F32) / total).astype(BF)
    heads = []
    for g in range(groups):
        part = qkv[g * group : (g + 1) * group]
        spread = jnp.concatenate([part[:, 2 * embed :]] * HEADS, axis=0) * own[...]
        heads.append(
            jnp.dot(attn[g * group : (g + 1) * group], spread, preferred_element_type=F32).astype(BF)
        )
    heads = jnp.concatenate(heads, axis=0)
    attended = jnp.dot(heads, w_out[...], preferred_element_type=F32).astype(BF)
    mixed = cells + attended.astype(F32)
    normed_two = layer_norm(mixed).astype(BF)
    up = jnp.dot(normed_two, w_up[...], preferred_element_type=F32)
    expanded = (0.5 * up * (1.0 + jnp.tanh(0.7978845608 * (up + 0.044715 * (up * up * up))))).astype(BF)
    result = mixed + jnp.dot(expanded, w_down[...], preferred_element_type=F32)
    for g in range(groups):
        back[pl.ds(g, group, stride=groups), :] = result[g * group : (g + 1) * group]
    out[...] = back[...].reshape(x.shape).astype(BF)


def block_step(moved, devices_y, devices_x, w_qkv, w_out, w_up, w_down):
    _, piece_y, piece_cols, width = moved.shape
    lanes = devices_y // GRID
    view = moved.reshape(GRID, lanes, devices_x, piece_y, piece_cols, width)
    tokens = GRID * devices_x * piece_cols
    spec = pl.BlockSpec(
        (GRID, None, devices_x, None, piece_cols, width), lambda i, j: (0, i, 0, j, 0, 0)
    )

    def whole(array):
        return pl.BlockSpec(array.shape, lambda i, j: (0,) * array.ndim)

    total = lanes * piece_y * tokens
    out = pl.pallas_call(
        block_kernel,
        grid=(lanes, piece_y),
        in_specs=[spec, whole(w_qkv), whole(w_out), whole(w_up), whole(w_down)],
        out_specs=spec,
        out_shape=jax.ShapeDtypeStruct(view.shape, BF),
        scratch_shapes=[
            pltpu.VMEM((tokens, width), F32),
            pltpu.VMEM((tokens, width), F32),
            pltpu.VMEM((HEADS * GRID * GRID, w_out.shape[0]), BF),
            pltpu.VMEM((HEADS * GRID * GRID, HEADS * GRID * GRID), BF),
        ],
        compiler_params=pltpu.CompilerParams(vmem_limit_bytes=VMEM_LIMIT),
        cost_estimate=pl.CostEstimate(
            flops=total * 3_000_000, bytes_accessed=total * width * 4 + 800_000, transcendentals=total * 1100
        ),
    )(view, w_qkv, w_out, w_up, w_down)
    return out.reshape(moved.shape)


def unpack_kernel(local_m, piece_x, *refs):
    src, out = refs[0], refs[-1]
    owners_y, owners_x, piece_y, _, width = src.shape
    for owner_y in range(owners_y):
        for row in range(piece_y):
            wide = src[owner_y, :, row].astype(F32)
            out[owner_y * piece_y + row] = jnp.concatenate(
                [wide[owner, m * piece_x : (m + 1) * piece_x] for m in range(local_m) for owner in range(owners_x)],
                axis=0,
            ).astype(BF)


def unpack_step(landed, carry, start, rows, cols, local_m, piece_x):
    owners_y, owners_x, piece_y, _, width = landed.shape
    depth = owners_y * piece_y
    specs = [pl.BlockSpec(landed.shape, lambda i: (0,) * landed.ndim)]
    operands = [landed]
    aliases = {}
    if carry is not None:
        specs.append(pl.BlockSpec(memory_space=pl.ANY))
        operands.append(carry)
        aliases = {1: 0}
    return pl.pallas_call(
        functools.partial(unpack_kernel, local_m, piece_x),
        grid=(1,),
        in_specs=specs,
        out_specs=pl.BlockSpec((depth, cols, width), lambda i: (start // depth, 0, 0)),
        out_shape=jax.ShapeDtypeStruct((rows, cols, width), BF),
        input_output_aliases=aliases,
        compiler_params=pltpu.CompilerParams(vmem_limit_bytes=VMEM_LIMIT),
        cost_estimate=pl.CostEstimate(flops=0, bytes_accessed=depth * cols * width * 4, transcendentals=0),
    )(*operands)


def body(frames, hidden_state, cell_state, w_gates, gate_bias, w_qkv, w_out, w_up, w_down):
    rows, cols, width = hidden_state.shape
    latent = frames.shape[2] // 2
    chans = latent + width
    held = chans + width
    devices_y, devices_x = lax.axis_size("gy"), lax.axis_size("gx")
    local_m = GRID // devices_x
    piece_x = cols // local_m // devices_x
    weights = w_gates.reshape(-1, w_gates.shape[3])
    bias = gate_bias.reshape(1, -1)

    def pack(row, col):
        return jnp.concatenate(
            [
                frames[row, col, :latent],
                hidden_state[row, col],
                cell_state[row, col].astype(BF),
                frames[row, col, latent:],
            ],
            axis=-1,
        )

    def shifted(value, axis, step):
        count = lax.axis_size(axis)
        pairs = [(i, i + step) for i in range(count) if 0 <= i + step < count]
        return lax.ppermute(value, axis, pairs)

    every = slice(None)
    side_left, side_right = pack(every, slice(0, 2)), pack(every, slice(cols - 2, cols))
    from_left = shifted(side_right, "gx", 1)
    from_right = shifted(side_left, "gx", -1)
    line_top, line_bot = pack(slice(0, 2), every), pack(slice(rows - 2, rows), every)
    from_up = shifted(jnp.concatenate([line_bot, from_left[-2:], from_right[-2:]], axis=1), "gy", 1)
    from_down = shifted(jnp.concatenate([line_top, from_left[:2], from_right[:2]], axis=1), "gy", -1)

    tile_shapes = (jax.ShapeDtypeStruct((rows, cols, width), BF), jax.ShapeDtypeStruct((rows, cols, width), F32))
    half = rows // STEP // 2
    hidden_one = cell_one = None
    for first, count in ((0, half), (half, rows // STEP - half)):
        spec = pl.BlockSpec((STEP, cols, width), lambda j, first=first: (first + jnp.maximum(j - 1, 0), 0, 0))
        hidden_one, cell_one = conv_step(
            frames, 0, hidden_state, cell_state, {}, weights, bias, (first, count), tile_shapes, (spec, spec),
            None, (hidden_one, cell_one),
        )

    def column(at, middle):
        return jnp.concatenate([from_up[:, at], middle, from_down[:, at]], axis=0)

    columns = [
        column(cols, from_left[:, 0]),
        column(cols + 1, from_left[:, 1]),
        column(0, side_left[:, 0]),
        column(1, side_left[:, 1]),
        column(cols - 2, side_right[:, 0]),
        column(cols - 1, side_right[:, 1]),
        column(cols + 2, from_right[:, 0]),
        column(cols + 3, from_right[:, 1]),
    ]
    length = -(-(rows + 4) // 16) * 16
    strips = jnp.stack(columns)[:, :, :held].reshape(2, 4, rows + 4, held)
    strips = jnp.pad(strips, ((0, 0), (0, 0), (0, length - rows - 4), (0, 0)))
    low, high = columns[1].astype(F32)[:, None], columns[6].astype(F32)[:, None]
    lines = jnp.stack(
        [
            jnp.concatenate([from_up[:, :cols, :held], line_top[:, :, :held]], axis=0),
            jnp.concatenate([line_bot[:, :, :held], from_down[:, :cols, :held]], axis=0),
        ]
    )
    ring_shapes = [jax.ShapeDtypeStruct((4, cols, width), F32)] * 2 + [jax.ShapeDtypeStruct((4, length, width), F32)] * 2
    line_hid, line_cell, strip_hid, strip_cell = pl.pallas_call(
        ring_kernel,
        out_shape=ring_shapes,
        compiler_params=pltpu.CompilerParams(vmem_limit_bytes=VMEM_LIMIT),
        cost_estimate=pl.CostEstimate(flops=16 * length * weights.size, bytes_accessed=2 * weights.size, transcendentals=0),
    )(lines, strips, low[:, :, :chans], high[:, :, :chans], weights, bias)

    def sided(strip, at):
        return strip[at, 1 : rows + 3][:, None]

    ring = {
        "left": jnp.concatenate([low[1:-1, :, held:], sided(strip_hid, 0)], axis=2),
        "right": jnp.concatenate([high[1:-1, :, held:], sided(strip_hid, 3)], axis=2),
        "first_col": sided(strip_hid, 1),
        "last_col": sided(strip_hid, 2),
        "first_cell": sided(strip_cell, 1),
        "last_cell": sided(strip_cell, 2),
        "lines": line_hid,
        "cell_lines": line_cell,
        "frame_top": from_up[1:, :cols, held:],
        "frame_bot": from_down[:1, :cols, held:],
    }

    pieces = rows // devices_y
    piece_cols = local_m * piece_x
    cell_out, moved, start = None, [], 0
    for piece_y in (pieces - pieces // 2, pieces // 2):
        first, count = start // STEP, piece_y * devices_y // STEP
        sent_shape = (devices_y, devices_x, piece_y, piece_cols, width)
        sent, cell_out = conv_step(
            frames, 1, hidden_one, cell_one, ring, weights, bias, (first, count),
            (jax.ShapeDtypeStruct(sent_shape, BF), tile_shapes[1]),
            (
                pl.BlockSpec(sent_shape, lambda j: (0,) * 5),
                pl.BlockSpec((STEP, cols, width), lambda j, first=first: (first + jnp.maximum(j - 1, 0), 0, 0)),
            ),
            (local_m, piece_x), (None, cell_out),
        )
        sent = sent.reshape(devices_y * devices_x, piece_y, piece_cols, width)
        moved.append((start, lax.all_to_all(sent, ("gy", "gx"), split_axis=0, concat_axis=0, tiled=True)))
        start += piece_y * devices_y
    landed = []
    for start, value in moved:
        done = block_step(value, devices_y, devices_x, w_qkv, w_out, w_up, w_down)
        landed.append((start, lax.all_to_all(done, ("gy", "gx"), split_axis=0, concat_axis=0, tiled=True)))
    result = None
    for start, value in landed:
        view = value.reshape(devices_y, devices_x, *value.shape[1:])
        result = unpack_step(view, result, start, rows, cols, local_m, piece_x)
    return result, cell_out


def solution(mesh):
    tiled = P("gy", "gx", None)
    in_specs = (tiled, tiled, tiled, P(), P(), P(), P(), P(), P())
    return jax.shard_map(body, mesh=mesh, in_specs=in_specs, out_specs=(tiled, tiled), check_vma=False)
```

time: 143 us -> 145 us (1.014)
  Pallas kernels: 54.4 us -> 74.9 us
  starting transfers between devices: 41.9 us -> 31.6 us
  local copies, waits for them, and re-layouts: 19.3 us -> 12.1 us
  waiting for transfers between devices: 22.5 us -> 18.4 us
  other arithmetic: 2.92 us -> 5.5 us
    pallas_call x5, Pallas kernels: 31.1 us -> 49.1 us  [the longest x4 43.8 us: conv_step(): pl.pallas_call(functools.partial(conv_kernel, first, count, last, refs, p...]
    unnamed x64 -> x32, local copies, waits for them, and re-layouts: 14.7 us -> 0.92 us
    all_to_all x3 -> x2, starting transfers between devices: 18.4 us -> 10.7 us  [body(): lax.all_to_all(sent, ('gy', 'gx'), split_axis=0, concat_axis=0, tiled=True)]
    ppermute x4, waiting for transfers between devices: 6.41 us -> 2.8 us  [shifted(): return lax.ppermute(value, axis, pairs)]
    all_to_all x3 -> x2, waiting for transfers between devices: 15.7 us -> 12.6 us  [body(): lax.all_to_all(done, ('gy', 'gx'), split_axis=0, concat_axis=0, tiled=True)]
    all_to_all x3 -> x2, waiting for transfers between devices: 0.34 us -> 3.05 us  [body(): lax.all_to_all(sent, ('gy', 'gx'), split_axis=0, concat_axis=0, tiled=True)]
    all_to_all x3 -> x2, starting transfers between devices: 10.9 us -> 8.41 us  [body(): lax.all_to_all(done, ('gy', 'gx'), split_axis=0, concat_axis=0, tiled=True)]
    slice x14 -> x9, local copies, waits for them, and re-layouts: 0.44 us -> 2.85 us  [the longest x1 0.96 us: pack(): frames[row, col, latent:]]
  transfers between devices with their start and end apart: 10 -> 8, of which waited for: 8 -> 6; matrix products, arithmetic and copies ran while one was open for 1% -> 2% of each run, Pallas kernels for 23% -> 39%
where the time goes in v1:
time: 145 us; the launch traced here: 144 us
  Pallas kernels  74.9 us (52%)
  starting transfers between devices  31.6 us (22%)
  waiting for transfers between devices  18.4 us (13%)
  local copies, waits for them, and re-layouts  12.1 us (8%)
  other arithmetic  5.5 us (4%)
    pallas_call x4, Pallas kernels, conv_step(): pl.pallas_call(functools.partial(conv_kernel, first, count, last, refs, p...  43.8 us
    pallas_call x2, Pallas kernels, block_step(): pl.pallas_call(block_kernel, grid=(lanes, piece_y), in_specs=[spec, whole...  22.2 us
    all_to_all x2, waiting for transfers between devices, body(): lax.all_to_all(done, ('gy', 'gx'), split_axis=0, concat_axis=0, tiled=True)  12.6 us
    ppermute x4, starting transfers between devices, shifted(): return lax.ppermute(value, axis, pairs)  12.5 us
    all_to_all x2, starting transfers between devices, body(): lax.all_to_all(sent, ('gy', 'gx'), split_axis=0, concat_axis=0, tiled=True)  10.7 us
    all_to_all x2, starting transfers between devices, body(): lax.all_to_all(done, ('gy', 'gx'), split_axis=0, concat_axis=0, tiled=True)  8.41 us
    pallas_call x1, Pallas kernels, body(): pl.pallas_call(ring_kernel, out_shape=ring_shapes, compiler_params=pltpu....  5.28 us
    pallas_call x2, Pallas kernels, unpack_step(): pl.pallas_call(functools.partial(unpack_kernel, local_m, piece_x), grid=(...  3.62 us
  transfers between devices with their start and end apart: 8, of which 6 were waited for; matrix products, arithmetic and copies ran while one was open for 2% of the time, Pallas kernels for 39%

profile of v1, /device:TPU:1, one launch (start us, length us, event | category | flops | bytes accessed | tf_op | source)
XLA Modules:
  0.0 143.7 jit_solution(15850051118486552955)
XLA Ops:
  0.6 1.4 fusion.10
  2.0 1.5 %convert.6 = bf16[48,64,128]{2,1,0:T(8,128)(2,1)S(1)} convert(f32[48,64,128]{2,1,0:T(8,128)} %args_6_.6) | non-fusion elementwise | flops 393216 | bytes 2359296 | tf_op jit(solution)/shard_map/convert.3
  4.8 1.3 collective-permute-start.1
  6.2 4.7 %collective-permute-start = (bf16[48,2,768]{2,1,0:T(2,128)(2,1)S(1)}, bf16[48,2,768]{2,1,0:T(2,128)(2,1)S(1)}, u32[]{:S(2)}, u32[]{:S(2)}) collective-permute-start(bf16[48,2,768]{2,1,0:T(2,128)(2,1)S(1)} %pad_maximum_fusion.3), channel_id=1, source_target_pairs={{0,1},{1,2},{2,3},{4,5},{5,6},{6,7},{8,9},{9,10},{10,11},{12,13},{... | collective-permute-start | bytes 442376 | tf_op jit(solution)/shard_map/ppermute | solution.py:399
  12.3 10.6 %shard_map.104 = (bf16[48,64,128]{2,1,0:T(8,128)(2,1)}, f32[48,64,128]{2,1,0:T(8,128)}) custom-call(bf16[48,64,512]{2,1,0:T(8,128)(2,1)} %args_2_.10, bf16[48,64,512]{2,1,0:T(8,128)(2,1)} %args_2_.10, bf16[48,64,512]{2,1,0:T(8,128)(2,1)} %args_2_.10, bf16[48,64,128]{2,1,0:T(8,128)(2,1)} %args_5_.6, bf16[48,64,128]{2,1,0:T(8,128)(2,1)} %args_5_.6, ...), custom_call_target="tpu_custom_call" | custom-call | flops 5435817984 | bytes 6684672 | tf_op jit(solution)/shard_map/pallas_call | solution.py:197
  23.0 10.6 %shard_map.105 = (bf16[48,64,128]{2,1,0:T(8,128)(2,1)}, f32[48,64,128]{2,1,0:T(8,128)}) custom-call(bf16[48,64,512]{2,1,0:T(8,128)(2,1)} %args_2_.10, bf16[48,64,512]{2,1,0:T(8,128)(2,1)} %args_2_.10, bf16[48,64,512]{2,1,0:T(8,128)(2,1)} %args_2_.10, bf16[48,64,128]{2,1,0:T(8,128)(2,1)} %args_5_.6, ...), custom_call_target="tpu_custom_call", output_to_operand_aliasing={{0}: (9, {}), {1}: (10, {})} | custom-call | flops 5435817984 | bytes 6684672 | tf_op jit(solution)/shard_map/pallas_call | solution.py:197
  34.5 3.0 %collective-permute-start.3 = (bf16[2,68,768]{2,1,0:T(8,128)(2,1)S(1)}, bf16[2,68,768]{2,1,0:T(8,128)(2,1)S(1)}, u32[]{:S(2)}, u32[]{:S(2)}) collective-permute-start(bf16[2,68,768]{2,1,0:T(8,128)(2,1)S(1)} %pad_maximum_fusion.2), channel_id=1, source_target_pairs={{4,0},{8,4},{12,8},{16,12},{20,16},{24,20},{28,24},{5,1},{9,5},{13... | collective-permute-start | bytes 626696 | tf_op jit(solution)/shard_map/ppermute | solution.py:399
  38.1 3.5 %collective-permute-start.2 = (bf16[2,68,768]{2,1,0:T(8,128)(2,1)S(1)}, bf16[2,68,768]{2,1,0:T(8,128)(2,1)S(1)}, u32[]{:S(2)}, u32[]{:S(2)}) collective-permute-start(bf16[2,68,768]{2,1,0:T(8,128)(2,1)S(1)} %pad_maximum_fusion.1), channel_id=1, source_target_pairs={{0,4},{4,8},{8,12},{12,16},{16,20},{20,24},{24,28},{1,5},{5,9},{9,... | collective-permute-start | bytes 626696 | tf_op jit(solution)/shard_map/ppermute | solution.py:399
  42.7 1.7 %collective-permute-done.2 = bf16[2,68,768]{2,1,0:T(8,128)(2,1)S(1)} collective-permute-done((bf16[2,68,768]{2,1,0:T(8,128)(2,1)S(1)}, bf16[2,68,768]{2,1,0:T(8,128)(2,1)S(1)}, u32[]{:S(2)}, u32[]{:S(2)}) %collective-permute-start.2) | collective-permute-done | bytes 208928 | tf_op jit(solution)/shard_map/ppermute | solution.py:399
  48.5 5.3 %shard_map.106 = (f32[4,64,128]{2,1,0:T(8,128)}, f32[4,64,128]{2,1,0:T(8,128)}, f32[4,64,128]{2,1,0:T(8,128)}, f32[4,64,128]{2,1,0:T(8,128)}) custom-call(bf16[2,4,64,512]{3,2,1,0:T(8,128)(2,1)} %pad_maximum_fusion.lines, bf16[2,4,64,512]{3,2,1,0:T(8,128)(2,1)} %pad.4.strips, f32[52,1,384]{2,1,0:T(1,128)} %fusion.8.left, f32[52,1,384]{2,1,0:T(1,128)} %slice.279.right, ...), custom_call_target="tpu_custom_call" | custom-call | flops 1811939328 | bytes 3538944 | tf_op jit(solution)/shard_map/pallas_call | solution.py:443
  59.8 11.3 %shard_map.107 = (bf16[8,4,3,16,128]{4,3,2,1,0:T(8,128)(2,1)}, f32[48,64,128]{2,1,0:T(8,128)}) custom-call(bf16[48,64,512]{2,1,0:T(8,128)(2,1)} %args_2_.10, bf16[48,64,512]{2,1,0:T(8,128)(2,1)} %args_2_.10, bf16[48,64,512]{2,1,0:T(8,128)(2,1)} %args_2_.10, bf16[48,64,128]{2,1,0:T(8,128)(2,1)} %get-tuple-element.16.args_3_.args_4_.args_5_, ...), custom_call_target="tpu_custom_call" | custom-call | flops 5435817984 | bytes 6684672 | tf_op jit(solution)/shard_map/pallas_call | solution.py:197
  71.1 6.3 %all-to-all-start.2 = ((bf16[32,3,16,128]{3,2,1,0:T(8,128)(2,1)}), bf16[32,3,16,128]{3,2,1,0:T(8,128)(2,1)S(1)}, u32[]{:S(2)}, u32[]{:S(2)}) async-start(bf16[32,3,16,128]{3,2,1,0:T(8,128)(2,1)} %bitcast.136), calls=%async_computation.2 | async-start | bytes 786432 | tf_op jit(solution)/shard_map/all_to_all | solution.py:482
  77.3 11.3 %shard_map.108 = (bf16[8,4,3,16,128]{4,3,2,1,0:T(8,128)(2,1)}, f32[48,64,128]{2,1,0:T(8,128)}) custom-call(bf16[48,64,512]{2,1,0:T(8,128)(2,1)} %args_2_.10, bf16[48,64,512]{2,1,0:T(8,128)(2,1)} %args_2_.10, bf16[48,64,512]{2,1,0:T(8,128)(2,1)} %args_2_.10, ...), custom_call_target="tpu_custom_call", output_to_operand_aliasing={{1}: (19, {})} | custom-call | flops 5435817984 | bytes 6684672 | tf_op jit(solution)/shard_map/pallas_call | solution.py:197
  88.7 1.4 all-to-all-done.2
  90.1 4.4 %all-to-all-start = ((bf16[32,3,16,128]{3,2,1,0:T(8,128)(2,1)}), bf16[32,3,16,128]{3,2,1,0:T(8,128)(2,1)S(1)}, u32[]{:S(2)}, u32[]{:S(2)}) async-start(bf16[32,3,16,128]{3,2,1,0:T(8,128)(2,1)} %bitcast.135), calls=%async_computation | async-start | bytes 786432 | tf_op jit(solution)/shard_map/all_to_all | solution.py:482
  94.5 11.1 %shard_map.110 = bf16[8,1,4,3,16,128]{5,4,3,2,1,0:T(8,128)(2,1)} custom-call(bf16[8,1,4,3,16,128]{5,4,3,2,1,0:T(8,128)(2,1)} %bitcast.134, bf16[128,768]{1,0:T(8,128)(2,1)} %w_qkv.3, bf16[256,128]{1,0:T(8,128)(2,1)} %w_out.3, bf16[128,512]{1,0:T(8,128)(2,1)} %w_up.3, bf16[512,128]{1,0:T(8,128)(2,1)} %w_down.3), custom_call_target="tpu_custom_call" | custom-call | flops 4608000000 | bytes 1586432 | tf_op jit(solution)/shard_map/pallas_call | solution.py:320
  105.6 1.6 %all-to-all-done = bf16[32,3,16,128]{3,2,1,0:T(8,128)(2,1)S(1)} async-done(((bf16[32,3,16,128]{3,2,1,0:T(8,128)(2,1)}), bf16[32,3,16,128]{3,2,1,0:T(8,128)(2,1)S(1)}, u32[]{:S(2)}, u32[]{:S(2)}) %all-to-all-start) | async-done | bytes 393248 | tf_op jit(solution)/shard_map/all_to_all | solution.py:482
  107.3 4.2 %all-to-all-start.3 = ((bf16[32,3,16,128]{3,2,1,0:T(8,128)(2,1)}), bf16[32,3,16,128]{3,2,1,0:T(8,128)(2,1)S(1)}, u32[]{:S(2)}, u32[]{:S(2)}) async-start(bf16[32,3,16,128]{3,2,1,0:T(8,128)(2,1)} %bitcast.138), calls=%async_computation.3 | async-start | bytes 786432 | tf_op jit(solution)/shard_map/all_to_all | solution.py:487
  111.5 11.1 %shard_map.109 = bf16[8,1,4,3,16,128]{5,4,3,2,1,0:T(8,128)(2,1)} custom-call(bf16[8,1,4,3,16,128]{5,4,3,2,1,0:T(8,128)(2,1)} %bitcast.137, bf16[128,768]{1,0:T(8,128)(2,1)} %w_qkv.3, bf16[256,128]{1,0:T(8,128)(2,1)} %w_out.3, bf16[128,512]{1,0:T(8,128)(2,1)} %w_up.3, bf16[512,128]{1,0:T(8,128)(2,1)} %w_down.3), custom_call_target="tpu_custom_call" | custom-call | flops 4608000000 | bytes 1586432 | tf_op jit(solution)/shard_map/pallas_call | solution.py:320
  122.6 1.7 %all-to-all-done.3 = bf16[32,3,16,128]{3,2,1,0:T(8,128)(2,1)S(1)} async-done(((bf16[32,3,16,128]{3,2,1,0:T(8,128)(2,1)}), bf16[32,3,16,128]{3,2,1,0:T(8,128)(2,1)S(1)}, u32[]{:S(2)}, u32[]{:S(2)}) %all-to-all-start.3) | async-done | bytes 393248 | tf_op jit(solution)/shard_map/all_to_all | solution.py:487
  124.3 4.2 %all-to-all-start.1 = ((bf16[32,3,16,128]{3,2,1,0:T(8,128)(2,1)}), bf16[32,3,16,128]{3,2,1,0:T(8,128)(2,1)S(1)}, u32[]{:S(2)}, u32[]{:S(2)}) async-start(bf16[32,3,16,128]{3,2,1,0:T(8,128)(2,1)} %bitcast.139), calls=%async_computation.1 | async-start | bytes 786432 | tf_op jit(solution)/shard_map/all_to_all | solution.py:487
  128.5 1.8 %shard_map.111.refs_1_ = bf16[48,64,128]{2,1,0:T(8,128)(2,1)} custom-call(bf16[8,4,3,16,128]{4,3,2,1,0:T(8,128)(2,1)} %bitcast.132), custom_call_target="tpu_custom_call" | custom-call | bytes 786432 | tf_op jit(solution)/shard_map/pallas_call | solution.py:362
  130.3 10.9 %all-to-all-done.1 = bf16[32,3,16,128]{3,2,1,0:T(8,128)(2,1)S(1)} async-done(((bf16[32,3,16,128]{3,2,1,0:T(8,128)(2,1)}), bf16[32,3,16,128]{3,2,1,0:T(8,128)(2,1)S(1)}, u32[]{:S(2)}, u32[]{:S(2)}) %all-to-all-start.1) | async-done | bytes 393248 | tf_op jit(solution)/shard_map/all_to_all | solution.py:487
  141.9 1.8 %shard_map.112 = bf16[48,64,128]{2,1,0:T(8,128)(2,1)} custom-call(bf16[8,4,3,16,128]{4,3,2,1,0:T(8,128)(2,1)} %bitcast.133, bf16[48,64,128]{2,1,0:T(8,128)(2,1)} %shard_map.111.refs_1_), custom_call_target="tpu_custom_call", output_to_operand_aliasing={{}: (1, {})} | custom-call | bytes 786432 | tf_op jit(solution)/shard_map/pallas_call | solution.py:362
  (78 shorter events, 15.8 us)
Async XLA Ops:
  4.8 29.6 %collective-permute-start.1 = (bf16[48,2,768]{2,1,0:T(2,128)(2,1)S(1)}, bf16[48,2,768]{2,1,0:T(2,128)(2,1)S(1)}, u32[]{:S(2)}, u32[]{:S(2)}) collective-permute-start(bf16[48,2,768]{2,1,0:T(2,128)(2,1)S(1)} %pad_maximum_fusion.4), channel_id=1, source_target_pairs={{1,0},{2,1},{3,2},{5,4},{6,5},{7,6},{9,8},{10,9},{11,10},{13,12},{... | collective-permute-start | bytes 442376 | tf_op jit(solution)/shard_map/ppermute | solution.py:399
  6.2 28.2 %collective-permute-start = (bf16[48,2,768]{2,1,0:T(2,128)(2,1)S(1)}, bf16[48,2,768]{2,1,0:T(2,128)(2,1)S(1)}, u32[]{:S(2)}, u32[]{:S(2)}) collective-permute-start(bf16[48,2,768]{2,1,0:T(2,128)(2,1)S(1)} %pad_maximum_fusion.3), channel_id=1, source_target_pairs={{0,1},{1,2},{2,3},{4,5},{5,6},{6,7},{8,9},{9,10},{10,11},{12,13},{... | collective-permute-start | bytes 442376 | tf_op jit(solution)/shard_map/ppermute | solution.py:399
  34.5 8.2 %collective-permute-start.3 = (bf16[2,68,768]{2,1,0:T(8,128)(2,1)S(1)}, bf16[2,68,768]{2,1,0:T(8,128)(2,1)S(1)}, u32[]{:S(2)}, u32[]{:S(2)}) collective-permute-start(bf16[2,68,768]{2,1,0:T(8,128)(2,1)S(1)} %pad_maximum_fusion.2), channel_id=1, source_target_pairs={{4,0},{8,4},{12,8},{16,12},{20,16},{24,20},{28,24},{5,1},{9,5},{13... | collective-permute-start | bytes 626696 | tf_op jit(solution)/shard_map/ppermute | solution.py:399
  38.1 6.3 %collective-permute-start.2 = (bf16[2,68,768]{2,1,0:T(8,128)(2,1)S(1)}, bf16[2,68,768]{2,1,0:T(8,128)(2,1)S(1)}, u32[]{:S(2)}, u32[]{:S(2)}) collective-permute-start(bf16[2,68,768]{2,1,0:T(8,128)(2,1)S(1)} %pad_maximum_fusion.1), channel_id=1, source_target_pairs={{0,4},{4,8},{8,12},{12,16},{16,20},{20,24},{24,28},{1,5},{5,9},{9,... | collective-permute-start | bytes 626696 | tf_op jit(solution)/shard_map/ppermute | solution.py:399
  71.1 19.0 %all-to-all-start.2 = ((bf16[32,3,16,128]{3,2,1,0:T(8,128)(2,1)}), bf16[32,3,16,128]{3,2,1,0:T(8,128)(2,1)S(1)}, u32[]{:S(2)}, u32[]{:S(2)}) async-start(bf16[32,3,16,128]{3,2,1,0:T(8,128)(2,1)} %bitcast.136), calls=%async_computation.2 | async-start | bytes 786432 | tf_op jit(solution)/shard_map/all_to_all | solution.py:482
  90.1 4.4 %copy-start.2 = (bf16[32,3,16,128]{3,2,1,0:T(8,128)(2,1)}, bf16[32,3,16,128]{3,2,1,0:T(8,128)(2,1)S(1)}, u32[]{:S(2)}) copy-start(bf16[32,3,16,128]{3,2,1,0:T(8,128)(2,1)S(1)} %all-to-all-done.2) | copy-start | bytes 1179652
  90.1 17.2 %all-to-all-start = ((bf16[32,3,16,128]{3,2,1,0:T(8,128)(2,1)}), bf16[32,3,16,128]{3,2,1,0:T(8,128)(2,1)S(1)}, u32[]{:S(2)}, u32[]{:S(2)}) async-start(bf16[32,3,16,128]{3,2,1,0:T(8,128)(2,1)} %bitcast.135), calls=%async_computation | async-start | bytes 786432 | tf_op jit(solution)/shard_map/all_to_all | solution.py:482
  107.3 4.2 %copy-start.3 = (bf16[32,3,16,128]{3,2,1,0:T(8,128)(2,1)}, bf16[32,3,16,128]{3,2,1,0:T(8,128)(2,1)S(1)}, u32[]{:S(2)}) copy-start(bf16[32,3,16,128]{3,2,1,0:T(8,128)(2,1)S(1)} %all-to-all-done) | copy-start | bytes 1179652
  107.3 17.0 %all-to-all-start.3 = ((bf16[32,3,16,128]{3,2,1,0:T(8,128)(2,1)}), bf16[32,3,16,128]{3,2,1,0:T(8,128)(2,1)S(1)}, u32[]{:S(2)}, u32[]{:S(2)}) async-start(bf16[32,3,16,128]{3,2,1,0:T(8,128)(2,1)} %bitcast.138), calls=%async_computation.3 | async-start | bytes 786432 | tf_op jit(solution)/shard_map/all_to_all | solution.py:487
  124.3 4.2 %copy-start = (bf16[32,3,16,128]{3,2,1,0:T(8,128)(2,1)}, bf16[32,3,16,128]{3,2,1,0:T(8,128)(2,1)S(1)}, u32[]{:S(2)}) copy-start(bf16[32,3,16,128]{3,2,1,0:T(8,128)(2,1)S(1)} %all-to-all-done.3) | copy-start | bytes 1179652
  124.3 16.9 %all-to-all-start.1 = ((bf16[32,3,16,128]{3,2,1,0:T(8,128)(2,1)}), bf16[32,3,16,128]{3,2,1,0:T(8,128)(2,1)S(1)}, u32[]{:S(2)}, u32[]{:S(2)}) async-start(bf16[32,3,16,128]{3,2,1,0:T(8,128)(2,1)} %bitcast.139), calls=%async_computation.1 | async-start | bytes 786432 | tf_op jit(solution)/shard_map/all_to_all | solution.py:487
  141.2 0.7 copy-start.1

commit v2 on v1

v2 whole, which is shorter than its diff:
```python
import functools

import jax
import jax.numpy as jnp
from jax import lax
from jax.experimental import pallas as pl
from jax.experimental.pallas import tpu as pltpu
from jax.sharding import PartitionSpec as P

HEADS = 8
HDIM = 32
GRID = 8
BF = jnp.bfloat16
F32 = jnp.float32
LOG2E = 1.4426950408889634
BF_MAX = 3.3895313892515355e38
VMEM_LIMIT = 60 * 1024 * 1024


def sigmoid(x):
    return 0.5 * jnp.tanh(0.5 * x) + 0.5


def lstm(gates, cell_prev):
    width = cell_prev.shape[-1]
    in_gate = sigmoid(gates[:, 0:width])
    forget_gate = sigmoid(gates[:, width : 2 * width])
    candidate = jnp.tanh(gates[:, 2 * width : 3 * width])
    out_gate = sigmoid(gates[:, 3 * width :])
    cell = forget_gate * cell_prev + in_gate * candidate
    return cell, out_gate * jnp.tanh(cell)


def layer_norm(values):
    center = values - jnp.mean(values, axis=-1, keepdims=True)
    spread = jnp.mean(center * center, axis=-1, keepdims=True)
    return center * lax.rsqrt(spread + 1e-05)


def three_columns(wide, left, right):
    count = wide.shape[0]
    place = lax.broadcasted_iota(jnp.int32, wide.shape, 0)
    before = jnp.where(place == 0, left, pltpu.roll(wide, 1, axis=0))
    after = jnp.where(place == count - 1, right, pltpu.roll(wide, count - 1, axis=0))
    return before.astype(BF), wide.astype(BF), after.astype(BF)


def conv_kernel(first, last, refs, packed, *args):
    ref = dict(zip(refs, args))
    frame, hid = ref["frame"], ref["hid"]
    hid_out, cell_out, spread = ref["hid_out"], ref["cell_out"], ref["spread"]
    ring = "strips_hid" in ref
    step = pl.program_id(0)
    depth, cols, latent = frame.shape
    width = hid.shape[2]
    chans = latent + width
    load = pltpu.make_async_copy(ref["weights"], ref["held"], ref["sem"])

    @pl.when(step == 0)
    def _():
        load.start()
        if ring:
            for side, strip, frames_beside in (("left", 0, "frame_left"), ("right", 3, "frame_right")):
                ref[side][:, :latent] = ref[frames_beside][0, 0].astype(F32)
                ref[side][:, latent:] = ref["strips_hid"][strip]

    block = first + step
    base = block * depth
    top, bot = block == 0, block == last
    for pos in range(depth + 2):
        if pos == 0:
            x, h = ref["frame_prev"][0].astype(F32), ref["hid_prev"][0].astype(F32)
        elif pos == depth + 1:
            x, h = ref["frame_next"][0].astype(F32), ref["hid_next"][0].astype(F32)
        else:
            x, h = frame[pos - 1].astype(F32), hid[pos - 1].astype(F32)
        low = high = jnp.zeros((1, chans), F32)
        if ring:
            here = pl.ds(base + pos + 1, 1)
            low, high = ref["left"][here, :], ref["right"][here, :]
            place = lax.broadcasted_iota(jnp.int32, h.shape, 0)
            h = jnp.where(place == 0, ref["strips_hid"][1, here, :], h)
            h = jnp.where(place == cols - 1, ref["strips_hid"][2, here, :], h)
            for spot, edge, line in ((0, top, 0), (1, top, 1), (depth, bot, 2), (depth + 1, bot, 3)):
                if pos == spot:
                    h = jnp.where(edge, ref["lines_hid"][line], h)
            if pos == 0:
                x = jnp.where(top, ref["frame_top"][0, :cols].astype(F32), x)
            if pos == depth + 1:
                x = jnp.where(bot, ref["frame_bot"][0, :cols].astype(F32), x)
        elif pos == 0:
            x, h = jnp.where(top, 0.0, x), jnp.where(top, 0.0, h)
        elif pos == depth + 1:
            x, h = jnp.where(bot, 0.0, x), jnp.where(bot, 0.0, h)
        for part, start in ((x, 0), (h, latent)):
            size = part.shape[1]
            pieces = three_columns(part, low[:, start : start + size], high[:, start : start + size])
            for tap in range(3):
                spread[pos, :, tap * chans + start : tap * chans + start + size] = pieces[tap]

    @pl.when(step == 0)
    def _():
        load.wait()

    lhs = jnp.concatenate(
        [spread[tap : tap + depth].reshape(depth * cols, 3 * chans) for tap in range(3)], axis=1
    )
    gates = jnp.dot(lhs, ref["held"][...], preferred_element_type=F32) + ref["bias"][...]
    for row in range(depth):
        cell_prev = ref["cell"][row]
        if ring:
            here = pl.ds(base + row + 2, 1)
            place = lax.broadcasted_iota(jnp.int32, cell_prev.shape, 0)
            cell_prev = jnp.where(place == 0, ref["strips_cell"][1, here, :], cell_prev)
            cell_prev = jnp.where(place == cols - 1, ref["strips_cell"][2, here, :], cell_prev)
            if row == 0:
                cell_prev = jnp.where(top, ref["lines_cell"][1], cell_prev)
            if row == depth - 1:
                cell_prev = jnp.where(bot, ref["lines_cell"][2], cell_prev)
        new_cell, new_hidden = lstm(gates[row * cols : (row + 1) * cols], cell_prev)
        cell_out[row] = new_cell
        if not packed:
            hid_out[row] = new_hidden.astype(BF)
            continue
        owners_x, piece_y = hid_out.shape[1:3]
        local_m, piece_x = packed
        line = step * depth + row
        for owner in range(owners_x):
            picked = [
                new_hidden[(m * owners_x + owner) * piece_x : (m * owners_x + owner + 1) * piece_x]
                for m in range(local_m)
            ]
            hid_out[lax.div(line, piece_y), owner, lax.rem(line, piece_y)] = jnp.concatenate(picked, axis=0).astype(BF)


def whole(array):
    return pl.BlockSpec(array.shape, lambda *step: (0,) * array.ndim)


def conv_step(frames, part, hid, cell, ring, weights, bias, extent, depth, out_shapes, out_specs, packed, carry):
    rows, cols, width = hid.shape
    latent = weights.shape[0] // 9 - width
    first, count = extent[0] // depth, extent[1] // depth
    last = rows // depth - 1

    def rowed(size, channels, channel, index):
        return pl.BlockSpec((size, cols, channels), lambda step: (index(first + step), 0, channel))

    def before(block):
        return jnp.maximum(block * depth - 1, 0)

    def after(block):
        return jnp.minimum(block * depth + depth, rows - 1)

    inputs = {
        "frame": (frames, rowed(depth, latent, part, lambda block: block)),
        "frame_prev": (frames, rowed(1, latent, part, before)),
        "frame_next": (frames, rowed(1, latent, part, after)),
        "hid": (hid, rowed(depth, width, 0, lambda block: block)),
        "hid_prev": (hid, rowed(1, width, 0, before)),
        "hid_next": (hid, rowed(1, width, 0, after)),
        "cell": (cell, rowed(depth, width, 0, lambda block: block)),
        "weights": (weights, pl.BlockSpec(memory_space=pl.ANY)),
        "bias": (bias, whole(bias)),
    }
    inputs |= ring
    aliases = {}
    for place, array in enumerate(carry):
        if array is not None:
            aliases[len(inputs)] = place
            inputs[f"carry{place}"] = (array, pl.BlockSpec(memory_space=pl.ANY))
    refs = [*inputs, "hid_out", "cell_out", "spread", "held", "sem"]
    scratch = [
        pltpu.VMEM((depth + 2, cols, 3 * (latent + width)), BF),
        pltpu.VMEM(weights.shape, BF),
        pltpu.SemaphoreType.DMA(()),
    ]
    if ring:
        refs += ["left", "right"]
        scratch += [pltpu.VMEM((ring["strips_hid"][0].shape[1], latent + width), F32)] * 2
    cells = extent[1] * cols
    return pl.pallas_call(
        functools.partial(conv_kernel, first, last, refs, packed),
        grid=(count,),
        in_specs=[spec for _, spec in inputs.values()],
        out_specs=out_specs,
        out_shape=out_shapes,
        scratch_shapes=scratch,
        input_output_aliases=aliases,
        compiler_params=pltpu.CompilerParams(vmem_limit_bytes=VMEM_LIMIT),
        cost_estimate=pl.CostEstimate(
            flops=2 * cells * weights.size, bytes_accessed=2 * weights.size + cells * 2048, transcendentals=cells * width * 5
        ),
    )(*(array for array, _ in inputs.values()))


def ring_kernel(
    rows, above, below, frame_top, frame_bot, hid_top, hid_bot, cell_top, cell_bot, strips, weights, bias,
    line_hid, line_cell, strip_hid, strip_cell,
):
    latent, width = frame_top.shape[2], hid_top.shape[2]
    chans = latent + width
    cols, length = frame_top.shape[1], strips.shape[2]
    low, high = strips[0, 1, :, :chans].astype(F32), strips[1, 2, :, :chans].astype(F32)

    def beside(ref, row):
        line = ref[row, :cols].astype(F32)
        return line[:, :chans], line[:, chans : chans + width]

    def within(frame, hid, cell, row):
        return jnp.concatenate([frame[row].astype(F32), hid[row].astype(F32)], axis=1), cell[row]

    tops = [beside(above, 0), beside(above, 1)] + [within(frame_top, hid_top, cell_top, row) for row in range(2)]
    bots = [within(frame_bot, hid_bot, cell_bot, row) for row in range(2)] + [beside(below, 0), beside(below, 1)]
    parts, held = [], []
    for lead, lines in ((0, tops), (rows, bots)):
        pieces = []
        for row in range(4):
            at = lead + row
            pieces.append(three_columns(lines[row][0], low[at : at + 1], high[at : at + 1]))
        for row in range(2):
            parts.append(jnp.concatenate([pieces[row + tap][col] for tap in range(3) for col in range(3)], axis=1))
            held.append(lines[row + 1][1])
    for side in range(2):
        rolled = []
        for col in range(4):
            wide = strips[side, col, :, :chans].astype(F32)
            rolled.append((pltpu.roll(wide, 1, axis=0), wide, pltpu.roll(wide, length - 1, axis=0)))
        for col in range(2):
            parts.append(
                jnp.concatenate([rolled[col + tap][row].astype(BF) for row in range(3) for tap in range(3)], axis=1)
            )
            held.append(strips[side, col + 1, :, chans : chans + width].astype(F32))
    row_at, col_at = lax.axis_index("gy"), lax.axis_index("gx")
    upper = (row_at > 0).astype(F32)
    lower = (row_at < lax.axis_size("gy") - 1).astype(F32)
    before = (col_at > 0).astype(F32)
    after = (col_at < lax.axis_size("gx") - 1).astype(F32)
    spot = lax.broadcasted_iota(jnp.int32, (length, width), 0)
    inside = jnp.where(spot == 1, upper, jnp.where(spot == rows + 2, lower, 1.0))
    keep = [upper, 1.0, 1.0, lower, inside * before, inside, inside, inside * after]
    lhs = jnp.concatenate(parts, axis=0)
    gates = jnp.dot(lhs, weights[...], preferred_element_type=F32) + bias[...]
    start = 0
    for place in range(8):
        hid, cell = (line_hid, line_cell) if place < 4 else (strip_hid, strip_cell)
        size = hid.shape[1]
        new_cell, hidden = lstm(gates[start : start + size], held[place])
        hid[place % 4] = hidden.astype(BF).astype(F32) * keep[place]
        cell[place % 4] = new_cell
        start += size


def block_kernel(x, w_qkv, w_out, w_up, w_down, out, flat, back, keys_t, own_low, own_high, own_values, ones):
    group = GRID * GRID
    embed = w_out.shape[0]
    tile = embed // 2

    @pl.when((pl.program_id(0) == 0) & (pl.program_id(1) == 0))
    def _():
        def fill(target, down, across, add):
            above = lax.broadcasted_iota(jnp.int32, target.shape, 0) // down
            along = lax.broadcasted_iota(jnp.int32, target.shape, 1) // across
            target[...] = (above == along + add).astype(F32).astype(BF)

        fill(own_low, HDIM, group, 0)
        fill(own_high, HDIM, group, HEADS // 4)
        fill(own_values, group, HDIM, 0)
        fill(ones, group, group, 0)
        keys_t[...] = w_qkv[:, embed : 2 * embed].astype(F32).T.astype(BF)

    flat[...] = x[...].astype(F32).reshape(flat.shape)
    groups = flat.shape[0] // group
    cells = jnp.concatenate([flat[pl.ds(g, group, stride=groups), :] for g in range(groups)], axis=0)
    normed = layer_norm(cells).astype(BF)
    queries = jnp.dot(normed, w_qkv[:, :embed], preferred_element_type=F32).astype(BF)
    values = jnp.dot(normed, w_qkv[:, 2 * embed :], preferred_element_type=F32).astype(BF)
    keys = lax.dot_general(keys_t[...], normed, (((1,), (1,)), ((), ())), preferred_element_type=F32)
    side = lax.broadcasted_iota(jnp.int32, (embed, 2 * group), 1) < group
    raised = [[], []]
    for pair in range(groups // 2):
        both = keys[:, pair * 2 * group : (pair + 1) * 2 * group]
        turned = pltpu.roll(both, group, axis=1)
        for place, twice in enumerate((jnp.where(side, both, turned), jnp.where(side, turned, both))):
            twice = twice.astype(BF)
            start = (2 * pair + place) * group
            for half in range(2):
                part = twice[half * tile : (half + 1) * tile]
                spread = jnp.concatenate([part * own_low[...], part * own_high[...]], axis=1)
                scores = jnp.dot(
                    queries[start : start + group, half * tile : (half + 1) * tile], spread, preferred_element_type=F32
                )
                raised[half].append(jnp.minimum(jnp.exp2(scores * (LOG2E * HDIM**-0.5)), BF_MAX).astype(BF))
    heads = []
    for half in range(2):
        part = jnp.concatenate(raised[half], axis=0)
        total = jnp.dot(part, ones[...], preferred_element_type=F32)
        attn = (part.astype(F32) * pl.reciprocal(total)).astype(BF)
        column = []
        for g in range(groups):
            held = values[g * group : (g + 1) * group, half * tile : (half + 1) * tile]
            spread = jnp.concatenate([held] * (HEADS // 2), axis=0) * own_values[...]
            column.append(
                jnp.dot(attn[g * group : (g + 1) * group], spread, preferred_element_type=F32).astype(BF)
            )
        heads.append(jnp.concatenate(column, axis=0))
    heads = jnp.concatenate(heads, axis=1)
    attended = jnp.dot(heads, w_out[...], preferred_element_type=F32).astype(BF)
    mixed = cells + attended.astype(F32)
    normed_two = layer_norm(mixed).astype(BF)
    up = jnp.dot(normed_two, w_up[...], preferred_element_type=F32)
    bent = jnp.tanh(up * (0.7978845608 + (0.7978845608 * 0.044715) * (up * up)))
    half_up = 0.5 * up
    expanded = (half_up + half_up * bent).astype(BF)
    result = mixed + jnp.dot(expanded, w_down[...], preferred_element_type=F32)
    for g in range(groups):
        back[pl.ds(g, group, stride=groups), :] = result[g * group : (g + 1) * group]
    out[...] = back[...].reshape(x.shape).astype(BF)


def block_step(moved, devices_y, devices_x, w_qkv, w_out, w_up, w_down):
    _, piece_y, piece_cols, width = moved.shape
    lanes = devices_y // GRID
    view = moved.reshape(GRID, lanes, devices_x, piece_y, piece_cols, width)
    tokens = GRID * devices_x * piece_cols
    spec = pl.BlockSpec(
        (GRID, None, devices_x, None, piece_cols, width), lambda i, j: (0, i, 0, j, 0, 0)
    )

    total = lanes * piece_y * tokens
    out = pl.pallas_call(
        block_kernel,
        grid=(lanes, piece_y),
        in_specs=[spec, whole(w_qkv), whole(w_out), whole(w_up), whole(w_down)],
        out_specs=spec,
        out_shape=jax.ShapeDtypeStruct(view.shape, BF),
        scratch_shapes=[
            pltpu.VMEM((tokens, width), F32),
            pltpu.VMEM((tokens, width), F32),
            pltpu.VMEM((w_out.shape[0], width), BF),
            pltpu.VMEM((HEADS // 2 * HDIM, 2 * GRID * GRID), BF),
            pltpu.VMEM((HEADS // 2 * HDIM, 2 * GRID * GRID), BF),
            pltpu.VMEM((HEADS // 2 * GRID * GRID, HEADS // 2 * HDIM), BF),
            pltpu.VMEM((HEADS // 2 * GRID * GRID, HEADS // 2 * GRID * GRID), BF),
        ],
        compiler_params=pltpu.CompilerParams(vmem_limit_bytes=VMEM_LIMIT),
        cost_estimate=pl.CostEstimate(
            flops=total * 3_000_000, bytes_accessed=total * width * 4 + 800_000, transcendentals=total * 1100
        ),
    )(view, w_qkv, w_out, w_up, w_down)
    return out.reshape(moved.shape)


def unpack_kernel(local_m, piece_x, *refs):
    src, out = refs[0], refs[-1]
    owners_y, owners_x, piece_y, _, width = src.shape
    for owner_y in range(owners_y):
        for row in range(piece_y):
            wide = src[owner_y, :, row].astype(F32)
            out[owner_y * piece_y + row] = jnp.concatenate(
                [wide[owner, m * piece_x : (m + 1) * piece_x] for m in range(local_m) for owner in range(owners_x)],
                axis=0,
            ).astype(BF)


def unpack_step(landed, carry, start, rows, cols, local_m, piece_x):
    owners_y, owners_x, piece_y, _, width = landed.shape
    depth = owners_y * piece_y
    specs = [pl.BlockSpec(landed.shape, lambda i: (0,) * landed.ndim)]
    operands = [landed]
    aliases = {}
    if carry is not None:
        specs.append(pl.BlockSpec(memory_space=pl.ANY))
        operands.append(carry)
        aliases = {1: 0}
    return pl.pallas_call(
        functools.partial(unpack_kernel, local_m, piece_x),
        grid=(1,),
        in_specs=specs,
        out_specs=pl.BlockSpec((depth, cols, width), lambda i: (start // depth, 0, 0)),
        out_shape=jax.ShapeDtypeStruct((rows, cols, width), BF),
        input_output_aliases=aliases,
        compiler_params=pltpu.CompilerParams(vmem_limit_bytes=VMEM_LIMIT),
        cost_estimate=pl.CostEstimate(flops=0, bytes_accessed=depth * cols * width * 4, transcendentals=0),
    )(*operands)


def step_rows(start, extent):
    return max(size for size in range(1, 17) if extent % size == 0 and start % size == 0)


def body(frames, hidden_state, cell_state, w_gates, gate_bias, w_qkv, w_out, w_up, w_down):
    rows, cols, width = hidden_state.shape
    latent = frames.shape[2] // 2
    chans = latent + width
    held = chans + width
    devices_y, devices_x = lax.axis_size("gy"), lax.axis_size("gx")
    local_m = GRID // devices_x
    piece_x = cols // local_m // devices_x
    weights = w_gates.reshape(-1, w_gates.shape[3])
    bias = gate_bias.reshape(1, -1)

    every, left_two, right_two = slice(None), slice(0, 2), slice(cols - 2, cols)
    top_two, bot_two = slice(0, 2), slice(rows - 2, rows)
    edges = ((every, left_two), (every, right_two), (top_two, every), (bot_two, every))
    edge_cells = lax.optimization_barrier(tuple(cell_state[edge] for edge in edges))

    def pack(edge, cells):
        return jnp.concatenate(
            [frames[edge][:, :, :latent], hidden_state[edge], cells.astype(BF), frames[edge][:, :, latent:]], axis=-1
        )

    def shifted(value, axis, step):
        count = lax.axis_size(axis)
        pairs = [(i, i + step) for i in range(count) if 0 <= i + step < count]
        return lax.ppermute(value, axis, pairs)

    side_left, side_right, line_top, line_bot = (pack(edge, cells) for edge, cells in zip(edges, edge_cells))
    from_left = shifted(side_right, "gx", 1)
    from_right = shifted(side_left, "gx", -1)
    from_up = shifted(jnp.concatenate([line_bot, from_left[-2:], from_right[-2:]], axis=1), "gy", 1)
    from_down = shifted(jnp.concatenate([line_top, from_left[:2], from_right[:2]], axis=1), "gy", -1)

    tile_shapes = (jax.ShapeDtypeStruct((rows, cols, width), BF), jax.ShapeDtypeStruct((rows, cols, width), F32))
    depth = step_rows(0, rows)
    spec = pl.BlockSpec((depth, cols, width), lambda step: (step, 0, 0))
    hidden_one, cell_one = conv_step(
        frames, 0, hidden_state, cell_state, {}, weights, bias, (0, rows), depth, tile_shapes, (spec, spec), None, ()
    )

    def column(at, middle):
        return jnp.concatenate([from_up[:, at], middle, from_down[:, at]], axis=0)

    columns = [
        column(cols, from_left[:, 0]),
        column(cols + 1, from_left[:, 1]),
        column(0, side_left[:, 0]),
        column(1, side_left[:, 1]),
        column(cols - 2, side_right[:, 0]),
        column(cols - 1, side_right[:, 1]),
        column(cols + 2, from_right[:, 0]),
        column(cols + 3, from_right[:, 1]),
    ]
    length = -(-(rows + 4) // 16) * 16
    strips = jnp.stack(columns).reshape(2, 4, rows + 4, held + latent)
    strips = jnp.pad(strips, ((0, 0), (0, 0), (0, length - rows - 4), (0, 0)))

    def two_rows(channels, at):
        return pl.BlockSpec((2, cols, channels), lambda step: (at, 0, 0))

    last_two = rows // 2 - 1
    line_shape = jax.ShapeDtypeStruct((4, cols, width), F32)
    strip_shape = jax.ShapeDtypeStruct((4, length, width), F32)
    line_hid, line_cell, strip_hid, strip_cell = pl.pallas_call(
        functools.partial(ring_kernel, rows),
        grid=(1,),
        in_specs=[
            whole(from_up), whole(from_down), two_rows(latent, 0), two_rows(latent, last_two), two_rows(width, 0),
            two_rows(width, last_two), two_rows(width, 0), two_rows(width, last_two), whole(strips), whole(weights),
            whole(bias),
        ],
        out_specs=[whole(line_shape), whole(line_shape), whole(strip_shape), whole(strip_shape)],
        out_shape=[line_shape, line_shape, strip_shape, strip_shape],
        compiler_params=pltpu.CompilerParams(vmem_limit_bytes=VMEM_LIMIT),
        cost_estimate=pl.CostEstimate(flops=16 * length * weights.size, bytes_accessed=2 * weights.size, transcendentals=0),
    )(
        from_up, from_down, frames, frames, hidden_state, hidden_state, cell_state, cell_state, strips, weights, bias
    )

    second = held // latent
    beside = (1, 1, length, latent)
    line = (1, from_up.shape[1], latent)
    ring = {name: (array, whole(array)) for name, array in (
        ("strips_hid", strip_hid), ("strips_cell", strip_cell), ("lines_hid", line_hid), ("lines_cell", line_cell)
    )}
    ring["frame_left"] = strips, pl.BlockSpec(beside, lambda step: (0, 1, 0, second))
    ring["frame_right"] = strips, pl.BlockSpec(beside, lambda step: (1, 2, 0, second))
    ring["frame_top"] = from_up, pl.BlockSpec(line, lambda step: (1, 0, second))
    ring["frame_bot"] = from_down, pl.BlockSpec(line, lambda step: (0, 0, second))

    pieces = rows // devices_y
    piece_cols = local_m * piece_x
    cell_out, moved, start = None, [], 0
    for piece_y in (pieces - pieces // 2, pieces // 2):
        extent = piece_y * devices_y
        depth = step_rows(start, extent)
        sent_shape = jax.ShapeDtypeStruct((devices_y, devices_x, piece_y, piece_cols, width), BF)
        sent, cell_out = conv_step(
            frames, 1, hidden_one, cell_one, ring, weights, bias, (start, extent), depth, (sent_shape, tile_shapes[1]),
            (
                whole(sent_shape),
                pl.BlockSpec((depth, cols, width), lambda step, first=start // depth: (first + step, 0, 0)),
            ),
            (local_m, piece_x), (None, cell_out),
        )
        sent = sent.reshape(devices_y * devices_x, piece_y, piece_cols, width)
        moved.append((start, lax.all_to_all(sent, ("gy", "gx"), split_axis=0, concat_axis=0, tiled=True)))
        start += extent
    landed = []
    for start, value in moved:
        done = block_step(value, devices_y, devices_x, w_qkv, w_out, w_up, w_down)
        landed.append((start, lax.all_to_all(done, ("gy", "gx"), split_axis=0, concat_axis=0, tiled=True)))
    result = None
    for start, value in landed:
        view = value.reshape(devices_y, devices_x, *value.shape[1:])
        result = unpack_step(view, result, start, rows, cols, local_m, piece_x)
    return result, cell_out


def solution(mesh):
    tiled = P("gy", "gx", None)
    in_specs = (tiled, tiled, tiled, P(), P(), P(), P(), P(), P())
    return jax.shard_map(body, mesh=mesh, in_specs=in_specs, out_specs=(tiled, tiled), check_vma=False)
```

time: 145 us -> 131 us (0.903)
  Pallas kernels: 74.9 us -> 66.8 us
  waiting for transfers between devices: 18.4 us -> 25.2 us
  other arithmetic: 5.5 us -> 0.6 us
  starting transfers between devices: 31.6 us -> 27.1 us
  local copies, waits for them, and re-layouts: 12.1 us -> 8.87 us
    pallas_call x2, Pallas kernels: 22.2 us -> 17.7 us  [block_step(): pl.pallas_call(block_kernel, grid=(lanes, piece_y), in_specs=[spec, whole...]
    pallas_call x5 -> x4, Pallas kernels: 49.1 us -> 45.4 us  [the longest x3 40 us: conv_step(): pl.pallas_call(functools.partial(conv_kernel, first, last, refs, packed),...]
    all_to_all x2, starting transfers between devices: 8.41 us -> 5.88 us  [body(): lax.all_to_all(done, ('gy', 'gx'), split_axis=0, concat_axis=0, tiled=True)]
    another operation x5 -> x1, other arithmetic: 2.47 us -> 0.03 us  [body(): strips = jnp.stack(columns).reshape(2, 4, rows + 4, held + latent)]
    all_to_all x2, waiting for transfers between devices: 3.05 us -> 5.39 us  [body(): lax.all_to_all(sent, ('gy', 'gx'), split_axis=0, concat_axis=0, tiled=True)]
    ppermute x4, waiting for transfers between devices: 2.8 us -> 5.03 us  [shifted(): return lax.ppermute(value, axis, pairs)]
    all_to_all x2, waiting for transfers between devices: 12.6 us -> 14.8 us  [body(): lax.all_to_all(done, ('gy', 'gx'), split_axis=0, concat_axis=0, tiled=True)]
    pallas_call x2 -> x0, local copies, waits for them, and re-layouts: 1.98 us -> none  [body(): pl.pallas_call(ring_kernel, out_shape=ring_shapes, compiler_params=pltpu....]
  transfers between devices with their start and end apart: 8 -> 8, of which waited for: 6 -> 6; matrix products, arithmetic and copies ran while one was open for 2% -> 2% of each run, Pallas kernels for 39% -> 37%
where the time goes in v2:
time: 131 us; the launch traced here: 130 us
  Pallas kernels  66.8 us (51%)
  starting transfers between devices  27.1 us (21%)
  waiting for transfers between devices  25.2 us (19%)
  local copies, waits for them, and re-layouts  8.87 us (7%)
    pallas_call x3, Pallas kernels, conv_step(): pl.pallas_call(functools.partial(conv_kernel, first, last, refs, packed),...  40 us
    pallas_call x2, Pallas kernels, block_step(): pl.pallas_call(block_kernel, grid=(lanes, piece_y), in_specs=[spec, whole...  17.7 us
    all_to_all x2, waiting for transfers between devices, body(): lax.all_to_all(done, ('gy', 'gx'), split_axis=0, concat_axis=0, tiled=True)  14.8 us
    ppermute x4, starting transfers between devices, shifted(): return lax.ppermute(value, axis, pairs)  12.3 us
    all_to_all x2, starting transfers between devices, body(): lax.all_to_all(sent, ('gy', 'gx'), split_axis=0, concat_axis=0, tiled=True)  8.99 us
    all_to_all x2, starting transfers between devices, body(): lax.all_to_all(done, ('gy', 'gx'), split_axis=0, concat_axis=0, tiled=True)  5.88 us
    pallas_call x1, Pallas kernels, body(): pl.pallas_call(functools.partial(ring_kernel, rows), grid=(1,), in_specs=...  5.4 us
    all_to_all x2, waiting for transfers between devices, body(): lax.all_to_all(sent, ('gy', 'gx'), split_axis=0, concat_axis=0, tiled=True)  5.39 us
  transfers between devices with their start and end apart: 8, of which 6 were waited for; matrix products, arithmetic and copies ran while one was open for 2% of the time, Pallas kernels for 37%

profile of v2, /device:TPU:1, one launch (start us, length us, event | category | flops | bytes accessed | tf_op | source)
XLA Modules:
  0.0 129.6 jit_solution(3312333005049760392)
XLA Ops:
  0.6 1.1 fusion.11
  2.6 1.0 fusion.13
  3.6 1.4 %fusion.9 = (bf16[48,2,256]{2,1,0:T(2,128)(2,1)S(1)}, bf16[48,2,256]{2,1,0:T(2,128)(2,1)S(1)}, bf16[48,2,256]{2,1,0:T(2,128)(2,1)S(1)}, bf16[48,2,256]{2,1,0:T(2,128)(2,1)S(1)}) fusion(bf16[48,64,512]{2,1,0:T(8,128)(2,1)} %args_2_.8), kind=kLoop, calls=%fused_computation.45 | loop fusion | bytes 393216 | tf_op jit(solution)/shard_map/slice | solution.py:410
  5.1 1.3 collective-permute-start.1
  6.6 4.7 %collective-permute-start = (bf16[48,2,768]{2,1,0:T(2,128)(2,1)S(1)}, bf16[48,2,768]{2,1,0:T(2,128)(2,1)S(1)}, u32[]{:S(2)}, u32[]{:S(2)}) collective-permute-start(bf16[48,2,768]{2,1,0:T(2,128)(2,1)S(1)} %pad_maximum_fusion.2), channel_id=1, source_target_pairs={{0,1},{1,2},{2,3},{4,5},{5,6},{6,7},{8,9},{9,10},{10,11},{12,13},{... | collective-permute-start | bytes 442376 | tf_op jit(solution)/shard_map/ppermute | solution.py:416
  12.7 17.6 %shard_map.104 = (bf16[48,64,128]{2,1,0:T(8,128)(2,1)}, f32[48,64,128]{2,1,0:T(8,128)}) custom-call(bf16[48,64,512]{2,1,0:T(8,128)(2,1)} %args_2_.8, bf16[48,64,512]{2,1,0:T(8,128)(2,1)} %args_2_.8, bf16[48,64,512]{2,1,0:T(8,128)(2,1)} %args_2_.8, bf16[48,64,128]{2,1,0:T(8,128)(2,1)} %hid_bot.1, bf16[48,64,128]{2,1,0:T(8,128)(2,1)} %hid_bot.1, ...), custom_call_target="tpu_custom_call" | custom-call | flops 10871635968 | bytes 9830400 | tf_op jit(solution)/shard_map/pallas_call | solution.py:182
  31.4 4.4 %collective-permute-start.2 = (bf16[2,68,768]{2,1,0:T(8,128)(2,1)S(1)}, bf16[2,68,768]{2,1,0:T(8,128)(2,1)S(1)}, u32[]{:S(2)}, u32[]{:S(2)}) collective-permute-start(bf16[2,68,768]{2,1,0:T(8,128)(2,1)S(1)} %pad_maximum_fusion), channel_id=1, source_target_pairs={{0,4},{4,8},{8,12},{12,16},{16,20},{20,24},{24,28},{1,5},{5,9},{9,... | collective-permute-start | bytes 626696 | tf_op jit(solution)/shard_map/ppermute | solution.py:416
  35.9 1.9 %collective-permute-start.3 = (bf16[2,68,768]{2,1,0:T(8,128)(2,1)S(1)}, bf16[2,68,768]{2,1,0:T(8,128)(2,1)S(1)}, u32[]{:S(2)}, u32[]{:S(2)}) collective-permute-start(bf16[2,68,768]{2,1,0:T(8,128)(2,1)S(1)} %pad_maximum_fusion.1), channel_id=1, source_target_pairs={{4,0},{8,4},{12,8},{16,12},{20,16},{24,20},{28,24},{5,1},{9,5},{13... | collective-permute-start | bytes 626696 | tf_op jit(solution)/shard_map/ppermute | solution.py:416
  38.7 4.4 %collective-permute-done.3.below.args_16_ = bf16[2,68,768]{2,1,0:T(8,128)(2,1)S(1)} collective-permute-done((bf16[2,68,768]{2,1,0:T(8,128)(2,1)S(1)}, bf16[2,68,768]{2,1,0:T(8,128)(2,1)S(1)}, u32[]{:S(2)}, u32[]{:S(2)}) %collective-permute-start.3) | collective-permute-done | bytes 208928 | tf_op jit(solution)/shard_map/ppermute | solution.py:416
  44.6 5.4 %shard_map.105 = (f32[4,64,128]{2,1,0:T(8,128)}, f32[4,64,128]{2,1,0:T(8,128)}, f32[4,64,128]{2,1,0:T(8,128)}, f32[4,64,128]{2,1,0:T(8,128)}) custom-call(bf16[2,68,768]{2,1,0:T(8,128)(2,1)} %copy-done.2, bf16[2,68,768]{2,1,0:T(8,128)(2,1)} %copy-done.3, bf16[48,64,512]{2,1,0:T(8,128)(2,1)} %args_2_.8, bf16[48,64,512]{2,1,0:T(8,128)(2,1)} %args_2_.8, ...), custom_call_target="tpu_custom_call" | custom-call | flops 1811939328 | bytes 3538944 | tf_op jit(solution)/shard_map/pallas_call | solution.py:454
  50.0 11.2 %shard_map.106 = (bf16[8,4,3,16,128]{4,3,2,1,0:T(8,128)(2,1)}, f32[48,64,128]{2,1,0:T(8,128)}) custom-call(bf16[48,64,512]{2,1,0:T(8,128)(2,1)} %args_2_.8, bf16[48,64,512]{2,1,0:T(8,128)(2,1)} %args_2_.8, bf16[48,64,512]{2,1,0:T(8,128)(2,1)} %args_2_.8, bf16[48,64,128]{2,1,0:T(8,128)(2,1)} %get-tuple-element.16.args_3_.args_4_.args_5_, ...), custom_call_target="tpu_custom_call" | custom-call | flops 5435817984 | bytes 6684672 | tf_op jit(solution)/shard_map/pallas_call | solution.py:182
  61.2 4.6 %all-to-all-start.2 = ((bf16[32,3,16,128]{3,2,1,0:T(8,128)(2,1)}), bf16[32,3,16,128]{3,2,1,0:T(8,128)(2,1)S(1)}, u32[]{:S(2)}, u32[]{:S(2)}) async-start(bf16[32,3,16,128]{3,2,1,0:T(8,128)(2,1)} %bitcast.106), calls=%async_computation.2 | async-start | bytes 786432 | tf_op jit(solution)/shard_map/all_to_all | solution.py:497
  65.8 11.2 %shard_map.107 = (bf16[8,4,3,16,128]{4,3,2,1,0:T(8,128)(2,1)}, f32[48,64,128]{2,1,0:T(8,128)}) custom-call(bf16[48,64,512]{2,1,0:T(8,128)(2,1)} %args_2_.8, bf16[48,64,512]{2,1,0:T(8,128)(2,1)} %args_2_.8, bf16[48,64,512]{2,1,0:T(8,128)(2,1)} %args_2_.8, ...), custom_call_target="tpu_custom_call", output_to_operand_aliasing={{1}: (17, {})} | custom-call | flops 5435817984 | bytes 6684672 | tf_op jit(solution)/shard_map/pallas_call | solution.py:182
  77.1 1.5 %all-to-all-done.2 = bf16[32,3,16,128]{3,2,1,0:T(8,128)(2,1)S(1)} async-done(((bf16[32,3,16,128]{3,2,1,0:T(8,128)(2,1)}), bf16[32,3,16,128]{3,2,1,0:T(8,128)(2,1)S(1)}, u32[]{:S(2)}, u32[]{:S(2)}) %all-to-all-start.2) | async-done | bytes 393248 | tf_op jit(solution)/shard_map/all_to_all | solution.py:497
  78.6 4.3 %all-to-all-start = ((bf16[32,3,16,128]{3,2,1,0:T(8,128)(2,1)}), bf16[32,3,16,128]{3,2,1,0:T(8,128)(2,1)S(1)}, u32[]{:S(2)}, u32[]{:S(2)}) async-start(bf16[32,3,16,128]{3,2,1,0:T(8,128)(2,1)} %bitcast.105), calls=%async_computation | async-start | bytes 786432 | tf_op jit(solution)/shard_map/all_to_all | solution.py:497
  83.0 8.9 %shard_map.109 = bf16[8,1,4,3,16,128]{5,4,3,2,1,0:T(8,128)(2,1)} custom-call(bf16[8,1,4,3,16,128]{5,4,3,2,1,0:T(8,128)(2,1)} %bitcast.104, bf16[128,768]{1,0:T(8,128)(2,1)} %w_qkv.3, bf16[256,128]{1,0:T(8,128)(2,1)} %w_out.3, bf16[128,512]{1,0:T(8,128)(2,1)} %w_up.3, bf16[512,128]{1,0:T(8,128)(2,1)} %w_down.3), custom_call_target="tpu_custom_call" | custom-call | flops 4608000000 | bytes 1586432 | tf_op jit(solution)/shard_map/pallas_call | solution.py:331
  91.8 3.9 %all-to-all-done = bf16[32,3,16,128]{3,2,1,0:T(8,128)(2,1)S(1)} async-done(((bf16[32,3,16,128]{3,2,1,0:T(8,128)(2,1)}), bf16[32,3,16,128]{3,2,1,0:T(8,128)(2,1)S(1)}, u32[]{:S(2)}, u32[]{:S(2)}) %all-to-all-start) | async-done | bytes 393248 | tf_op jit(solution)/shard_map/all_to_all | solution.py:497
  95.7 2.9 %all-to-all-start.3 = ((bf16[32,3,16,128]{3,2,1,0:T(8,128)(2,1)}), bf16[32,3,16,128]{3,2,1,0:T(8,128)(2,1)S(1)}, u32[]{:S(2)}, u32[]{:S(2)}) async-start(bf16[32,3,16,128]{3,2,1,0:T(8,128)(2,1)} %bitcast.108), calls=%async_computation.3 | async-start | bytes 786432 | tf_op jit(solution)/shard_map/all_to_all | solution.py:502
  98.6 8.9 %shard_map.108 = bf16[8,1,4,3,16,128]{5,4,3,2,1,0:T(8,128)(2,1)} custom-call(bf16[8,1,4,3,16,128]{5,4,3,2,1,0:T(8,128)(2,1)} %bitcast.107, bf16[128,768]{1,0:T(8,128)(2,1)} %w_qkv.3, bf16[256,128]{1,0:T(8,128)(2,1)} %w_out.3, bf16[128,512]{1,0:T(8,128)(2,1)} %w_up.3, bf16[512,128]{1,0:T(8,128)(2,1)} %w_down.3), custom_call_target="tpu_custom_call" | custom-call | flops 4608000000 | bytes 1586432 | tf_op jit(solution)/shard_map/pallas_call | solution.py:331
  107.5 3.9 %all-to-all-done.3 = bf16[32,3,16,128]{3,2,1,0:T(8,128)(2,1)S(1)} async-done(((bf16[32,3,16,128]{3,2,1,0:T(8,128)(2,1)}), bf16[32,3,16,128]{3,2,1,0:T(8,128)(2,1)S(1)}, u32[]{:S(2)}, u32[]{:S(2)}) %all-to-all-start.3) | async-done | bytes 393248 | tf_op jit(solution)/shard_map/all_to_all | solution.py:502
  111.4 2.9 %all-to-all-start.1 = ((bf16[32,3,16,128]{3,2,1,0:T(8,128)(2,1)}), bf16[32,3,16,128]{3,2,1,0:T(8,128)(2,1)S(1)}, u32[]{:S(2)}, u32[]{:S(2)}) async-start(bf16[32,3,16,128]{3,2,1,0:T(8,128)(2,1)} %bitcast.109), calls=%async_computation.1 | async-start | bytes 786432 | tf_op jit(solution)/shard_map/all_to_all | solution.py:502
  114.3 1.8 %shard_map.110.refs_1_ = bf16[48,64,128]{2,1,0:T(8,128)(2,1)} custom-call(bf16[8,4,3,16,128]{4,3,2,1,0:T(8,128)(2,1)} %bitcast.101), custom_call_target="tpu_custom_call" | custom-call | bytes 786432 | tf_op jit(solution)/shard_map/pallas_call | solution.py:376
  116.1 10.9 %all-to-all-done.1 = bf16[32,3,16,128]{3,2,1,0:T(8,128)(2,1)S(1)} async-done(((bf16[32,3,16,128]{3,2,1,0:T(8,128)(2,1)}), bf16[32,3,16,128]{3,2,1,0:T(8,128)(2,1)S(1)}, u32[]{:S(2)}, u32[]{:S(2)}) %all-to-all-start.1) | async-done | bytes 393248 | tf_op jit(solution)/shard_map/all_to_all | solution.py:502
  127.8 1.8 %shard_map.111 = bf16[48,64,128]{2,1,0:T(8,128)(2,1)} custom-call(bf16[8,4,3,16,128]{4,3,2,1,0:T(8,128)(2,1)} %bitcast.102, bf16[48,64,128]{2,1,0:T(8,128)(2,1)} %shard_map.110.refs_1_), custom_call_target="tpu_custom_call", output_to_operand_aliasing={{}: (1, {})} | custom-call | bytes 786432 | tf_op jit(solution)/shard_map/pallas_call | solution.py:376
  (54 shorter events, 6.7 us)
Async XLA Ops:
  5.1 26.0 %collective-permute-start.1 = (bf16[48,2,768]{2,1,0:T(2,128)(2,1)S(1)}, bf16[48,2,768]{2,1,0:T(2,128)(2,1)S(1)}, u32[]{:S(2)}, u32[]{:S(2)}) collective-permute-start(bf16[48,2,768]{2,1,0:T(2,128)(2,1)S(1)} %pad_maximum_fusion.3), channel_id=1, source_target_pairs={{1,0},{2,1},{3,2},{5,4},{6,5},{7,6},{9,8},{10,9},{11,10},{13,12},{... | collective-permute-start | bytes 442376 | tf_op jit(solution)/shard_map/ppermute | solution.py:416
  6.6 24.8 %collective-permute-start = (bf16[48,2,768]{2,1,0:T(2,128)(2,1)S(1)}, bf16[48,2,768]{2,1,0:T(2,128)(2,1)S(1)}, u32[]{:S(2)}, u32[]{:S(2)}) collective-permute-start(bf16[48,2,768]{2,1,0:T(2,128)(2,1)S(1)} %pad_maximum_fusion.2), channel_id=1, source_target_pairs={{0,1},{1,2},{2,3},{4,5},{5,6},{6,7},{8,9},{9,10},{10,11},{12,13},{... | collective-permute-start | bytes 442376 | tf_op jit(solution)/shard_map/ppermute | solution.py:416
  31.4 7.3 %collective-permute-start.2 = (bf16[2,68,768]{2,1,0:T(8,128)(2,1)S(1)}, bf16[2,68,768]{2,1,0:T(8,128)(2,1)S(1)}, u32[]{:S(2)}, u32[]{:S(2)}) collective-permute-start(bf16[2,68,768]{2,1,0:T(8,128)(2,1)S(1)} %pad_maximum_fusion), channel_id=1, source_target_pairs={{0,4},{4,8},{8,12},{12,16},{16,20},{20,24},{24,28},{1,5},{5,9},{9,... | collective-permute-start | bytes 626696 | tf_op jit(solution)/shard_map/ppermute | solution.py:416
  35.9 7.3 %collective-permute-start.3 = (bf16[2,68,768]{2,1,0:T(8,128)(2,1)S(1)}, bf16[2,68,768]{2,1,0:T(8,128)(2,1)S(1)}, u32[]{:S(2)}, u32[]{:S(2)}) collective-permute-start(bf16[2,68,768]{2,1,0:T(8,128)(2,1)S(1)} %pad_maximum_fusion.1), channel_id=1, source_target_pairs={{4,0},{8,4},{12,8},{16,12},{20,16},{24,20},{28,24},{5,1},{9,5},{13... | collective-permute-start | bytes 626696 | tf_op jit(solution)/shard_map/ppermute | solution.py:416
  38.7 5.9 %copy-start.2 = (bf16[2,68,768]{2,1,0:T(8,128)(2,1)}, bf16[2,68,768]{2,1,0:T(8,128)(2,1)S(1)}, u32[]{:S(2)}) copy-start(bf16[2,68,768]{2,1,0:T(8,128)(2,1)S(1)} %collective-permute-done.2.above.args_15_) | copy-start | bytes 626692
  43.1 1.4 %copy-start.3 = (bf16[2,68,768]{2,1,0:T(8,128)(2,1)}, bf16[2,68,768]{2,1,0:T(8,128)(2,1)S(1)}, u32[]{:S(2)}) copy-start(bf16[2,68,768]{2,1,0:T(8,128)(2,1)S(1)} %collective-permute-done.3.below.args_16_) | copy-start | bytes 626692
  61.2 17.4 %all-to-all-start.2 = ((bf16[32,3,16,128]{3,2,1,0:T(8,128)(2,1)}), bf16[32,3,16,128]{3,2,1,0:T(8,128)(2,1)S(1)}, u32[]{:S(2)}, u32[]{:S(2)}) async-start(bf16[32,3,16,128]{3,2,1,0:T(8,128)(2,1)} %bitcast.106), calls=%async_computation.2 | async-start | bytes 786432 | tf_op jit(solution)/shard_map/all_to_all | solution.py:497
  78.6 4.4 %copy-start.4 = (bf16[32,3,16,128]{3,2,1,0:T(8,128)(2,1)}, bf16[32,3,16,128]{3,2,1,0:T(8,128)(2,1)S(1)}, u32[]{:S(2)}) copy-start(bf16[32,3,16,128]{3,2,1,0:T(8,128)(2,1)S(1)} %all-to-all-done.2) | copy-start | bytes 1179652
  78.6 17.1 %all-to-all-start = ((bf16[32,3,16,128]{3,2,1,0:T(8,128)(2,1)}), bf16[32,3,16,128]{3,2,1,0:T(8,128)(2,1)S(1)}, u32[]{:S(2)}, u32[]{:S(2)}) async-start(bf16[32,3,16,128]{3,2,1,0:T(8,128)(2,1)} %bitcast.105), calls=%async_computation | async-start | bytes 786432 | tf_op jit(solution)/shard_map/all_to_all | solution.py:497
  95.7 3.0 %copy-start.5 = (bf16[32,3,16,128]{3,2,1,0:T(8,128)(2,1)}, bf16[32,3,16,128]{3,2,1,0:T(8,128)(2,1)S(1)}, u32[]{:S(2)}) copy-start(bf16[32,3,16,128]{3,2,1,0:T(8,128)(2,1)S(1)} %all-to-all-done) | copy-start | bytes 1179652
  95.7 15.7 %all-to-all-start.3 = ((bf16[32,3,16,128]{3,2,1,0:T(8,128)(2,1)}), bf16[32,3,16,128]{3,2,1,0:T(8,128)(2,1)S(1)}, u32[]{:S(2)}, u32[]{:S(2)}) async-start(bf16[32,3,16,128]{3,2,1,0:T(8,128)(2,1)} %bitcast.108), calls=%async_computation.3 | async-start | bytes 786432 | tf_op jit(solution)/shard_map/all_to_all | solution.py:502
  111.4 3.0 %copy-start = (bf16[32,3,16,128]{3,2,1,0:T(8,128)(2,1)}, bf16[32,3,16,128]{3,2,1,0:T(8,128)(2,1)S(1)}, u32[]{:S(2)}) copy-start(bf16[32,3,16,128]{3,2,1,0:T(8,128)(2,1)S(1)} %all-to-all-done.3) | copy-start | bytes 1179652
  111.4 15.7 %all-to-all-start.1 = ((bf16[32,3,16,128]{3,2,1,0:T(8,128)(2,1)}), bf16[32,3,16,128]{3,2,1,0:T(8,128)(2,1)S(1)}, u32[]{:S(2)}, u32[]{:S(2)}) async-start(bf16[32,3,16,128]{3,2,1,0:T(8,128)(2,1)} %bitcast.109), calls=%async_computation.1 | async-start | bytes 786432 | tf_op jit(solution)/shard_map/all_to_all | solution.py:502
  127.1 0.7 copy-start.1

commit v3 on v2

--- a/solution.py
+++ b/solution.py
@@ -14,7 +14,9 @@
 F32 = jnp.float32
 LOG2E = 1.4426950408889634
 BF_MAX = 3.3895313892515355e38
-VMEM_LIMIT = 60 * 1024 * 1024
+VMEM_LIMIT = 32 * 1024 * 1024
+VMEM_ALL = 60 * 1024 * 1024
+LOADS = 9
 
 
 def sigmoid(x):
@@ -48,18 +50,32 @@
 def conv_kernel(first, last, refs, packed, *args):
     ref = dict(zip(refs, args))
     frame, hid = ref["frame"], ref["hid"]
-    hid_out, cell_out, spread = ref["hid_out"], ref["cell_out"], ref["spread"]
+    cell_out, spread = ref["cell_out"], ref["spread"]
     ring = "strips_hid" in ref
     step = pl.program_id(0)
     depth, cols, latent = frame.shape
     width = hid.shape[2]
     chans = latent + width
-    load = pltpu.make_async_copy(ref["weights"], ref["held"], ref["sem"])
-
-    @pl.when(step == 0)
-    def _():
-        load.start()
-        if ring:
+    loads = []
+    if "weights" in ref:
+        size = ref["weights"].shape[0] // LOADS
+        for place in range(LOADS):
+            part = pl.ds(place * size, size)
+            loads.append(
+                pltpu.make_async_copy(ref["weights"].at[part], ref["held"].at[part], ref["sem"].at[place])
+            )
+
+    if loads:
+
+        @pl.when(step == 0)
+        def _():
+            for load in loads:
+                load.start()
+
+    if ring:
+
+        @pl.when(step == 0)
+        def _():
             for side, strip, frames_beside in (("left", 0, "frame_left"), ("right", 3, "frame_right")):
                 ref[side][:, :latent] = ref[frames_beside][0, 0].astype(F32)
                 ref[side][:, latent:] = ref["strips_hid"][strip]
@@ -98,9 +114,12 @@
             for tap in range(3):
                 spread[pos, :, tap * chans + start : tap * chans + start + size] = pieces[tap]
 
-    @pl.when(step == 0)
-    def _():
-        load.wait()
+    if loads:
+
+        @pl.when(step == 0)
+        def _():
+            for load in loads:
+                load.wait()
 
     lhs = jnp.concatenate(
         [spread[tap : tap + depth].reshape(depth * cols, 3 * chans) for tap in range(3)], axis=1
@@ -119,6 +138,7 @@
                 cell_prev = jnp.where(bot, ref["lines_cell"][2], cell_prev)
         new_cell, new_hidden = lstm(gates[row * cols : (row + 1) * cols], cell_prev)
         cell_out[row] = new_cell
+        hid_out = ref["hid_out"]
         if not packed:
             hid_out[row] = new_hidden.astype(BF)
             continue
@@ -137,7 +157,7 @@
     return pl.BlockSpec(array.shape, lambda *step: (0,) * array.ndim)
 
 
-def conv_step(frames, part, hid, cell, ring, weights, bias, extent, depth, out_shapes, out_specs, packed, carry):
+def conv_step(frames, part, hid, cell, ring, weights, bias, extent, depth, names, out_shapes, out_specs, packed, carry, load):
     rows, cols, width = hid.shape
     latent = weights.shape[0] // 9 - width
     first, count = extent[0] // depth, extent[1] // depth
@@ -160,24 +180,26 @@
         "hid_prev": (hid, rowed(1, width, 0, before)),
         "hid_next": (hid, rowed(1, width, 0, after)),
         "cell": (cell, rowed(depth, width, 0, lambda block: block)),
-        "weights": (weights, pl.BlockSpec(memory_space=pl.ANY)),
         "bias": (bias, whole(bias)),
     }
+    if load:
+        inputs["weights"] = weights, pl.BlockSpec(memory_space=pl.ANY)
+    else:
+        inputs["held"] = weights, pl.BlockSpec(memory_space=pltpu.VMEM)
     inputs |= ring
     aliases = {}
     for place, array in enumerate(carry):
         if array is not None:
             aliases[len(inputs)] = place
             inputs[f"carry{place}"] = (array, pl.BlockSpec(memory_space=pl.ANY))
-    refs = [*inputs, "hid_out", "cell_out", "spread", "held", "sem"]
-    scratch = [
-        pltpu.VMEM((depth + 2, cols, 3 * (latent + width)), BF),
-        pltpu.VMEM(weights.shape, BF),
-        pltpu.SemaphoreType.DMA(()),
-    ]
+    refs = [*inputs, *names, "spread"]
+    scratch = [pltpu.VMEM((depth + 2, cols, 3 * (latent + width)), BF)]
     if ring:
         refs += ["left", "right"]
         scratch += [pltpu.VMEM((ring["strips_hid"][0].shape[1], latent + width), F32)] * 2
+    if load:
+        refs += ["held", "sem"]
+        scratch += [pltpu.VMEM(weights.shape, BF), pltpu.SemaphoreType.DMA((LOADS,))]
     cells = extent[1] * cols
     return pl.pallas_call(
         functools.partial(conv_kernel, first, last, refs, packed),
@@ -187,7 +209,7 @@
         out_shape=out_shapes,
         scratch_shapes=scratch,
         input_output_aliases=aliases,
-        compiler_params=pltpu.CompilerParams(vmem_limit_bytes=VMEM_LIMIT),
+        compiler_params=pltpu.CompilerParams(vmem_limit_bytes=VMEM_ALL if load else VMEM_LIMIT),
         cost_estimate=pl.CostEstimate(
             flops=2 * cells * weights.size, bytes_accessed=2 * weights.size + cells * 2048, transcendentals=cells * width * 5
         ),
@@ -418,15 +440,22 @@
     side_left, side_right, line_top, line_bot = (pack(edge, cells) for edge, cells in zip(edges, edge_cells))
     from_left = shifted(side_right, "gx", 1)
     from_right = shifted(side_left, "gx", -1)
-    from_up = shifted(jnp.concatenate([line_bot, from_left[-2:], from_right[-2:]], axis=1), "gy", 1)
-    from_down = shifted(jnp.concatenate([line_top, from_left[:2], from_right[:2]], axis=1), "gy", -1)
+    to_down = jnp.concatenate([line_bot, from_left[-2:], from_right[-2:]], axis=1)
+    to_up = jnp.concatenate([line_top, from_left[:2], from_right[:2]], axis=1)
 
     tile_shapes = (jax.ShapeDtypeStruct((rows, cols, width), BF), jax.ShapeDtypeStruct((rows, cols, width), F32))
-    depth = step_rows(0, rows)
-    spec = pl.BlockSpec((depth, cols, width), lambda step: (step, 0, 0))
-    hidden_one, cell_one = conv_step(
-        frames, 0, hidden_state, cell_state, {}, weights, bias, (0, rows), depth, tile_shapes, (spec, spec), None, ()
-    )
+    carry = ()
+    for start, extent in ((0, rows // 2), (rows // 2, rows - rows // 2)):
+        depth = step_rows(start, extent)
+        spec = pl.BlockSpec((depth, cols, width), lambda step, first=start // depth: (first + step, 0, 0))
+        if carry:
+            *carry, to_down, to_up = lax.optimization_barrier((*carry, to_down, to_up))
+            from_up, from_down = shifted(to_down, "gy", 1), shifted(to_up, "gy", -1)
+        carry = conv_step(
+            frames, 0, hidden_state, cell_state, {}, weights, bias, (start, extent), depth, ("hid_out", "cell_out"),
+            tile_shapes, (spec, spec), None, carry, False,
+        )
+    hidden_one, cell_one = carry
 
     def column(at, middle):
         return jnp.concatenate([from_up[:, at], middle, from_down[:, at]], axis=0)
@@ -456,8 +485,8 @@
         grid=(1,),
         in_specs=[
             whole(from_up), whole(from_down), two_rows(latent, 0), two_rows(latent, last_two), two_rows(width, 0),
-            two_rows(width, last_two), two_rows(width, 0), two_rows(width, last_two), whole(strips), whole(weights),
-            whole(bias),
+            two_rows(width, last_two), two_rows(width, 0), two_rows(width, last_two), whole(strips),
+            pl.BlockSpec(memory_space=pltpu.VMEM),            whole(bias),
         ],
         out_specs=[whole(line_shape), whole(line_shape), whole(strip_shape), whole(strip_shape)],
         out_shape=[line_shape, line_shape, strip_shape, strip_shape],
@@ -480,19 +509,17 @@
 
     pieces = rows // devices_y
     piece_cols = local_m * piece_x
-    cell_out, moved, start = None, [], 0
+    moved, start, carry = [], 0, ()
     for piece_y in (pieces - pieces // 2, pieces // 2):
         extent = piece_y * devices_y
         depth = step_rows(start, extent)
         sent_shape = jax.ShapeDtypeStruct((devices_y, devices_x, piece_y, piece_cols, width), BF)
+        spec = pl.BlockSpec((depth, cols, width), lambda step, first=start // depth: (first + step, 0, 0))
         sent, cell_out = conv_step(
-            frames, 1, hidden_one, cell_one, ring, weights, bias, (start, extent), depth, (sent_shape, tile_shapes[1]),
-            (
-                whole(sent_shape),
-                pl.BlockSpec((depth, cols, width), lambda step, first=start // depth: (first + step, 0, 0)),
-            ),
-            (local_m, piece_x), (None, cell_out),
+            frames, 1, hidden_one, cell_one, ring, weights, bias, (start, extent), depth, ("hid_out", "cell_out"),
+            (sent_shape, tile_shapes[1]), (whole(sent_shape), spec), (local_m, piece_x), carry, bool(carry),
         )
+        carry = (None, cell_out)
         sent = sent.reshape(devices_y * devices_x, piece_y, piece_cols, width)
         moved.append((start, lax.all_to_all(sent, ("gy", "gx"), split_axis=0, concat_axis=0, tiled=True)))
         start += extent

time: 131 us -> 118 us (0.901)
  Pallas kernels: 66.8 us -> 50.9 us
  local copies, waits for them, and re-layouts: 8.87 us -> 12.9 us
  waiting for transfers between devices: 25.2 us -> 23.4 us
    pallas_call x3 -> x4, Pallas kernels: 40 us -> 31.7 us  [conv_step(): pl.pallas_call(functools.partial(conv_kernel, first, last, refs, packed),...]
    unnamed x27 -> x64, local copies, waits for them, and re-layouts: 0.92 us -> 6.58 us
    ppermute x4, waiting for transfers between devices: 5.03 us -> 0.01 us  [shifted(): return lax.ppermute(value, axis, pairs)]
    pallas_call x1, Pallas kernels: 5.4 us -> 2.2 us  [body(): pl.pallas_call(functools.partial(ring_kernel, rows), grid=(1,), in_specs=...]
    pallas_call x2, Pallas kernels: 17.7 us -> 15.3 us  [block_step(): pl.pallas_call(block_kernel, grid=(lanes, piece_y), in_specs=[spec, whole...]
    all_to_all x2, waiting for transfers between devices: 14.8 us -> 17 us  [body(): lax.all_to_all(done, ('gy', 'gx'), split_axis=0, concat_axis=0, tiled=True)]
    pallas_call x2, Pallas kernels: 3.62 us -> 1.63 us  [unpack_step(): pl.pallas_call(functools.partial(unpack_kernel, local_m, piece_x), grid=(...]
  transfers between devices with their start and end apart: 8 -> 8, of which waited for: 6 -> 4; matrix products, arithmetic and copies ran while one was open for 2% -> 2% of each run, Pallas kernels for 37% -> 35%
where the time goes in v3:
time: 118 us; the launch traced here: 117 us
  Pallas kernels  50.9 us (43%)
  starting transfers between devices  28.1 us (24%)
  waiting for transfers between devices  23.4 us (20%)
  local copies, waits for them, and re-layouts  12.9 us (11%)
  between operations  1.35 us (1%)
    pallas_call x4, Pallas kernels, conv_step(): pl.pallas_call(functools.partial(conv_kernel, first, last, refs, packed),...  31.7 us
    all_to_all x2, waiting for transfers between devices, body(): lax.all_to_all(done, ('gy', 'gx'), split_axis=0, concat_axis=0, tiled=True)  17 us
    pallas_call x2, Pallas kernels, block_step(): pl.pallas_call(block_kernel, grid=(lanes, piece_y), in_specs=[spec, whole...  15.3 us
    ppermute x4, starting transfers between devices, shifted(): return lax.ppermute(value, axis, pairs)  12.5 us
    all_to_all x2, starting transfers between devices, body(): lax.all_to_all(sent, ('gy', 'gx'), split_axis=0, concat_axis=0, tiled=True)  9.69 us
    unnamed x64, local copies, waits for them, and re-layouts  6.58 us
    all_to_all x2, waiting for transfers between devices, body(): lax.all_to_all(sent, ('gy', 'gx'), split_axis=0, concat_axis=0, tiled=True)  6.41 us
    all_to_all x2, starting transfers between devices, body(): lax.all_to_all(done, ('gy', 'gx'), split_axis=0, concat_axis=0, tiled=True)  5.88 us
  transfers between devices with their start and end apart: 8, of which 4 were waited for; matrix products, arithmetic and copies ran while one was open for 2% of the time, Pallas kernels for 35%

profile of v3, /device:TPU:1, one launch (start us, length us, event | category | flops | bytes accessed | tf_op | source)
XLA Modules:
  0.0 117.2 jit_solution(18143633562762825842)
XLA Ops:
  0.6 1.1 fusion.11
  3.6 1.4 %fusion.9 = (bf16[48,2,256]{2,1,0:T(2,128)(2,1)S(1)}, bf16[48,2,256]{2,1,0:T(2,128)(2,1)S(1)}, bf16[48,2,256]{2,1,0:T(2,128)(2,1)S(1)}, bf16[48,2,256]{2,1,0:T(2,128)(2,1)S(1)}) fusion(bf16[48,64,512]{2,1,0:T(8,128)(2,1)} %args_2_.10), kind=kLoop, calls=%fused_computation.45 | loop fusion | bytes 393216 | tf_op jit(solution)/shard_map/slice | solution.py:432
  5.1 1.6 %collective-permute-start.1 = (bf16[48,2,768]{2,1,0:T(2,128)(2,1)S(1)}, bf16[48,2,768]{2,1,0:T(2,128)(2,1)S(1)}, u32[]{:S(2)}, u32[]{:S(2)}) collective-permute-start(bf16[48,2,768]{2,1,0:T(2,128)(2,1)S(1)} %pad_maximum_fusion.3), channel_id=1, source_target_pairs={{1,0},{2,1},{3,2},{5,4},{6,5},{7,6},{9,8},{10,9},{11,10},{13,12},{... | collective-permute-start | bytes 442376 | tf_op jit(solution)/shard_map/ppermute | solution.py:438
  6.9 4.7 %collective-permute-start = (bf16[48,2,768]{2,1,0:T(2,128)(2,1)S(1)}, bf16[48,2,768]{2,1,0:T(2,128)(2,1)S(1)}, u32[]{:S(2)}, u32[]{:S(2)}) collective-permute-start(bf16[48,2,768]{2,1,0:T(2,128)(2,1)S(1)} %pad_maximum_fusion.2), channel_id=1, source_target_pairs={{0,1},{1,2},{2,3},{4,5},{5,6},{6,7},{8,9},{9,10},{10,11},{12,13},{... | collective-permute-start | bytes 442376 | tf_op jit(solution)/shard_map/ppermute | solution.py:438
  13.0 2.0 %copy-done.1 = bf16[3,3,384,512]{3,2,1,0:T(8,128)(2,1)S(1)} copy-done((bf16[3,3,384,512]{3,2,1,0:T(8,128)(2,1)S(1)}, bf16[3,3,384,512]{3,2,1,0:T(8,128)(2,1)}, u32[]{:S(2)}) %copy-start.1) | copy-done | bytes 3538968
  15.0 1.4 %copy-done.5 = f32[48,64,128]{2,1,0:T(8,128)S(1)} copy-done((f32[48,64,128]{2,1,0:T(8,128)S(1)}, f32[48,64,128]{2,1,0:T(8,128)}, u32[]{:S(2)}) %copy-start.5) | copy-done | bytes 1572888
  16.4 1.1 copy-done.6
  17.6 6.5 %shard_map.104 = (bf16[48,64,128]{2,1,0:T(8,128)(2,1)S(1)}, f32[48,64,128]{2,1,0:T(8,128)S(1)}) custom-call(bf16[48,64,512]{2,1,0:T(8,128)(2,1)S(1)} %copy-done, bf16[48,64,512]{2,1,0:T(8,128)(2,1)S(1)} %copy-done, bf16[48,64,512]{2,1,0:T(8,128)(2,1)S(1)} %copy-done, bf16[48,64,128]{2,1,0:T(8,128)(2,1)S(1)} %copy-done.6, bf16[48,64,128]{2,1,0:T(8,128)(2,1)S(1)} %copy-done.6, ...), custom_call_target="tpu_custom_call" | custom-call | flops 5435817984 | bytes 6684672 | tf_op jit(solution)/shard_map/pallas_call | solution.py:204
  24.4 4.4 %collective-permute-start.2 = (bf16[2,68,768]{2,1,0:T(8,128)(2,1)S(1)}, bf16[2,68,768]{2,1,0:T(8,128)(2,1)S(1)}, u32[]{:S(2)}, u32[]{:S(2)}) collective-permute-start(bf16[2,68,768]{2,1,0:T(8,128)(2,1)S(1)} %get-tuple-element.32), channel_id=1, source_target_pairs={{0,4},{4,8},{8,12},{12,16},{16,20},{20,24},{24,28},{1,5},{5,9},{9,... | collective-permute-start | bytes 626696 | tf_op jit(solution)/shard_map/ppermute | solution.py:438
  28.9 1.9 %collective-permute-start.3 = (bf16[2,68,768]{2,1,0:T(8,128)(2,1)S(1)}, bf16[2,68,768]{2,1,0:T(8,128)(2,1)S(1)}, u32[]{:S(2)}, u32[]{:S(2)}) collective-permute-start(bf16[2,68,768]{2,1,0:T(8,128)(2,1)S(1)} %get-tuple-element.33), channel_id=1, source_target_pairs={{4,0},{8,4},{12,8},{16,12},{20,16},{24,20},{28,24},{5,1},{9,5},{13... | collective-permute-start | bytes 626696 | tf_op jit(solution)/shard_map/ppermute | solution.py:438
  30.8 6.5 %shard_map.105 = (bf16[48,64,128]{2,1,0:T(8,128)(2,1)S(1)}, f32[48,64,128]{2,1,0:T(8,128)S(1)}) custom-call(bf16[48,64,512]{2,1,0:T(8,128)(2,1)S(1)} %copy-done, bf16[48,64,512]{2,1,0:T(8,128)(2,1)S(1)} %copy-done, bf16[48,64,512]{2,1,0:T(8,128)(2,1)S(1)} %copy-done, ...), custom_call_target="tpu_custom_call", output_to_operand_aliasing={{0}: (9, {}), {1}: (10, {})} | custom-call | flops 5435817984 | bytes 6684672 | tf_op jit(solution)/shard_map/pallas_call | solution.py:204
  39.4 2.2 %shard_map.106 = (f32[4,64,128]{2,1,0:T(8,128)S(1)}, f32[4,64,128]{2,1,0:T(8,128)S(1)}, f32[4,64,128]{2,1,0:T(8,128)S(1)}, f32[4,64,128]{2,1,0:T(8,128)S(1)}) custom-call(bf16[2,68,768]{2,1,0:T(8,128)(2,1)S(1)} %collective-permute-done.2.above.args_15_, bf16[2,68,768]{2,1,0:T(8,128)(2,1)S(1)} %collective-permute-done.3.below.args_16_, ...), custom_call_target="tpu_custom_call" | custom-call | flops 1811939328 | bytes 3538944 | tf_op jit(solution)/shard_map/pallas_call | solution.py:483
  41.7 7.3 %shard_map.107 = (bf16[8,4,3,16,128]{4,3,2,1,0:T(8,128)(2,1)S(1)}, f32[48,64,128]{2,1,0:T(8,128)}) custom-call(bf16[48,64,512]{2,1,0:T(8,128)(2,1)S(1)} %copy-done, bf16[48,64,512]{2,1,0:T(8,128)(2,1)S(1)} %copy-done, bf16[48,64,512]{2,1,0:T(8,128)(2,1)S(1)} %copy-done, bf16[48,64,128]{2,1,0:T(8,128)(2,1)S(1)} %get-tuple-element.30.args_3_.args_4_.args_5_, ...), custom_call_target="tpu_custom_call" | custom-call | flops 5435817984 | bytes 6684672 | tf_op jit(solution)/shard_map/pallas_call | solution.py:204
  49.8 5.2 %all-to-all-start.2 = ((bf16[32,3,16,128]{3,2,1,0:T(8,128)(2,1)}), bf16[32,3,16,128]{3,2,1,0:T(8,128)(2,1)S(1)}, u32[]{:S(2)}, u32[]{:S(2)}) async-start(bf16[32,3,16,128]{3,2,1,0:T(8,128)(2,1)} %bitcast.119), calls=%async_computation.2 | async-start | bytes 786432 | tf_op jit(solution)/shard_map/all_to_all | solution.py:524
  55.1 11.3 %shard_map.108 = (bf16[8,4,3,16,128]{4,3,2,1,0:T(8,128)(2,1)}, f32[48,64,128]{2,1,0:T(8,128)}) custom-call(bf16[48,64,512]{2,1,0:T(8,128)(2,1)} %args_2_.10, bf16[48,64,512]{2,1,0:T(8,128)(2,1)} %args_2_.10, bf16[48,64,512]{2,1,0:T(8,128)(2,1)} %args_2_.10, bf16[48,64,128]{2,1,0:T(8,128)(2,1)} %copy-done.4, ...), custom_call_target="tpu_custom_call", output_to_operand_aliasing={{1}: (17, {})} | custom-call | flops 5435817984 | bytes 6684672 | tf_op jit(solution)/shard_map/pallas_call | solution.py:204
  66.4 1.4 %all-to-all-done.2 = bf16[32,3,16,128]{3,2,1,0:T(8,128)(2,1)S(1)} async-done(((bf16[32,3,16,128]{3,2,1,0:T(8,128)(2,1)}), bf16[32,3,16,128]{3,2,1,0:T(8,128)(2,1)S(1)}, u32[]{:S(2)}, u32[]{:S(2)}) %all-to-all-start.2) | async-done | bytes 393248 | tf_op jit(solution)/shard_map/all_to_all | solution.py:524
  67.8 4.5 %all-to-all-start = ((bf16[32,3,16,128]{3,2,1,0:T(8,128)(2,1)}), bf16[32,3,16,128]{3,2,1,0:T(8,128)(2,1)S(1)}, u32[]{:S(2)}, u32[]{:S(2)}) async-start(bf16[32,3,16,128]{3,2,1,0:T(8,128)(2,1)} %bitcast.127), calls=%async_computation | async-start | bytes 786432 | tf_op jit(solution)/shard_map/all_to_all | solution.py:524
  72.3 7.7 %shard_map.110 = bf16[8,1,4,3,16,128]{5,4,3,2,1,0:T(8,128)(2,1)} custom-call(bf16[8,1,4,3,16,128]{5,4,3,2,1,0:T(8,128)(2,1)S(1)} %bitcast.118, bf16[128,768]{1,0:T(8,128)(2,1)S(1)} %copy-done.17, bf16[256,128]{1,0:T(8,128)(2,1)S(1)} %copy-done.20, bf16[128,512]{1,0:T(8,128)(2,1)S(1)} %copy-done.18, bf16[512,128]{1,0:T(8,128)(2,1)S(1)} %copy-done.19), custom_call_target="tpu_custom_call" | custom-call | flops 4608000000 | bytes 1586432 | tf_op jit(solution)/shard_map/pallas_call | solution.py:353
  80.0 5.0 %all-to-all-done = bf16[32,3,16,128]{3,2,1,0:T(8,128)(2,1)S(1)} async-done(((bf16[32,3,16,128]{3,2,1,0:T(8,128)(2,1)}), bf16[32,3,16,128]{3,2,1,0:T(8,128)(2,1)S(1)}, u32[]{:S(2)}, u32[]{:S(2)}) %all-to-all-start) | async-done | bytes 393248 | tf_op jit(solution)/shard_map/all_to_all | solution.py:524
  85.0 2.9 %all-to-all-start.3 = ((bf16[32,3,16,128]{3,2,1,0:T(8,128)(2,1)}), bf16[32,3,16,128]{3,2,1,0:T(8,128)(2,1)S(1)}, u32[]{:S(2)}, u32[]{:S(2)}) async-start(bf16[32,3,16,128]{3,2,1,0:T(8,128)(2,1)} %bitcast.17), calls=%async_computation.3 | async-start | bytes 786432 | tf_op jit(solution)/shard_map/all_to_all | solution.py:529
  88.0 7.7 %shard_map.109 = bf16[8,1,4,3,16,128]{5,4,3,2,1,0:T(8,128)(2,1)} custom-call(bf16[8,1,4,3,16,128]{5,4,3,2,1,0:T(8,128)(2,1)S(1)} %bitcast.120, bf16[128,768]{1,0:T(8,128)(2,1)S(1)} %copy-done.17, bf16[256,128]{1,0:T(8,128)(2,1)S(1)} %copy-done.20, bf16[128,512]{1,0:T(8,128)(2,1)S(1)} %copy-done.18, bf16[512,128]{1,0:T(8,128)(2,1)S(1)} %copy-done.19), custom_call_target="tpu_custom_call" | custom-call | flops 4608000000 | bytes 1586432 | tf_op jit(solution)/shard_map/pallas_call | solution.py:353
  95.6 5.1 %all-to-all-done.3 = bf16[32,3,16,128]{3,2,1,0:T(8,128)(2,1)S(1)} async-done(((bf16[32,3,16,128]{3,2,1,0:T(8,128)(2,1)}), bf16[32,3,16,128]{3,2,1,0:T(8,128)(2,1)S(1)}, u32[]{:S(2)}, u32[]{:S(2)}) %all-to-all-start.3) | async-done | bytes 393248 | tf_op jit(solution)/shard_map/all_to_all | solution.py:529
  100.7 2.9 %all-to-all-start.1 = ((bf16[32,3,16,128]{3,2,1,0:T(8,128)(2,1)}), bf16[32,3,16,128]{3,2,1,0:T(8,128)(2,1)S(1)}, u32[]{:S(2)}, u32[]{:S(2)}) async-start(bf16[32,3,16,128]{3,2,1,0:T(8,128)(2,1)} %bitcast.13), calls=%async_computation.1 | async-start | bytes 786432 | tf_op jit(solution)/shard_map/all_to_all | solution.py:529
  104.5 11.9 %all-to-all-done.1 = bf16[32,3,16,128]{3,2,1,0:T(8,128)(2,1)S(1)} async-done(((bf16[32,3,16,128]{3,2,1,0:T(8,128)(2,1)}), bf16[32,3,16,128]{3,2,1,0:T(8,128)(2,1)S(1)}, u32[]{:S(2)}, u32[]{:S(2)}) %all-to-all-start.1) | async-done | bytes 393248 | tf_op jit(solution)/shard_map/all_to_all | solution.py:529
  (91 shorter events, 8.1 us)
Async XLA Ops:
  5.0 8.0 %copy-start = (bf16[48,64,512]{2,1,0:T(8,128)(2,1)S(1)}, bf16[48,64,512]{2,1,0:T(8,128)(2,1)}, u32[]{:S(2)}) copy-start(bf16[48,64,512]{2,1,0:T(8,128)(2,1)} %args_2_.10) | copy-start | bytes 9437188
  5.0 8.0 %copy-start.16 = (f32[512]{0:T(512)S(1)}, f32[512]{0:T(512)}, u32[]{:S(2)}) copy-start(f32[512]{0:T(512)} %param.13) | copy-start | bytes 6148
  5.1 18.9 %collective-permute-start.1 = (bf16[48,2,768]{2,1,0:T(2,128)(2,1)S(1)}, bf16[48,2,768]{2,1,0:T(2,128)(2,1)S(1)}, u32[]{:S(2)}, u32[]{:S(2)}) collective-permute-start(bf16[48,2,768]{2,1,0:T(2,128)(2,1)S(1)} %pad_maximum_fusion.3), channel_id=1, source_target_pairs={{1,0},{2,1},{3,2},{5,4},{6,5},{7,6},{9,8},{10,9},{11,10},{13,12},{... | collective-permute-start | bytes 442376 | tf_op jit(solution)/shard_map/ppermute | solution.py:438
  6.9 17.5 %collective-permute-start = (bf16[48,2,768]{2,1,0:T(2,128)(2,1)S(1)}, bf16[48,2,768]{2,1,0:T(2,128)(2,1)S(1)}, u32[]{:S(2)}, u32[]{:S(2)}) collective-permute-start(bf16[48,2,768]{2,1,0:T(2,128)(2,1)S(1)} %pad_maximum_fusion.2), channel_id=1, source_target_pairs={{0,1},{1,2},{2,3},{4,5},{5,6},{6,7},{8,9},{9,10},{10,11},{12,13},{... | collective-permute-start | bytes 442376 | tf_op jit(solution)/shard_map/ppermute | solution.py:438
  24.4 13.1 %collective-permute-start.2 = (bf16[2,68,768]{2,1,0:T(8,128)(2,1)S(1)}, bf16[2,68,768]{2,1,0:T(8,128)(2,1)S(1)}, u32[]{:S(2)}, u32[]{:S(2)}) collective-permute-start(bf16[2,68,768]{2,1,0:T(8,128)(2,1)S(1)} %get-tuple-element.32), channel_id=1, source_target_pairs={{0,4},{4,8},{8,12},{12,16},{16,20},{20,24},{24,28},{1,5},{5,9},{9,... | collective-permute-start | bytes 626696 | tf_op jit(solution)/shard_map/ppermute | solution.py:438
  28.9 8.9 %collective-permute-start.3 = (bf16[2,68,768]{2,1,0:T(8,128)(2,1)S(1)}, bf16[2,68,768]{2,1,0:T(8,128)(2,1)S(1)}, u32[]{:S(2)}, u32[]{:S(2)}) collective-permute-start(bf16[2,68,768]{2,1,0:T(8,128)(2,1)S(1)} %get-tuple-element.33), channel_id=1, source_target_pairs={{4,0},{8,4},{12,8},{16,12},{20,16},{24,20},{28,24},{5,1},{9,5},{13... | collective-permute-start | bytes 626696 | tf_op jit(solution)/shard_map/ppermute | solution.py:438
  37.3 4.3 %copy-start.4 = (bf16[48,64,128]{2,1,0:T(8,128)(2,1)}, bf16[48,64,128]{2,1,0:T(8,128)(2,1)S(1)}, u32[]{:S(2)}) copy-start(bf16[48,64,128]{2,1,0:T(8,128)(2,1)S(1)} %get-tuple-element.30.args_3_.args_4_.args_5_) | copy-start | bytes 2359300
  37.3 4.3 %copy-start.8 = (f32[48,64,128]{2,1,0:T(8,128)}, f32[48,64,128]{2,1,0:T(8,128)S(1)}, u32[]{:S(2)}) copy-start(f32[48,64,128]{2,1,0:T(8,128)S(1)} %get-tuple-element.31.args_6_) | copy-start | bytes 4718596
  37.6 4.0 %copy-start.9 = (bf16[2,68,768]{2,1,0:T(8,128)(2,1)}, bf16[2,68,768]{2,1,0:T(8,128)(2,1)S(1)}, u32[]{:S(2)}) copy-start(bf16[2,68,768]{2,1,0:T(8,128)(2,1)S(1)} %collective-permute-done.2.above.args_15_) | copy-start | bytes 626692
  37.8 3.9 %copy-start.10 = (bf16[2,68,768]{2,1,0:T(8,128)(2,1)}, bf16[2,68,768]{2,1,0:T(8,128)(2,1)S(1)}, u32[]{:S(2)}) copy-start(bf16[2,68,768]{2,1,0:T(8,128)(2,1)S(1)} %collective-permute-done.3.below.args_16_) | copy-start | bytes 626692
  39.4 2.3 %copy-start.3 = (bf16[2,4,64,768]{3,2,1,0:T(8,128)(2,1)}, bf16[2,4,64,768]{3,2,1,0:T(8,128)(2,1)S(1)}, u32[]{:S(2)}) copy-start(bf16[2,4,64,768]{3,2,1,0:T(8,128)(2,1)S(1)} %pad.4.strips.args_13_.args_14_) | copy-start | bytes 2359300
  39.4 2.3 %copy-start.2 = (bf16[3,3,384,512]{3,2,1,0:T(8,128)(2,1)S(1)}, bf16[3,3,384,512]{3,2,1,0:T(8,128)(2,1)}, u32[]{:S(2)}) copy-start(bf16[3,3,384,512]{3,2,1,0:T(8,128)(2,1)} %param.12) | copy-start | bytes 10616836
  41.6 7.4 %copy-start.12 = (f32[4,64,128]{2,1,0:T(8,128)}, f32[4,64,128]{2,1,0:T(8,128)S(1)}, u32[]{:S(2)}) copy-start(f32[4,64,128]{2,1,0:T(8,128)S(1)} %get-tuple-element.36.args_11_) | copy-start | bytes 393220
  41.6 7.4 %copy-start.13 = (f32[4,64,128]{2,1,0:T(8,128)}, f32[4,64,128]{2,1,0:T(8,128)S(1)}, u32[]{:S(2)}) copy-start(f32[4,64,128]{2,1,0:T(8,128)S(1)} %get-tuple-element.37.args_12_) | copy-start | bytes 393220
  41.6 7.4 %copy-start.14 = (f32[4,64,128]{2,1,0:T(8,128)}, f32[4,64,128]{2,1,0:T(8,128)S(1)}, u32[]{:S(2)}) copy-start(f32[4,64,128]{2,1,0:T(8,128)S(1)} %get-tuple-element.34.args_9_) | copy-start | bytes 393220
  41.6 7.4 %copy-start.15 = (f32[4,64,128]{2,1,0:T(8,128)}, f32[4,64,128]{2,1,0:T(8,128)S(1)}, u32[]{:S(2)}) copy-start(f32[4,64,128]{2,1,0:T(8,128)S(1)} %get-tuple-element.35.args_10_) | copy-start | bytes 393220
  49.8 18.0 %all-to-all-start.2 = ((bf16[32,3,16,128]{3,2,1,0:T(8,128)(2,1)}), bf16[32,3,16,128]{3,2,1,0:T(8,128)(2,1)S(1)}, u32[]{:S(2)}, u32[]{:S(2)}) async-start(bf16[32,3,16,128]{3,2,1,0:T(8,128)(2,1)} %bitcast.119), calls=%async_computation.2 | async-start | bytes 786432 | tf_op jit(solution)/shard_map/all_to_all | solution.py:524
  55.0 17.2 %copy-start.17 = (bf16[128,768]{1,0:T(8,128)(2,1)S(1)}, bf16[128,768]{1,0:T(8,128)(2,1)}, u32[]{:S(2)}) copy-start(bf16[128,768]{1,0:T(8,128)(2,1)} %w_qkv.3) | copy-start | bytes 589828
  55.0 17.2 %copy-start.18 = (bf16[128,512]{1,0:T(8,128)(2,1)S(1)}, bf16[128,512]{1,0:T(8,128)(2,1)}, u32[]{:S(2)}) copy-start(bf16[128,512]{1,0:T(8,128)(2,1)} %w_up.3) | copy-start | bytes 393220
  55.1 17.2 %copy-start.19 = (bf16[512,128]{1,0:T(8,128)(2,1)S(1)}, bf16[512,128]{1,0:T(8,128)(2,1)}, u32[]{:S(2)}) copy-start(bf16[512,128]{1,0:T(8,128)(2,1)} %w_down.3) | copy-start | bytes 393220
  55.1 17.2 %copy-start.20 = (bf16[256,128]{1,0:T(8,128)(2,1)S(1)}, bf16[256,128]{1,0:T(8,128)(2,1)}, u32[]{:S(2)}) copy-start(bf16[256,128]{1,0:T(8,128)(2,1)} %w_out.3) | copy-start | bytes 196612
  67.8 17.2 %all-to-all-start = ((bf16[32,3,16,128]{3,2,1,0:T(8,128)(2,1)}), bf16[32,3,16,128]{3,2,1,0:T(8,128)(2,1)S(1)}, u32[]{:S(2)}, u32[]{:S(2)}) async-start(bf16[32,3,16,128]{3,2,1,0:T(8,128)(2,1)} %bitcast.127), calls=%async_computation | async-start | bytes 786432 | tf_op jit(solution)/shard_map/all_to_all | solution.py:524
  85.0 15.7 %all-to-all-start.3 = ((bf16[32,3,16,128]{3,2,1,0:T(8,128)(2,1)}), bf16[32,3,16,128]{3,2,1,0:T(8,128)(2,1)S(1)}, u32[]{:S(2)}, u32[]{:S(2)}) async-start(bf16[32,3,16,128]{3,2,1,0:T(8,128)(2,1)} %bitcast.17), calls=%async_computation.3 | async-start | bytes 786432 | tf_op jit(solution)/shard_map/all_to_all | solution.py:529
  100.7 15.7 %all-to-all-start.1 = ((bf16[32,3,16,128]{3,2,1,0:T(8,128)(2,1)}), bf16[32,3,16,128]{3,2,1,0:T(8,128)(2,1)S(1)}, u32[]{:S(2)}, u32[]{:S(2)}) async-start(bf16[32,3,16,128]{3,2,1,0:T(8,128)(2,1)} %bitcast.13), calls=%async_computation.1 | async-start | bytes 786432 | tf_op jit(solution)/shard_map/all_to_all | solution.py:529
  (5 other events, 7.0 us)

commit v4 on v3

--- a/solution.py
+++ b/solution.py
@@ -17,6 +17,7 @@
 VMEM_LIMIT = 32 * 1024 * 1024
 VMEM_ALL = 60 * 1024 * 1024
 LOADS = 9
+LANES = 128
 
 
 def sigmoid(x):
@@ -76,9 +77,9 @@
 
         @pl.when(step == 0)
         def _():
-            for side, strip, frames_beside in (("left", 0, "frame_left"), ("right", 3, "frame_right")):
-                ref[side][:, :latent] = ref[frames_beside][0, 0].astype(F32)
-                ref[side][:, latent:] = ref["strips_hid"][strip]
+            for place, side in enumerate(("left", "right")):
+                ref[side][:, :latent] = ref["beside"][place]
+                ref[side][:, latent:] = ref["strips_hid"][3 * place]
 
     block = first + step
     base = block * depth
@@ -216,24 +217,97 @@
     )(*(array for array, _ in inputs.values()))
 
 
+def pack_kernel(
+    frame_low, frame_high, frame_top, frame_bot, hid_low, hid_high, hid_top, hid_bot,
+    cell_low, cell_high, cell_top, cell_bot, side_low, side_high, line_top, line_bot, flat,
+):
+    latent, width = frame_low.shape[2] // 2, hid_low.shape[2]
+    chans = latent + width
+    places = ((0, 0, latent), (chans + width, latent, latent))
+    for out, frame, hid, cell in (
+        (line_top, frame_top, hid_top, cell_top),
+        (line_bot, frame_bot, hid_bot, cell_bot),
+    ):
+        for to, start, size in places:
+            out[:, :, to : to + size] = frame[:, :, start : start + size]
+        out[:, :, latent:chans] = hid[...]
+        out[:, :, chans : chans + width] = cell[...].astype(BF)
+    for out, frame, hid, cell, first, start in (
+        (side_low, frame_low, hid_low, cell_low, 0, 0),
+        (side_high, frame_high, hid_high, cell_high, frame_high.shape[1] - 8, 6),
+    ):
+        tall = frame.shape[0]
+        near = slice(first, first + 8)
+        for slab in range(out.shape[2] // LANES):
+            to = slab * LANES
+            if to < latent or to >= chans + width:
+                begin = to if to < latent else to - 2 * width
+                part = frame[:, near, begin : begin + LANES].astype(F32)
+            elif to < chans:
+                part = hid[:, near, to - latent : to - latent + LANES].astype(F32)
+            else:
+                part = cell[:, :, to - chans : to - chans + LANES]
+            flat[...] = part.reshape(tall * 8, LANES)
+            for place in range(2):
+                out[place, :, to : to + LANES] = flat[pl.ds(start + place, tall, stride=8), :].astype(BF)
+
+
+def pack_step(frames, hid, cell):
+    rows, cols, width = hid.shape
+    span = frames.shape[2]
+    near = 16
+
+    def edge(array, size):
+        deep = array.shape[2]
+        return [
+            pl.BlockSpec((rows, size, deep), lambda step: (0, 0, 0)),
+            pl.BlockSpec((rows, size, deep), lambda step: (0, cols // size - 1, 0)),
+            pl.BlockSpec((2, cols, deep), lambda step: (0, 0, 0)),
+            pl.BlockSpec((2, cols, deep), lambda step: (rows // 2 - 1, 0, 0)),
+        ]
+
+    deep = span + 2 * width
+    shapes = [jax.ShapeDtypeStruct((2, rows, deep), BF)] * 2 + [jax.ShapeDtypeStruct((2, cols, deep), BF)] * 2
+    return pl.pallas_call(
+        pack_kernel,
+        grid=(1,),
+        in_specs=[*edge(frames, near), *edge(hid, near), *edge(cell, 8)],
+        out_specs=[whole(shape) for shape in shapes],
+        out_shape=shapes,
+        scratch_shapes=[pltpu.VMEM((rows * 8, LANES), F32)],
+        compiler_params=pltpu.CompilerParams(vmem_limit_bytes=VMEM_ALL),
+        cost_estimate=pl.CostEstimate(flops=0, bytes_accessed=4_000_000, transcendentals=0),
+    )(*[frames] * 4, *[hid] * 4, *[cell] * 4)
+
+
 def ring_kernel(
-    rows, above, below, frame_top, frame_bot, hid_top, hid_bot, cell_top, cell_bot, strips, weights, bias,
-    line_hid, line_cell, strip_hid, strip_cell,
+    above, below, line_top, line_bot, from_left, from_right, side_left, side_right, weights, bias,
+    line_hid, line_cell, strip_hid, strip_cell, beside, strips,
 ):
-    latent, width = frame_top.shape[2], hid_top.shape[2]
-    chans = latent + width
-    cols, length = frame_top.shape[1], strips.shape[2]
-    low, high = strips[0, 1, :, :chans].astype(F32), strips[1, 2, :, :chans].astype(F32)
-
-    def beside(ref, row):
-        line = ref[row, :cols].astype(F32)
-        return line[:, :chans], line[:, chans : chans + width]
-
-    def within(frame, hid, cell, row):
-        return jnp.concatenate([frame[row].astype(F32), hid[row].astype(F32)], axis=1), cell[row]
-
-    tops = [beside(above, 0), beside(above, 1)] + [within(frame_top, hid_top, cell_top, row) for row in range(2)]
-    bots = [within(frame_bot, hid_bot, cell_bot, row) for row in range(2)] + [beside(below, 0), beside(below, 1)]
+    width = line_hid.shape[2]
+    chans = weights.shape[0] // 9
+    cols, length = line_top.shape[1], strip_hid.shape[1]
+    rows = from_left.shape[1]
+    columns = (
+        (from_left, 0, cols), (from_left, 1, cols + 1), (side_left, 0, 0), (side_left, 1, 1),
+        (side_right, 0, cols - 2), (side_right, 1, cols - 1), (from_right, 0, cols + 2), (from_right, 1, cols + 3),
+    )
+    ends = [(ref[row].astype(F32), at + row) for ref, at in ((above, 0), (below, rows + 2)) for row in range(2)]
+    strips[:, rows + 4 :, :] = jnp.zeros((8, length - rows - 4, strips.shape[2]), F32)
+    for place, (source, at, end) in enumerate(columns):
+        strips[place, 2 : rows + 2, :] = source[at].astype(F32)
+        for value, spot in ends:
+            strips[place, spot : spot + 1, :] = value[end : end + 1]
+    beside[0] = strips[1, :, chans + width :]
+    beside[1] = strips[6, :, chans + width :]
+    low, high = strips[1, :, :chans], strips[6, :, :chans]
+
+    def line(ref, row):
+        held = ref[row, :cols].astype(F32)
+        return held[:, :chans], held[:, chans : chans + width]
+
+    tops = [line(above, 0), line(above, 1), line(line_top, 0), line(line_top, 1)]
+    bots = [line(line_bot, 0), line(line_bot, 1), line(below, 0), line(below, 1)]
     parts, held = [], []
     for lead, lines in ((0, tops), (rows, bots)):
         pieces = []
@@ -246,13 +320,13 @@
     for side in range(2):
         rolled = []
         for col in range(4):
-            wide = strips[side, col, :, :chans].astype(F32)
+            wide = strips[4 * side + col, :, :chans]
             rolled.append((pltpu.roll(wide, 1, axis=0), wide, pltpu.roll(wide, length - 1, axis=0)))
         for col in range(2):
             parts.append(
                 jnp.concatenate([rolled[col + tap][row].astype(BF) for row in range(3) for tap in range(3)], axis=1)
             )
-            held.append(strips[side, col + 1, :, chans : chans + width].astype(F32))
+            held.append(strips[4 * side + col + 1, :, chans : chans + width])
     row_at, col_at = lax.axis_index("gy"), lax.axis_index("gx")
     upper = (row_at > 0).astype(F32)
     lower = (row_at < lax.axis_size("gy") - 1).astype(F32)
@@ -273,7 +347,8 @@
         start += size
 
 
-def block_kernel(x, w_qkv, w_out, w_up, w_down, out, flat, back, keys_t, own_low, own_high, own_values, ones):
+def block_kernel(x, w_qkv, w_out, w_up, w_down, *rest):
+    out, flat, back, keys_t, own_low, own_high, own_values, ones = rest[-8:]
     group = GRID * GRID
     embed = w_out.shape[0]
     tile = embed // 2
@@ -340,22 +415,26 @@
     out[...] = back[...].reshape(x.shape).astype(BF)
 
 
-def block_step(moved, devices_y, devices_x, w_qkv, w_out, w_up, w_down):
+def block_step(moved, carry, first, pieces, devices_y, devices_x, w_qkv, w_out, w_up, w_down):
     _, piece_y, piece_cols, width = moved.shape
     lanes = devices_y // GRID
     view = moved.reshape(GRID, lanes, devices_x, piece_y, piece_cols, width)
     tokens = GRID * devices_x * piece_cols
-    spec = pl.BlockSpec(
-        (GRID, None, devices_x, None, piece_cols, width), lambda i, j: (0, i, 0, j, 0, 0)
-    )
-
+    block = (GRID, None, devices_x, None, piece_cols, width)
+    operands = [view, w_qkv, w_out, w_up, w_down]
+    in_specs = [pl.BlockSpec(block, lambda i, j: (0, i, 0, j, 0, 0)), *(whole(array) for array in operands[1:])]
+    aliases = {}
+    if carry is not None:
+        aliases = {len(operands): 0}
+        operands.append(carry)
+        in_specs.append(pl.BlockSpec(memory_space=pl.ANY))
     total = lanes * piece_y * tokens
-    out = pl.pallas_call(
+    return pl.pallas_call(
         block_kernel,
         grid=(lanes, piece_y),
-        in_specs=[spec, whole(w_qkv), whole(w_out), whole(w_up), whole(w_down)],
-        out_specs=spec,
-        out_shape=jax.ShapeDtypeStruct(view.shape, BF),
+        in_specs=in_specs,
+        out_specs=pl.BlockSpec(block, lambda i, j: (0, i, 0, first + j, 0, 0)),
+        out_shape=jax.ShapeDtypeStruct((GRID, lanes, devices_x, pieces, piece_cols, width), BF),
         scratch_shapes=[
             pltpu.VMEM((tokens, width), F32),
             pltpu.VMEM((tokens, width), F32),
@@ -365,50 +444,50 @@
             pltpu.VMEM((HEADS // 2 * GRID * GRID, HEADS // 2 * HDIM), BF),
             pltpu.VMEM((HEADS // 2 * GRID * GRID, HEADS // 2 * GRID * GRID), BF),
         ],
+        input_output_aliases=aliases,
         compiler_params=pltpu.CompilerParams(vmem_limit_bytes=VMEM_LIMIT),
         cost_estimate=pl.CostEstimate(
             flops=total * 3_000_000, bytes_accessed=total * width * 4 + 800_000, transcendentals=total * 1100
         ),
-    )(view, w_qkv, w_out, w_up, w_down)
-    return out.reshape(moved.shape)
-
-
-def unpack_kernel(local_m, piece_x, *refs):
-    src, out = refs[0], refs[-1]
-    owners_y, owners_x, piece_y, _, width = src.shape
-    for owner_y in range(owners_y):
-        for row in range(piece_y):
-            wide = src[owner_y, :, row].astype(F32)
-            out[owner_y * piece_y + row] = jnp.concatenate(
-                [wide[owner, m * piece_x : (m + 1) * piece_x] for m in range(local_m) for owner in range(owners_x)],
-                axis=0,
-            ).astype(BF)
-
-
-def unpack_step(landed, carry, start, rows, cols, local_m, piece_x):
-    owners_y, owners_x, piece_y, _, width = landed.shape
-    depth = owners_y * piece_y
-    specs = [pl.BlockSpec(landed.shape, lambda i: (0,) * landed.ndim)]
-    operands = [landed]
-    aliases = {}
-    if carry is not None:
-        specs.append(pl.BlockSpec(memory_space=pl.ANY))
-        operands.append(carry)
-        aliases = {1: 0}
+    )(*operands)
+
+
+def unpack_kernel(shares, local_m, piece_x, src, out):
+    owners_y, owners_x = src.shape[:2]
+    unit = out.shape[0]
+    lines, first = [], 0
+    for share in shares:
+        lines += [(owner_y, first + piece) for owner_y in range(owners_y) for piece in range(share)]
+        first += share
+    for step in range(len(lines) // unit):
+
+        @pl.when(pl.program_id(0) == step)
+        def _():
+            for row, (owner_y, piece) in enumerate(lines[step * unit : (step + 1) * unit]):
+                wide = src[owner_y, :, piece].astype(F32)
+                parts = [
+                    wide[owner, m * piece_x : (m + 1) * piece_x] for m in range(local_m) for owner in range(owners_x)
+                ]
+                out[row] = jnp.concatenate(parts, axis=0).astype(BF)
+
+
+def unpack_step(landed, shares, cols, local_m, piece_x):
+    owners_y, _, pieces, _, width = landed.shape
+    rows = owners_y * pieces
+    unit = 16 if rows % 16 == 0 else rows
     return pl.pallas_call(
-        functools.partial(unpack_kernel, local_m, piece_x),
-        grid=(1,),
-        in_specs=specs,
-        out_specs=pl.BlockSpec((depth, cols, width), lambda i: (start // depth, 0, 0)),
+        functools.partial(unpack_kernel, shares, local_m, piece_x),
+        grid=(rows // unit,),
+        in_specs=[pl.BlockSpec(memory_space=pltpu.VMEM)],
+        out_specs=pl.BlockSpec((unit, cols, width), lambda step: (step, 0, 0)),
         out_shape=jax.ShapeDtypeStruct((rows, cols, width), BF),
-        input_output_aliases=aliases,
         compiler_params=pltpu.CompilerParams(vmem_limit_bytes=VMEM_LIMIT),
-        cost_estimate=pl.CostEstimate(flops=0, bytes_accessed=depth * cols * width * 4, transcendentals=0),
-    )(*operands)
-
-
-def step_rows(start, extent):
-    return max(size for size in range(1, 17) if extent % size == 0 and start % size == 0)
+        cost_estimate=pl.CostEstimate(flops=0, bytes_accessed=rows * cols * width * 4, transcendentals=0),
+    )(landed)
+
+
+def step_rows(start, extent, most=16):
+    return max(size for size in range(1, most + 1) if extent % size == 0 and start % size == 0)
 
 
 def body(frames, hidden_state, cell_state, w_gates, gate_bias, w_qkv, w_out, w_up, w_down):
@@ -422,26 +501,18 @@
     weights = w_gates.reshape(-1, w_gates.shape[3])
     bias = gate_bias.reshape(1, -1)
 
-    every, left_two, right_two = slice(None), slice(0, 2), slice(cols - 2, cols)
-    top_two, bot_two = slice(0, 2), slice(rows - 2, rows)
-    edges = ((every, left_two), (every, right_two), (top_two, every), (bot_two, every))
-    edge_cells = lax.optimization_barrier(tuple(cell_state[edge] for edge in edges))
-
-    def pack(edge, cells):
-        return jnp.concatenate(
-            [frames[edge][:, :, :latent], hidden_state[edge], cells.astype(BF), frames[edge][:, :, latent:]], axis=-1
-        )
-
     def shifted(value, axis, step):
         count = lax.axis_size(axis)
         pairs = [(i, i + step) for i in range(count) if 0 <= i + step < count]
         return lax.ppermute(value, axis, pairs)
 
-    side_left, side_right, line_top, line_bot = (pack(edge, cells) for edge, cells in zip(edges, edge_cells))
+    side_left, side_right, line_top, line_bot = pack_step(frames, hidden_state, cell_state)
     from_left = shifted(side_right, "gx", 1)
     from_right = shifted(side_left, "gx", -1)
-    to_down = jnp.concatenate([line_bot, from_left[-2:], from_right[-2:]], axis=1)
-    to_up = jnp.concatenate([line_top, from_left[:2], from_right[:2]], axis=1)
+    from_left, from_right = lax.optimization_barrier((from_left, from_right))
+    beside = jnp.concatenate([from_left, from_right], axis=0)
+    to_down = jnp.concatenate([line_bot, beside[:, -2:].transpose(1, 0, 2)], axis=1)
+    to_up = jnp.concatenate([line_top, beside[:, :2].transpose(1, 0, 2)], axis=1)
 
     tile_shapes = (jax.ShapeDtypeStruct((rows, cols, width), BF), jax.ShapeDtypeStruct((rows, cols, width), F32))
     carry = ()
@@ -457,80 +528,57 @@
         )
     hidden_one, cell_one = carry
 
-    def column(at, middle):
-        return jnp.concatenate([from_up[:, at], middle, from_down[:, at]], axis=0)
-
-    columns = [
-        column(cols, from_left[:, 0]),
-        column(cols + 1, from_left[:, 1]),
-        column(0, side_left[:, 0]),
-        column(1, side_left[:, 1]),
-        column(cols - 2, side_right[:, 0]),
-        column(cols - 1, side_right[:, 1]),
-        column(cols + 2, from_right[:, 0]),
-        column(cols + 3, from_right[:, 1]),
-    ]
     length = -(-(rows + 4) // 16) * 16
-    strips = jnp.stack(columns).reshape(2, 4, rows + 4, held + latent)
-    strips = jnp.pad(strips, ((0, 0), (0, 0), (0, length - rows - 4), (0, 0)))
-
-    def two_rows(channels, at):
-        return pl.BlockSpec((2, cols, channels), lambda step: (at, 0, 0))
-
-    last_two = rows // 2 - 1
     line_shape = jax.ShapeDtypeStruct((4, cols, width), F32)
     strip_shape = jax.ShapeDtypeStruct((4, length, width), F32)
-    line_hid, line_cell, strip_hid, strip_cell = pl.pallas_call(
-        functools.partial(ring_kernel, rows),
+    beside_shape = jax.ShapeDtypeStruct((2, length, latent), F32)
+    shapes = (line_shape, line_shape, strip_shape, strip_shape, beside_shape)
+    around = (from_up, from_down, line_top, line_bot, from_left, from_right, side_left, side_right)
+    line_hid, line_cell, strip_hid, strip_cell, beside = pl.pallas_call(
+        ring_kernel,
         grid=(1,),
-        in_specs=[
-            whole(from_up), whole(from_down), two_rows(latent, 0), two_rows(latent, last_two), two_rows(width, 0),
-            two_rows(width, last_two), two_rows(width, 0), two_rows(width, last_two), whole(strips),
-            pl.BlockSpec(memory_space=pltpu.VMEM),            whole(bias),
-        ],
-        out_specs=[whole(line_shape), whole(line_shape), whole(strip_shape), whole(strip_shape)],
-        out_shape=[line_shape, line_shape, strip_shape, strip_shape],
+        in_specs=[*(whole(array) for array in around), pl.BlockSpec(memory_space=pltpu.VMEM), whole(bias)],
+        out_specs=[whole(shape) for shape in shapes],
+        out_shape=shapes,
+        scratch_shapes=[pltpu.VMEM((8, length, held + latent), F32)],
         compiler_params=pltpu.CompilerParams(vmem_limit_bytes=VMEM_LIMIT),
         cost_estimate=pl.CostEstimate(flops=16 * length * weights.size, bytes_accessed=2 * weights.size, transcendentals=0),
-    )(
-        from_up, from_down, frames, frames, hidden_state, hidden_state, cell_state, cell_state, strips, weights, bias
-    )
+    )(*around, weights, bias)
 
     second = held // latent
-    beside = (1, 1, length, latent)
     line = (1, from_up.shape[1], latent)
     ring = {name: (array, whole(array)) for name, array in (
-        ("strips_hid", strip_hid), ("strips_cell", strip_cell), ("lines_hid", line_hid), ("lines_cell", line_cell)
+        ("strips_hid", strip_hid), ("strips_cell", strip_cell), ("lines_hid", line_hid), ("lines_cell", line_cell),
+        ("beside", beside),
     )}
-    ring["frame_left"] = strips, pl.BlockSpec(beside, lambda step: (0, 1, 0, second))
-    ring["frame_right"] = strips, pl.BlockSpec(beside, lambda step: (1, 2, 0, second))
     ring["frame_top"] = from_up, pl.BlockSpec(line, lambda step: (1, 0, second))
     ring["frame_bot"] = from_down, pl.BlockSpec(line, lambda step: (0, 0, second))
 
     pieces = rows // devices_y
     piece_cols = local_m * piece_x
+    shares = (pieces - pieces // 3, pieces // 3)
     moved, start, carry = [], 0, ()
-    for piece_y in (pieces - pieces // 2, pieces // 2):
+    for piece_y in shares:
         extent = piece_y * devices_y
-        depth = step_rows(start, extent)
+        depth = step_rows(start, extent, 8 if carry else 16)
         sent_shape = jax.ShapeDtypeStruct((devices_y, devices_x, piece_y, piece_cols, width), BF)
         spec = pl.BlockSpec((depth, cols, width), lambda step, first=start // depth: (first + step, 0, 0))
         sent, cell_out = conv_step(
-            frames, 1, hidden_one, cell_one, ring, weights, bias, (start, extent), depth, ("hid_out", "cell_out"),
-            (sent_shape, tile_shapes[1]), (whole(sent_shape), spec), (local_m, piece_x), carry, bool(carry),
+            frames, 1, hidden_one, cell_one, ring, weights, bias, (start, extent), depth,
+            ("hid_out", "cell_out"), (sent_shape, tile_shapes[1]), (whole(sent_shape), spec), (local_m, piece_x), carry,
+            bool(carry),
         )
         carry = (None, cell_out)
         sent = sent.reshape(devices_y * devices_x, piece_y, piece_cols, width)
-        moved.append((start, lax.all_to_all(sent, ("gy", "gx"), split_axis=0, concat_axis=0, tiled=True)))
+        moved.append(lax.all_to_all(sent, ("gy", "gx"), split_axis=0, concat_axis=0, tiled=True))
         start += extent
-    landed = []
-    for start, value in moved:
-        done = block_step(value, devices_y, devices_x, w_qkv, w_out, w_up, w_down)
-        landed.append((start, lax.all_to_all(done, ("gy", "gx"), split_axis=0, concat_axis=0, tiled=True)))
-    result = None
-    for start, value in landed:
-        view = value.reshape(devices_y, devices_x, *value.shape[1:])
-        result = unpack_step(view, result, start, rows, cols, local_m, piece_x)
+    done, first = None, 0
+    for piece_y, value in zip(shares, moved):
+        done = block_step(value, done, first, pieces, devices_y, devices_x, w_qkv, w_out, w_up, w_down)
+        first += piece_y
+    done = done.reshape(devices_y * devices_x, pieces, piece_cols, width)
+    landed = lax.all_to_all(done, ("gy", "gx"), split_axis=0, concat_axis=0, tiled=True)
+    result = unpack_step(landed.reshape(devices_y, devices_x, *landed.shape[1:]), shares, cols, local_m, piece_x)
     return result, cell_out
 
 

time: 118 us -> 115 us (0.975)
  blocking collectives: 0 us -> 25.6 us
  waiting for transfers between devices: 23.4 us -> 7.1 us
  starting transfers between devices: 28.1 us -> 20.9 us
  local copies, waits for them, and re-layouts: 12.9 us -> 7.51 us
  Pallas kernels: 50.9 us -> 52.3 us
    all_to_all x0 -> x1, blocking collectives: none -> 25.6 us  [body(): lax.all_to_all(done, ('gy', 'gx'), split_axis=0, concat_axis=0, tiled=True)]
    all_to_all x2 -> x0, waiting for transfers between devices: 17 us -> none  [body(): lax.all_to_all(done, ('gy', 'gx'), split_axis=0, concat_axis=0, tiled=True)]
    slice x14 -> x0, local copies, waits for them, and re-layouts: 6.23 us -> none  [the longest x2 2.35 us: pack(): frames[edge][:, :, :latent]]
    all_to_all x2 -> x0, starting transfers between devices: 5.88 us -> none  [body(): lax.all_to_all(done, ('gy', 'gx'), split_axis=0, concat_axis=0, tiled=True)]
    pallas_call x0 -> x2, local copies, waits for them, and re-layouts: none -> 2.05 us  [pack_step(): pl.pallas_call(pack_kernel, grid=(1,), in_specs=[*edge(frames, near), *ed...]
    pallas_call x5, Pallas kernels: 19.2 us -> 20.8 us  [the longest x2 14.1 us: block_step(): pl.pallas_call(block_kernel, grid=(lanes, piece_y), in_specs=in_specs, ou...]
    all_to_all x2, starting transfers between devices: 9.69 us -> 8.38 us  [body(): lax.all_to_all(sent, ('gy', 'gx'), split_axis=0, concat_axis=0, tiled=True)]
    unnamed x64 -> x48, local copies, waits for them, and re-layouts: 6.58 us -> 5.43 us
  transfers between devices with their start and end apart: 8 -> 6, of which waited for: 4 -> 2; matrix products, arithmetic and copies ran while one was open for 2% -> 1% of each run, Pallas kernels for 35% -> 27%
where the time goes in v4:
time: 115 us
  Pallas kernels  52.3 us (45%)
  blocking collectives  25.6 us (22%)
  starting transfers between devices  20.9 us (18%)
  local copies, waits for them, and re-layouts  7.51 us (7%)
  waiting for transfers between devices  7.1 us (6%)
    pallas_call x4, Pallas kernels, conv_step(): pl.pallas_call(functools.partial(conv_kernel, first, last, refs, packed),...  31.5 us
    all_to_all x1, blocking collectives, body(): lax.all_to_all(done, ('gy', 'gx'), split_axis=0, concat_axis=0, tiled=True)  25.6 us
    pallas_call x2, Pallas kernels, block_step(): pl.pallas_call(block_kernel, grid=(lanes, piece_y), in_specs=in_specs, ou...  14.1 us
    ppermute x4, starting transfers between devices, shifted(): return lax.ppermute(value, axis, pairs)  12.5 us
    all_to_all x2, starting transfers between devices, body(): lax.all_to_all(sent, ('gy', 'gx'), split_axis=0, concat_axis=0, tiled=True)  8.38 us
    all_to_all x2, waiting for transfers between devices, body(): lax.all_to_all(sent, ('gy', 'gx'), split_axis=0, concat_axis=0, tiled=True)  7.09 us
    unnamed x48, local copies, waits for them, and re-layouts  5.43 us
    pallas_call x1, Pallas kernels, pack_step(): pl.pallas_call(pack_kernel, grid=(1,), in_specs=[*edge(frames, near), *ed...  3.02 us
  transfers between devices with their start and end apart: 6, of which 2 were waited for; matrix products, arithmetic and copies ran while one was open for 1% of the time, Pallas kernels for 27%

profile of v4, /device:TPU:1, one launch (start us, length us, event | category | flops | bytes accessed | tf_op | source)
XLA Modules:
  0.0 114.6 jit_solution(17890515408649623503)
XLA Ops:
  0.7 3.0 %shard_map.105 = (bf16[2,48,768]{2,1,0:T(8,128)(2,1)}, bf16[2,48,768]{2,1,0:T(8,128)(2,1)}, bf16[2,64,768]{2,1,0:T(8,128)(2,1)}, bf16[2,64,768]{2,1,0:T(8,128)(2,1)}) custom-call(bf16[48,64,512]{2,1,0:T(8,128)(2,1)} %args_2_.10, bf16[48,64,512]{2,1,0:T(8,128)(2,1)} %args_2_.10, bf16[48,64,512]{2,1,0:T(8,128)(2,1)} %args_2_.10, ...), custom_call_target="tpu_custom_call" | custom-call | bytes 4000000 | tf_op jit(solution)/shard_map/pallas_call | solution.py:271
  3.7 1.0 copy.16
  4.7 1.3 %collective-permute-start.1 = (bf16[2,48,768]{2,0,1:T(2,128)(2,1)S(1)}, bf16[2,48,768]{2,0,1:T(2,128)(2,1)S(1)}, u32[]{:S(2)}, u32[]{:S(2)}) collective-permute-start(bf16[2,48,768]{2,0,1:T(2,128)(2,1)S(1)} %copy.16), channel_id=1, source_target_pairs={{1,0},{2,1},{3,2},{5,4},{6,5},{7,6},{9,8},{10,9},{11,10},{13,12},{... | collective-permute-start | bytes 442376 | tf_op jit(solution)/shard_map/ppermute | solution.py:507
  6.0 1.0 copy.15
  7.0 4.7 %collective-permute-start = (bf16[2,48,768]{2,0,1:T(2,128)(2,1)S(1)}, bf16[2,48,768]{2,0,1:T(2,128)(2,1)S(1)}, u32[]{:S(2)}, u32[]{:S(2)}) collective-permute-start(bf16[2,48,768]{2,0,1:T(2,128)(2,1)S(1)} %copy.15), channel_id=1, source_target_pairs={{0,1},{1,2},{2,3},{4,5},{5,6},{6,7},{8,9},{9,10},{10,11},{12,13},{... | collective-permute-start | bytes 442376 | tf_op jit(solution)/shard_map/ppermute | solution.py:507
  11.7 1.4 %copy-done.1 = f32[48,64,128]{2,1,0:T(8,128)S(1)} copy-done((f32[48,64,128]{2,1,0:T(8,128)S(1)}, f32[48,64,128]{2,1,0:T(8,128)}, u32[]{:S(2)}) %copy-start.1) | copy-done | bytes 1572888
  13.1 1.1 copy-done.2
  14.3 2.0 %copy-done.4 = bf16[3,3,384,512]{3,2,1,0:T(8,128)(2,1)S(1)} copy-done((bf16[3,3,384,512]{3,2,1,0:T(8,128)(2,1)S(1)}, bf16[3,3,384,512]{3,2,1,0:T(8,128)(2,1)}, u32[]{:S(2)}) %copy-start.4) | copy-done | bytes 3538968
  16.3 6.5 %shard_map.104 = (bf16[48,64,128]{2,1,0:T(8,128)(2,1)S(1)}, f32[48,64,128]{2,1,0:T(8,128)S(1)}) custom-call(bf16[48,64,512]{2,1,0:T(8,128)(2,1)S(1)} %copy-done, bf16[48,64,512]{2,1,0:T(8,128)(2,1)S(1)} %copy-done, bf16[48,64,512]{2,1,0:T(8,128)(2,1)S(1)} %copy-done, bf16[48,64,128]{2,1,0:T(8,128)(2,1)S(1)} %copy-done.2, bf16[48,64,128]{2,1,0:T(8,128)(2,1)S(1)} %copy-done.2, ...), custom_call_target="tpu_custom_call" | custom-call | flops 5435817984 | bytes 6684672 | tf_op jit(solution)/shard_map/pallas_call | solution.py:205
  22.9 4.7 %collective-permute-start.2 = (bf16[2,68,768]{2,1,0:T(8,128)(2,1)S(1)}, bf16[2,68,768]{2,1,0:T(8,128)(2,1)S(1)}, u32[]{:S(2)}, u32[]{:S(2)}) collective-permute-start(bf16[2,68,768]{2,1,0:T(8,128)(2,1)S(1)} %get-tuple-element.37), channel_id=1, source_target_pairs={{0,4},{4,8},{8,12},{12,16},{16,20},{20,24},{24,28},{1,5},{5,9},{9,... | collective-permute-start | bytes 626696 | tf_op jit(solution)/shard_map/ppermute | solution.py:507
  27.6 1.9 %collective-permute-start.3 = (bf16[2,68,768]{2,1,0:T(8,128)(2,1)S(1)}, bf16[2,68,768]{2,1,0:T(8,128)(2,1)S(1)}, u32[]{:S(2)}, u32[]{:S(2)}) collective-permute-start(bf16[2,68,768]{2,1,0:T(8,128)(2,1)S(1)} %get-tuple-element.38), channel_id=1, source_target_pairs={{4,0},{8,4},{12,8},{16,12},{20,16},{24,20},{28,24},{5,1},{9,5},{13... | collective-permute-start | bytes 626696 | tf_op jit(solution)/shard_map/ppermute | solution.py:507
  29.5 6.5 %shard_map.106 = (bf16[48,64,128]{2,1,0:T(8,128)(2,1)S(1)}, f32[48,64,128]{2,1,0:T(8,128)S(1)}) custom-call(bf16[48,64,512]{2,1,0:T(8,128)(2,1)S(1)} %copy-done, bf16[48,64,512]{2,1,0:T(8,128)(2,1)S(1)} %copy-done, bf16[48,64,512]{2,1,0:T(8,128)(2,1)S(1)} %copy-done, ...), custom_call_target="tpu_custom_call", output_to_operand_aliasing={{0}: (9, {}), {1}: (10, {})} | custom-call | flops 5435817984 | bytes 6684672 | tf_op jit(solution)/shard_map/pallas_call | solution.py:205
  36.2 2.2 %shard_map.107 = (f32[4,64,128]{2,1,0:T(8,128)S(1)}, f32[4,64,128]{2,1,0:T(8,128)S(1)}, f32[4,64,128]{2,1,0:T(8,128)S(1)}, f32[4,64,128]{2,1,0:T(8,128)S(1)}, f32[2,64,256]{2,1,0:T(8,128)S(1)}) custom-call(bf16[2,68,768]{2,1,0:T(8,128)(2,1)S(1)} %collective-permute-done.2.above.args_14_, bf16[2,68,768]{2,1,0:T(8,128)(2,1)S(1)} %collective-permute-done.3.below.args_15_, ...), custom_call_target="tpu_custom_call" | custom-call | flops 1811939328 | bytes 3538944 | tf_op jit(solution)/shard_map/pallas_call | solution.py:537
  38.5 9.4 %shard_map.108 = (bf16[8,4,4,16,128]{4,3,2,1,0:T(8,128)(2,1)S(1)}, f32[48,64,128]{2,1,0:T(8,128)}) custom-call(bf16[48,64,512]{2,1,0:T(8,128)(2,1)S(1)} %copy-done, bf16[48,64,512]{2,1,0:T(8,128)(2,1)S(1)} %copy-done, bf16[48,64,512]{2,1,0:T(8,128)(2,1)S(1)} %copy-done, bf16[48,64,128]{2,1,0:T(8,128)(2,1)S(1)} %get-tuple-element.35.args_3_.args_4_.args_5_, ...), custom_call_target="tpu_custom_call" | custom-call | flops 7247757312 | bytes 7733248 | tf_op jit(solution)/shard_map/pallas_call | solution.py:205
  48.0 0.8 copy-done.7
  48.7 5.2 %all-to-all-start.1 = ((bf16[32,4,16,128]{3,2,1,0:T(8,128)(2,1)}), bf16[32,4,16,128]{3,2,1,0:T(8,128)(2,1)S(1)}, u32[]{:S(2)}, u32[]{:S(2)}) async-start(bf16[32,4,16,128]{3,2,1,0:T(8,128)(2,1)} %bitcast.20), calls=%async_computation.1 | async-start | bytes 1048576 | tf_op jit(solution)/shard_map/all_to_all | solution.py:573
  54.0 9.1 %shard_map.109 = (bf16[8,4,2,16,128]{4,3,2,1,0:T(8,128)(2,1)}, f32[48,64,128]{2,1,0:T(8,128)}) custom-call(bf16[48,64,512]{2,1,0:T(8,128)(2,1)} %args_2_.10, bf16[48,64,512]{2,1,0:T(8,128)(2,1)} %args_2_.10, bf16[48,64,512]{2,1,0:T(8,128)(2,1)} %args_2_.10, bf16[48,64,128]{2,1,0:T(8,128)(2,1)} %copy-done.3, ...), custom_call_target="tpu_custom_call", output_to_operand_aliasing={{1}: (16, {})} | custom-call | flops 3623878656 | bytes 5636096 | tf_op jit(solution)/shard_map/pallas_call | solution.py:205
  63.1 6.2 %all-to-all-done.1 = bf16[32,4,16,128]{3,2,1,0:T(8,128)(2,1)S(1)} async-done(((bf16[32,4,16,128]{3,2,1,0:T(8,128)(2,1)}), bf16[32,4,16,128]{3,2,1,0:T(8,128)(2,1)S(1)}, u32[]{:S(2)}, u32[]{:S(2)}) %all-to-all-start.1) | async-done | bytes 524320 | tf_op jit(solution)/shard_map/all_to_all | solution.py:573
  69.3 3.2 %all-to-all-start = ((bf16[32,2,16,128]{3,2,1,0:T(8,128)(2,1)}), bf16[32,2,16,128]{3,2,1,0:T(8,128)(2,1)S(1)}, u32[]{:S(2)}, u32[]{:S(2)}) async-start(bf16[32,2,16,128]{3,2,1,0:T(8,128)(2,1)} %bitcast.27), calls=%async_computation | async-start | bytes 524288 | tf_op jit(solution)/shard_map/all_to_all | solution.py:573
  72.5 9.4 %shard_map.110.rest_0_ = bf16[8,1,4,6,16,128]{5,4,3,2,1,0:T(8,128)(2,1)S(1)} custom-call(bf16[8,1,4,4,16,128]{5,4,3,2,1,0:T(8,128)(2,1)S(1)} %bitcast.19, bf16[128,768]{1,0:T(8,128)(2,1)S(1)} %copy-done.20, bf16[256,128]{1,0:T(8,128)(2,1)S(1)} %copy-done.23, bf16[128,512]{1,0:T(8,128)(2,1)S(1)} %copy-done.21, bf16[512,128]{1,0:T(8,128)(2,1)S(1)} %copy-done.22), custom_call_target="tpu_custom_call" | custom-call | flops 6144000000 | bytes 1848576 | tf_op jit(solution)/shard_map/pallas_call | solution.py:432
  81.9 0.9 all-to-all-done
  82.8 4.7 %shard_map.111 = bf16[8,1,4,6,16,128]{5,4,3,2,1,0:T(8,128)(2,1)S(1)} custom-call(bf16[8,1,4,2,16,128]{5,4,3,2,1,0:T(8,128)(2,1)S(1)} %bitcast.21, bf16[128,768]{1,0:T(8,128)(2,1)S(1)} %copy-done.20, bf16[256,128]{1,0:T(8,128)(2,1)S(1)} %copy-done.23, bf16[128,512]{1,0:T(8,128)(2,1)S(1)} %copy-done.21, ...), custom_call_target="tpu_custom_call", output_to_operand_aliasing={{}: (5, {})} | custom-call | flops 3072000000 | bytes 1324288 | tf_op jit(solution)/shard_map/pallas_call | solution.py:432
  87.5 25.6 %all_to_all.15 = bf16[32,6,16,128]{3,2,1,0:T(8,128)(2,1)S(1)} all-to-all(bf16[32,6,16,128]{3,2,1,0:T(8,128)(2,1)S(1)} %bitcast.18), channel_id=1, replica_groups=mesh['gy'=8,'gx'=4] {'gy','gx'}, dimensions={0} | all-to-all | bytes 1572864 | tf_op jit(solution)/shard_map/all_to_all | solution.py:580
  113.1 1.5 %shard_map.112 = bf16[48,64,128]{2,1,0:T(8,128)(2,1)} custom-call(bf16[8,4,6,16,128]{4,3,2,1,0:T(8,128)(2,1)S(1)} %bitcast.17), custom_call_target="tpu_custom_call" | custom-call | bytes 1572864 | tf_op jit(solution)/shard_map/pallas_call | solution.py:478
  (52 shorter events, 0.2 us)
Async XLA Ops:
  0.6 11.1 %copy-start = (bf16[48,64,512]{2,1,0:T(8,128)(2,1)S(1)}, bf16[48,64,512]{2,1,0:T(8,128)(2,1)}, u32[]{:S(2)}) copy-start(bf16[48,64,512]{2,1,0:T(8,128)(2,1)} %args_2_.10) | copy-start | bytes 9437188
  0.6 11.1 %copy-start.19 = (f32[512]{0:T(512)S(1)}, f32[512]{0:T(512)}, u32[]{:S(2)}) copy-start(f32[512]{0:T(512)} %param.13) | copy-start | bytes 6148
  4.7 18.1 %collective-permute-start.1 = (bf16[2,48,768]{2,0,1:T(2,128)(2,1)S(1)}, bf16[2,48,768]{2,0,1:T(2,128)(2,1)S(1)}, u32[]{:S(2)}, u32[]{:S(2)}) collective-permute-start(bf16[2,48,768]{2,0,1:T(2,128)(2,1)S(1)} %copy.16), channel_id=1, source_target_pairs={{1,0},{2,1},{3,2},{5,4},{6,5},{7,6},{9,8},{10,9},{11,10},{13,12},{... | collective-permute-start | bytes 442376 | tf_op jit(solution)/shard_map/ppermute | solution.py:507
  7.0 15.8 %collective-permute-start = (bf16[2,48,768]{2,0,1:T(2,128)(2,1)S(1)}, bf16[2,48,768]{2,0,1:T(2,128)(2,1)S(1)}, u32[]{:S(2)}, u32[]{:S(2)}) collective-permute-start(bf16[2,48,768]{2,0,1:T(2,128)(2,1)S(1)} %copy.15), channel_id=1, source_target_pairs={{0,1},{1,2},{2,3},{4,5},{5,6},{6,7},{8,9},{9,10},{10,11},{12,13},{... | collective-permute-start | bytes 442376 | tf_op jit(solution)/shard_map/ppermute | solution.py:507
  16.3 6.6 %copy-start.10 = (bf16[2,64,768]{2,1,0:T(8,128)(2,1)S(1)}, bf16[2,64,768]{2,1,0:T(8,128)(2,1)}, u32[]{:S(2)}) copy-start(bf16[2,64,768]{2,1,0:T(8,128)(2,1)} %get-tuple-element.32.line_top) | copy-start | bytes 589828
  16.3 6.6 %copy-start.11 = (bf16[2,64,768]{2,1,0:T(8,128)(2,1)S(1)}, bf16[2,64,768]{2,1,0:T(8,128)(2,1)}, u32[]{:S(2)}) copy-start(bf16[2,64,768]{2,1,0:T(8,128)(2,1)} %get-tuple-element.27.line_bot) | copy-start | bytes 589828
  22.9 13.3 %copy-start.5 = (bf16[3,3,384,512]{3,2,1,0:T(8,128)(2,1)S(1)}, bf16[3,3,384,512]{3,2,1,0:T(8,128)(2,1)}, u32[]{:S(2)}) copy-start(bf16[3,3,384,512]{3,2,1,0:T(8,128)(2,1)} %param.12) | copy-start | bytes 10616836
  22.9 13.3 %copy-start.12 = (bf16[2,48,768]{2,1,0:T(8,128)(2,1)S(1)}, bf16[2,48,768]{2,1,0:T(8,128)(2,1)}, u32[]{:S(2)}) copy-start(bf16[2,48,768]{2,1,0:T(8,128)(2,1)} %get-tuple-element.29.side_left) | copy-start | bytes 442372
  22.9 13.3 %copy-start.13 = (bf16[2,48,768]{2,1,0:T(8,128)(2,1)S(1)}, bf16[2,48,768]{2,1,0:T(8,128)(2,1)}, u32[]{:S(2)}) copy-start(bf16[2,48,768]{2,1,0:T(8,128)(2,1)} %get-tuple-element.28.side_right) | copy-start | bytes 442372
  22.9 13.2 %collective-permute-start.2 = (bf16[2,68,768]{2,1,0:T(8,128)(2,1)S(1)}, bf16[2,68,768]{2,1,0:T(8,128)(2,1)S(1)}, u32[]{:S(2)}, u32[]{:S(2)}) collective-permute-start(bf16[2,68,768]{2,1,0:T(8,128)(2,1)S(1)} %get-tuple-element.37), channel_id=1, source_target_pairs={{0,4},{4,8},{8,12},{12,16},{16,20},{20,24},{24,28},{1,5},{5,9},{9,... | collective-permute-start | bytes 626696 | tf_op jit(solution)/shard_map/ppermute | solution.py:507
  27.6 8.6 %collective-permute-start.3 = (bf16[2,68,768]{2,1,0:T(8,128)(2,1)S(1)}, bf16[2,68,768]{2,1,0:T(8,128)(2,1)S(1)}, u32[]{:S(2)}, u32[]{:S(2)}) collective-permute-start(bf16[2,68,768]{2,1,0:T(8,128)(2,1)S(1)} %get-tuple-element.38), channel_id=1, source_target_pairs={{4,0},{8,4},{12,8},{16,12},{20,16},{24,20},{28,24},{5,1},{9,5},{13... | collective-permute-start | bytes 626696 | tf_op jit(solution)/shard_map/ppermute | solution.py:507
  36.1 2.4 %copy-start.3 = (bf16[48,64,128]{2,1,0:T(8,128)(2,1)}, bf16[48,64,128]{2,1,0:T(8,128)(2,1)S(1)}, u32[]{:S(2)}) copy-start(bf16[48,64,128]{2,1,0:T(8,128)(2,1)S(1)} %get-tuple-element.35.args_3_.args_4_.args_5_) | copy-start | bytes 2359300
  36.1 2.4 %copy-start.6 = (f32[48,64,128]{2,1,0:T(8,128)}, f32[48,64,128]{2,1,0:T(8,128)S(1)}, u32[]{:S(2)}) copy-start(f32[48,64,128]{2,1,0:T(8,128)S(1)} %get-tuple-element.36.args_6_) | copy-start | bytes 4718596
  38.4 9.5 %copy-start.14 = (f32[4,64,128]{2,1,0:T(8,128)}, f32[4,64,128]{2,1,0:T(8,128)S(1)}, u32[]{:S(2)}) copy-start(f32[4,64,128]{2,1,0:T(8,128)S(1)} %get-tuple-element.41.args_11_) | copy-start | bytes 393220
  38.5 9.5 %copy-start.15 = (f32[4,64,128]{2,1,0:T(8,128)}, f32[4,64,128]{2,1,0:T(8,128)S(1)}, u32[]{:S(2)}) copy-start(f32[4,64,128]{2,1,0:T(8,128)S(1)} %get-tuple-element.42.args_12_) | copy-start | bytes 393220
  38.5 9.5 %copy-start.16 = (f32[4,64,128]{2,1,0:T(8,128)}, f32[4,64,128]{2,1,0:T(8,128)S(1)}, u32[]{:S(2)}) copy-start(f32[4,64,128]{2,1,0:T(8,128)S(1)} %get-tuple-element.39.args_9_) | copy-start | bytes 393220
  38.5 9.4 %copy-start.17 = (f32[4,64,128]{2,1,0:T(8,128)}, f32[4,64,128]{2,1,0:T(8,128)S(1)}, u32[]{:S(2)}) copy-start(f32[4,64,128]{2,1,0:T(8,128)S(1)} %get-tuple-element.40.args_10_) | copy-start | bytes 393220
  38.5 9.4 %copy-start.18 = (f32[2,64,256]{2,1,0:T(8,128)}, f32[2,64,256]{2,1,0:T(8,128)S(1)}, u32[]{:S(2)}) copy-start(f32[2,64,256]{2,1,0:T(8,128)S(1)} %get-tuple-element.43.args_13_) | copy-start | bytes 393220
  48.7 20.5 %all-to-all-start.1 = ((bf16[32,4,16,128]{3,2,1,0:T(8,128)(2,1)}), bf16[32,4,16,128]{3,2,1,0:T(8,128)(2,1)S(1)}, u32[]{:S(2)}, u32[]{:S(2)}) async-start(bf16[32,4,16,128]{3,2,1,0:T(8,128)(2,1)} %bitcast.20), calls=%async_computation.1 | async-start | bytes 1048576 | tf_op jit(solution)/shard_map/all_to_all | solution.py:573
  54.0 18.5 %copy-start.20 = (bf16[128,768]{1,0:T(8,128)(2,1)S(1)}, bf16[128,768]{1,0:T(8,128)(2,1)}, u32[]{:S(2)}) copy-start(bf16[128,768]{1,0:T(8,128)(2,1)} %w_qkv.3) | copy-start | bytes 589828
  54.0 18.5 %copy-start.21 = (bf16[128,512]{1,0:T(8,128)(2,1)S(1)}, bf16[128,512]{1,0:T(8,128)(2,1)}, u32[]{:S(2)}) copy-start(bf16[128,512]{1,0:T(8,128)(2,1)} %w_up.3) | copy-start | bytes 393220
  54.0 18.5 %copy-start.22 = (bf16[512,128]{1,0:T(8,128)(2,1)S(1)}, bf16[512,128]{1,0:T(8,128)(2,1)}, u32[]{:S(2)}) copy-start(bf16[512,128]{1,0:T(8,128)(2,1)} %w_down.3) | copy-start | bytes 393220
  54.0 18.5 %copy-start.23 = (bf16[256,128]{1,0:T(8,128)(2,1)S(1)}, bf16[256,128]{1,0:T(8,128)(2,1)}, u32[]{:S(2)}) copy-start(bf16[256,128]{1,0:T(8,128)(2,1)} %w_out.3) | copy-start | bytes 196612
  69.3 13.5 %all-to-all-start = ((bf16[32,2,16,128]{3,2,1,0:T(8,128)(2,1)}), bf16[32,2,16,128]{3,2,1,0:T(8,128)(2,1)S(1)}, u32[]{:S(2)}, u32[]{:S(2)}) async-start(bf16[32,2,16,128]{3,2,1,0:T(8,128)(2,1)} %bitcast.27), calls=%async_computation | async-start | bytes 524288 | tf_op jit(solution)/shard_map/all_to_all | solution.py:573
  (6 other events, 10.0 us)

commit v5 on v4

--- a/solution.py
+++ b/solution.py
@@ -112,6 +112,8 @@
         for part, start in ((x, 0), (h, latent)):
             size = part.shape[1]
             pieces = three_columns(part, low[:, start : start + size], high[:, start : start + size])
+            if 0 < pos <= depth and (start == 0 or not ring):
+                pieces = pieces[0], (frame, hid)[start > 0][pos - 1], pieces[2]
             for tap in range(3):
                 spread[pos, :, tap * chans + start : tap * chans + start + size] = pieces[tap]
 
@@ -122,10 +124,11 @@
             for load in loads:
                 load.wait()
 
-    lhs = jnp.concatenate(
-        [spread[tap : tap + depth].reshape(depth * cols, 3 * chans) for tap in range(3)], axis=1
-    )
-    gates = jnp.dot(lhs, ref["held"][...], preferred_element_type=F32) + ref["bias"][...]
+    gates = ref["bias"][...]
+    for tap in range(3):
+        lhs = spread[tap : tap + depth].reshape(depth * cols, 3 * chans)
+        taps = ref["held"][tap * 3 * chans : (tap + 1) * 3 * chans, :]
+        gates = gates + jnp.dot(lhs, taps, preferred_element_type=F32)
     for row in range(depth):
         cell_prev = ref["cell"][row]
         if ring:
@@ -219,7 +222,7 @@
 
 def pack_kernel(
     frame_low, frame_high, frame_top, frame_bot, hid_low, hid_high, hid_top, hid_bot,
-    cell_low, cell_high, cell_top, cell_bot, side_low, side_high, line_top, line_bot, flat,
+    cell_low, cell_high, cell_top, cell_bot, send_low, send_high, side_low, side_high, line_top, line_bot, flat,
 ):
     latent, width = frame_low.shape[2] // 2, hid_low.shape[2]
     chans = latent + width
@@ -232,9 +235,9 @@
             out[:, :, to : to + size] = frame[:, :, start : start + size]
         out[:, :, latent:chans] = hid[...]
         out[:, :, chans : chans + width] = cell[...].astype(BF)
-    for out, frame, hid, cell, first, start in (
-        (side_low, frame_low, hid_low, cell_low, 0, 0),
-        (side_high, frame_high, hid_high, cell_high, frame_high.shape[1] - 8, 6),
+    for out, send, frame, hid, cell, first, start in (
+        (side_low, send_low, frame_low, hid_low, cell_low, 0, 0),
+        (side_high, send_high, frame_high, hid_high, cell_high, frame_high.shape[1] - 8, 6),
     ):
         tall = frame.shape[0]
         near = slice(first, first + 8)
@@ -247,6 +250,7 @@
                 part = hid[:, near, to - latent : to - latent + LANES].astype(F32)
             else:
                 part = cell[:, :, to - chans : to - chans + LANES]
+            send[:, :, to : to + LANES] = part[:, start : start + 2].astype(BF)
             flat[...] = part.reshape(tall * 8, LANES)
             for place in range(2):
                 out[place, :, to : to + LANES] = flat[pl.ds(start + place, tall, stride=8), :].astype(BF)
@@ -267,7 +271,8 @@
         ]
 
     deep = span + 2 * width
-    shapes = [jax.ShapeDtypeStruct((2, rows, deep), BF)] * 2 + [jax.ShapeDtypeStruct((2, cols, deep), BF)] * 2
+    shapes = [jax.ShapeDtypeStruct((rows, 2, deep), BF)] * 2 + [jax.ShapeDtypeStruct((2, rows, deep), BF)] * 2
+    shapes += [jax.ShapeDtypeStruct((2, cols, deep), BF)] * 2
     return pl.pallas_call(
         pack_kernel,
         grid=(1,),
@@ -392,7 +397,8 @@
     for half in range(2):
         part = jnp.concatenate(raised[half], axis=0)
         total = jnp.dot(part, ones[...], preferred_element_type=F32)
-        attn = (part.astype(F32) * pl.reciprocal(total)).astype(BF)
+        guess = pl.reciprocal(total, approx=True)
+        attn = (part.astype(F32) * (guess * (2.0 - total * guess))).astype(BF)
         column = []
         for g in range(groups):
             held = values[g * group : (g + 1) * group, half * tile : (half + 1) * tile]
@@ -506,13 +512,11 @@
         pairs = [(i, i + step) for i in range(count) if 0 <= i + step < count]
         return lax.ppermute(value, axis, pairs)
 
-    side_left, side_right, line_top, line_bot = pack_step(frames, hidden_state, cell_state)
-    from_left = shifted(side_right, "gx", 1)
-    from_right = shifted(side_left, "gx", -1)
-    from_left, from_right = lax.optimization_barrier((from_left, from_right))
-    beside = jnp.concatenate([from_left, from_right], axis=0)
-    to_down = jnp.concatenate([line_bot, beside[:, -2:].transpose(1, 0, 2)], axis=1)
-    to_up = jnp.concatenate([line_top, beside[:, :2].transpose(1, 0, 2)], axis=1)
+    send_left, send_right, side_left, side_right, line_top, line_bot = pack_step(frames, hidden_state, cell_state)
+    from_left = shifted(send_right, "gx", 1)
+    from_right = shifted(send_left, "gx", -1)
+    to_down = jnp.concatenate([line_bot, from_left[-2:], from_right[-2:]], axis=1)
+    to_up = jnp.concatenate([line_top, from_left[:2], from_right[:2]], axis=1)
 
     tile_shapes = (jax.ShapeDtypeStruct((rows, cols, width), BF), jax.ShapeDtypeStruct((rows, cols, width), F32))
     carry = ()
@@ -533,7 +537,8 @@
     strip_shape = jax.ShapeDtypeStruct((4, length, width), F32)
     beside_shape = jax.ShapeDtypeStruct((2, length, latent), F32)
     shapes = (line_shape, line_shape, strip_shape, strip_shape, beside_shape)
-    around = (from_up, from_down, line_top, line_bot, from_left, from_right, side_left, side_right)
+    turned = from_left.transpose(1, 0, 2), from_right.transpose(1, 0, 2)
+    around = (from_up, from_down, line_top, line_bot, *turned, side_left, side_right)
     line_hid, line_cell, strip_hid, strip_cell, beside = pl.pallas_call(
         ring_kernel,
         grid=(1,),

time: 115 us -> 116 us (level)
  local copies, waits for them, and re-layouts: 7.51 us -> 5.5 us
  Pallas kernels: 52.3 us -> 54.3 us
    all_to_all x2, starting transfers between devices: 8.38 us -> 10.5 us  [body(): lax.all_to_all(sent, ('gy', 'gx'), split_axis=0, concat_axis=0, tiled=True)]
    pallas_call x2 -> x0, local copies, waits for them, and re-layouts: 2.05 us -> none  [pack_step(): pl.pallas_call(pack_kernel, grid=(1,), in_specs=[*edge(frames, near), *ed...]
    pallas_call x4, Pallas kernels: 31.5 us -> 33.2 us  [conv_step(): pl.pallas_call(functools.partial(conv_kernel, first, last, refs, packed),...]
  transfers between devices with their start and end apart: 6 -> 6, of which waited for: 2 -> 2; matrix products, arithmetic and copies ran while one was open for 1% -> 0% of each run, Pallas kernels for 27% -> 28%
where the time goes in v5:
time: 116 us; the launch traced here: 115 us
  Pallas kernels  54.3 us (47%)
  blocking collectives  25.6 us (22%)
  starting transfers between devices  21.9 us (19%)
  waiting for transfers between devices  6.8 us (6%)
  local copies, waits for them, and re-layouts  5.5 us (5%)
    pallas_call x4, Pallas kernels, conv_step(): pl.pallas_call(functools.partial(conv_kernel, first, last, refs, packed),...  33.2 us
    all_to_all x1, blocking collectives, body(): lax.all_to_all(done, ('gy', 'gx'), split_axis=0, concat_axis=0, tiled=True)  25.6 us
    pallas_call x2, Pallas kernels, block_step(): pl.pallas_call(block_kernel, grid=(lanes, piece_y), in_specs=in_specs, ou...  14.2 us
    ppermute x4, starting transfers between devices, shifted(): return lax.ppermute(value, axis, pairs)  11.5 us
    all_to_all x2, starting transfers between devices, body(): lax.all_to_all(sent, ('gy', 'gx'), split_axis=0, concat_axis=0, tiled=True)  10.5 us
    all_to_all x2, waiting for transfers between devices, body(): lax.all_to_all(sent, ('gy', 'gx'), split_axis=0, concat_axis=0, tiled=True)  6.79 us
    unnamed x48, local copies, waits for them, and re-layouts  5.44 us
    pallas_call x1, Pallas kernels, pack_step(): pl.pallas_call(pack_kernel, grid=(1,), in_specs=[*edge(frames, near), *ed...  3.28 us
  transfers between devices with their start and end apart: 6, of which 2 were waited for; matrix products, arithmetic and copies ran while one was open for 0% of the time, Pallas kernels for 28%

profile of v5, /device:TPU:1, one launch (start us, length us, event | category | flops | bytes accessed | tf_op | source)
XLA Modules:
  0.0 115.3 jit_solution(5899747366911306735)
XLA Ops:
  0.6 0.0 copy-start
  0.7 3.3 %shard_map.105 = (bf16[48,2,768]{2,1,0:T(2,128)(2,1)}, bf16[48,2,768]{2,1,0:T(2,128)(2,1)}, bf16[2,48,768]{2,1,0:T(8,128)(2,1)}, bf16[2,48,768]{2,1,0:T(8,128)(2...) custom-call(bf16[48,64,512]{2,1,0:T(8,128)(2,1)} %args_2_.10, bf16[48,64,512]{2,1,0:T(8,128)(2,1)} %args_2_.10, ...), custom_call_target="tpu_custom_call" | custom-call | bytes 4000000 | tf_op jit(solution)/shard_map/pallas_call | solution.py:276
  3.9 4.0 %collective-permute-start = (bf16[48,2,768]{2,1,0:T(2,128)(2,1)}, bf16[48,2,768]{2,1,0:T(2,128)(2,1)S(1)}, u32[]{:S(2)}, u32[]{:S(2)}) collective-permute-start(bf16[48,2,768]{2,1,0:T(2,128)(2,1)} %get-tuple-element.28), channel_id=1, source_target_pairs={{0,1},{1,2},{2,3},{4,5},{5,6},{6,7},{8,9},{9,10},{10,11},{12,13},{... | collective-permute-start | bytes 442376 | tf_op jit(solution)/shard_map/ppermute | solution.py:513
  8.0 1.3 %collective-permute-start.1 = (bf16[48,2,768]{2,1,0:T(2,128)(2,1)}, bf16[48,2,768]{2,1,0:T(2,128)(2,1)S(1)}, u32[]{:S(2)}, u32[]{:S(2)}) collective-permute-start(bf16[48,2,768]{2,1,0:T(2,128)(2,1)} %get-tuple-element.29), channel_id=1, source_target_pairs={{1,0},{2,1},{3,2},{5,4},{6,5},{7,6},{9,8},{10,9},{11,10},{13,12},{... | collective-permute-start | bytes 442376 | tf_op jit(solution)/shard_map/ppermute | solution.py:513
  9.3 0.0 copy-start.1
  9.3 1.4 %copy-done.1 = f32[48,64,128]{2,1,0:T(8,128)S(1)} copy-done((f32[48,64,128]{2,1,0:T(8,128)S(1)}, f32[48,64,128]{2,1,0:T(8,128)}, u32[]{:S(2)}) %copy-start.1) | copy-done | bytes 1572888
  10.7 1.1 copy-done.2
  11.8 2.0 %copy-done.4 = bf16[3,3,384,512]{3,2,1,0:T(8,128)(2,1)S(1)} copy-done((bf16[3,3,384,512]{3,2,1,0:T(8,128)(2,1)S(1)}, bf16[3,3,384,512]{3,2,1,0:T(8,128)(2,1)}, u32[]{:S(2)}) %copy-start.4) | copy-done | bytes 3538968
  13.8 6.9 %shard_map.104 = (bf16[48,64,128]{2,1,0:T(8,128)(2,1)S(1)}, f32[48,64,128]{2,1,0:T(8,128)S(1)}) custom-call(bf16[48,64,512]{2,1,0:T(8,128)(2,1)S(1)} %copy-done, bf16[48,64,512]{2,1,0:T(8,128)(2,1)S(1)} %copy-done, bf16[48,64,512]{2,1,0:T(8,128)(2,1)S(1)} %copy-done, bf16[48,64,128]{2,1,0:T(8,128)(2,1)S(1)} %copy-done.2, bf16[48,64,128]{2,1,0:T(8,128)(2,1)S(1)} %copy-done.2, ...), custom_call_target="tpu_custom_call" | custom-call | flops 5435817984 | bytes 6684672 | tf_op jit(solution)/shard_map/pallas_call | solution.py:208
  20.9 4.2 %collective-permute-start.2 = (bf16[2,68,768]{2,1,0:T(8,128)(2,1)S(1)}, bf16[2,68,768]{2,1,0:T(8,128)(2,1)S(1)}, u32[]{:S(2)}, u32[]{:S(2)}) collective-permute-start(bf16[2,68,768]{2,1,0:T(8,128)(2,1)S(1)} %get-tuple-element.35), channel_id=1, source_target_pairs={{0,4},{4,8},{8,12},{12,16},{16,20},{20,24},{24,28},{1,5},{5,9},{9,... | collective-permute-start | bytes 626696 | tf_op jit(solution)/shard_map/ppermute | solution.py:513
  25.2 1.9 %collective-permute-start.3 = (bf16[2,68,768]{2,1,0:T(8,128)(2,1)S(1)}, bf16[2,68,768]{2,1,0:T(8,128)(2,1)S(1)}, u32[]{:S(2)}, u32[]{:S(2)}) collective-permute-start(bf16[2,68,768]{2,1,0:T(8,128)(2,1)S(1)} %get-tuple-element.36), channel_id=1, source_target_pairs={{4,0},{8,4},{12,8},{16,12},{20,16},{24,20},{28,24},{5,1},{9,5},{13... | collective-permute-start | bytes 626696 | tf_op jit(solution)/shard_map/ppermute | solution.py:513
  27.1 7.0 %shard_map.106 = (bf16[48,64,128]{2,1,0:T(8,128)(2,1)S(1)}, f32[48,64,128]{2,1,0:T(8,128)S(1)}) custom-call(bf16[48,64,512]{2,1,0:T(8,128)(2,1)S(1)} %copy-done, bf16[48,64,512]{2,1,0:T(8,128)(2,1)S(1)} %copy-done, bf16[48,64,512]{2,1,0:T(8,128)(2,1)S(1)} %copy-done, ...), custom_call_target="tpu_custom_call", output_to_operand_aliasing={{0}: (9, {}), {1}: (10, {})} | custom-call | flops 5435817984 | bytes 6684672 | tf_op jit(solution)/shard_map/pallas_call | solution.py:208
  34.2 2.2 %shard_map.107 = (f32[4,64,128]{2,1,0:T(8,128)S(1)}, f32[4,64,128]{2,1,0:T(8,128)S(1)}, f32[4,64,128]{2,1,0:T(8,128)S(1)}, f32[4,64,128]{2,1,0:T(8,128)S(1)}, f32[2,64,256]{2,1,0:T(8,128)S(1)}) custom-call(bf16[2,68,768]{2,1,0:T(8,128)(2,1)S(1)} %collective-permute-done.2.above.args_14_, bf16[2,68,768]{2,1,0:T(8,128)(2,1)S(1)} %collective-permute-done.3.below.args_15_, ...), custom_call_target="tpu_custom_call" | custom-call | flops 1811939328 | bytes 3538944 | tf_op jit(solution)/shard_map/pallas_call | solution.py:542
  36.5 9.9 %shard_map.108 = (bf16[8,4,4,16,128]{4,3,2,1,0:T(8,128)(2,1)S(1)}, f32[48,64,128]{2,1,0:T(8,128)}) custom-call(bf16[48,64,512]{2,1,0:T(8,128)(2,1)S(1)} %copy-done, bf16[48,64,512]{2,1,0:T(8,128)(2,1)S(1)} %copy-done, bf16[48,64,512]{2,1,0:T(8,128)(2,1)S(1)} %copy-done, bf16[48,64,128]{2,1,0:T(8,128)(2,1)S(1)} %get-tuple-element.33.args_3_.args_4_.args_5_, ...), custom_call_target="tpu_custom_call" | custom-call | flops 7247757312 | bytes 7733248 | tf_op jit(solution)/shard_map/pallas_call | solution.py:208
  46.5 0.8 copy-done.7
  47.3 7.3 %all-to-all-start.1 = ((bf16[32,4,16,128]{3,2,1,0:T(8,128)(2,1)}), bf16[32,4,16,128]{3,2,1,0:T(8,128)(2,1)S(1)}, u32[]{:S(2)}, u32[]{:S(2)}) async-start(bf16[32,4,16,128]{3,2,1,0:T(8,128)(2,1)} %bitcast.18), calls=%async_computation.1 | async-start | bytes 1048576 | tf_op jit(solution)/shard_map/all_to_all | solution.py:578
  54.6 9.3 %shard_map.109 = (bf16[8,4,2,16,128]{4,3,2,1,0:T(8,128)(2,1)}, f32[48,64,128]{2,1,0:T(8,128)}) custom-call(bf16[48,64,512]{2,1,0:T(8,128)(2,1)} %args_2_.10, bf16[48,64,512]{2,1,0:T(8,128)(2,1)} %args_2_.10, bf16[48,64,512]{2,1,0:T(8,128)(2,1)} %args_2_.10, bf16[48,64,128]{2,1,0:T(8,128)(2,1)} %copy-done.3, ...), custom_call_target="tpu_custom_call", output_to_operand_aliasing={{1}: (16, {})} | custom-call | flops 3623878656 | bytes 5636096 | tf_op jit(solution)/shard_map/pallas_call | solution.py:208
  64.0 5.9 %all-to-all-done.1 = bf16[32,4,16,128]{3,2,1,0:T(8,128)(2,1)S(1)} async-done(((bf16[32,4,16,128]{3,2,1,0:T(8,128)(2,1)}), bf16[32,4,16,128]{3,2,1,0:T(8,128)(2,1)S(1)}, u32[]{:S(2)}, u32[]{:S(2)}) %all-to-all-start.1) | async-done | bytes 524320 | tf_op jit(solution)/shard_map/all_to_all | solution.py:578
  69.9 3.2 %all-to-all-start = ((bf16[32,2,16,128]{3,2,1,0:T(8,128)(2,1)}), bf16[32,2,16,128]{3,2,1,0:T(8,128)(2,1)S(1)}, u32[]{:S(2)}, u32[]{:S(2)}) async-start(bf16[32,2,16,128]{3,2,1,0:T(8,128)(2,1)} %bitcast.25), calls=%async_computation | async-start | bytes 524288 | tf_op jit(solution)/shard_map/all_to_all | solution.py:578
  73.1 9.4 %shard_map.110.rest_0_ = bf16[8,1,4,6,16,128]{5,4,3,2,1,0:T(8,128)(2,1)S(1)} custom-call(bf16[8,1,4,4,16,128]{5,4,3,2,1,0:T(8,128)(2,1)S(1)} %bitcast.17, bf16[128,768]{1,0:T(8,128)(2,1)S(1)} %copy-done.18, bf16[256,128]{1,0:T(8,128)(2,1)S(1)} %copy-done.23, bf16[128,512]{1,0:T(8,128)(2,1)S(1)} %copy-done.21, bf16[512,128]{1,0:T(8,128)(2,1)S(1)} %copy-done.22), custom_call_target="tpu_custom_call" | custom-call | flops 6144000000 | bytes 1848576 | tf_op jit(solution)/shard_map/pallas_call | solution.py:438
  82.5 0.9 all-to-all-done
  83.4 4.8 %shard_map.111 = bf16[8,1,4,6,16,128]{5,4,3,2,1,0:T(8,128)(2,1)S(1)} custom-call(bf16[8,1,4,2,16,128]{5,4,3,2,1,0:T(8,128)(2,1)S(1)} %bitcast.19, bf16[128,768]{1,0:T(8,128)(2,1)S(1)} %copy-done.18, bf16[256,128]{1,0:T(8,128)(2,1)S(1)} %copy-done.23, bf16[128,512]{1,0:T(8,128)(2,1)S(1)} %copy-done.21, ...), custom_call_target="tpu_custom_call", output_to_operand_aliasing={{}: (5, {})} | custom-call | flops 3072000000 | bytes 1324288 | tf_op jit(solution)/shard_map/pallas_call | solution.py:438
  88.2 25.6 %all_to_all.15 = bf16[32,6,16,128]{3,2,1,0:T(8,128)(2,1)S(1)} all-to-all(bf16[32,6,16,128]{3,2,1,0:T(8,128)(2,1)S(1)} %bitcast.16), channel_id=1, replica_groups=mesh['gy'=8,'gx'=4] {'gy','gx'}, dimensions={0} | all-to-all | bytes 1572864 | tf_op jit(solution)/shard_map/all_to_all | solution.py:585
  113.8 1.5 %shard_map.112 = bf16[48,64,128]{2,1,0:T(8,128)(2,1)} custom-call(bf16[8,4,6,16,128]{4,3,2,1,0:T(8,128)(2,1)S(1)} %bitcast.15), custom_call_target="tpu_custom_call" | custom-call | bytes 1572864 | tf_op jit(solution)/shard_map/pallas_call | solution.py:484
  (51 shorter events, 0.2 us)
Async XLA Ops:
  0.6 8.6 %copy-start = (bf16[48,64,512]{2,1,0:T(8,128)(2,1)S(1)}, bf16[48,64,512]{2,1,0:T(8,128)(2,1)}, u32[]{:S(2)}) copy-start(bf16[48,64,512]{2,1,0:T(8,128)(2,1)} %args_2_.10) | copy-start | bytes 9437188
  0.6 8.6 %copy-start.17 = (f32[512]{0:T(512)S(1)}, f32[512]{0:T(512)}, u32[]{:S(2)}) copy-start(f32[512]{0:T(512)} %param.13) | copy-start | bytes 6148
  3.9 16.8 %collective-permute-start = (bf16[48,2,768]{2,1,0:T(2,128)(2,1)}, bf16[48,2,768]{2,1,0:T(2,128)(2,1)S(1)}, u32[]{:S(2)}, u32[]{:S(2)}) collective-permute-start(bf16[48,2,768]{2,1,0:T(2,128)(2,1)} %get-tuple-element.28), channel_id=1, source_target_pairs={{0,1},{1,2},{2,3},{4,5},{5,6},{6,7},{8,9},{9,10},{10,11},{12,13},{... | collective-permute-start | bytes 442376 | tf_op jit(solution)/shard_map/ppermute | solution.py:513
  8.0 12.8 %collective-permute-start.1 = (bf16[48,2,768]{2,1,0:T(2,128)(2,1)}, bf16[48,2,768]{2,1,0:T(2,128)(2,1)S(1)}, u32[]{:S(2)}, u32[]{:S(2)}) collective-permute-start(bf16[48,2,768]{2,1,0:T(2,128)(2,1)} %get-tuple-element.29), channel_id=1, source_target_pairs={{1,0},{2,1},{3,2},{5,4},{6,5},{7,6},{9,8},{10,9},{11,10},{13,12},{... | collective-permute-start | bytes 442376 | tf_op jit(solution)/shard_map/ppermute | solution.py:513
  13.8 7.0 %copy-start.10 = (bf16[2,64,768]{2,1,0:T(8,128)(2,1)S(1)}, bf16[2,64,768]{2,1,0:T(8,128)(2,1)}, u32[]{:S(2)}) copy-start(bf16[2,64,768]{2,1,0:T(8,128)(2,1)} %get-tuple-element.30.line_top) | copy-start | bytes 589828
  13.8 7.0 %copy-start.11 = (bf16[2,64,768]{2,1,0:T(8,128)(2,1)S(1)}, bf16[2,64,768]{2,1,0:T(8,128)(2,1)}, u32[]{:S(2)}) copy-start(bf16[2,64,768]{2,1,0:T(8,128)(2,1)} %get-tuple-element.27.line_bot) | copy-start | bytes 589828
  20.9 13.3 %copy-start.5 = (bf16[3,3,384,512]{3,2,1,0:T(8,128)(2,1)S(1)}, bf16[3,3,384,512]{3,2,1,0:T(8,128)(2,1)}, u32[]{:S(2)}) copy-start(bf16[3,3,384,512]{3,2,1,0:T(8,128)(2,1)} %param.12) | copy-start | bytes 10616836
  20.9 13.3 %copy-start.19 = (bf16[2,48,768]{2,1,0:T(8,128)(2,1)S(1)}, bf16[2,48,768]{2,1,0:T(8,128)(2,1)}, u32[]{:S(2)}) copy-start(bf16[2,48,768]{2,1,0:T(8,128)(2,1)} %get-tuple-element.37.side_left) | copy-start | bytes 442372
  20.9 13.3 %copy-start.20 = (bf16[2,48,768]{2,1,0:T(8,128)(2,1)S(1)}, bf16[2,48,768]{2,1,0:T(8,128)(2,1)}, u32[]{:S(2)}) copy-start(bf16[2,48,768]{2,1,0:T(8,128)(2,1)} %get-tuple-element.38.side_right) | copy-start | bytes 442372
  20.9 13.2 %collective-permute-start.2 = (bf16[2,68,768]{2,1,0:T(8,128)(2,1)S(1)}, bf16[2,68,768]{2,1,0:T(8,128)(2,1)S(1)}, u32[]{:S(2)}, u32[]{:S(2)}) collective-permute-start(bf16[2,68,768]{2,1,0:T(8,128)(2,1)S(1)} %get-tuple-element.35), channel_id=1, source_target_pairs={{0,4},{4,8},{8,12},{12,16},{16,20},{20,24},{24,28},{1,5},{5,9},{9,... | collective-permute-start | bytes 626696 | tf_op jit(solution)/shard_map/ppermute | solution.py:513
  25.2 9.0 %collective-permute-start.3 = (bf16[2,68,768]{2,1,0:T(8,128)(2,1)S(1)}, bf16[2,68,768]{2,1,0:T(8,128)(2,1)S(1)}, u32[]{:S(2)}, u32[]{:S(2)}) collective-permute-start(bf16[2,68,768]{2,1,0:T(8,128)(2,1)S(1)} %get-tuple-element.36), channel_id=1, source_target_pairs={{4,0},{8,4},{12,8},{16,12},{20,16},{24,20},{28,24},{5,1},{9,5},{13... | collective-permute-start | bytes 626696 | tf_op jit(solution)/shard_map/ppermute | solution.py:513
  34.1 2.4 %copy-start.3 = (bf16[48,64,128]{2,1,0:T(8,128)(2,1)}, bf16[48,64,128]{2,1,0:T(8,128)(2,1)S(1)}, u32[]{:S(2)}) copy-start(bf16[48,64,128]{2,1,0:T(8,128)(2,1)S(1)} %get-tuple-element.33.args_3_.args_4_.args_5_) | copy-start | bytes 2359300
  34.1 2.4 %copy-start.6 = (f32[48,64,128]{2,1,0:T(8,128)}, f32[48,64,128]{2,1,0:T(8,128)S(1)}, u32[]{:S(2)}) copy-start(f32[48,64,128]{2,1,0:T(8,128)S(1)} %get-tuple-element.34.args_6_) | copy-start | bytes 4718596
  36.4 10.0 %copy-start.12 = (f32[4,64,128]{2,1,0:T(8,128)}, f32[4,64,128]{2,1,0:T(8,128)S(1)}, u32[]{:S(2)}) copy-start(f32[4,64,128]{2,1,0:T(8,128)S(1)} %get-tuple-element.41.args_11_) | copy-start | bytes 393220
  36.4 10.0 %copy-start.13 = (f32[4,64,128]{2,1,0:T(8,128)}, f32[4,64,128]{2,1,0:T(8,128)S(1)}, u32[]{:S(2)}) copy-start(f32[4,64,128]{2,1,0:T(8,128)S(1)} %get-tuple-element.42.args_12_) | copy-start | bytes 393220
  36.4 10.0 %copy-start.14 = (f32[4,64,128]{2,1,0:T(8,128)}, f32[4,64,128]{2,1,0:T(8,128)S(1)}, u32[]{:S(2)}) copy-start(f32[4,64,128]{2,1,0:T(8,128)S(1)} %get-tuple-element.39.args_9_) | copy-start | bytes 393220
  36.4 10.0 %copy-start.15 = (f32[4,64,128]{2,1,0:T(8,128)}, f32[4,64,128]{2,1,0:T(8,128)S(1)}, u32[]{:S(2)}) copy-start(f32[4,64,128]{2,1,0:T(8,128)S(1)} %get-tuple-element.40.args_10_) | copy-start | bytes 393220
  36.5 10.0 %copy-start.16 = (f32[2,64,256]{2,1,0:T(8,128)}, f32[2,64,256]{2,1,0:T(8,128)S(1)}, u32[]{:S(2)}) copy-start(f32[2,64,256]{2,1,0:T(8,128)S(1)} %get-tuple-element.43.args_13_) | copy-start | bytes 393220
  47.3 22.6 %all-to-all-start.1 = ((bf16[32,4,16,128]{3,2,1,0:T(8,128)(2,1)}), bf16[32,4,16,128]{3,2,1,0:T(8,128)(2,1)S(1)}, u32[]{:S(2)}, u32[]{:S(2)}) async-start(bf16[32,4,16,128]{3,2,1,0:T(8,128)(2,1)} %bitcast.18), calls=%async_computation.1 | async-start | bytes 1048576 | tf_op jit(solution)/shard_map/all_to_all | solution.py:578
  54.6 18.5 %copy-start.18 = (bf16[128,768]{1,0:T(8,128)(2,1)S(1)}, bf16[128,768]{1,0:T(8,128)(2,1)}, u32[]{:S(2)}) copy-start(bf16[128,768]{1,0:T(8,128)(2,1)} %w_qkv.3) | copy-start | bytes 589828
  54.6 18.5 %copy-start.21 = (bf16[128,512]{1,0:T(8,128)(2,1)S(1)}, bf16[128,512]{1,0:T(8,128)(2,1)}, u32[]{:S(2)}) copy-start(bf16[128,512]{1,0:T(8,128)(2,1)} %w_up.3) | copy-start | bytes 393220
  54.6 18.5 %copy-start.22 = (bf16[512,128]{1,0:T(8,128)(2,1)S(1)}, bf16[512,128]{1,0:T(8,128)(2,1)}, u32[]{:S(2)}) copy-start(bf16[512,128]{1,0:T(8,128)(2,1)} %w_down.3) | copy-start | bytes 393220
  54.6 18.5 %copy-start.23 = (bf16[256,128]{1,0:T(8,128)(2,1)S(1)}, bf16[256,128]{1,0:T(8,128)(2,1)}, u32[]{:S(2)}) copy-start(bf16[256,128]{1,0:T(8,128)(2,1)} %w_out.3) | copy-start | bytes 196612
  69.9 13.5 %all-to-all-start = ((bf16[32,2,16,128]{3,2,1,0:T(8,128)(2,1)}), bf16[32,2,16,128]{3,2,1,0:T(8,128)(2,1)S(1)}, u32[]{:S(2)}, u32[]{:S(2)}) async-start(bf16[32,2,16,128]{3,2,1,0:T(8,128)(2,1)} %bitcast.25), calls=%async_computation | async-start | bytes 524288 | tf_op jit(solution)/shard_map/all_to_all | solution.py:578
  (6 other events, 10.0 us)

commit v6 on v5

--- a/solution.py
+++ b/solution.py
@@ -48,15 +48,15 @@
     return before.astype(BF), wide.astype(BF), after.astype(BF)
 
 
-def conv_kernel(first, last, refs, packed, *args):
+def conv_kernel(start, rows, refs, packed, *args):
     ref = dict(zip(refs, args))
-    frame, hid = ref["frame"], ref["hid"]
-    cell_out, spread = ref["cell_out"], ref["spread"]
+    frame, hid, spread = ref["frame"], ref["hid"], ref["spread"]
+    hid_out, cell_out = ref["hid_out"], ref["cell_out"]
     ring = "strips_hid" in ref
-    step = pl.program_id(0)
-    depth, cols, latent = frame.shape
+    extent, cols, latent = frame.shape
     width = hid.shape[2]
     chans = latent + width
+    top, bot = start == 0, start + extent == rows
     loads = []
     if "weights" in ref:
         size = ref["weights"].shape[0] // LOADS
@@ -65,125 +65,122 @@
             loads.append(
                 pltpu.make_async_copy(ref["weights"].at[part], ref["held"].at[part], ref["sem"].at[place])
             )
-
-    if loads:
-
-        @pl.when(step == 0)
-        def _():
-            for load in loads:
-                load.start()
-
-    if ring:
-
-        @pl.when(step == 0)
-        def _():
-            for place, side in enumerate(("left", "right")):
-                ref[side][:, :latent] = ref["beside"][place]
-                ref[side][:, latent:] = ref["strips_hid"][3 * place]
-
-    block = first + step
-    base = block * depth
-    top, bot = block == 0, block == last
+    for load in loads:
+        load.start()
+
+    def beside(row):
+        if not ring:
+            return jnp.zeros((1, chans), F32), jnp.zeros((1, chans), F32)
+        at = row + 2
+        return tuple(
+            jnp.concatenate(
+                [ref["beside"][place, at : at + 1, :], ref["strips_hid"][3 * place, at : at + 1, :]], axis=1
+            )
+            for place in range(2)
+        )
+
+    def build(pos):
+        row = start + pos - 1
+        raw = None
+        if pos == 0 or pos == extent + 1:
+            name, outside = ("prev", top) if pos == 0 else ("next", bot)
+            if outside and not ring:
+                spread[pos] = jnp.zeros(spread.shape[1:], BF)
+                return
+            x, h = ref["frame_" + name][0].astype(F32), ref["hid_" + name][0].astype(F32)
+            if outside:
+                x = ref["frame_top" if pos == 0 else "frame_bot"][0, :cols].astype(F32)
+        else:
+            raw = frame[pos - 1], hid[pos - 1]
+            x, h = raw[0].astype(F32), raw[1].astype(F32)
+        low, high = beside(row)
+        if ring:
+            at = row + 2
+            place = lax.broadcasted_iota(jnp.int32, h.shape, 0)
+            h = jnp.where(place == 0, ref["strips_hid"][1, at : at + 1, :], h)
+            h = jnp.where(place == cols - 1, ref["strips_hid"][2, at : at + 1, :], h)
+            for spot, line in ((-1, 0), (0, 1), (rows - 1, 2), (rows, 3)):
+                if row == spot:
+                    h = ref["lines_hid"][line]
+        for part, (value, first) in enumerate(((x, 0), (h, latent))):
+            size = value.shape[1]
+            pieces = three_columns(value, low[:, first : first + size], high[:, first : first + size])
+            if raw is not None and (part == 0 or not ring):
+                pieces = pieces[0], raw[part], pieces[2]
+            for tap in range(3):
+                spread[pos, :, tap * chans + first : tap * chans + first + size] = pieces[tap]
+
+    def multiply(first, depth):
+        lhs = jnp.concatenate(
+            [spread[first + tap : first + tap + depth].reshape(depth * cols, 3 * chans) for tap in range(3)], axis=1
+        )
+        return jnp.dot(lhs, ref["held"][...], preferred_element_type=F32)
+
+    def activate(first, depth, gates):
+        for line in range(first, first + depth):
+            row = start + line
+            cell_prev = ref["cell"][line]
+            if ring:
+                at = row + 2
+                place = lax.broadcasted_iota(jnp.int32, cell_prev.shape, 0)
+                cell_prev = jnp.where(place == 0, ref["strips_cell"][1, at : at + 1, :], cell_prev)
+                cell_prev = jnp.where(place == cols - 1, ref["strips_cell"][2, at : at + 1, :], cell_prev)
+                if row == 0:
+                    cell_prev = ref["lines_cell"][1]
+                if row == rows - 1:
+                    cell_prev = ref["lines_cell"][2]
+            own = gates[(line - first) * cols : (line - first + 1) * cols] + ref["bias"][...]
+            new_cell, new_hidden = lstm(own, cell_prev)
+            cell_out[line] = new_cell
+            if not packed:
+                hid_out[line] = new_hidden.astype(BF)
+                continue
+            owners_x, piece_y = hid_out.shape[1:3]
+            local_m, piece_x = packed
+            for owner in range(owners_x):
+                picked = [
+                    new_hidden[(m * owners_x + owner) * piece_x : (m * owners_x + owner + 1) * piece_x]
+                    for m in range(local_m)
+                ]
+                hid_out[line // piece_y, owner, line % piece_y] = jnp.concatenate(picked, axis=0).astype(BF)
+
+    depth = step_rows(0, extent, 12)
     for pos in range(depth + 2):
-        if pos == 0:
-            x, h = ref["frame_prev"][0].astype(F32), ref["hid_prev"][0].astype(F32)
-        elif pos == depth + 1:
-            x, h = ref["frame_next"][0].astype(F32), ref["hid_next"][0].astype(F32)
-        else:
-            x, h = frame[pos - 1].astype(F32), hid[pos - 1].astype(F32)
-        low = high = jnp.zeros((1, chans), F32)
-        if ring:
-            here = pl.ds(base + pos + 1, 1)
-            low, high = ref["left"][here, :], ref["right"][here, :]
-            place = lax.broadcasted_iota(jnp.int32, h.shape, 0)
-            h = jnp.where(place == 0, ref["strips_hid"][1, here, :], h)
-            h = jnp.where(place == cols - 1, ref["strips_hid"][2, here, :], h)
-            for spot, edge, line in ((0, top, 0), (1, top, 1), (depth, bot, 2), (depth + 1, bot, 3)):
-                if pos == spot:
-                    h = jnp.where(edge, ref["lines_hid"][line], h)
-            if pos == 0:
-                x = jnp.where(top, ref["frame_top"][0, :cols].astype(F32), x)
-            if pos == depth + 1:
-                x = jnp.where(bot, ref["frame_bot"][0, :cols].astype(F32), x)
-        elif pos == 0:
-            x, h = jnp.where(top, 0.0, x), jnp.where(top, 0.0, h)
-        elif pos == depth + 1:
-            x, h = jnp.where(bot, 0.0, x), jnp.where(bot, 0.0, h)
-        for part, start in ((x, 0), (h, latent)):
-            size = part.shape[1]
-            pieces = three_columns(part, low[:, start : start + size], high[:, start : start + size])
-            if 0 < pos <= depth and (start == 0 or not ring):
-                pieces = pieces[0], (frame, hid)[start > 0][pos - 1], pieces[2]
-            for tap in range(3):
-                spread[pos, :, tap * chans + start : tap * chans + start + size] = pieces[tap]
-
-    if loads:
-
-        @pl.when(step == 0)
-        def _():
-            for load in loads:
-                load.wait()
-
-    gates = ref["bias"][...]
-    for tap in range(3):
-        lhs = spread[tap : tap + depth].reshape(depth * cols, 3 * chans)
-        taps = ref["held"][tap * 3 * chans : (tap + 1) * 3 * chans, :]
-        gates = gates + jnp.dot(lhs, taps, preferred_element_type=F32)
-    for row in range(depth):
-        cell_prev = ref["cell"][row]
-        if ring:
-            here = pl.ds(base + row + 2, 1)
-            place = lax.broadcasted_iota(jnp.int32, cell_prev.shape, 0)
-            cell_prev = jnp.where(place == 0, ref["strips_cell"][1, here, :], cell_prev)
-            cell_prev = jnp.where(place == cols - 1, ref["strips_cell"][2, here, :], cell_prev)
-            if row == 0:
-                cell_prev = jnp.where(top, ref["lines_cell"][1], cell_prev)
-            if row == depth - 1:
-                cell_prev = jnp.where(bot, ref["lines_cell"][2], cell_prev)
-        new_cell, new_hidden = lstm(gates[row * cols : (row + 1) * cols], cell_prev)
-        cell_out[row] = new_cell
-        hid_out = ref["hid_out"]
-        if not packed:
-            hid_out[row] = new_hidden.astype(BF)
-            continue
-        owners_x, piece_y = hid_out.shape[1:3]
-        local_m, piece_x = packed
-        line = step * depth + row
-        for owner in range(owners_x):
-            picked = [
-                new_hidden[(m * owners_x + owner) * piece_x : (m * owners_x + owner + 1) * piece_x]
-                for m in range(local_m)
-            ]
-            hid_out[lax.div(line, piece_y), owner, lax.rem(line, piece_y)] = jnp.concatenate(picked, axis=0).astype(BF)
+        build(pos)
+    for load in loads:
+        load.wait()
+    waiting = None
+    for first in range(0, extent, depth):
+        for pos in range(first + depth + 2, min(first + 2 * depth, extent) + 2):
+            build(pos)
+        gates = multiply(first, depth)
+        if waiting:
+            activate(*waiting)
+        waiting = first, depth, gates
+    activate(*waiting)
 
 
 def whole(array):
     return pl.BlockSpec(array.shape, lambda *step: (0,) * array.ndim)
 
 
-def conv_step(frames, part, hid, cell, ring, weights, bias, extent, depth, names, out_shapes, out_specs, packed, carry, load):
+def conv_step(frames, part, hid, cell, ring, weights, bias, rows_of, names, out_shapes, out_specs, packed, carry, load):
     rows, cols, width = hid.shape
     latent = weights.shape[0] // 9 - width
-    first, count = extent[0] // depth, extent[1] // depth
-    last = rows // depth - 1
-
-    def rowed(size, channels, channel, index):
-        return pl.BlockSpec((size, cols, channels), lambda step: (index(first + step), 0, channel))
-
-    def before(block):
-        return jnp.maximum(block * depth - 1, 0)
-
-    def after(block):
-        return jnp.minimum(block * depth + depth, rows - 1)
-
+    start, extent = rows_of
+
+    def rowed(size, channels, channel, row):
+        return pl.BlockSpec((size, cols, channels), lambda step: (row // size, 0, channel))
+
+    before, after = max(start - 1, 0), min(start + extent, rows - 1)
     inputs = {
-        "frame": (frames, rowed(depth, latent, part, lambda block: block)),
+        "frame": (frames, rowed(extent, latent, part, start)),
         "frame_prev": (frames, rowed(1, latent, part, before)),
         "frame_next": (frames, rowed(1, latent, part, after)),
-        "hid": (hid, rowed(depth, width, 0, lambda block: block)),
+        "hid": (hid, rowed(extent, width, 0, start)),
         "hid_prev": (hid, rowed(1, width, 0, before)),
         "hid_next": (hid, rowed(1, width, 0, after)),
-        "cell": (cell, rowed(depth, width, 0, lambda block: block)),
+        "cell": (cell, rowed(extent, width, 0, start)),
         "bias": (bias, whole(bias)),
     }
     if load:
@@ -197,17 +194,14 @@
             aliases[len(inputs)] = place
             inputs[f"carry{place}"] = (array, pl.BlockSpec(memory_space=pl.ANY))
     refs = [*inputs, *names, "spread"]
-    scratch = [pltpu.VMEM((depth + 2, cols, 3 * (latent + width)), BF)]
-    if ring:
-        refs += ["left", "right"]
-        scratch += [pltpu.VMEM((ring["strips_hid"][0].shape[1], latent + width), F32)] * 2
+    scratch = [pltpu.VMEM((extent + 2, cols, 3 * (latent + width)), BF)]
     if load:
         refs += ["held", "sem"]
         scratch += [pltpu.VMEM(weights.shape, BF), pltpu.SemaphoreType.DMA((LOADS,))]
-    cells = extent[1] * cols
+    cells = extent * cols
     return pl.pallas_call(
-        functools.partial(conv_kernel, first, last, refs, packed),
-        grid=(count,),
+        functools.partial(conv_kernel, start, rows, refs, packed),
+        grid=(1,),
         in_specs=[spec for _, spec in inputs.values()],
         out_specs=out_specs,
         out_shape=out_shapes,
@@ -521,13 +515,12 @@
     tile_shapes = (jax.ShapeDtypeStruct((rows, cols, width), BF), jax.ShapeDtypeStruct((rows, cols, width), F32))
     carry = ()
     for start, extent in ((0, rows // 2), (rows // 2, rows - rows // 2)):
-        depth = step_rows(start, extent)
-        spec = pl.BlockSpec((depth, cols, width), lambda step, first=start // depth: (first + step, 0, 0))
+        spec = pl.BlockSpec((extent, cols, width), lambda step, place=start // extent: (place, 0, 0))
         if carry:
             *carry, to_down, to_up = lax.optimization_barrier((*carry, to_down, to_up))
             from_up, from_down = shifted(to_down, "gy", 1), shifted(to_up, "gy", -1)
         carry = conv_step(
-            frames, 0, hidden_state, cell_state, {}, weights, bias, (start, extent), depth, ("hid_out", "cell_out"),
+            frames, 0, hidden_state, cell_state, {}, weights, bias, (start, extent), ("hid_out", "cell_out"),
             tile_shapes, (spec, spec), None, carry, False,
         )
     hidden_one, cell_one = carry
@@ -565,11 +558,10 @@
     moved, start, carry = [], 0, ()
     for piece_y in shares:
         extent = piece_y * devices_y
-        depth = step_rows(start, extent, 8 if carry else 16)
         sent_shape = jax.ShapeDtypeStruct((devices_y, devices_x, piece_y, piece_cols, width), BF)
-        spec = pl.BlockSpec((depth, cols, width), lambda step, first=start // depth: (first + step, 0, 0))
+        spec = pl.BlockSpec((extent, cols, width), lambda step, place=start // extent: (place, 0, 0))
         sent, cell_out = conv_step(
-            frames, 1, hidden_one, cell_one, ring, weights, bias, (start, extent), depth,
+            frames, 1, hidden_one, cell_one, ring, weights, bias, (start, extent),
             ("hid_out", "cell_out"), (sent_shape, tile_shapes[1]), (whole(sent_shape), spec), (local_m, piece_x), carry,
             bool(carry),
         )

time: 116 us -> 114 us (0.983)
  Pallas kernels: 54.3 us -> 51.6 us
    pallas_call x4, Pallas kernels: 33.2 us -> 30.5 us  [conv_step(): pl.pallas_call(functools.partial(conv_kernel, start, rows, refs, packed),...]
  transfers between devices with their start and end apart: 6 -> 6, of which waited for: 2 -> 2; matrix products, arithmetic and copies ran while one was open for 0% -> 0% of each run, Pallas kernels for 28% -> 27%
where the time goes in v6:
time: 114 us; the launch traced here: 113 us
  Pallas kernels  51.6 us (45%)
  blocking collectives  25.6 us (22%)
  starting transfers between devices  22.1 us (19%)
  waiting for transfers between devices  7.39 us (6%)
  local copies, waits for them, and re-layouts  5.5 us (5%)
    pallas_call x4, Pallas kernels, conv_step(): pl.pallas_call(functools.partial(conv_kernel, start, rows, refs, packed),...  30.5 us
    all_to_all x1, blocking collectives, body(): lax.all_to_all(done, ('gy', 'gx'), split_axis=0, concat_axis=0, tiled=True)  25.6 us
    pallas_call x2, Pallas kernels, block_step(): pl.pallas_call(block_kernel, grid=(lanes, piece_y), in_specs=in_specs, ou...  14.2 us
    ppermute x4, starting transfers between devices, shifted(): return lax.ppermute(value, axis, pairs)  11.6 us
    all_to_all x2, starting transfers between devices, body(): lax.all_to_all(sent, ('gy', 'gx'), split_axis=0, concat_axis=0, tiled=True)  10.5 us
    all_to_all x2, waiting for transfers between devices, body(): lax.all_to_all(sent, ('gy', 'gx'), split_axis=0, concat_axis=0, tiled=True)  7.38 us
    unnamed x48, local copies, waits for them, and re-layouts  5.44 us
    pallas_call x1, Pallas kernels, pack_step(): pl.pallas_call(pack_kernel, grid=(1,), in_specs=[*edge(frames, near), *ed...  3.28 us
  transfers between devices with their start and end apart: 6, of which 2 were waited for; matrix products, arithmetic and copies ran while one was open for 0% of the time, Pallas kernels for 27%

profile of v6, /device:TPU:1, one launch (start us, length us, event | category | flops | bytes accessed | tf_op | source)
XLA Modules:
  0.0 113.4 jit_solution(7255022008890562024)
XLA Ops:
  0.6 0.0 copy-start
  0.7 3.3 %shard_map.105 = (bf16[48,2,768]{2,1,0:T(2,128)(2,1)}, bf16[48,2,768]{2,1,0:T(2,128)(2,1)}, bf16[2,48,768]{2,1,0:T(8,128)(2,1)}, bf16[2,48,768]{2,1,0:T(8,128)(2...) custom-call(bf16[48,64,512]{2,1,0:T(8,128)(2,1)} %args_2_.10, bf16[48,64,512]{2,1,0:T(8,128)(2,1)} %args_2_.10, ...), custom_call_target="tpu_custom_call" | custom-call | bytes 4000000 | tf_op jit(solution)/shard_map/pallas_call | solution.py:270
  3.9 4.0 %collective-permute-start = (bf16[48,2,768]{2,1,0:T(2,128)(2,1)}, bf16[48,2,768]{2,1,0:T(2,128)(2,1)S(1)}, u32[]{:S(2)}, u32[]{:S(2)}) collective-permute-start(bf16[48,2,768]{2,1,0:T(2,128)(2,1)} %get-tuple-element.28), channel_id=1, source_target_pairs={{0,1},{1,2},{2,3},{4,5},{5,6},{6,7},{8,9},{9,10},{10,11},{12,13},{... | collective-permute-start | bytes 442376 | tf_op jit(solution)/shard_map/ppermute | solution.py:507
  8.0 1.3 %collective-permute-start.1 = (bf16[48,2,768]{2,1,0:T(2,128)(2,1)}, bf16[48,2,768]{2,1,0:T(2,128)(2,1)S(1)}, u32[]{:S(2)}, u32[]{:S(2)}) collective-permute-start(bf16[48,2,768]{2,1,0:T(2,128)(2,1)} %get-tuple-element.29), channel_id=1, source_target_pairs={{1,0},{2,1},{3,2},{5,4},{6,5},{7,6},{9,8},{10,9},{11,10},{13,12},{... | collective-permute-start | bytes 442376 | tf_op jit(solution)/shard_map/ppermute | solution.py:507
  9.3 0.0 copy-start.1
  9.3 1.4 %copy-done.1 = f32[48,64,128]{2,1,0:T(8,128)S(1)} copy-done((f32[48,64,128]{2,1,0:T(8,128)S(1)}, f32[48,64,128]{2,1,0:T(8,128)}, u32[]{:S(2)}) %copy-start.1) | copy-done | bytes 1572888
  10.7 1.1 copy-done.2
  11.8 2.0 %copy-done.4 = bf16[3,3,384,512]{3,2,1,0:T(8,128)(2,1)S(1)} copy-done((bf16[3,3,384,512]{3,2,1,0:T(8,128)(2,1)S(1)}, bf16[3,3,384,512]{3,2,1,0:T(8,128)(2,1)}, u32[]{:S(2)}) %copy-start.4) | copy-done | bytes 3538968
  13.8 6.2 %shard_map.104 = (bf16[48,64,128]{2,1,0:T(8,128)(2,1)S(1)}, f32[48,64,128]{2,1,0:T(8,128)S(1)}) custom-call(bf16[48,64,512]{2,1,0:T(8,128)(2,1)S(1)} %copy-done, bf16[48,64,512]{2,1,0:T(8,128)(2,1)S(1)} %copy-done, bf16[48,64,512]{2,1,0:T(8,128)(2,1)S(1)} %copy-done, bf16[48,64,128]{2,1,0:T(8,128)(2,1)S(1)} %copy-done.2, bf16[48,64,128]{2,1,0:T(8,128)(2,1)S(1)} %copy-done.2, ...), custom_call_target="tpu_custom_call" | custom-call | flops 5435817984 | bytes 6684672 | tf_op jit(solution)/shard_map/pallas_call | solution.py:202
  20.2 4.2 %collective-permute-start.2 = (bf16[2,68,768]{2,1,0:T(8,128)(2,1)S(1)}, bf16[2,68,768]{2,1,0:T(8,128)(2,1)S(1)}, u32[]{:S(2)}, u32[]{:S(2)}) collective-permute-start(bf16[2,68,768]{2,1,0:T(8,128)(2,1)S(1)} %get-tuple-element.35), channel_id=1, source_target_pairs={{0,4},{4,8},{8,12},{12,16},{16,20},{20,24},{24,28},{1,5},{5,9},{9,... | collective-permute-start | bytes 626696 | tf_op jit(solution)/shard_map/ppermute | solution.py:507
  24.4 2.1 %collective-permute-start.3 = (bf16[2,68,768]{2,1,0:T(8,128)(2,1)S(1)}, bf16[2,68,768]{2,1,0:T(8,128)(2,1)S(1)}, u32[]{:S(2)}, u32[]{:S(2)}) collective-permute-start(bf16[2,68,768]{2,1,0:T(8,128)(2,1)S(1)} %get-tuple-element.36), channel_id=1, source_target_pairs={{4,0},{8,4},{12,8},{16,12},{20,16},{24,20},{28,24},{5,1},{9,5},{13... | collective-permute-start | bytes 626696 | tf_op jit(solution)/shard_map/ppermute | solution.py:507
  26.5 6.2 %shard_map.106 = (bf16[48,64,128]{2,1,0:T(8,128)(2,1)S(1)}, f32[48,64,128]{2,1,0:T(8,128)S(1)}) custom-call(bf16[48,64,512]{2,1,0:T(8,128)(2,1)S(1)} %copy-done, bf16[48,64,512]{2,1,0:T(8,128)(2,1)S(1)} %copy-done, bf16[48,64,512]{2,1,0:T(8,128)(2,1)S(1)} %copy-done, ...), custom_call_target="tpu_custom_call", output_to_operand_aliasing={{0}: (9, {}), {1}: (10, {})} | custom-call | flops 5435817984 | bytes 6684672 | tf_op jit(solution)/shard_map/pallas_call | solution.py:202
  32.9 2.2 %shard_map.107 = (f32[4,64,128]{2,1,0:T(8,128)S(1)}, f32[4,64,128]{2,1,0:T(8,128)S(1)}, f32[4,64,128]{2,1,0:T(8,128)S(1)}, f32[4,64,128]{2,1,0:T(8,128)S(1)}, f32[2,64,256]{2,1,0:T(8,128)S(1)}) custom-call(bf16[2,68,768]{2,1,0:T(8,128)(2,1)S(1)} %collective-permute-done.2.above.args_14_, bf16[2,68,768]{2,1,0:T(8,128)(2,1)S(1)} %collective-permute-done.3.below.args_15_, ...), custom_call_target="tpu_custom_call" | custom-call | flops 1811939328 | bytes 3538944 | tf_op jit(solution)/shard_map/pallas_call | solution.py:535
  35.2 9.3 %shard_map.108 = (bf16[8,4,4,16,128]{4,3,2,1,0:T(8,128)(2,1)S(1)}, f32[48,64,128]{2,1,0:T(8,128)}) custom-call(bf16[48,64,512]{2,1,0:T(8,128)(2,1)S(1)} %copy-done, bf16[48,64,512]{2,1,0:T(8,128)(2,1)S(1)} %copy-done, bf16[48,64,512]{2,1,0:T(8,128)(2,1)S(1)} %copy-done, bf16[48,64,128]{2,1,0:T(8,128)(2,1)S(1)} %get-tuple-element.33.args_3_.args_4_.args_5_, ...), custom_call_target="tpu_custom_call" | custom-call | flops 7247757312 | bytes 7733248 | tf_op jit(solution)/shard_map/pallas_call | solution.py:202
  44.6 0.8 copy-done.7
  45.4 7.3 %all-to-all-start.1 = ((bf16[32,4,16,128]{3,2,1,0:T(8,128)(2,1)}), bf16[32,4,16,128]{3,2,1,0:T(8,128)(2,1)S(1)}, u32[]{:S(2)}, u32[]{:S(2)}) async-start(bf16[32,4,16,128]{3,2,1,0:T(8,128)(2,1)} %bitcast.18), calls=%async_computation.1 | async-start | bytes 1048576 | tf_op jit(solution)/shard_map/all_to_all | solution.py:570
  52.7 8.7 %shard_map.109 = (bf16[8,4,2,16,128]{4,3,2,1,0:T(8,128)(2,1)}, f32[48,64,128]{2,1,0:T(8,128)}) custom-call(bf16[48,64,512]{2,1,0:T(8,128)(2,1)} %args_2_.10, bf16[48,64,512]{2,1,0:T(8,128)(2,1)} %args_2_.10, bf16[48,64,512]{2,1,0:T(8,128)(2,1)} %args_2_.10, bf16[48,64,128]{2,1,0:T(8,128)(2,1)} %copy-done.3, ...), custom_call_target="tpu_custom_call", output_to_operand_aliasing={{1}: (16, {})} | custom-call | flops 3623878656 | bytes 5636096 | tf_op jit(solution)/shard_map/pallas_call | solution.py:202
  61.5 6.5 %all-to-all-done.1 = bf16[32,4,16,128]{3,2,1,0:T(8,128)(2,1)S(1)} async-done(((bf16[32,4,16,128]{3,2,1,0:T(8,128)(2,1)}), bf16[32,4,16,128]{3,2,1,0:T(8,128)(2,1)S(1)}, u32[]{:S(2)}, u32[]{:S(2)}) %all-to-all-start.1) | async-done | bytes 524320 | tf_op jit(solution)/shard_map/all_to_all | solution.py:570
  68.0 3.2 %all-to-all-start = ((bf16[32,2,16,128]{3,2,1,0:T(8,128)(2,1)}), bf16[32,2,16,128]{3,2,1,0:T(8,128)(2,1)S(1)}, u32[]{:S(2)}, u32[]{:S(2)}) async-start(bf16[32,2,16,128]{3,2,1,0:T(8,128)(2,1)} %bitcast.25), calls=%async_computation | async-start | bytes 524288 | tf_op jit(solution)/shard_map/all_to_all | solution.py:570
  71.2 9.4 %shard_map.110.rest_0_ = bf16[8,1,4,6,16,128]{5,4,3,2,1,0:T(8,128)(2,1)S(1)} custom-call(bf16[8,1,4,4,16,128]{5,4,3,2,1,0:T(8,128)(2,1)S(1)} %bitcast.17, bf16[128,768]{1,0:T(8,128)(2,1)S(1)} %copy-done.18, bf16[256,128]{1,0:T(8,128)(2,1)S(1)} %copy-done.23, bf16[128,512]{1,0:T(8,128)(2,1)S(1)} %copy-done.21, bf16[512,128]{1,0:T(8,128)(2,1)S(1)} %copy-done.22), custom_call_target="tpu_custom_call" | custom-call | flops 6144000000 | bytes 1848576 | tf_op jit(solution)/shard_map/pallas_call | solution.py:432
  80.6 0.9 all-to-all-done
  81.5 4.8 %shard_map.111 = bf16[8,1,4,6,16,128]{5,4,3,2,1,0:T(8,128)(2,1)S(1)} custom-call(bf16[8,1,4,2,16,128]{5,4,3,2,1,0:T(8,128)(2,1)S(1)} %bitcast.19, bf16[128,768]{1,0:T(8,128)(2,1)S(1)} %copy-done.18, bf16[256,128]{1,0:T(8,128)(2,1)S(1)} %copy-done.23, bf16[128,512]{1,0:T(8,128)(2,1)S(1)} %copy-done.21, ...), custom_call_target="tpu_custom_call", output_to_operand_aliasing={{}: (5, {})} | custom-call | flops 3072000000 | bytes 1324288 | tf_op jit(solution)/shard_map/pallas_call | solution.py:432
  86.2 25.6 %all_to_all.15 = bf16[32,6,16,128]{3,2,1,0:T(8,128)(2,1)S(1)} all-to-all(bf16[32,6,16,128]{3,2,1,0:T(8,128)(2,1)S(1)} %bitcast.16), channel_id=1, replica_groups=mesh['gy'=8,'gx'=4] {'gy','gx'}, dimensions={0} | all-to-all | bytes 1572864 | tf_op jit(solution)/shard_map/all_to_all | solution.py:577
  111.9 1.5 %shard_map.112 = bf16[48,64,128]{2,1,0:T(8,128)(2,1)} custom-call(bf16[8,4,6,16,128]{4,3,2,1,0:T(8,128)(2,1)S(1)} %bitcast.15), custom_call_target="tpu_custom_call" | custom-call | bytes 1572864 | tf_op jit(solution)/shard_map/pallas_call | solution.py:478
  (51 shorter events, 0.2 us)
Async XLA Ops:
  0.6 8.6 %copy-start = (bf16[48,64,512]{2,1,0:T(8,128)(2,1)S(1)}, bf16[48,64,512]{2,1,0:T(8,128)(2,1)}, u32[]{:S(2)}) copy-start(bf16[48,64,512]{2,1,0:T(8,128)(2,1)} %args_2_.10) | copy-start | bytes 9437188
  0.6 8.6 %copy-start.17 = (f32[512]{0:T(512)S(1)}, f32[512]{0:T(512)}, u32[]{:S(2)}) copy-start(f32[512]{0:T(512)} %param.13) | copy-start | bytes 6148
  3.9 16.1 %collective-permute-start = (bf16[48,2,768]{2,1,0:T(2,128)(2,1)}, bf16[48,2,768]{2,1,0:T(2,128)(2,1)S(1)}, u32[]{:S(2)}, u32[]{:S(2)}) collective-permute-start(bf16[48,2,768]{2,1,0:T(2,128)(2,1)} %get-tuple-element.28), channel_id=1, source_target_pairs={{0,1},{1,2},{2,3},{4,5},{5,6},{6,7},{8,9},{9,10},{10,11},{12,13},{... | collective-permute-start | bytes 442376 | tf_op jit(solution)/shard_map/ppermute | solution.py:507
  8.0 12.1 %collective-permute-start.1 = (bf16[48,2,768]{2,1,0:T(2,128)(2,1)}, bf16[48,2,768]{2,1,0:T(2,128)(2,1)S(1)}, u32[]{:S(2)}, u32[]{:S(2)}) collective-permute-start(bf16[48,2,768]{2,1,0:T(2,128)(2,1)} %get-tuple-element.29), channel_id=1, source_target_pairs={{1,0},{2,1},{3,2},{5,4},{6,5},{7,6},{9,8},{10,9},{11,10},{13,12},{... | collective-permute-start | bytes 442376 | tf_op jit(solution)/shard_map/ppermute | solution.py:507
  13.8 6.3 %copy-start.10 = (bf16[2,64,768]{2,1,0:T(8,128)(2,1)S(1)}, bf16[2,64,768]{2,1,0:T(8,128)(2,1)}, u32[]{:S(2)}) copy-start(bf16[2,64,768]{2,1,0:T(8,128)(2,1)} %get-tuple-element.30.line_top) | copy-start | bytes 589828
  13.8 6.3 %copy-start.11 = (bf16[2,64,768]{2,1,0:T(8,128)(2,1)S(1)}, bf16[2,64,768]{2,1,0:T(8,128)(2,1)}, u32[]{:S(2)}) copy-start(bf16[2,64,768]{2,1,0:T(8,128)(2,1)} %get-tuple-element.27.line_bot) | copy-start | bytes 589828
  20.2 12.7 %copy-start.5 = (bf16[3,3,384,512]{3,2,1,0:T(8,128)(2,1)S(1)}, bf16[3,3,384,512]{3,2,1,0:T(8,128)(2,1)}, u32[]{:S(2)}) copy-start(bf16[3,3,384,512]{3,2,1,0:T(8,128)(2,1)} %param.12) | copy-start | bytes 10616836
  20.2 12.7 %copy-start.19 = (bf16[2,48,768]{2,1,0:T(8,128)(2,1)S(1)}, bf16[2,48,768]{2,1,0:T(8,128)(2,1)}, u32[]{:S(2)}) copy-start(bf16[2,48,768]{2,1,0:T(8,128)(2,1)} %get-tuple-element.37.side_left) | copy-start | bytes 442372
  20.2 12.7 %copy-start.20 = (bf16[2,48,768]{2,1,0:T(8,128)(2,1)S(1)}, bf16[2,48,768]{2,1,0:T(8,128)(2,1)}, u32[]{:S(2)}) copy-start(bf16[2,48,768]{2,1,0:T(8,128)(2,1)} %get-tuple-element.38.side_right) | copy-start | bytes 442372
  20.2 12.6 %collective-permute-start.2 = (bf16[2,68,768]{2,1,0:T(8,128)(2,1)S(1)}, bf16[2,68,768]{2,1,0:T(8,128)(2,1)S(1)}, u32[]{:S(2)}, u32[]{:S(2)}) collective-permute-start(bf16[2,68,768]{2,1,0:T(8,128)(2,1)S(1)} %get-tuple-element.35), channel_id=1, source_target_pairs={{0,4},{4,8},{8,12},{12,16},{16,20},{20,24},{24,28},{1,5},{5,9},{9,... | collective-permute-start | bytes 626696 | tf_op jit(solution)/shard_map/ppermute | solution.py:507
  24.4 8.4 %collective-permute-start.3 = (bf16[2,68,768]{2,1,0:T(8,128)(2,1)S(1)}, bf16[2,68,768]{2,1,0:T(8,128)(2,1)S(1)}, u32[]{:S(2)}, u32[]{:S(2)}) collective-permute-start(bf16[2,68,768]{2,1,0:T(8,128)(2,1)S(1)} %get-tuple-element.36), channel_id=1, source_target_pairs={{4,0},{8,4},{12,8},{16,12},{20,16},{24,20},{28,24},{5,1},{9,5},{13... | collective-permute-start | bytes 626696 | tf_op jit(solution)/shard_map/ppermute | solution.py:507
  32.7 2.4 %copy-start.3 = (bf16[48,64,128]{2,1,0:T(8,128)(2,1)}, bf16[48,64,128]{2,1,0:T(8,128)(2,1)S(1)}, u32[]{:S(2)}) copy-start(bf16[48,64,128]{2,1,0:T(8,128)(2,1)S(1)} %get-tuple-element.33.args_3_.args_4_.args_5_) | copy-start | bytes 2359300
  32.8 2.4 %copy-start.6 = (f32[48,64,128]{2,1,0:T(8,128)}, f32[48,64,128]{2,1,0:T(8,128)S(1)}, u32[]{:S(2)}) copy-start(f32[48,64,128]{2,1,0:T(8,128)S(1)} %get-tuple-element.34.args_6_) | copy-start | bytes 4718596
  35.1 9.4 %copy-start.12 = (f32[4,64,128]{2,1,0:T(8,128)}, f32[4,64,128]{2,1,0:T(8,128)S(1)}, u32[]{:S(2)}) copy-start(f32[4,64,128]{2,1,0:T(8,128)S(1)} %get-tuple-element.41.args_11_) | copy-start | bytes 393220
  35.1 9.4 %copy-start.13 = (f32[4,64,128]{2,1,0:T(8,128)}, f32[4,64,128]{2,1,0:T(8,128)S(1)}, u32[]{:S(2)}) copy-start(f32[4,64,128]{2,1,0:T(8,128)S(1)} %get-tuple-element.42.args_12_) | copy-start | bytes 393220
  35.1 9.4 %copy-start.14 = (f32[4,64,128]{2,1,0:T(8,128)}, f32[4,64,128]{2,1,0:T(8,128)S(1)}, u32[]{:S(2)}) copy-start(f32[4,64,128]{2,1,0:T(8,128)S(1)} %get-tuple-element.39.args_9_) | copy-start | bytes 393220
  35.1 9.4 %copy-start.15 = (f32[4,64,128]{2,1,0:T(8,128)}, f32[4,64,128]{2,1,0:T(8,128)S(1)}, u32[]{:S(2)}) copy-start(f32[4,64,128]{2,1,0:T(8,128)S(1)} %get-tuple-element.40.args_10_) | copy-start | bytes 393220
  35.1 9.4 %copy-start.16 = (f32[2,64,256]{2,1,0:T(8,128)}, f32[2,64,256]{2,1,0:T(8,128)S(1)}, u32[]{:S(2)}) copy-start(f32[2,64,256]{2,1,0:T(8,128)S(1)} %get-tuple-element.43.args_13_) | copy-start | bytes 393220
  45.4 22.6 %all-to-all-start.1 = ((bf16[32,4,16,128]{3,2,1,0:T(8,128)(2,1)}), bf16[32,4,16,128]{3,2,1,0:T(8,128)(2,1)S(1)}, u32[]{:S(2)}, u32[]{:S(2)}) async-start(bf16[32,4,16,128]{3,2,1,0:T(8,128)(2,1)} %bitcast.18), calls=%async_computation.1 | async-start | bytes 1048576 | tf_op jit(solution)/shard_map/all_to_all | solution.py:570
  52.7 18.5 %copy-start.18 = (bf16[128,768]{1,0:T(8,128)(2,1)S(1)}, bf16[128,768]{1,0:T(8,128)(2,1)}, u32[]{:S(2)}) copy-start(bf16[128,768]{1,0:T(8,128)(2,1)} %w_qkv.3) | copy-start | bytes 589828
  52.7 18.5 %copy-start.21 = (bf16[128,512]{1,0:T(8,128)(2,1)S(1)}, bf16[128,512]{1,0:T(8,128)(2,1)}, u32[]{:S(2)}) copy-start(bf16[128,512]{1,0:T(8,128)(2,1)} %w_up.3) | copy-start | bytes 393220
  52.7 18.4 %copy-start.22 = (bf16[512,128]{1,0:T(8,128)(2,1)S(1)}, bf16[512,128]{1,0:T(8,128)(2,1)}, u32[]{:S(2)}) copy-start(bf16[512,128]{1,0:T(8,128)(2,1)} %w_down.3) | copy-start | bytes 393220
  52.7 18.4 %copy-start.23 = (bf16[256,128]{1,0:T(8,128)(2,1)S(1)}, bf16[256,128]{1,0:T(8,128)(2,1)}, u32[]{:S(2)}) copy-start(bf16[256,128]{1,0:T(8,128)(2,1)} %w_out.3) | copy-start | bytes 196612
  68.0 13.5 %all-to-all-start = ((bf16[32,2,16,128]{3,2,1,0:T(8,128)(2,1)}), bf16[32,2,16,128]{3,2,1,0:T(8,128)(2,1)S(1)}, u32[]{:S(2)}, u32[]{:S(2)}) async-start(bf16[32,2,16,128]{3,2,1,0:T(8,128)(2,1)} %bitcast.25), calls=%async_computation | async-start | bytes 524288 | tf_op jit(solution)/shard_map/all_to_all | solution.py:570
  (6 other events, 10.0 us)

commit v7 on v6

--- a/solution.py
+++ b/solution.py
@@ -48,23 +48,32 @@
     return before.astype(BF), wide.astype(BF), after.astype(BF)
 
 
-def conv_kernel(start, rows, refs, packed, *args):
+def conv_kernel(start, rows, part, refs, packed, *args):
     ref = dict(zip(refs, args))
-    frame, hid, spread = ref["frame"], ref["hid"], ref["spread"]
-    hid_out, cell_out = ref["hid_out"], ref["cell_out"]
+    spread, hid_out, cell_out = ref["spread"], ref["hid_out"], ref["cell_out"]
     ring = "strips_hid" in ref
-    extent, cols, latent = frame.shape
-    width = hid.shape[2]
-    chans = latent + width
+    extent = spread.shape[0] - 2
+    cols, width = ref["hid"].shape[1:]
+    chans = spread.shape[2] // 3
+    latent = chans - width
     top, bot = start == 0, start + extent == rows
+
+    def row_of(name, row):
+        channels = slice(part * latent, (part + 1) * latent) if name == "frame" else slice(None)
+        if ref[name].shape[0] == rows:
+            return ref[name][row, :, channels]
+        if row == start - 1:
+            return ref[name + "_prev"][0]
+        if row == start + extent:
+            return ref[name + "_next"][0]
+        return ref[name][row - start]
+
     loads = []
     if "weights" in ref:
         size = ref["weights"].shape[0] // LOADS
         for place in range(LOADS):
-            part = pl.ds(place * size, size)
-            loads.append(
-                pltpu.make_async_copy(ref["weights"].at[part], ref["held"].at[part], ref["sem"].at[place])
-            )
+            run = pl.ds(place * size, size)
+            loads.append(pltpu.make_async_copy(ref["weights"].at[run], ref["held"].at[run], ref["sem"].at[place]))
     for load in loads:
         load.start()
 
@@ -82,17 +91,14 @@
     def build(pos):
         row = start + pos - 1
         raw = None
-        if pos == 0 or pos == extent + 1:
-            name, outside = ("prev", top) if pos == 0 else ("next", bot)
-            if outside and not ring:
-                spread[pos] = jnp.zeros(spread.shape[1:], BF)
-                return
-            x, h = ref["frame_" + name][0].astype(F32), ref["hid_" + name][0].astype(F32)
-            if outside:
-                x = ref["frame_top" if pos == 0 else "frame_bot"][0, :cols].astype(F32)
+        if 0 <= row < rows:
+            raw = row_of("frame", row), row_of("hid", row)
+            x, h = raw[0].astype(F32), raw[1].astype(F32)
+        elif ring:
+            x, h = ref["frame_top" if row < 0 else "frame_bot"][0, :cols].astype(F32), ref["lines_hid"][3 * (row > 0)]
         else:
-            raw = frame[pos - 1], hid[pos - 1]
-            x, h = raw[0].astype(F32), raw[1].astype(F32)
+            spread[pos] = jnp.zeros(spread.shape[1:], BF)
+            return
         low, high = beside(row)
         if ring:
             at = row + 2
@@ -102,11 +108,11 @@
             for spot, line in ((-1, 0), (0, 1), (rows - 1, 2), (rows, 3)):
                 if row == spot:
                     h = ref["lines_hid"][line]
-        for part, (value, first) in enumerate(((x, 0), (h, latent))):
+        for side, (value, first) in enumerate(((x, 0), (h, latent))):
             size = value.shape[1]
             pieces = three_columns(value, low[:, first : first + size], high[:, first : first + size])
-            if raw is not None and (part == 0 or not ring):
-                pieces = pieces[0], raw[part], pieces[2]
+            if raw is not None and (side == 0 or not ring):
+                pieces = pieces[0], raw[side], pieces[2]
             for tap in range(3):
                 spread[pos, :, tap * chans + first : tap * chans + first + size] = pieces[tap]
 
@@ -119,7 +125,7 @@
     def activate(first, depth, gates):
         for line in range(first, first + depth):
             row = start + line
-            cell_prev = ref["cell"][line]
+            cell_prev = row_of("cell", row)
             if ring:
                 at = row + 2
                 place = lax.broadcasted_iota(jnp.int32, cell_prev.shape, 0)
@@ -131,10 +137,11 @@
                     cell_prev = ref["lines_cell"][2]
             own = gates[(line - first) * cols : (line - first + 1) * cols] + ref["bias"][...]
             new_cell, new_hidden = lstm(own, cell_prev)
-            cell_out[line] = new_cell
             if not packed:
-                hid_out[line] = new_hidden.astype(BF)
+                cell_out[row] = new_cell
+                hid_out[row] = new_hidden.astype(BF)
                 continue
+            ref["cell_rows"][line] = new_cell
             owners_x, piece_y = hid_out.shape[1:3]
             local_m, piece_x = packed
             for owner in range(owners_x):
@@ -144,6 +151,15 @@
                 ]
                 hid_out[line // piece_y, owner, line % piece_y] = jnp.concatenate(picked, axis=0).astype(BF)
 
+        if packed:
+            done = pl.ds(first, depth)
+            leave = pltpu.make_async_copy(
+                ref["cell_rows"].at[done], cell_out.at[pl.ds(start + first, depth)], ref["left"].at[first // depth]
+            )
+            leave.start()
+            leaving.append(leave)
+
+    leaving = []
     depth = step_rows(0, extent, 12)
     for pos in range(depth + 2):
         build(pos)
@@ -158,6 +174,8 @@
             activate(*waiting)
         waiting = first, depth, gates
     activate(*waiting)
+    for leave in leaving:
+        leave.wait()
 
 
 def whole(array):
@@ -173,34 +191,41 @@
         return pl.BlockSpec((size, cols, channels), lambda step: (row // size, 0, channel))
 
     before, after = max(start - 1, 0), min(start + extent, rows - 1)
-    inputs = {
-        "frame": (frames, rowed(extent, latent, part, start)),
-        "frame_prev": (frames, rowed(1, latent, part, before)),
-        "frame_next": (frames, rowed(1, latent, part, after)),
-        "hid": (hid, rowed(extent, width, 0, start)),
-        "hid_prev": (hid, rowed(1, width, 0, before)),
-        "hid_next": (hid, rowed(1, width, 0, after)),
-        "cell": (cell, rowed(extent, width, 0, start)),
-        "bias": (bias, whole(bias)),
-    }
+    near = pl.BlockSpec(memory_space=pltpu.VMEM)
+    if load:
+        inputs = {
+            "frame": (frames, rowed(extent, latent, part, start)),
+            "frame_prev": (frames, rowed(1, latent, part, before)),
+            "frame_next": (frames, rowed(1, latent, part, after)),
+            "hid": (hid, rowed(extent, width, 0, start)),
+            "hid_prev": (hid, rowed(1, width, 0, before)),
+            "hid_next": (hid, rowed(1, width, 0, after)),
+            "cell": (cell, rowed(extent, width, 0, start)),
+        }
+    else:
+        inputs = {"frame": (frames, near), "hid": (hid, near), "cell": (cell, near)}
+    inputs["bias"] = bias, whole(bias)
     if load:
         inputs["weights"] = weights, pl.BlockSpec(memory_space=pl.ANY)
     else:
-        inputs["held"] = weights, pl.BlockSpec(memory_space=pltpu.VMEM)
+        inputs["held"] = weights, near
     inputs |= ring
     aliases = {}
     for place, array in enumerate(carry):
         if array is not None:
             aliases[len(inputs)] = place
-            inputs[f"carry{place}"] = (array, pl.BlockSpec(memory_space=pl.ANY))
+            inputs[f"carry{place}"] = (array, pl.BlockSpec(memory_space=pl.ANY) if packed else near)
     refs = [*inputs, *names, "spread"]
     scratch = [pltpu.VMEM((extent + 2, cols, 3 * (latent + width)), BF)]
     if load:
         refs += ["held", "sem"]
         scratch += [pltpu.VMEM(weights.shape, BF), pltpu.SemaphoreType.DMA((LOADS,))]
+    if packed:
+        refs += ["cell_rows", "left"]
+        scratch += [pltpu.VMEM((extent, cols, width), F32), pltpu.SemaphoreType.DMA((extent,))]
     cells = extent * cols
     return pl.pallas_call(
-        functools.partial(conv_kernel, start, rows, refs, packed),
+        functools.partial(conv_kernel, start, rows, part, refs, packed),
         grid=(1,),
         in_specs=[spec for _, spec in inputs.values()],
         out_specs=out_specs,
@@ -214,69 +239,51 @@
     )(*(array for array, _ in inputs.values()))
 
 
-def pack_kernel(
-    frame_low, frame_high, frame_top, frame_bot, hid_low, hid_high, hid_top, hid_bot,
-    cell_low, cell_high, cell_top, cell_bot, send_low, send_high, side_low, side_high, line_top, line_bot, flat,
-):
-    latent, width = frame_low.shape[2] // 2, hid_low.shape[2]
+def pack_kernel(frames, hids, cells, send_low, send_high, side_low, side_high, line_top, line_bot, flat):
+    rows, cols, width = hids.shape
+    latent = frames.shape[2] // 2
     chans = latent + width
     places = ((0, 0, latent), (chans + width, latent, latent))
-    for out, frame, hid, cell in (
-        (line_top, frame_top, hid_top, cell_top),
-        (line_bot, frame_bot, hid_bot, cell_bot),
+    for out, near in ((line_top, slice(0, 2)), (line_bot, slice(rows - 2, rows))):
+        for to, start, size in places:
+            out[:, :, to : to + size] = frames[near, :, start : start + size]
+        out[:, :, latent:chans] = hids[near]
+        out[:, :, chans : chans + width] = cells[near].astype(BF)
+    for out, send, near, start in (
+        (side_low, send_low, slice(0, 8), 0),
+        (side_high, send_high, slice(cols - 8, cols), 6),
     ):
-        for to, start, size in places:
-            out[:, :, to : to + size] = frame[:, :, start : start + size]
-        out[:, :, latent:chans] = hid[...]
-        out[:, :, chans : chans + width] = cell[...].astype(BF)
-    for out, send, frame, hid, cell, first, start in (
-        (side_low, send_low, frame_low, hid_low, cell_low, 0, 0),
-        (side_high, send_high, frame_high, hid_high, cell_high, frame_high.shape[1] - 8, 6),
-    ):
-        tall = frame.shape[0]
-        near = slice(first, first + 8)
         for slab in range(out.shape[2] // LANES):
             to = slab * LANES
             if to < latent or to >= chans + width:
                 begin = to if to < latent else to - 2 * width
-                part = frame[:, near, begin : begin + LANES].astype(F32)
+                part = frames[:, near, begin : begin + LANES].astype(F32)
             elif to < chans:
-                part = hid[:, near, to - latent : to - latent + LANES].astype(F32)
+                part = hids[:, near, to - latent : to - latent + LANES].astype(F32)
             else:
-                part = cell[:, :, to - chans : to - chans + LANES]
+                part = cells[:, near, to - chans : to - chans + LANES]
             send[:, :, to : to + LANES] = part[:, start : start + 2].astype(BF)
-            flat[...] = part.reshape(tall * 8, LANES)
+            flat[...] = part.reshape(rows * 8, LANES)
             for place in range(2):
-                out[place, :, to : to + LANES] = flat[pl.ds(start + place, tall, stride=8), :].astype(BF)
+                out[place, :, to : to + LANES] = flat[pl.ds(start + place, rows, stride=8), :].astype(BF)
 
 
 def pack_step(frames, hid, cell):
     rows, cols, width = hid.shape
     span = frames.shape[2]
-    near = 16
-
-    def edge(array, size):
-        deep = array.shape[2]
-        return [
-            pl.BlockSpec((rows, size, deep), lambda step: (0, 0, 0)),
-            pl.BlockSpec((rows, size, deep), lambda step: (0, cols // size - 1, 0)),
-            pl.BlockSpec((2, cols, deep), lambda step: (0, 0, 0)),
-            pl.BlockSpec((2, cols, deep), lambda step: (rows // 2 - 1, 0, 0)),
-        ]
-
     deep = span + 2 * width
     shapes = [jax.ShapeDtypeStruct((rows, 2, deep), BF)] * 2 + [jax.ShapeDtypeStruct((2, rows, deep), BF)] * 2
     shapes += [jax.ShapeDtypeStruct((2, cols, deep), BF)] * 2
     return pl.pallas_call(
         pack_kernel,
         grid=(1,),
-        in_specs=[*edge(frames, near), *edge(hid, near), *edge(cell, 8)],
+        in_specs=[pl.BlockSpec(memory_space=pltpu.VMEM)] * 3,
         out_specs=[whole(shape) for shape in shapes],
         out_shape=shapes,
         scratch_shapes=[pltpu.VMEM((rows * 8, LANES), F32)],
-        compiler_params=pltpu.CompilerParams(vmem_limit_bytes=VMEM_ALL),
+        compiler_params=pltpu.CompilerParams(vmem_limit_bytes=VMEM_LIMIT),
         cost_estimate=pl.CostEstimate(flops=0, bytes_accessed=4_000_000, transcendentals=0),
-    )(*[frames] * 4, *[hid] * 4, *[cell] * 4)
+    )(frames, hid, cell)
 
 
 def ring_kernel(
@@ -515,7 +522,7 @@
     tile_shapes = (jax.ShapeDtypeStruct((rows, cols, width), BF), jax.ShapeDtypeStruct((rows, cols, width), F32))
     carry = ()
     for start, extent in ((0, rows // 2), (rows // 2, rows - rows // 2)):
-        spec = pl.BlockSpec((extent, cols, width), lambda step, place=start // extent: (place, 0, 0))
+        spec = pl.BlockSpec(memory_space=pltpu.VMEM)
         if carry:
             *carry, to_down, to_up = lax.optimization_barrier((*carry, to_down, to_up))
             from_up, from_down = shifted(to_down, "gy", 1), shifted(to_up, "gy", -1)
@@ -559,7 +566,7 @@
     for piece_y in shares:
         extent = piece_y * devices_y
         sent_shape = jax.ShapeDtypeStruct((devices_y, devices_x, piece_y, piece_cols, width), BF)
-        spec = pl.BlockSpec((extent, cols, width), lambda step, place=start // extent: (place, 0, 0))
+        spec = pl.BlockSpec(memory_space=pl.ANY)
         sent, cell_out = conv_step(
             frames, 1, hidden_one, cell_one, ring, weights, bias, (start, extent),
             ("hid_out", "cell_out"), (sent_shape, tile_shapes[1]), (whole(sent_shape), spec), (local_m, piece_x), carry,

time: 114 us -> 111 us (0.974)
  Pallas kernels: 51.6 us -> 49.5 us
    pallas_call x5, Pallas kernels: 33.8 us -> 31.6 us  [the longest x4 31 us: conv_step(): pl.pallas_call(functools.partial(conv_kernel, start, rows, part, refs, pa...]
    unnamed x48 -> x40, local copies, waits for them, and re-layouts: 5.44 us -> 5.77 us
  transfers between devices with their start and end apart: 6 -> 6, of which waited for: 2 -> 2; matrix products, arithmetic and copies ran while one was open for 0% -> 0% of each run, Pallas kernels for 27% -> 28%
where the time goes in v7:
time: 111 us
  Pallas kernels  49.5 us (45%)
  blocking collectives  25.6 us (23%)
  starting transfers between devices  22 us (20%)
  waiting for transfers between devices  6.74 us (6%)
  local copies, waits for them, and re-layouts  5.83 us (5%)
    pallas_call x4, Pallas kernels, conv_step(): pl.pallas_call(functools.partial(conv_kernel, start, rows, part, refs, pa...  31 us
    all_to_all x1, blocking collectives, body(): lax.all_to_all(done, ('gy', 'gx'), split_axis=0, concat_axis=0, tiled=True)  25.6 us
    pallas_call x2, Pallas kernels, block_step(): pl.pallas_call(block_kernel, grid=(lanes, piece_y), in_specs=in_specs, ou...  14.2 us
    ppermute x4, starting transfers between devices, shifted(): return lax.ppermute(value, axis, pairs)  11.5 us
    all_to_all x2, starting transfers between devices, body(): lax.all_to_all(sent, ('gy', 'gx'), split_axis=0, concat_axis=0, tiled=True)  10.5 us
    all_to_all x2, waiting for transfers between devices, body(): lax.all_to_all(sent, ('gy', 'gx'), split_axis=0, concat_axis=0, tiled=True)  6.73 us
    unnamed x40, local copies, waits for them, and re-layouts  5.77 us
  transfers between devices with their start and end apart: 6, of which 2 were waited for; matrix products, arithmetic and copies ran while one was open for 0% of the time, Pallas kernels for 28%

profile of v7, /device:TPU:1, one launch (start us, length us, event | category | flops | bytes accessed | tf_op | source)
XLA Modules:
  0.0 110.8 jit_solution(4014795304414505368)
XLA Ops:
  0.6 1.9 %copy-done = bf16[48,64,512]{2,1,0:T(8,128)(2,1)S(1)} copy-done((bf16[48,64,512]{2,1,0:T(8,128)(2,1)S(1)}, bf16[48,64,512]{2,1,0:T(8,128)(2,1)}, u32[]{:S(2)}) %copy-start) | copy-done | bytes 3145752
  2.5 1.4 %copy-done.5 = f32[48,64,128]{2,1,0:T(8,128)S(1)} copy-done((f32[48,64,128]{2,1,0:T(8,128)S(1)}, f32[48,64,128]{2,1,0:T(8,128)}, u32[]{:S(2)}) %copy-start.5) | copy-done | bytes 1572888
  3.9 1.1 %copy-done.6 = bf16[48,64,128]{2,1,0:T(8,128)(2,1)S(1)} copy-done((bf16[48,64,128]{2,1,0:T(8,128)(2,1)S(1)}, bf16[48,64,128]{2,1,0:T(8,128)(2,1)}, u32[]{:S(2)}) %copy-start.6) | copy-done | bytes 786456
  5.1 0.6 shard_map.105
  5.7 4.2 %collective-permute-start = (bf16[48,2,768]{2,1,0:T(2,128)(2,1)S(1)}, bf16[48,2,768]{2,1,0:T(2,128)(2,1)S(1)}, u32[]{:S(2)}, u32[]{:S(2)}) collective-permute-start(bf16[48,2,768]{2,1,0:T(2,128)(2,1)S(1)} %get-tuple-element.28), channel_id=1, source_target_pairs={{0,1},{1,2},{2,3},{4,5},{5,6},{6,7},{8,9},{9,10},{10,11},{12,13},{... | collective-permute-start | bytes 442376 | tf_op jit(solution)/shard_map/ppermute | solution.py:514
  9.9 1.3 %collective-permute-start.1 = (bf16[48,2,768]{2,1,0:T(2,128)(2,1)S(1)}, bf16[48,2,768]{2,1,0:T(2,128)(2,1)S(1)}, u32[]{:S(2)}, u32[]{:S(2)}) collective-permute-start(bf16[48,2,768]{2,1,0:T(2,128)(2,1)S(1)} %get-tuple-element.29), channel_id=1, source_target_pairs={{1,0},{2,1},{3,2},{5,4},{6,5},{7,6},{9,8},{10,9},{11,10},{13,12},{... | collective-permute-start | bytes 442376 | tf_op jit(solution)/shard_map/ppermute | solution.py:514
  11.2 6.2 %shard_map.104 = (bf16[48,64,128]{2,1,0:T(8,128)(2,1)S(1)}, f32[48,64,128]{2,1,0:T(8,128)S(1)}) custom-call(bf16[48,64,512]{2,1,0:T(8,128)(2,1)S(1)} %copy-done, bf16[48,64,128]{2,1,0:T(8,128)(2,1)S(1)} %copy-done.6, f32[48,64,128]{2,1,0:T(8,128)S(1)} %copy-done.5, f32[1,512]{1,0:T(1,128)S(1)} %bitcast.21, bf16[3456,512]{1,0:T(8,128)(2,1)S(1)} %bitcast.11), custom_call_target="tpu_custom_call" | custom-call | flops 5435817984 | bytes 6684672 | tf_op jit(solution)/shard_map/pallas_call | solution.py:227
  17.5 4.0 %collective-permute-start.2 = (bf16[2,68,768]{2,1,0:T(8,128)(2,1)S(1)}, bf16[2,68,768]{2,1,0:T(8,128)(2,1)S(1)}, u32[]{:S(2)}, u32[]{:S(2)}) collective-permute-start(bf16[2,68,768]{2,1,0:T(8,128)(2,1)S(1)} %get-tuple-element.35), channel_id=1, source_target_pairs={{0,4},{4,8},{8,12},{12,16},{16,20},{20,24},{24,28},{1,5},{5,9},{9,... | collective-permute-start | bytes 626696 | tf_op jit(solution)/shard_map/ppermute | solution.py:514
  21.5 2.1 %collective-permute-start.3 = (bf16[2,68,768]{2,1,0:T(8,128)(2,1)S(1)}, bf16[2,68,768]{2,1,0:T(8,128)(2,1)S(1)}, u32[]{:S(2)}, u32[]{:S(2)}) collective-permute-start(bf16[2,68,768]{2,1,0:T(8,128)(2,1)S(1)} %get-tuple-element.36), channel_id=1, source_target_pairs={{4,0},{8,4},{12,8},{16,12},{20,16},{24,20},{28,24},{5,1},{9,5},{13... | collective-permute-start | bytes 626696 | tf_op jit(solution)/shard_map/ppermute | solution.py:514
  23.6 6.2 %shard_map.106 = (bf16[48,64,128]{2,1,0:T(8,128)(2,1)S(1)}, f32[48,64,128]{2,1,0:T(8,128)S(1)}) custom-call(bf16[48,64,512]{2,1,0:T(8,128)(2,1)S(1)} %copy-done, bf16[48,64,128]{2,1,0:T(8,128)(2,1)S(1)} %copy-done.6, f32[48,64,128]{2,1,0:T(8,128)S(1)} %copy-done.5, f32[1,512]{1,0:T(1,128)S(1)} %bitcast.22, ...), custom_call_target="tpu_custom_call", output_to_operand_aliasing={{0}: (5, {}), {1}: (6, {})} | custom-call | flops 5435817984 | bytes 6684672 | tf_op jit(solution)/shard_map/pallas_call | solution.py:227
  29.9 0.0 copy-start.1
  29.9 2.2 %shard_map.107 = (f32[4,64,128]{2,1,0:T(8,128)S(1)}, f32[4,64,128]{2,1,0:T(8,128)S(1)}, f32[4,64,128]{2,1,0:T(8,128)S(1)}, f32[4,64,128]{2,1,0:T(8,128)S(1)}, f32[2,64,256]{2,1,0:T(8,128)S(1)}) custom-call(bf16[2,68,768]{2,1,0:T(8,128)(2,1)S(1)} %collective-permute-done.2.above.args_10_.args_14_, ...), custom_call_target="tpu_custom_call" | custom-call | flops 1811939328 | bytes 3538944 | tf_op jit(solution)/shard_map/pallas_call | solution.py:542
  32.2 0.5 copy-done.1
  32.7 9.3 %shard_map.108 = (bf16[8,4,4,16,128]{4,3,2,1,0:T(8,128)(2,1)S(1)}, f32[48,64,128]{2,1,0:T(8,128)}) custom-call(bf16[48,64,512]{2,1,0:T(8,128)(2,1)S(1)} %copy-done.1, bf16[48,64,128]{2,1,0:T(8,128)(2,1)S(1)} %get-tuple-element.33.args_1_.args_3_.args_4_.args_5_, f32[48,64,128]{2,1,0:T(8,128)S(1)} %get-tuple-element.34.args_2_.args_6_, ...), custom_call_target="tpu_custom_call" | custom-call | flops 7247757312 | bytes 7733248 | tf_op jit(solution)/shard_map/pallas_call | solution.py:227
  42.0 0.8 copy-done.7
  42.8 7.3 %all-to-all-start.1 = ((bf16[32,4,16,128]{3,2,1,0:T(8,128)(2,1)}), bf16[32,4,16,128]{3,2,1,0:T(8,128)(2,1)S(1)}, u32[]{:S(2)}, u32[]{:S(2)}) async-start(bf16[32,4,16,128]{3,2,1,0:T(8,128)(2,1)} %bitcast.18), calls=%async_computation.1 | async-start | bytes 1048576 | tf_op jit(solution)/shard_map/all_to_all | solution.py:577
  50.2 9.4 %shard_map.109 = (bf16[8,4,2,16,128]{4,3,2,1,0:T(8,128)(2,1)}, f32[48,64,128]{2,1,0:T(8,128)}) custom-call(bf16[48,64,512]{2,1,0:T(8,128)(2,1)} %args_2_.8, bf16[48,64,512]{2,1,0:T(8,128)(2,1)} %args_2_.8, bf16[48,64,512]{2,1,0:T(8,128)(2,1)} %args_2_.8, bf16[48,64,128]{2,1,0:T(8,128)(2,1)} %copy-done.2, ...), custom_call_target="tpu_custom_call", output_to_operand_aliasing={{1}: (16, {})} | custom-call | flops 3623878656 | bytes 5636096 | tf_op jit(solution)/shard_map/pallas_call | solution.py:227
  59.6 5.8 %all-to-all-done.1 = bf16[32,4,16,128]{3,2,1,0:T(8,128)(2,1)S(1)} async-done(((bf16[32,4,16,128]{3,2,1,0:T(8,128)(2,1)}), bf16[32,4,16,128]{3,2,1,0:T(8,128)(2,1)S(1)}, u32[]{:S(2)}, u32[]{:S(2)}) %all-to-all-start.1) | async-done | bytes 524320 | tf_op jit(solution)/shard_map/all_to_all | solution.py:577
  65.4 3.2 %all-to-all-start = ((bf16[32,2,16,128]{3,2,1,0:T(8,128)(2,1)}), bf16[32,2,16,128]{3,2,1,0:T(8,128)(2,1)S(1)}, u32[]{:S(2)}, u32[]{:S(2)}) async-start(bf16[32,2,16,128]{3,2,1,0:T(8,128)(2,1)} %bitcast.25), calls=%async_computation | async-start | bytes 524288 | tf_op jit(solution)/shard_map/all_to_all | solution.py:577
  68.6 9.4 %shard_map.110.rest_0_ = bf16[8,1,4,6,16,128]{5,4,3,2,1,0:T(8,128)(2,1)S(1)} custom-call(bf16[8,1,4,4,16,128]{5,4,3,2,1,0:T(8,128)(2,1)S(1)} %bitcast.17, bf16[128,768]{1,0:T(8,128)(2,1)S(1)} %copy-done.16, bf16[256,128]{1,0:T(8,128)(2,1)S(1)} %copy-done.19, bf16[128,512]{1,0:T(8,128)(2,1)S(1)} %copy-done.17, bf16[512,128]{1,0:T(8,128)(2,1)S(1)} %copy-done.18), custom_call_target="tpu_custom_call" | custom-call | flops 6144000000 | bytes 1848576 | tf_op jit(solution)/shard_map/pallas_call | solution.py:439
  78.0 0.9 all-to-all-done
  78.9 4.8 %shard_map.111 = bf16[8,1,4,6,16,128]{5,4,3,2,1,0:T(8,128)(2,1)S(1)} custom-call(bf16[8,1,4,2,16,128]{5,4,3,2,1,0:T(8,128)(2,1)S(1)} %bitcast.19, bf16[128,768]{1,0:T(8,128)(2,1)S(1)} %copy-done.16, bf16[256,128]{1,0:T(8,128)(2,1)S(1)} %copy-done.19, bf16[128,512]{1,0:T(8,128)(2,1)S(1)} %copy-done.17, ...), custom_call_target="tpu_custom_call", output_to_operand_aliasing={{}: (5, {})} | custom-call | flops 3072000000 | bytes 1324288 | tf_op jit(solution)/shard_map/pallas_call | solution.py:439
  83.7 25.6 %all_to_all.15 = bf16[32,6,16,128]{3,2,1,0:T(8,128)(2,1)S(1)} all-to-all(bf16[32,6,16,128]{3,2,1,0:T(8,128)(2,1)S(1)} %bitcast.16), channel_id=1, replica_groups=mesh['gy'=8,'gx'=4] {'gy','gx'}, dimensions={0} | all-to-all | bytes 1572864 | tf_op jit(solution)/shard_map/all_to_all | solution.py:584
  109.3 1.5 %shard_map.112 = bf16[48,64,128]{2,1,0:T(8,128)(2,1)} custom-call(bf16[8,4,6,16,128]{4,3,2,1,0:T(8,128)(2,1)S(1)} %bitcast.15), custom_call_target="tpu_custom_call" | custom-call | bytes 1572864 | tf_op jit(solution)/shard_map/pallas_call | solution.py:485
  (43 shorter events, 0.2 us)
Async XLA Ops:
  0.6 1.9 %copy-start = (bf16[48,64,512]{2,1,0:T(8,128)(2,1)S(1)}, bf16[48,64,512]{2,1,0:T(8,128)(2,1)}, u32[]{:S(2)}) copy-start(bf16[48,64,512]{2,1,0:T(8,128)(2,1)} %args_2_.8) | copy-start | bytes 9437188
  2.5 1.4 %copy-start.5 = (f32[48,64,128]{2,1,0:T(8,128)S(1)}, f32[48,64,128]{2,1,0:T(8,128)}, u32[]{:S(2)}) copy-start(f32[48,64,128]{2,1,0:T(8,128)} %args_2_.7) | copy-start | bytes 4718596
  5.1 6.1 %copy-start.3 = (bf16[3,3,384,512]{3,2,1,0:T(8,128)(2,1)S(1)}, bf16[3,3,384,512]{3,2,1,0:T(8,128)(2,1)}, u32[]{:S(2)}) copy-start(bf16[3,3,384,512]{3,2,1,0:T(8,128)(2,1)} %param.12) | copy-start | bytes 10616836
  5.1 6.1 %copy-start.15 = (f32[512]{0:T(512)S(1)}, f32[512]{0:T(512)}, u32[]{:S(2)}) copy-start(f32[512]{0:T(512)} %param.13) | copy-start | bytes 6148
  5.7 11.7 %collective-permute-start = (bf16[48,2,768]{2,1,0:T(2,128)(2,1)S(1)}, bf16[48,2,768]{2,1,0:T(2,128)(2,1)S(1)}, u32[]{:S(2)}, u32[]{:S(2)}) collective-permute-start(bf16[48,2,768]{2,1,0:T(2,128)(2,1)S(1)} %get-tuple-element.28), channel_id=1, source_target_pairs={{0,1},{1,2},{2,3},{4,5},{5,6},{6,7},{8,9},{9,10},{10,11},{12,13},{... | collective-permute-start | bytes 442376 | tf_op jit(solution)/shard_map/ppermute | solution.py:514
  9.9 7.5 %collective-permute-start.1 = (bf16[48,2,768]{2,1,0:T(2,128)(2,1)S(1)}, bf16[48,2,768]{2,1,0:T(2,128)(2,1)S(1)}, u32[]{:S(2)}, u32[]{:S(2)}) collective-permute-start(bf16[48,2,768]{2,1,0:T(2,128)(2,1)S(1)} %get-tuple-element.29), channel_id=1, source_target_pairs={{1,0},{2,1},{3,2},{5,4},{6,5},{7,6},{9,8},{10,9},{11,10},{13,12},{... | collective-permute-start | bytes 442376 | tf_op jit(solution)/shard_map/ppermute | solution.py:514
  17.5 12.3 %collective-permute-start.2 = (bf16[2,68,768]{2,1,0:T(8,128)(2,1)S(1)}, bf16[2,68,768]{2,1,0:T(8,128)(2,1)S(1)}, u32[]{:S(2)}, u32[]{:S(2)}) collective-permute-start(bf16[2,68,768]{2,1,0:T(8,128)(2,1)S(1)} %get-tuple-element.35), channel_id=1, source_target_pairs={{0,4},{4,8},{8,12},{12,16},{16,20},{20,24},{24,28},{1,5},{5,9},{9,... | collective-permute-start | bytes 626696 | tf_op jit(solution)/shard_map/ppermute | solution.py:514
  21.5 8.4 %collective-permute-start.3 = (bf16[2,68,768]{2,1,0:T(8,128)(2,1)S(1)}, bf16[2,68,768]{2,1,0:T(8,128)(2,1)S(1)}, u32[]{:S(2)}, u32[]{:S(2)}) collective-permute-start(bf16[2,68,768]{2,1,0:T(8,128)(2,1)S(1)} %get-tuple-element.36), channel_id=1, source_target_pairs={{4,0},{8,4},{12,8},{16,12},{20,16},{24,20},{28,24},{5,1},{9,5},{13... | collective-permute-start | bytes 626696 | tf_op jit(solution)/shard_map/ppermute | solution.py:514
  29.8 2.4 %copy-start.2 = (bf16[48,64,128]{2,1,0:T(8,128)(2,1)}, bf16[48,64,128]{2,1,0:T(8,128)(2,1)S(1)}, u32[]{:S(2)}) copy-start(bf16[48,64,128]{2,1,0:T(8,128)(2,1)S(1)} %get-tuple-element.33.args_1_.args_3_.args_4_.args_5_) | copy-start | bytes 2359300
  29.8 2.4 %copy-start.4 = (f32[48,64,128]{2,1,0:T(8,128)}, f32[48,64,128]{2,1,0:T(8,128)S(1)}, u32[]{:S(2)}) copy-start(f32[48,64,128]{2,1,0:T(8,128)S(1)} %get-tuple-element.34.args_2_.args_6_) | copy-start | bytes 4718596
  29.8 2.3 %copy-start.8 = (bf16[2,68,768]{2,1,0:T(8,128)(2,1)}, bf16[2,68,768]{2,1,0:T(8,128)(2,1)S(1)}, u32[]{:S(2)}) copy-start(bf16[2,68,768]{2,1,0:T(8,128)(2,1)S(1)} %collective-permute-done.2.above.args_10_.args_14_) | copy-start | bytes 626692
  29.9 2.3 %copy-start.9 = (bf16[2,68,768]{2,1,0:T(8,128)(2,1)}, bf16[2,68,768]{2,1,0:T(8,128)(2,1)S(1)}, u32[]{:S(2)}) copy-start(bf16[2,68,768]{2,1,0:T(8,128)(2,1)S(1)} %collective-permute-done.3.below.args_11_.args_15_) | copy-start | bytes 626692
  29.9 2.8 %copy-start.1 = (bf16[48,64,512]{2,1,0:T(8,128)(2,1)S(1)}, bf16[48,64,512]{2,1,0:T(8,128)(2,1)}, u32[]{:S(2)}) copy-start(bf16[48,64,512]{2,1,0:T(8,128)(2,1)} %args_2_.8) | copy-start | bytes 9437188
  32.1 9.8 %copy-start.10 = (f32[4,64,128]{2,1,0:T(8,128)}, f32[4,64,128]{2,1,0:T(8,128)S(1)}, u32[]{:S(2)}) copy-start(f32[4,64,128]{2,1,0:T(8,128)S(1)} %get-tuple-element.41.args_7_.args_11_) | copy-start | bytes 393220
  32.1 9.8 %copy-start.11 = (f32[4,64,128]{2,1,0:T(8,128)}, f32[4,64,128]{2,1,0:T(8,128)S(1)}, u32[]{:S(2)}) copy-start(f32[4,64,128]{2,1,0:T(8,128)S(1)} %get-tuple-element.42.args_8_.args_12_) | copy-start | bytes 393220
  32.1 9.8 %copy-start.12 = (f32[4,64,128]{2,1,0:T(8,128)}, f32[4,64,128]{2,1,0:T(8,128)S(1)}, u32[]{:S(2)}) copy-start(f32[4,64,128]{2,1,0:T(8,128)S(1)} %get-tuple-element.39.args_5_.args_9_) | copy-start | bytes 393220
  32.1 9.8 %copy-start.13 = (f32[4,64,128]{2,1,0:T(8,128)}, f32[4,64,128]{2,1,0:T(8,128)S(1)}, u32[]{:S(2)}) copy-start(f32[4,64,128]{2,1,0:T(8,128)S(1)} %get-tuple-element.40.args_6_.args_10_) | copy-start | bytes 393220
  32.1 9.8 %copy-start.14 = (f32[2,64,256]{2,1,0:T(8,128)}, f32[2,64,256]{2,1,0:T(8,128)S(1)}, u32[]{:S(2)}) copy-start(f32[2,64,256]{2,1,0:T(8,128)S(1)} %get-tuple-element.43.args_9_.args_13_) | copy-start | bytes 393220
  42.8 22.6 %all-to-all-start.1 = ((bf16[32,4,16,128]{3,2,1,0:T(8,128)(2,1)}), bf16[32,4,16,128]{3,2,1,0:T(8,128)(2,1)S(1)}, u32[]{:S(2)}, u32[]{:S(2)}) async-start(bf16[32,4,16,128]{3,2,1,0:T(8,128)(2,1)} %bitcast.18), calls=%async_computation.1 | async-start | bytes 1048576 | tf_op jit(solution)/shard_map/all_to_all | solution.py:577
  50.1 18.5 %copy-start.16 = (bf16[128,768]{1,0:T(8,128)(2,1)S(1)}, bf16[128,768]{1,0:T(8,128)(2,1)}, u32[]{:S(2)}) copy-start(bf16[128,768]{1,0:T(8,128)(2,1)} %w_qkv.3) | copy-start | bytes 589828
  50.1 18.5 %copy-start.17 = (bf16[128,512]{1,0:T(8,128)(2,1)S(1)}, bf16[128,512]{1,0:T(8,128)(2,1)}, u32[]{:S(2)}) copy-start(bf16[128,512]{1,0:T(8,128)(2,1)} %w_up.3) | copy-start | bytes 393220
  50.1 18.4 %copy-start.18 = (bf16[512,128]{1,0:T(8,128)(2,1)S(1)}, bf16[512,128]{1,0:T(8,128)(2,1)}, u32[]{:S(2)}) copy-start(bf16[512,128]{1,0:T(8,128)(2,1)} %w_down.3) | copy-start | bytes 393220
  50.1 18.4 %copy-start.19 = (bf16[256,128]{1,0:T(8,128)(2,1)S(1)}, bf16[256,128]{1,0:T(8,128)(2,1)}, u32[]{:S(2)}) copy-start(bf16[256,128]{1,0:T(8,128)(2,1)} %w_out.3) | copy-start | bytes 196612
  65.4 13.5 %all-to-all-start = ((bf16[32,2,16,128]{3,2,1,0:T(8,128)(2,1)}), bf16[32,2,16,128]{3,2,1,0:T(8,128)(2,1)S(1)}, u32[]{:S(2)}, u32[]{:S(2)}) async-start(bf16[32,2,16,128]{3,2,1,0:T(8,128)(2,1)} %bitcast.25), calls=%async_computation | async-start | bytes 524288 | tf_op jit(solution)/shard_map/all_to_all | solution.py:577
  (2 other events, 1.9 us)

commit v8 on v7

--- a/solution.py
+++ b/solution.py
@@ -160,7 +160,7 @@
             leaving.append(leave)
 
     leaving = []
-    depth = step_rows(0, extent, 12)
+    depth = step_rows(0, extent, 24)
     for pos in range(depth + 2):
         build(pos)
     for load in loads:
@@ -493,7 +493,7 @@
     )(landed)
 
 
-def step_rows(start, extent, most=16):
+def step_rows(start, extent, most):
     return max(size for size in range(1, most + 1) if extent % size == 0 and start % size == 0)
 
 

time: 111 us -> 111 us (level)
  no operation moved by 1% of the time
where the time goes in v8:
time: 111 us
  Pallas kernels  49.7 us (45%)
  blocking collectives  25.6 us (23%)
  starting transfers between devices  22 us (20%)
  waiting for transfers between devices  6.71 us (6%)
  local copies, waits for them, and re-layouts  5.83 us (5%)
    pallas_call x4, Pallas kernels, conv_step(): pl.pallas_call(functools.partial(conv_kernel, start, rows, part, refs, pa...  31.1 us
    all_to_all x1, blocking collectives, body(): lax.all_to_all(done, ('gy', 'gx'), split_axis=0, concat_axis=0, tiled=True)  25.6 us
    pallas_call x2, Pallas kernels, block_step(): pl.pallas_call(block_kernel, grid=(lanes, piece_y), in_specs=in_specs, ou...  14.2 us
    ppermute x4, starting transfers between devices, shifted(): return lax.ppermute(value, axis, pairs)  11.5 us
    all_to_all x2, starting transfers between devices, body(): lax.all_to_all(sent, ('gy', 'gx'), split_axis=0, concat_axis=0, tiled=True)  10.5 us
    all_to_all x2, waiting for transfers between devices, body(): lax.all_to_all(sent, ('gy', 'gx'), split_axis=0, concat_axis=0, tiled=True)  6.7 us
    unnamed x40, local copies, waits for them, and re-layouts  5.77 us
  transfers between devices with their start and end apart: 6, of which 2 were waited for; matrix products, arithmetic and copies ran while one was open for 0% of the time, Pallas kernels for 28%

profile of v8, /device:TPU:1, one launch (start us, length us, event | category | flops | bytes accessed | tf_op | source)
XLA Modules:
  0.0 110.9 jit_solution(4566181077309312147)
XLA Ops:
  0.6 1.9 %copy-done = bf16[48,64,512]{2,1,0:T(8,128)(2,1)S(1)} copy-done((bf16[48,64,512]{2,1,0:T(8,128)(2,1)S(1)}, bf16[48,64,512]{2,1,0:T(8,128)(2,1)}, u32[]{:S(2)}) %copy-start) | copy-done | bytes 3145752
  2.5 1.4 %copy-done.5 = f32[48,64,128]{2,1,0:T(8,128)S(1)} copy-done((f32[48,64,128]{2,1,0:T(8,128)S(1)}, f32[48,64,128]{2,1,0:T(8,128)}, u32[]{:S(2)}) %copy-start.5) | copy-done | bytes 1572888
  3.9 1.1 %copy-done.6 = bf16[48,64,128]{2,1,0:T(8,128)(2,1)S(1)} copy-done((bf16[48,64,128]{2,1,0:T(8,128)(2,1)S(1)}, bf16[48,64,128]{2,1,0:T(8,128)(2,1)}, u32[]{:S(2)}) %copy-start.6) | copy-done | bytes 786456
  5.1 0.6 shard_map.105
  5.7 4.2 %collective-permute-start = (bf16[48,2,768]{2,1,0:T(2,128)(2,1)S(1)}, bf16[48,2,768]{2,1,0:T(2,128)(2,1)S(1)}, u32[]{:S(2)}, u32[]{:S(2)}) collective-permute-start(bf16[48,2,768]{2,1,0:T(2,128)(2,1)S(1)} %get-tuple-element.28), channel_id=1, source_target_pairs={{0,1},{1,2},{2,3},{4,5},{5,6},{6,7},{8,9},{9,10},{10,11},{12,13},{... | collective-permute-start | bytes 442376 | tf_op jit(solution)/shard_map/ppermute | solution.py:514
  9.9 1.3 %collective-permute-start.1 = (bf16[48,2,768]{2,1,0:T(2,128)(2,1)S(1)}, bf16[48,2,768]{2,1,0:T(2,128)(2,1)S(1)}, u32[]{:S(2)}, u32[]{:S(2)}) collective-permute-start(bf16[48,2,768]{2,1,0:T(2,128)(2,1)S(1)} %get-tuple-element.29), channel_id=1, source_target_pairs={{1,0},{2,1},{3,2},{5,4},{6,5},{7,6},{9,8},{10,9},{11,10},{13,12},{... | collective-permute-start | bytes 442376 | tf_op jit(solution)/shard_map/ppermute | solution.py:514
  11.2 6.3 %shard_map.104 = (bf16[48,64,128]{2,1,0:T(8,128)(2,1)S(1)}, f32[48,64,128]{2,1,0:T(8,128)S(1)}) custom-call(bf16[48,64,512]{2,1,0:T(8,128)(2,1)S(1)} %copy-done, bf16[48,64,128]{2,1,0:T(8,128)(2,1)S(1)} %copy-done.6, f32[48,64,128]{2,1,0:T(8,128)S(1)} %copy-done.5, f32[1,512]{1,0:T(1,128)S(1)} %bitcast.21, bf16[3456,512]{1,0:T(8,128)(2,1)S(1)} %bitcast.11), custom_call_target="tpu_custom_call" | custom-call | flops 5435817984 | bytes 6684672 | tf_op jit(solution)/shard_map/pallas_call | solution.py:227
  17.6 4.0 %collective-permute-start.2 = (bf16[2,68,768]{2,1,0:T(8,128)(2,1)S(1)}, bf16[2,68,768]{2,1,0:T(8,128)(2,1)S(1)}, u32[]{:S(2)}, u32[]{:S(2)}) collective-permute-start(bf16[2,68,768]{2,1,0:T(8,128)(2,1)S(1)} %get-tuple-element.35), channel_id=1, source_target_pairs={{0,4},{4,8},{8,12},{12,16},{16,20},{20,24},{24,28},{1,5},{5,9},{9,... | collective-permute-start | bytes 626696 | tf_op jit(solution)/shard_map/ppermute | solution.py:514
  21.6 2.1 %collective-permute-start.3 = (bf16[2,68,768]{2,1,0:T(8,128)(2,1)S(1)}, bf16[2,68,768]{2,1,0:T(8,128)(2,1)S(1)}, u32[]{:S(2)}, u32[]{:S(2)}) collective-permute-start(bf16[2,68,768]{2,1,0:T(8,128)(2,1)S(1)} %get-tuple-element.36), channel_id=1, source_target_pairs={{4,0},{8,4},{12,8},{16,12},{20,16},{24,20},{28,24},{5,1},{9,5},{13... | collective-permute-start | bytes 626696 | tf_op jit(solution)/shard_map/ppermute | solution.py:514
  23.7 6.3 %shard_map.106 = (bf16[48,64,128]{2,1,0:T(8,128)(2,1)S(1)}, f32[48,64,128]{2,1,0:T(8,128)S(1)}) custom-call(bf16[48,64,512]{2,1,0:T(8,128)(2,1)S(1)} %copy-done, bf16[48,64,128]{2,1,0:T(8,128)(2,1)S(1)} %copy-done.6, f32[48,64,128]{2,1,0:T(8,128)S(1)} %copy-done.5, f32[1,512]{1,0:T(1,128)S(1)} %bitcast.22, ...), custom_call_target="tpu_custom_call", output_to_operand_aliasing={{0}: (5, {}), {1}: (6, {})} | custom-call | flops 5435817984 | bytes 6684672 | tf_op jit(solution)/shard_map/pallas_call | solution.py:227
  29.9 0.0 copy-start.2
  30.1 2.2 %shard_map.107 = (f32[4,64,128]{2,1,0:T(8,128)S(1)}, f32[4,64,128]{2,1,0:T(8,128)S(1)}, f32[4,64,128]{2,1,0:T(8,128)S(1)}, f32[4,64,128]{2,1,0:T(8,128)S(1)}, f32[2,64,256]{2,1,0:T(8,128)S(1)}) custom-call(bf16[2,68,768]{2,1,0:T(8,128)(2,1)S(1)} %collective-permute-done.2.above.args_10_.args_14_, ...), custom_call_target="tpu_custom_call" | custom-call | flops 1811939328 | bytes 3538944 | tf_op jit(solution)/shard_map/pallas_call | solution.py:542
  32.4 0.5 copy-done.1
  32.8 9.2 %shard_map.108 = (bf16[8,4,4,16,128]{4,3,2,1,0:T(8,128)(2,1)S(1)}, f32[48,64,128]{2,1,0:T(8,128)}) custom-call(bf16[48,64,512]{2,1,0:T(8,128)(2,1)S(1)} %copy-done.1, bf16[48,64,128]{2,1,0:T(8,128)(2,1)S(1)} %get-tuple-element.33.args_1_.args_3_.args_4_.args_5_, f32[48,64,128]{2,1,0:T(8,128)S(1)} %get-tuple-element.34.args_2_.args_6_, ...), custom_call_target="tpu_custom_call" | custom-call | flops 7247757312 | bytes 7733248 | tf_op jit(solution)/shard_map/pallas_call | solution.py:227
  42.1 0.8 copy-done.7
  42.9 7.3 %all-to-all-start.1 = ((bf16[32,4,16,128]{3,2,1,0:T(8,128)(2,1)}), bf16[32,4,16,128]{3,2,1,0:T(8,128)(2,1)S(1)}, u32[]{:S(2)}, u32[]{:S(2)}) async-start(bf16[32,4,16,128]{3,2,1,0:T(8,128)(2,1)} %bitcast.18), calls=%async_computation.1 | async-start | bytes 1048576 | tf_op jit(solution)/shard_map/all_to_all | solution.py:577
  50.3 9.4 %shard_map.109 = (bf16[8,4,2,16,128]{4,3,2,1,0:T(8,128)(2,1)}, f32[48,64,128]{2,1,0:T(8,128)}) custom-call(bf16[48,64,512]{2,1,0:T(8,128)(2,1)} %args_2_.8, bf16[48,64,512]{2,1,0:T(8,128)(2,1)} %args_2_.8, bf16[48,64,512]{2,1,0:T(8,128)(2,1)} %args_2_.8, bf16[48,64,128]{2,1,0:T(8,128)(2,1)} %copy-done.2, ...), custom_call_target="tpu_custom_call", output_to_operand_aliasing={{1}: (16, {})} | custom-call | flops 3623878656 | bytes 5636096 | tf_op jit(solution)/shard_map/pallas_call | solution.py:227
  59.7 5.8 %all-to-all-done.1 = bf16[32,4,16,128]{3,2,1,0:T(8,128)(2,1)S(1)} async-done(((bf16[32,4,16,128]{3,2,1,0:T(8,128)(2,1)}), bf16[32,4,16,128]{3,2,1,0:T(8,128)(2,1)S(1)}, u32[]{:S(2)}, u32[]{:S(2)}) %all-to-all-start.1) | async-done | bytes 524320 | tf_op jit(solution)/shard_map/all_to_all | solution.py:577
  65.5 3.2 %all-to-all-start = ((bf16[32,2,16,128]{3,2,1,0:T(8,128)(2,1)}), bf16[32,2,16,128]{3,2,1,0:T(8,128)(2,1)S(1)}, u32[]{:S(2)}, u32[]{:S(2)}) async-start(bf16[32,2,16,128]{3,2,1,0:T(8,128)(2,1)} %bitcast.25), calls=%async_computation | async-start | bytes 524288 | tf_op jit(solution)/shard_map/all_to_all | solution.py:577
  68.7 9.4 %shard_map.110.rest_0_ = bf16[8,1,4,6,16,128]{5,4,3,2,1,0:T(8,128)(2,1)S(1)} custom-call(bf16[8,1,4,4,16,128]{5,4,3,2,1,0:T(8,128)(2,1)S(1)} %bitcast.17, bf16[128,768]{1,0:T(8,128)(2,1)S(1)} %copy-done.16, bf16[256,128]{1,0:T(8,128)(2,1)S(1)} %copy-done.19, bf16[128,512]{1,0:T(8,128)(2,1)S(1)} %copy-done.17, bf16[512,128]{1,0:T(8,128)(2,1)S(1)} %copy-done.18), custom_call_target="tpu_custom_call" | custom-call | flops 6144000000 | bytes 1848576 | tf_op jit(solution)/shard_map/pallas_call | solution.py:439
  78.1 0.9 all-to-all-done
  79.0 4.8 %shard_map.111 = bf16[8,1,4,6,16,128]{5,4,3,2,1,0:T(8,128)(2,1)S(1)} custom-call(bf16[8,1,4,2,16,128]{5,4,3,2,1,0:T(8,128)(2,1)S(1)} %bitcast.19, bf16[128,768]{1,0:T(8,128)(2,1)S(1)} %copy-done.16, bf16[256,128]{1,0:T(8,128)(2,1)S(1)} %copy-done.19, bf16[128,512]{1,0:T(8,128)(2,1)S(1)} %copy-done.17, ...), custom_call_target="tpu_custom_call", output_to_operand_aliasing={{}: (5, {})} | custom-call | flops 3072000000 | bytes 1324288 | tf_op jit(solution)/shard_map/pallas_call | solution.py:439
  83.8 25.6 %all_to_all.15 = bf16[32,6,16,128]{3,2,1,0:T(8,128)(2,1)S(1)} all-to-all(bf16[32,6,16,128]{3,2,1,0:T(8,128)(2,1)S(1)} %bitcast.16), channel_id=1, replica_groups=mesh['gy'=8,'gx'=4] {'gy','gx'}, dimensions={0} | all-to-all | bytes 1572864 | tf_op jit(solution)/shard_map/all_to_all | solution.py:584
  109.4 1.5 %shard_map.112 = bf16[48,64,128]{2,1,0:T(8,128)(2,1)} custom-call(bf16[8,4,6,16,128]{4,3,2,1,0:T(8,128)(2,1)S(1)} %bitcast.15), custom_call_target="tpu_custom_call" | custom-call | bytes 1572864 | tf_op jit(solution)/shard_map/pallas_call | solution.py:485
  (43 shorter events, 0.2 us)
Async XLA Ops:
  0.6 1.9 %copy-start = (bf16[48,64,512]{2,1,0:T(8,128)(2,1)S(1)}, bf16[48,64,512]{2,1,0:T(8,128)(2,1)}, u32[]{:S(2)}) copy-start(bf16[48,64,512]{2,1,0:T(8,128)(2,1)} %args_2_.8) | copy-start | bytes 9437188
  2.5 1.4 %copy-start.5 = (f32[48,64,128]{2,1,0:T(8,128)S(1)}, f32[48,64,128]{2,1,0:T(8,128)}, u32[]{:S(2)}) copy-start(f32[48,64,128]{2,1,0:T(8,128)} %args_2_.7) | copy-start | bytes 4718596
  5.1 6.1 %copy-start.3 = (bf16[3,3,384,512]{3,2,1,0:T(8,128)(2,1)S(1)}, bf16[3,3,384,512]{3,2,1,0:T(8,128)(2,1)}, u32[]{:S(2)}) copy-start(bf16[3,3,384,512]{3,2,1,0:T(8,128)(2,1)} %param.12) | copy-start | bytes 10616836
  5.1 6.1 %copy-start.15 = (f32[512]{0:T(512)S(1)}, f32[512]{0:T(512)}, u32[]{:S(2)}) copy-start(f32[512]{0:T(512)} %param.13) | copy-start | bytes 6148
  5.7 11.8 %collective-permute-start = (bf16[48,2,768]{2,1,0:T(2,128)(2,1)S(1)}, bf16[48,2,768]{2,1,0:T(2,128)(2,1)S(1)}, u32[]{:S(2)}, u32[]{:S(2)}) collective-permute-start(bf16[48,2,768]{2,1,0:T(2,128)(2,1)S(1)} %get-tuple-element.28), channel_id=1, source_target_pairs={{0,1},{1,2},{2,3},{4,5},{5,6},{6,7},{8,9},{9,10},{10,11},{12,13},{... | collective-permute-start | bytes 442376 | tf_op jit(solution)/shard_map/ppermute | solution.py:514
  9.9 7.6 %collective-permute-start.1 = (bf16[48,2,768]{2,1,0:T(2,128)(2,1)S(1)}, bf16[48,2,768]{2,1,0:T(2,128)(2,1)S(1)}, u32[]{:S(2)}, u32[]{:S(2)}) collective-permute-start(bf16[48,2,768]{2,1,0:T(2,128)(2,1)S(1)} %get-tuple-element.29), channel_id=1, source_target_pairs={{1,0},{2,1},{3,2},{5,4},{6,5},{7,6},{9,8},{10,9},{11,10},{13,12},{... | collective-permute-start | bytes 442376 | tf_op jit(solution)/shard_map/ppermute | solution.py:514
  17.6 12.4 %collective-permute-start.2 = (bf16[2,68,768]{2,1,0:T(8,128)(2,1)S(1)}, bf16[2,68,768]{2,1,0:T(8,128)(2,1)S(1)}, u32[]{:S(2)}, u32[]{:S(2)}) collective-permute-start(bf16[2,68,768]{2,1,0:T(8,128)(2,1)S(1)} %get-tuple-element.35), channel_id=1, source_target_pairs={{0,4},{4,8},{8,12},{12,16},{16,20},{20,24},{24,28},{1,5},{5,9},{9,... | collective-permute-start | bytes 626696 | tf_op jit(solution)/shard_map/ppermute | solution.py:514
  21.6 8.5 %collective-permute-start.3 = (bf16[2,68,768]{2,1,0:T(8,128)(2,1)S(1)}, bf16[2,68,768]{2,1,0:T(8,128)(2,1)S(1)}, u32[]{:S(2)}, u32[]{:S(2)}) collective-permute-start(bf16[2,68,768]{2,1,0:T(8,128)(2,1)S(1)} %get-tuple-element.36), channel_id=1, source_target_pairs={{4,0},{8,4},{12,8},{16,12},{20,16},{24,20},{28,24},{5,1},{9,5},{13... | collective-permute-start | bytes 626696 | tf_op jit(solution)/shard_map/ppermute | solution.py:514
  29.9 2.4 %copy-start.2 = (bf16[48,64,128]{2,1,0:T(8,128)(2,1)}, bf16[48,64,128]{2,1,0:T(8,128)(2,1)S(1)}, u32[]{:S(2)}) copy-start(bf16[48,64,128]{2,1,0:T(8,128)(2,1)S(1)} %get-tuple-element.33.args_1_.args_3_.args_4_.args_5_) | copy-start | bytes 2359300
  29.9 2.4 %copy-start.4 = (f32[48,64,128]{2,1,0:T(8,128)}, f32[48,64,128]{2,1,0:T(8,128)S(1)}, u32[]{:S(2)}) copy-start(f32[48,64,128]{2,1,0:T(8,128)S(1)} %get-tuple-element.34.args_2_.args_6_) | copy-start | bytes 4718596
  30.0 2.3 %copy-start.8 = (bf16[2,68,768]{2,1,0:T(8,128)(2,1)}, bf16[2,68,768]{2,1,0:T(8,128)(2,1)S(1)}, u32[]{:S(2)}) copy-start(bf16[2,68,768]{2,1,0:T(8,128)(2,1)S(1)} %collective-permute-done.2.above.args_10_.args_14_) | copy-start | bytes 626692
  30.0 2.3 %copy-start.9 = (bf16[2,68,768]{2,1,0:T(8,128)(2,1)}, bf16[2,68,768]{2,1,0:T(8,128)(2,1)S(1)}, u32[]{:S(2)}) copy-start(bf16[2,68,768]{2,1,0:T(8,128)(2,1)S(1)} %collective-permute-done.3.below.args_11_.args_15_) | copy-start | bytes 626692
  30.0 2.8 %copy-start.1 = (bf16[48,64,512]{2,1,0:T(8,128)(2,1)S(1)}, bf16[48,64,512]{2,1,0:T(8,128)(2,1)}, u32[]{:S(2)}) copy-start(bf16[48,64,512]{2,1,0:T(8,128)(2,1)} %args_2_.8) | copy-start | bytes 9437188
  32.3 9.8 %copy-start.10 = (f32[4,64,128]{2,1,0:T(8,128)}, f32[4,64,128]{2,1,0:T(8,128)S(1)}, u32[]{:S(2)}) copy-start(f32[4,64,128]{2,1,0:T(8,128)S(1)} %get-tuple-element.41.args_7_.args_11_) | copy-start | bytes 393220
  32.3 9.8 %copy-start.11 = (f32[4,64,128]{2,1,0:T(8,128)}, f32[4,64,128]{2,1,0:T(8,128)S(1)}, u32[]{:S(2)}) copy-start(f32[4,64,128]{2,1,0:T(8,128)S(1)} %get-tuple-element.42.args_8_.args_12_) | copy-start | bytes 393220
  32.3 9.8 %copy-start.12 = (f32[4,64,128]{2,1,0:T(8,128)}, f32[4,64,128]{2,1,0:T(8,128)S(1)}, u32[]{:S(2)}) copy-start(f32[4,64,128]{2,1,0:T(8,128)S(1)} %get-tuple-element.39.args_5_.args_9_) | copy-start | bytes 393220
  32.3 9.8 %copy-start.13 = (f32[4,64,128]{2,1,0:T(8,128)}, f32[4,64,128]{2,1,0:T(8,128)S(1)}, u32[]{:S(2)}) copy-start(f32[4,64,128]{2,1,0:T(8,128)S(1)} %get-tuple-element.40.args_6_.args_10_) | copy-start | bytes 393220
  32.3 9.8 %copy-start.14 = (f32[2,64,256]{2,1,0:T(8,128)}, f32[2,64,256]{2,1,0:T(8,128)S(1)}, u32[]{:S(2)}) copy-start(f32[2,64,256]{2,1,0:T(8,128)S(1)} %get-tuple-element.43.args_9_.args_13_) | copy-start | bytes 393220
  42.9 22.6 %all-to-all-start.1 = ((bf16[32,4,16,128]{3,2,1,0:T(8,128)(2,1)}), bf16[32,4,16,128]{3,2,1,0:T(8,128)(2,1)S(1)}, u32[]{:S(2)}, u32[]{:S(2)}) async-start(bf16[32,4,16,128]{3,2,1,0:T(8,128)(2,1)} %bitcast.18), calls=%async_computation.1 | async-start | bytes 1048576 | tf_op jit(solution)/shard_map/all_to_all | solution.py:577
  50.2 18.5 %copy-start.16 = (bf16[128,768]{1,0:T(8,128)(2,1)S(1)}, bf16[128,768]{1,0:T(8,128)(2,1)}, u32[]{:S(2)}) copy-start(bf16[128,768]{1,0:T(8,128)(2,1)} %w_qkv.3) | copy-start | bytes 589828
  50.2 18.5 %copy-start.17 = (bf16[128,512]{1,0:T(8,128)(2,1)S(1)}, bf16[128,512]{1,0:T(8,128)(2,1)}, u32[]{:S(2)}) copy-start(bf16[128,512]{1,0:T(8,128)(2,1)} %w_up.3) | copy-start | bytes 393220
  50.3 18.4 %copy-start.18 = (bf16[512,128]{1,0:T(8,128)(2,1)S(1)}, bf16[512,128]{1,0:T(8,128)(2,1)}, u32[]{:S(2)}) copy-start(bf16[512,128]{1,0:T(8,128)(2,1)} %w_down.3) | copy-start | bytes 393220
  50.3 18.4 %copy-start.19 = (bf16[256,128]{1,0:T(8,128)(2,1)S(1)}, bf16[256,128]{1,0:T(8,128)(2,1)}, u32[]{:S(2)}) copy-start(bf16[256,128]{1,0:T(8,128)(2,1)} %w_out.3) | copy-start | bytes 196612
  65.5 13.5 %all-to-all-start = ((bf16[32,2,16,128]{3,2,1,0:T(8,128)(2,1)}), bf16[32,2,16,128]{3,2,1,0:T(8,128)(2,1)S(1)}, u32[]{:S(2)}, u32[]{:S(2)}) async-start(bf16[32,2,16,128]{3,2,1,0:T(8,128)(2,1)} %bitcast.25), calls=%async_computation | async-start | bytes 524288 | tf_op jit(solution)/shard_map/all_to_all | solution.py:577
  (2 other events, 1.9 us)

commit v9 on v7

--- a/solution.py
+++ b/solution.py
@@ -40,11 +40,20 @@
     return center * lax.rsqrt(spread + 1e-05)
 
 
+def with_first(wide, row):
+    place = lax.broadcasted_iota(jnp.int32, (8, wide.shape[1]), 0)
+    return jnp.concatenate([jnp.where(place == 0, row, wide[:8]), wide[8:]], axis=0)
+
+
+def with_last(wide, row):
+    place = lax.broadcasted_iota(jnp.int32, (8, wide.shape[1]), 0)
+    return jnp.concatenate([wide[:-8], jnp.where(place == 7, row, wide[-8:])], axis=0)
+
+
 def three_columns(wide, left, right):
     count = wide.shape[0]
-    place = lax.broadcasted_iota(jnp.int32, wide.shape, 0)
-    before = jnp.where(place == 0, left, pltpu.roll(wide, 1, axis=0))
-    after = jnp.where(place == count - 1, right, pltpu.roll(wide, count - 1, axis=0))
+    before = with_first(pltpu.roll(wide, 1, axis=0), left)
+    after = with_last(pltpu.roll(wide, count - 1, axis=0), right)
     return before.astype(BF), wide.astype(BF), after.astype(BF)
 
 
@@ -102,9 +111,8 @@
         low, high = beside(row)
         if ring:
             at = row + 2
-            place = lax.broadcasted_iota(jnp.int32, h.shape, 0)
-            h = jnp.where(place == 0, ref["strips_hid"][1, at : at + 1, :], h)
-            h = jnp.where(place == cols - 1, ref["strips_hid"][2, at : at + 1, :], h)
+            h = with_first(h, ref["strips_hid"][1, at : at + 1, :])
+            h = with_last(h, ref["strips_hid"][2, at : at + 1, :])
             for spot, line in ((-1, 0), (0, 1), (rows - 1, 2), (rows, 3)):
                 if row == spot:
                     h = ref["lines_hid"][line]
@@ -128,9 +136,8 @@
             cell_prev = row_of("cell", row)
             if ring:
                 at = row + 2
-                place = lax.broadcasted_iota(jnp.int32, cell_prev.shape, 0)
-                cell_prev = jnp.where(place == 0, ref["strips_cell"][1, at : at + 1, :], cell_prev)
-                cell_prev = jnp.where(place == cols - 1, ref["strips_cell"][2, at : at + 1, :], cell_prev)
+                cell_prev = with_first(cell_prev, ref["strips_cell"][1, at : at + 1, :])
+                cell_prev = with_last(cell_prev, ref["strips_cell"][2, at : at + 1, :])
                 if row == 0:
                     cell_prev = ref["lines_cell"][1]
                 if row == rows - 1:
@@ -514,22 +521,28 @@
         return lax.ppermute(value, axis, pairs)
 
     send_left, send_right, side_left, side_right, line_top, line_bot = pack_step(frames, hidden_state, cell_state)
+    tile_shapes = (jax.ShapeDtypeStruct((rows, cols, width), BF), jax.ShapeDtypeStruct((rows, cols, width), F32))
+    near = pl.BlockSpec(memory_space=pltpu.VMEM)
+    carry = ()
+
+    def first_conv(start, extent, *others):
+        done = conv_step(
+            frames, 0, hidden_state, cell_state, {}, weights, bias, (start, extent), ("hid_out", "cell_out"),
+            tile_shapes, (near, near), None, carry, False,
+        )
+        return lax.optimization_barrier((tuple(done), others))
+
+    quarter = rows // 4
     from_left = shifted(send_right, "gx", 1)
+    carry, (send_left,) = first_conv(0, quarter, send_left)
     from_right = shifted(send_left, "gx", -1)
+    carry, (line_top, line_bot) = first_conv(quarter, quarter, line_top, line_bot)
     to_down = jnp.concatenate([line_bot, from_left[-2:], from_right[-2:]], axis=1)
     to_up = jnp.concatenate([line_top, from_left[:2], from_right[:2]], axis=1)
-
-    tile_shapes = (jax.ShapeDtypeStruct((rows, cols, width), BF), jax.ShapeDtypeStruct((rows, cols, width), F32))
-    carry = ()
-    for start, extent in ((0, rows // 2), (rows // 2, rows - rows // 2)):
-        spec = pl.BlockSpec(memory_space=pltpu.VMEM)
-        if carry:
-            *carry, to_down, to_up = lax.optimization_barrier((*carry, to_down, to_up))
-            from_up, from_down = shifted(to_down, "gy", 1), shifted(to_up, "gy", -1)
-        carry = conv_step(
-            frames, 0, hidden_state, cell_state, {}, weights, bias, (start, extent), ("hid_out", "cell_out"),
-            tile_shapes, (spec, spec), None, carry, False,
-        )
+    from_up = shifted(to_down, "gy", 1)
+    carry, (to_up,) = first_conv(2 * quarter, quarter, to_up)
+    from_down = shifted(to_up, "gy", -1)
+    carry, _ = first_conv(3 * quarter, rows - 3 * quarter)
     hidden_one, cell_one = carry
 
     length = -(-(rows + 4) // 16) * 16

time: 111 us -> 112 us (level)
    pallas_call x4 -> x6, Pallas kernels: 31 us -> 31.4 us  [conv_step(): pl.pallas_call(functools.partial(conv_kernel, start, rows, part, refs, pa...]
where the time goes in v9:
time: 112 us; the launch traced here: 111 us
  Pallas kernels  49.9 us (45%)
  blocking collectives  25.6 us (23%)
  starting transfers between devices  21.9 us (20%)
  waiting for transfers between devices  6.73 us (6%)
  local copies, waits for them, and re-layouts  5.89 us (5%)
    pallas_call x6, Pallas kernels, conv_step(): pl.pallas_call(functools.partial(conv_kernel, start, rows, part, refs, pa...  31.4 us
    all_to_all x1, blocking collectives, body(): lax.all_to_all(done, ('gy', 'gx'), split_axis=0, concat_axis=0, tiled=True)  25.6 us
    pallas_call x2, Pallas kernels, block_step(): pl.pallas_call(block_kernel, grid=(lanes, piece_y), in_specs=in_specs, ou...  14.2 us
    ppermute x4, starting transfers between devices, shifted(): return lax.ppermute(value, axis, pairs)  11.5 us
    all_to_all x2, starting transfers between devices, body(): lax.all_to_all(sent, ('gy', 'gx'), split_axis=0, concat_axis=0, tiled=True)  10.4 us
    all_to_all x2, waiting for transfers between devices, body(): lax.all_to_all(sent, ('gy', 'gx'), split_axis=0, concat_axis=0, tiled=True)  6.72 us
    unnamed x40, local copies, waits for them, and re-layouts  5.83 us
  transfers between devices with their start and end apart: 6, of which 2 were waited for; matrix products, arithmetic and copies ran while one was open for 0% of the time, Pallas kernels for 28%

profile of v9, /device:TPU:1, one launch (start us, length us, event | category | flops | bytes accessed | tf_op | source)
XLA Modules:
  0.0 111.2 jit_solution(3540754342079584148)
XLA Ops:
  0.6 1.9 %copy-done = bf16[48,64,512]{2,1,0:T(8,128)(2,1)S(1)} copy-done((bf16[48,64,512]{2,1,0:T(8,128)(2,1)S(1)}, bf16[48,64,512]{2,1,0:T(8,128)(2,1)}, u32[]{:S(2)}) %copy-start) | copy-done | bytes 3145752
  2.5 1.4 %copy-done.5 = f32[48,64,128]{2,1,0:T(8,128)S(1)} copy-done((f32[48,64,128]{2,1,0:T(8,128)S(1)}, f32[48,64,128]{2,1,0:T(8,128)}, u32[]{:S(2)}) %copy-start.5) | copy-done | bytes 1572888
  3.9 1.1 %copy-done.6 = bf16[48,64,128]{2,1,0:T(8,128)(2,1)S(1)} copy-done((bf16[48,64,128]{2,1,0:T(8,128)(2,1)S(1)}, bf16[48,64,128]{2,1,0:T(8,128)(2,1)}, u32[]{:S(2)}) %copy-start.6) | copy-done | bytes 786456
  5.1 0.6 shard_map.105
  5.7 4.2 %collective-permute-start = (bf16[48,2,768]{2,1,0:T(2,128)(2,1)S(1)}, bf16[48,2,768]{2,1,0:T(2,128)(2,1)S(1)}, u32[]{:S(2)}, u32[]{:S(2)}) collective-permute-start(bf16[48,2,768]{2,1,0:T(2,128)(2,1)S(1)} %get-tuple-element.49), channel_id=1, source_target_pairs={{0,1},{1,2},{2,3},{4,5},{5,6},{6,7},{8,9},{9,10},{10,11},{12,13},{... | collective-permute-start | bytes 442376 | tf_op jit(solution)/shard_map/ppermute | solution.py:521
  9.9 3.2 %shard_map.104 = (bf16[48,64,128]{2,1,0:T(8,128)(2,1)S(1)}, f32[48,64,128]{2,1,0:T(8,128)S(1)}) custom-call(bf16[48,64,512]{2,1,0:T(8,128)(2,1)S(1)} %copy-done, bf16[48,64,128]{2,1,0:T(8,128)(2,1)S(1)} %copy-done.6, f32[48,64,128]{2,1,0:T(8,128)S(1)} %copy-done.5, f32[1,512]{1,0:T(1,128)S(1)} %bitcast.23, bf16[3456,512]{1,0:T(8,128)(2,1)S(1)} %bitcast.11), custom_call_target="tpu_custom_call" | custom-call | flops 2717908992 | bytes 5111808 | tf_op jit(solution)/shard_map/pallas_call | solution.py:234
  13.1 1.3 %collective-permute-start.1 = (bf16[48,2,768]{2,1,0:T(2,128)(2,1)S(1)}, bf16[48,2,768]{2,1,0:T(2,128)(2,1)S(1)}, u32[]{:S(2)}, u32[]{:S(2)}) collective-permute-start(bf16[48,2,768]{2,1,0:T(2,128)(2,1)S(1)} %get-tuple-element.50), channel_id=1, source_target_pairs={{1,0},{2,1},{3,2},{5,4},{6,5},{7,6},{9,8},{10,9},{11,10},{13,12},{... | collective-permute-start | bytes 442376 | tf_op jit(solution)/shard_map/ppermute | solution.py:521
  14.4 3.2 %shard_map.106 = (bf16[48,64,128]{2,1,0:T(8,128)(2,1)S(1)}, f32[48,64,128]{2,1,0:T(8,128)S(1)}) custom-call(bf16[48,64,512]{2,1,0:T(8,128)(2,1)S(1)} %copy-done, bf16[48,64,128]{2,1,0:T(8,128)(2,1)S(1)} %copy-done.6, f32[48,64,128]{2,1,0:T(8,128)S(1)} %copy-done.5, f32[1,512]{1,0:T(1,128)S(1)} %bitcast.24, ...), custom_call_target="tpu_custom_call", output_to_operand_aliasing={{0}: (5, {}), {1}: (6, {})} | custom-call | flops 2717908992 | bytes 5111808 | tf_op jit(solution)/shard_map/pallas_call | solution.py:234
  17.6 3.2 %shard_map.107 = (bf16[48,64,128]{2,1,0:T(8,128)(2,1)S(1)}, f32[48,64,128]{2,1,0:T(8,128)S(1)}) custom-call(bf16[48,64,512]{2,1,0:T(8,128)(2,1)S(1)} %copy-done, bf16[48,64,128]{2,1,0:T(8,128)(2,1)S(1)} %copy-done.6, f32[48,64,128]{2,1,0:T(8,128)S(1)} %copy-done.5, f32[1,512]{1,0:T(1,128)S(1)} %bitcast.25, ...), custom_call_target="tpu_custom_call", output_to_operand_aliasing={{0}: (5, {}), {1}: (6, {})} | custom-call | flops 2717908992 | bytes 5111808 | tf_op jit(solution)/shard_map/pallas_call | solution.py:234
  20.9 2.8 %collective-permute-start.3 = (bf16[2,68,768]{2,1,0:T(8,128)(2,1)S(1)}, bf16[2,68,768]{2,1,0:T(8,128)(2,1)S(1)}, u32[]{:S(2)}, u32[]{:S(2)}) collective-permute-start(bf16[2,68,768]{2,1,0:T(8,128)(2,1)S(1)} %pad_maximum_fusion), channel_id=1, source_target_pairs={{4,0},{8,4},{12,8},{16,12},{20,16},{24,20},{28,24},{5,1},{9,5},{13... | collective-permute-start | bytes 626696 | tf_op jit(solution)/shard_map/ppermute | solution.py:521
  23.8 3.2 %collective-permute-start.2 = (bf16[2,68,768]{2,1,0:T(8,128)(2,1)S(1)}, bf16[2,68,768]{2,1,0:T(8,128)(2,1)S(1)}, u32[]{:S(2)}, u32[]{:S(2)}) collective-permute-start(bf16[2,68,768]{2,1,0:T(8,128)(2,1)S(1)} %pad_maximum_fusion.1), channel_id=1, source_target_pairs={{0,4},{4,8},{8,12},{12,16},{16,20},{20,24},{24,28},{1,5},{5,9},{9,... | collective-permute-start | bytes 626696 | tf_op jit(solution)/shard_map/ppermute | solution.py:521
  27.0 3.1 %shard_map.108 = (bf16[48,64,128]{2,1,0:T(8,128)(2,1)S(1)}, f32[48,64,128]{2,1,0:T(8,128)S(1)}) custom-call(bf16[48,64,512]{2,1,0:T(8,128)(2,1)S(1)} %copy-done, bf16[48,64,128]{2,1,0:T(8,128)(2,1)S(1)} %copy-done.6, f32[48,64,128]{2,1,0:T(8,128)S(1)} %copy-done.5, f32[1,512]{1,0:T(1,128)S(1)} %bitcast.26, ...), custom_call_target="tpu_custom_call", output_to_operand_aliasing={{0}: (5, {}), {1}: (6, {})} | custom-call | flops 2717908992 | bytes 5111808 | tf_op jit(solution)/shard_map/pallas_call | solution.py:234
  30.2 2.2 %shard_map.109 = (f32[4,64,128]{2,1,0:T(8,128)S(1)}, f32[4,64,128]{2,1,0:T(8,128)S(1)}, f32[4,64,128]{2,1,0:T(8,128)S(1)}, f32[4,64,128]{2,1,0:T(8,128)S(1)}, f32[2,64,256]{2,1,0:T(8,128)S(1)}) custom-call(bf16[2,68,768]{2,1,0:T(8,128)(2,1)S(1)} %collective-permute-done.2.above.args_10_.args_14_, ...), custom_call_target="tpu_custom_call" | custom-call | flops 1811939328 | bytes 3538944 | tf_op jit(solution)/shard_map/pallas_call | solution.py:555
  33.1 9.4 %shard_map.110 = (bf16[8,4,4,16,128]{4,3,2,1,0:T(8,128)(2,1)S(1)}, f32[48,64,128]{2,1,0:T(8,128)}) custom-call(bf16[48,64,512]{2,1,0:T(8,128)(2,1)S(1)} %copy-done.1, bf16[48,64,128]{2,1,0:T(8,128)(2,1)S(1)} %get-tuple-element.53.args_1_.args_3_.args_4_.args_5_, f32[48,64,128]{2,1,0:T(8,128)S(1)} %get-tuple-element.54.args_2_.args_6_, ...), custom_call_target="tpu_custom_call" | custom-call | flops 7247757312 | bytes 7733248 | tf_op jit(solution)/shard_map/pallas_call | solution.py:234
  42.5 0.8 copy-done.7
  43.3 7.2 %all-to-all-start.1 = ((bf16[32,4,16,128]{3,2,1,0:T(8,128)(2,1)}), bf16[32,4,16,128]{3,2,1,0:T(8,128)(2,1)S(1)}, u32[]{:S(2)}, u32[]{:S(2)}) async-start(bf16[32,4,16,128]{3,2,1,0:T(8,128)(2,1)} %bitcast.20), calls=%async_computation.1 | async-start | bytes 1048576 | tf_op jit(solution)/shard_map/all_to_all | solution.py:590
  50.6 9.4 %shard_map.111 = (bf16[8,4,2,16,128]{4,3,2,1,0:T(8,128)(2,1)}, f32[48,64,128]{2,1,0:T(8,128)}) custom-call(bf16[48,64,512]{2,1,0:T(8,128)(2,1)} %args_2_.12, bf16[48,64,512]{2,1,0:T(8,128)(2,1)} %args_2_.12, bf16[48,64,512]{2,1,0:T(8,128)(2,1)} %args_2_.12, bf16[48,64,128]{2,1,0:T(8,128)(2,1)} %copy-done.3, ...), custom_call_target="tpu_custom_call", output_to_operand_aliasing={{1}: (16, {})} | custom-call | flops 3623878656 | bytes 5636096 | tf_op jit(solution)/shard_map/pallas_call | solution.py:234
  60.0 5.8 %all-to-all-done.1 = bf16[32,4,16,128]{3,2,1,0:T(8,128)(2,1)S(1)} async-done(((bf16[32,4,16,128]{3,2,1,0:T(8,128)(2,1)}), bf16[32,4,16,128]{3,2,1,0:T(8,128)(2,1)S(1)}, u32[]{:S(2)}, u32[]{:S(2)}) %all-to-all-start.1) | async-done | bytes 524320 | tf_op jit(solution)/shard_map/all_to_all | solution.py:590
  65.8 3.2 %all-to-all-start = ((bf16[32,2,16,128]{3,2,1,0:T(8,128)(2,1)}), bf16[32,2,16,128]{3,2,1,0:T(8,128)(2,1)S(1)}, u32[]{:S(2)}, u32[]{:S(2)}) async-start(bf16[32,2,16,128]{3,2,1,0:T(8,128)(2,1)} %bitcast.29), calls=%async_computation | async-start | bytes 524288 | tf_op jit(solution)/shard_map/all_to_all | solution.py:590
  69.0 9.4 %shard_map.112.rest_0_ = bf16[8,1,4,6,16,128]{5,4,3,2,1,0:T(8,128)(2,1)S(1)} custom-call(bf16[8,1,4,4,16,128]{5,4,3,2,1,0:T(8,128)(2,1)S(1)} %bitcast.19, bf16[128,768]{1,0:T(8,128)(2,1)S(1)} %copy-done.16, bf16[256,128]{1,0:T(8,128)(2,1)S(1)} %copy-done.19, bf16[128,512]{1,0:T(8,128)(2,1)S(1)} %copy-done.17, bf16[512,128]{1,0:T(8,128)(2,1)S(1)} %copy-done.18), custom_call_target="tpu_custom_call" | custom-call | flops 6144000000 | bytes 1848576 | tf_op jit(solution)/shard_map/pallas_call | solution.py:446
  78.4 0.9 all-to-all-done
  79.3 4.8 %shard_map.113 = bf16[8,1,4,6,16,128]{5,4,3,2,1,0:T(8,128)(2,1)S(1)} custom-call(bf16[8,1,4,2,16,128]{5,4,3,2,1,0:T(8,128)(2,1)S(1)} %bitcast.21, bf16[128,768]{1,0:T(8,128)(2,1)S(1)} %copy-done.16, bf16[256,128]{1,0:T(8,128)(2,1)S(1)} %copy-done.19, bf16[128,512]{1,0:T(8,128)(2,1)S(1)} %copy-done.17, ...), custom_call_target="tpu_custom_call", output_to_operand_aliasing={{}: (5, {})} | custom-call | flops 3072000000 | bytes 1324288 | tf_op jit(solution)/shard_map/pallas_call | solution.py:446
  84.1 25.6 %all_to_all.15 = bf16[32,6,16,128]{3,2,1,0:T(8,128)(2,1)S(1)} all-to-all(bf16[32,6,16,128]{3,2,1,0:T(8,128)(2,1)S(1)} %bitcast.18), channel_id=1, replica_groups=mesh['gy'=8,'gx'=4] {'gy','gx'}, dimensions={0} | all-to-all | bytes 1572864 | tf_op jit(solution)/shard_map/all_to_all | solution.py:597
  109.7 1.5 %shard_map.114 = bf16[48,64,128]{2,1,0:T(8,128)(2,1)} custom-call(bf16[8,4,6,16,128]{4,3,2,1,0:T(8,128)(2,1)S(1)} %bitcast.17), custom_call_target="tpu_custom_call" | custom-call | bytes 1572864 | tf_op jit(solution)/shard_map/pallas_call | solution.py:492
  (46 shorter events, 0.8 us)
Async XLA Ops:
  0.6 1.9 %copy-start = (bf16[48,64,512]{2,1,0:T(8,128)(2,1)S(1)}, bf16[48,64,512]{2,1,0:T(8,128)(2,1)}, u32[]{:S(2)}) copy-start(bf16[48,64,512]{2,1,0:T(8,128)(2,1)} %args_2_.12) | copy-start | bytes 9437188
  2.5 1.4 %copy-start.5 = (f32[48,64,128]{2,1,0:T(8,128)S(1)}, f32[48,64,128]{2,1,0:T(8,128)}, u32[]{:S(2)}) copy-start(f32[48,64,128]{2,1,0:T(8,128)} %args_2_.11) | copy-start | bytes 4718596
  5.1 4.8 %copy-start.2 = (bf16[3,3,384,512]{3,2,1,0:T(8,128)(2,1)S(1)}, bf16[3,3,384,512]{3,2,1,0:T(8,128)(2,1)}, u32[]{:S(2)}) copy-start(bf16[3,3,384,512]{3,2,1,0:T(8,128)(2,1)} %param.12) | copy-start | bytes 10616836
  5.1 4.8 %copy-start.15 = (f32[512]{0:T(512)S(1)}, f32[512]{0:T(512)}, u32[]{:S(2)}) copy-start(f32[512]{0:T(512)} %param.13) | copy-start | bytes 6148
  5.7 15.1 %collective-permute-start = (bf16[48,2,768]{2,1,0:T(2,128)(2,1)S(1)}, bf16[48,2,768]{2,1,0:T(2,128)(2,1)S(1)}, u32[]{:S(2)}, u32[]{:S(2)}) collective-permute-start(bf16[48,2,768]{2,1,0:T(2,128)(2,1)S(1)} %get-tuple-element.49), channel_id=1, source_target_pairs={{0,1},{1,2},{2,3},{4,5},{5,6},{6,7},{8,9},{9,10},{10,11},{12,13},{... | collective-permute-start | bytes 442376 | tf_op jit(solution)/shard_map/ppermute | solution.py:521
  13.1 7.7 %collective-permute-start.1 = (bf16[48,2,768]{2,1,0:T(2,128)(2,1)S(1)}, bf16[48,2,768]{2,1,0:T(2,128)(2,1)S(1)}, u32[]{:S(2)}, u32[]{:S(2)}) collective-permute-start(bf16[48,2,768]{2,1,0:T(2,128)(2,1)S(1)} %get-tuple-element.50), channel_id=1, source_target_pairs={{1,0},{2,1},{3,2},{5,4},{6,5},{7,6},{9,8},{10,9},{11,10},{13,12},{... | collective-permute-start | bytes 442376 | tf_op jit(solution)/shard_map/ppermute | solution.py:521
  20.9 9.3 %collective-permute-start.3 = (bf16[2,68,768]{2,1,0:T(8,128)(2,1)S(1)}, bf16[2,68,768]{2,1,0:T(8,128)(2,1)S(1)}, u32[]{:S(2)}, u32[]{:S(2)}) collective-permute-start(bf16[2,68,768]{2,1,0:T(8,128)(2,1)S(1)} %pad_maximum_fusion), channel_id=1, source_target_pairs={{4,0},{8,4},{12,8},{16,12},{20,16},{24,20},{28,24},{5,1},{9,5},{13... | collective-permute-start | bytes 626696 | tf_op jit(solution)/shard_map/ppermute | solution.py:521
  23.8 6.4 %collective-permute-start.2 = (bf16[2,68,768]{2,1,0:T(8,128)(2,1)S(1)}, bf16[2,68,768]{2,1,0:T(8,128)(2,1)S(1)}, u32[]{:S(2)}, u32[]{:S(2)}) collective-permute-start(bf16[2,68,768]{2,1,0:T(8,128)(2,1)S(1)} %pad_maximum_fusion.1), channel_id=1, source_target_pairs={{0,4},{4,8},{8,12},{12,16},{16,20},{20,24},{24,28},{1,5},{5,9},{9,... | collective-permute-start | bytes 626696 | tf_op jit(solution)/shard_map/ppermute | solution.py:521
  30.1 2.3 %copy-start.3 = (bf16[48,64,128]{2,1,0:T(8,128)(2,1)}, bf16[48,64,128]{2,1,0:T(8,128)(2,1)S(1)}, u32[]{:S(2)}) copy-start(bf16[48,64,128]{2,1,0:T(8,128)(2,1)S(1)} %get-tuple-element.53.args_1_.args_3_.args_4_.args_5_) | copy-start | bytes 2359300
  30.2 2.3 %copy-start.4 = (f32[48,64,128]{2,1,0:T(8,128)}, f32[48,64,128]{2,1,0:T(8,128)S(1)}, u32[]{:S(2)}) copy-start(f32[48,64,128]{2,1,0:T(8,128)S(1)} %get-tuple-element.54.args_2_.args_6_) | copy-start | bytes 4718596
  30.2 2.3 %copy-start.8 = (bf16[2,68,768]{2,1,0:T(8,128)(2,1)}, bf16[2,68,768]{2,1,0:T(8,128)(2,1)S(1)}, u32[]{:S(2)}) copy-start(bf16[2,68,768]{2,1,0:T(8,128)(2,1)S(1)} %collective-permute-done.3.below.args_11_.args_15_) | copy-start | bytes 626692
  30.2 2.3 %copy-start.9 = (bf16[2,68,768]{2,1,0:T(8,128)(2,1)}, bf16[2,68,768]{2,1,0:T(8,128)(2,1)S(1)}, u32[]{:S(2)}) copy-start(bf16[2,68,768]{2,1,0:T(8,128)(2,1)S(1)} %collective-permute-done.2.above.args_10_.args_14_) | copy-start | bytes 626692
  30.2 2.9 %copy-start.1 = (bf16[48,64,512]{2,1,0:T(8,128)(2,1)S(1)}, bf16[48,64,512]{2,1,0:T(8,128)(2,1)}, u32[]{:S(2)}) copy-start(bf16[48,64,512]{2,1,0:T(8,128)(2,1)} %args_2_.12) | copy-start | bytes 9437188
  32.4 10.0 %copy-start.10 = (f32[4,64,128]{2,1,0:T(8,128)}, f32[4,64,128]{2,1,0:T(8,128)S(1)}, u32[]{:S(2)}) copy-start(f32[4,64,128]{2,1,0:T(8,128)S(1)} %get-tuple-element.61.args_7_.args_11_) | copy-start | bytes 393220
  32.4 10.0 %copy-start.11 = (f32[4,64,128]{2,1,0:T(8,128)}, f32[4,64,128]{2,1,0:T(8,128)S(1)}, u32[]{:S(2)}) copy-start(f32[4,64,128]{2,1,0:T(8,128)S(1)} %get-tuple-element.62.args_8_.args_12_) | copy-start | bytes 393220
  32.4 10.0 %copy-start.12 = (f32[4,64,128]{2,1,0:T(8,128)}, f32[4,64,128]{2,1,0:T(8,128)S(1)}, u32[]{:S(2)}) copy-start(f32[4,64,128]{2,1,0:T(8,128)S(1)} %get-tuple-element.59.args_5_.args_9_) | copy-start | bytes 393220
  32.5 10.0 %copy-start.13 = (f32[4,64,128]{2,1,0:T(8,128)}, f32[4,64,128]{2,1,0:T(8,128)S(1)}, u32[]{:S(2)}) copy-start(f32[4,64,128]{2,1,0:T(8,128)S(1)} %get-tuple-element.60.args_6_.args_10_) | copy-start | bytes 393220
  32.5 10.0 %copy-start.14 = (f32[2,64,256]{2,1,0:T(8,128)}, f32[2,64,256]{2,1,0:T(8,128)S(1)}, u32[]{:S(2)}) copy-start(f32[2,64,256]{2,1,0:T(8,128)S(1)} %get-tuple-element.63.args_9_.args_13_) | copy-start | bytes 393220
  43.3 22.5 %all-to-all-start.1 = ((bf16[32,4,16,128]{3,2,1,0:T(8,128)(2,1)}), bf16[32,4,16,128]{3,2,1,0:T(8,128)(2,1)S(1)}, u32[]{:S(2)}, u32[]{:S(2)}) async-start(bf16[32,4,16,128]{3,2,1,0:T(8,128)(2,1)} %bitcast.20), calls=%async_computation.1 | async-start | bytes 1048576 | tf_op jit(solution)/shard_map/all_to_all | solution.py:590
  50.5 18.5 %copy-start.16 = (bf16[128,768]{1,0:T(8,128)(2,1)S(1)}, bf16[128,768]{1,0:T(8,128)(2,1)}, u32[]{:S(2)}) copy-start(bf16[128,768]{1,0:T(8,128)(2,1)} %w_qkv.3) | copy-start | bytes 589828
  50.5 18.5 %copy-start.17 = (bf16[128,512]{1,0:T(8,128)(2,1)S(1)}, bf16[128,512]{1,0:T(8,128)(2,1)}, u32[]{:S(2)}) copy-start(bf16[128,512]{1,0:T(8,128)(2,1)} %w_up.3) | copy-start | bytes 393220
  50.5 18.5 %copy-start.18 = (bf16[512,128]{1,0:T(8,128)(2,1)S(1)}, bf16[512,128]{1,0:T(8,128)(2,1)}, u32[]{:S(2)}) copy-start(bf16[512,128]{1,0:T(8,128)(2,1)} %w_down.3) | copy-start | bytes 393220
  50.5 18.5 %copy-start.19 = (bf16[256,128]{1,0:T(8,128)(2,1)S(1)}, bf16[256,128]{1,0:T(8,128)(2,1)}, u32[]{:S(2)}) copy-start(bf16[256,128]{1,0:T(8,128)(2,1)} %w_out.3) | copy-start | bytes 196612
  65.8 13.5 %all-to-all-start = ((bf16[32,2,16,128]{3,2,1,0:T(8,128)(2,1)}), bf16[32,2,16,128]{3,2,1,0:T(8,128)(2,1)S(1)}, u32[]{:S(2)}, u32[]{:S(2)}) async-start(bf16[32,2,16,128]{3,2,1,0:T(8,128)(2,1)} %bitcast.29), calls=%async_computation | async-start | bytes 524288 | tf_op jit(solution)/shard_map/all_to_all | solution.py:590
  (2 other events, 1.9 us)

commit v10 on v7

--- a/solution.py
+++ b/solution.py
@@ -48,27 +48,14 @@
     return before.astype(BF), wide.astype(BF), after.astype(BF)
 
 
-def conv_kernel(start, rows, part, refs, packed, *args):
+def conv_kernel(start, rows, part, tail, refs, packed, *args):
     ref = dict(zip(refs, args))
-    spread, hid_out, cell_out = ref["spread"], ref["hid_out"], ref["cell_out"]
-    ring = "strips_hid" in ref
-    extent = spread.shape[0] - 2
+    hid_out, cell_out = ref["hid_out"], ref["cell_out"]
+    extent = ref["spread"].shape[0] - 2
     cols, width = ref["hid"].shape[1:]
-    chans = spread.shape[2] // 3
+    chans = ref["spread"].shape[2] // 3
     latent = chans - width
-    top, bot = start == 0, start + extent == rows
-
-    def row_of(name, row):
-        channels = slice(part * latent, (part + 1) * latent) if name == "frame" else slice(None)
-        if ref[name].shape[0] == rows:
-            return ref[name][row, :, channels]
-        if row == start - 1:
-            return ref[name + "_prev"][0]
-        if row == start + extent:
-            return ref[name + "_next"][0]
-        return ref[name][row - start]
-
-    loads = []
+    loads, leaving = [], []
     if "weights" in ref:
         size = ref["weights"].shape[0] // LOADS
         for place in range(LOADS):
@@ -77,112 +64,148 @@
     for load in loads:
         load.start()
 
-    def beside(row):
-        if not ring:
-            return jnp.zeros((1, chans), F32), jnp.zeros((1, chans), F32)
-        at = row + 2
-        return tuple(
-            jnp.concatenate(
-                [ref["beside"][place, at : at + 1, :], ref["strips_hid"][3 * place, at : at + 1, :]], axis=1
+    def reader(prefix, first, count):
+        def row_of(name, row):
+            array = ref[prefix + name]
+            if array.shape[0] == rows:
+                channels = slice(part * latent, (part + 1) * latent) if name == "frame" else slice(None)
+                return array[row, :, channels]
+            if prefix != "tail_" and tail and row >= tail and name != "frame":
+                return ref["late_" + name][row - tail]
+            if row == first - 1:
+                return ref[prefix + name + "_prev"][0]
+            if row == first + count:
+                return ref[prefix + name + "_next"][0]
+            return array[row - first]
+
+        return row_of
+
+    def convolve(spread, start, extent, row_of, ring, write, leave):
+        def beside(row):
+            if not ring:
+                return jnp.zeros((1, chans), F32), jnp.zeros((1, chans), F32)
+            at = row + 2
+            return tuple(
+                jnp.concatenate(
+                    [ref["beside"][place, at : at + 1, :], ref["strips_hid"][3 * place, at : at + 1, :]], axis=1
+                )
+                for place in range(2)
             )
-            for place in range(2)
-        )
-
-    def build(pos):
-        row = start + pos - 1
-        raw = None
-        if 0 <= row < rows:
-            raw = row_of("frame", row), row_of("hid", row)
-            x, h = raw[0].astype(F32), raw[1].astype(F32)
-        elif ring:
-            x, h = ref["frame_top" if row < 0 else "frame_bot"][0, :cols].astype(F32), ref["lines_hid"][3 * (row > 0)]
-        else:
-            spread[pos] = jnp.zeros(spread.shape[1:], BF)
-            return
-        low, high = beside(row)
-        if ring:
-            at = row + 2
-            place = lax.broadcasted_iota(jnp.int32, h.shape, 0)
-            h = jnp.where(place == 0, ref["strips_hid"][1, at : at + 1, :], h)
-            h = jnp.where(place == cols - 1, ref["strips_hid"][2, at : at + 1, :], h)
-            for spot, line in ((-1, 0), (0, 1), (rows - 1, 2), (rows, 3)):
-                if row == spot:
-                    h = ref["lines_hid"][line]
-        for side, (value, first) in enumerate(((x, 0), (h, latent))):
-            size = value.shape[1]
-            pieces = three_columns(value, low[:, first : first + size], high[:, first : first + size])
-            if raw is not None and (side == 0 or not ring):
-                pieces = pieces[0], raw[side], pieces[2]
-            for tap in range(3):
-                spread[pos, :, tap * chans + first : tap * chans + first + size] = pieces[tap]
-
-    def multiply(first, depth):
-        lhs = jnp.concatenate(
-            [spread[first + tap : first + tap + depth].reshape(depth * cols, 3 * chans) for tap in range(3)], axis=1
-        )
-        return jnp.dot(lhs, ref["held"][...], preferred_element_type=F32)
-
-    def activate(first, depth, gates):
-        for line in range(first, first + depth):
-            row = start + line
-            cell_prev = row_of("cell", row)
+
+        def build(pos):
+            row = start + pos - 1
+            raw = None
+            if 0 <= row < rows:
+                raw = row_of("frame", row), row_of("hid", row)
+                x, h = raw[0].astype(F32), raw[1].astype(F32)
+            elif ring:
+                x = ref["frame_top" if row < 0 else "frame_bot"][0, :cols].astype(F32)
+                h = ref["lines_hid"][3 * (row > 0)]
+            else:
+                spread[pos] = jnp.zeros(spread.shape[1:], BF)
+                return
+            low, high = beside(row)
             if ring:
                 at = row + 2
-                place = lax.broadcasted_iota(jnp.int32, cell_prev.shape, 0)
-                cell_prev = jnp.where(place == 0, ref["strips_cell"][1, at : at + 1, :], cell_prev)
-                cell_prev = jnp.where(place == cols - 1, ref["strips_cell"][2, at : at + 1, :], cell_prev)
-                if row == 0:
-                    cell_prev = ref["lines_cell"][1]
-                if row == rows - 1:
-                    cell_prev = ref["lines_cell"][2]
-            own = gates[(line - first) * cols : (line - first + 1) * cols] + ref["bias"][...]
-            new_cell, new_hidden = lstm(own, cell_prev)
-            if not packed:
-                cell_out[row] = new_cell
-                hid_out[row] = new_hidden.astype(BF)
-                continue
-            ref["cell_rows"][line] = new_cell
-            owners_x, piece_y = hid_out.shape[1:3]
-            local_m, piece_x = packed
-            for owner in range(owners_x):
-                picked = [
-                    new_hidden[(m * owners_x + owner) * piece_x : (m * owners_x + owner + 1) * piece_x]
-                    for m in range(local_m)
-                ]
-                hid_out[line // piece_y, owner, line % piece_y] = jnp.concatenate(picked, axis=0).astype(BF)
-
-        if packed:
-            done = pl.ds(first, depth)
-            leave = pltpu.make_async_copy(
-                ref["cell_rows"].at[done], cell_out.at[pl.ds(start + first, depth)], ref["left"].at[first // depth]
+                place = lax.broadcasted_iota(jnp.int32, h.shape, 0)
+                h = jnp.where(place == 0, ref["strips_hid"][1, at : at + 1, :], h)
+                h = jnp.where(place == cols - 1, ref["strips_hid"][2, at : at + 1, :], h)
+                for spot, line in ((0, 1), (rows - 1, 2)):
+                    if row == spot:
+                        h = ref["lines_hid"][line]
+            for side, (value, first) in enumerate(((x, 0), (h, latent))):
+                size = value.shape[1]
+                pieces = three_columns(value, low[:, first : first + size], high[:, first : first + size])
+                if raw is not None and (side == 0 or not ring):
+                    pieces = pieces[0], raw[side], pieces[2]
+                for tap in range(3):
+                    spread[pos, :, tap * chans + first : tap * chans + first + size] = pieces[tap]
+
+        def multiply(first, depth):
+            lhs = jnp.concatenate(
+                [spread[first + tap : first + tap + depth].reshape(depth * cols, 3 * chans) for tap in range(3)], axis=1
             )
-            leave.start()
-            leaving.append(leave)
-
-    leaving = []
-    depth = step_rows(0, extent, 12)
-    for pos in range(depth + 2):
-        build(pos)
-    for load in loads:
-        load.wait()
-    waiting = None
-    for first in range(0, extent, depth):
-        for pos in range(first + depth + 2, min(first + 2 * depth, extent) + 2):
+            return jnp.dot(lhs, ref["held"][...], preferred_element_type=F32)
+
+        def activate(first, depth, gates):
+            for line in range(first, first + depth):
+                row = start + line
+                cell_prev = row_of("cell", row)
+                if ring:
+                    at = row + 2
+                    place = lax.broadcasted_iota(jnp.int32, cell_prev.shape, 0)
+                    cell_prev = jnp.where(place == 0, ref["strips_cell"][1, at : at + 1, :], cell_prev)
+                    cell_prev = jnp.where(place == cols - 1, ref["strips_cell"][2, at : at + 1, :], cell_prev)
+                    if row == 0:
+                        cell_prev = ref["lines_cell"][1]
+                    if row == rows - 1:
+                        cell_prev = ref["lines_cell"][2]
+                own = gates[(line - first) * cols : (line - first + 1) * cols] + ref["bias"][...]
+                new_cell, new_hidden = lstm(own, cell_prev)
+                write(row, new_cell, new_hidden)
+            leave(first, depth)
+
+        depth = step_rows(0, extent, 12)
+        for pos in range(depth + 2):
             build(pos)
-        gates = multiply(first, depth)
-        if waiting:
-            activate(*waiting)
-        waiting = first, depth, gates
-    activate(*waiting)
-    for leave in leaving:
-        leave.wait()
+        while loads:
+            loads.pop().wait()
+        waiting = None
+        for first in range(0, extent, depth):
+            for pos in range(first + depth + 2, min(first + 2 * depth, extent) + 2):
+                build(pos)
+            gates = multiply(first, depth)
+            if waiting:
+                activate(*waiting)
+            waiting = first, depth, gates
+        activate(*waiting)
+
+    def keep(row, new_cell, new_hidden):
+        cell_out[row] = new_cell
+        hid_out[row] = new_hidden.astype(BF)
+
+    def keep_late(row, new_cell, new_hidden):
+        ref["late_cell"][row - tail] = new_cell
+        ref["late_hid"][row - tail] = new_hidden.astype(BF)
+
+    def send(row, new_cell, new_hidden):
+        line = row - start
+        ref["cell_rows"][line] = new_cell
+        owners_x, piece_y = hid_out.shape[1:3]
+        local_m, piece_x = packed
+        for owner in range(owners_x):
+            picked = [
+                new_hidden[(m * owners_x + owner) * piece_x : (m * owners_x + owner + 1) * piece_x]
+                for m in range(local_m)
+            ]
+            hid_out[line // piece_y, owner, line % piece_y] = jnp.concatenate(picked, axis=0).astype(BF)
+
+    def leave(first, depth):
+        copy = pltpu.make_async_copy(
+            ref["cell_rows"].at[pl.ds(first, depth)], cell_out.at[pl.ds(start + first, depth)],
+            ref["left"].at[first // depth],
+        )
+        copy.start()
+        leaving.append(copy)
+
+    def stay(first, depth):
+        pass
+
+    if not packed:
+        convolve(ref["spread"], start, extent, reader("", start, extent), False, keep, stay)
+        return
+    if tail:
+        convolve(ref["late_spread"], tail, rows - tail, reader("tail_", tail, rows - tail), False, keep_late, stay)
+    convolve(ref["spread"], start, extent, reader("", start, extent), True, send, leave)
+    for copy in leaving:
+        copy.wait()
 
 
 def whole(array):
     return pl.BlockSpec(array.shape, lambda *step: (0,) * array.ndim)
 
 
-def conv_step(frames, part, hid, cell, ring, weights, bias, rows_of, names, out_shapes, out_specs, packed, carry, load):
+def conv_step(frames, part, hid, cell, ring, weights, bias, rows_of, names, out_shapes, out_specs, packed, carry, late):
     rows, cols, width = hid.shape
     latent = weights.shape[0] // 9 - width
     start, extent = rows_of
@@ -190,22 +213,28 @@
     def rowed(size, channels, channel, row):
         return pl.BlockSpec((size, cols, channels), lambda step: (row // size, 0, channel))
 
-    before, after = max(start - 1, 0), min(start + extent, rows - 1)
+    def windows(prefix, hid, cell, channel, start, extent):
+        before, after = max(start - 1, 0), min(start + extent, rows - 1)
+        return {
+            prefix + "frame": (frames, rowed(extent, latent, channel, start)),
+            prefix + "frame_prev": (frames, rowed(1, latent, channel, before)),
+            prefix + "frame_next": (frames, rowed(1, latent, channel, after)),
+            prefix + "hid": (hid, rowed(extent, width, 0, start)),
+            prefix + "hid_prev": (hid, rowed(1, width, 0, before)),
+            prefix + "hid_next": (hid, rowed(1, width, 0, after)),
+            prefix + "cell": (cell, rowed(extent, width, 0, start)),
+        }
+
     near = pl.BlockSpec(memory_space=pltpu.VMEM)
-    if load:
-        inputs = {
-            "frame": (frames, rowed(extent, latent, part, start)),
-            "frame_prev": (frames, rowed(1, latent, part, before)),
-            "frame_next": (frames, rowed(1, latent, part, after)),
-            "hid": (hid, rowed(extent, width, 0, start)),
-            "hid_prev": (hid, rowed(1, width, 0, before)),
-            "hid_next": (hid, rowed(1, width, 0, after)),
-            "cell": (cell, rowed(extent, width, 0, start)),
-        }
+    tail = 0
+    if late:
+        tail, *first = late
+        inputs = windows("", hid, cell, part, start, extent)
+        inputs |= windows("tail_", *first, 0, tail, rows - tail)
     else:
         inputs = {"frame": (frames, near), "hid": (hid, near), "cell": (cell, near)}
     inputs["bias"] = bias, whole(bias)
-    if load:
+    if late:
         inputs["weights"] = weights, pl.BlockSpec(memory_space=pl.ANY)
     else:
         inputs["held"] = weights, near
@@ -217,22 +246,28 @@
             inputs[f"carry{place}"] = (array, pl.BlockSpec(memory_space=pl.ANY) if packed else near)
     refs = [*inputs, *names, "spread"]
     scratch = [pltpu.VMEM((extent + 2, cols, 3 * (latent + width)), BF)]
-    if load:
-        refs += ["held", "sem"]
-        scratch += [pltpu.VMEM(weights.shape, BF), pltpu.SemaphoreType.DMA((LOADS,))]
+    if late:
+        refs += ["held", "sem", "late_spread", "late_hid", "late_cell"]
+        scratch += [
+            pltpu.VMEM(weights.shape, BF),
+            pltpu.SemaphoreType.DMA((LOADS,)),
+            pltpu.VMEM((rows - tail + 2, cols, 3 * (latent + width)), BF),
+            pltpu.VMEM((rows - tail, cols, width), BF),
+            pltpu.VMEM((rows - tail, cols, width), F32),
+        ]
     if packed:
         refs += ["cell_rows", "left"]
         scratch += [pltpu.VMEM((extent, cols, width), F32), pltpu.SemaphoreType.DMA((extent,))]
     cells = extent * cols
     return pl.pallas_call(
-        functools.partial(conv_kernel, start, rows, part, refs, packed),
+        functools.partial(conv_kernel, start, rows, part, tail, refs, packed),
         grid=(1,),
         in_specs=[spec for _, spec in inputs.values()],
         out_specs=out_specs,
         out_shape=out_shapes,
         scratch_shapes=scratch,
         input_output_aliases=aliases,
-        compiler_params=pltpu.CompilerParams(vmem_limit_bytes=VMEM_ALL if load else VMEM_LIMIT),
+        compiler_params=pltpu.CompilerParams(vmem_limit_bytes=VMEM_ALL if late else VMEM_LIMIT),
         cost_estimate=pl.CostEstimate(
             flops=2 * cells * weights.size, bytes_accessed=2 * weights.size + cells * 2048, transcendentals=cells * width * 5
         ),
@@ -519,16 +554,21 @@
     to_down = jnp.concatenate([line_bot, from_left[-2:], from_right[-2:]], axis=1)
     to_up = jnp.concatenate([line_top, from_left[:2], from_right[:2]], axis=1)
 
+    pieces = rows // devices_y
+    piece_cols = local_m * piece_x
+    shares = (pieces - pieces // 3, pieces // 3)
+    ahead = rows - max(size for size in range(1, 13) if rows % size == 0 and rows - size > shares[0] * devices_y)
     tile_shapes = (jax.ShapeDtypeStruct((rows, cols, width), BF), jax.ShapeDtypeStruct((rows, cols, width), F32))
     carry = ()
-    for start, extent in ((0, rows // 2), (rows // 2, rows - rows // 2)):
+    half = -(-ahead // 8) * 4
+    for start, extent in ((0, half), (half, ahead - half)):
         spec = pl.BlockSpec(memory_space=pltpu.VMEM)
         if carry:
             *carry, to_down, to_up = lax.optimization_barrier((*carry, to_down, to_up))
             from_up, from_down = shifted(to_down, "gy", 1), shifted(to_up, "gy", -1)
         carry = conv_step(
             frames, 0, hidden_state, cell_state, {}, weights, bias, (start, extent), ("hid_out", "cell_out"),
-            tile_shapes, (spec, spec), None, carry, False,
+            tile_shapes, (spec, spec), None, carry, None,
         )
     hidden_one, cell_one = carry
 
@@ -559,9 +599,6 @@
     ring["frame_top"] = from_up, pl.BlockSpec(line, lambda step: (1, 0, second))
     ring["frame_bot"] = from_down, pl.BlockSpec(line, lambda step: (0, 0, second))
 
-    pieces = rows // devices_y
-    piece_cols = local_m * piece_x
-    shares = (pieces - pieces // 3, pieces // 3)
     moved, start, carry = [], 0, ()
     for piece_y in shares:
         extent = piece_y * devices_y
@@ -570,7 +607,7 @@
         sent, cell_out = conv_step(
             frames, 1, hidden_one, cell_one, ring, weights, bias, (start, extent),
             ("hid_out", "cell_out"), (sent_shape, tile_shapes[1]), (whole(sent_shape), spec), (local_m, piece_x), carry,
-            bool(carry),
+            (ahead, hidden_state, cell_state) if carry else None,
         )
         carry = (None, cell_out)
         sent = sent.reshape(devices_y * devices_x, piece_y, piece_cols, width)

time: 111 us -> 109 us (0.982)
  waiting for transfers between devices: 6.74 us -> 4.31 us
    all_to_all x2, waiting for transfers between devices: 6.73 us -> 3.4 us  [body(): lax.all_to_all(sent, ('gy', 'gx'), split_axis=0, concat_axis=0, tiled=True)]
  transfers between devices with their start and end apart: 6 -> 6, of which waited for: 2 -> 3; matrix products, arithmetic and copies ran while one was open for 0% -> 0% of each run, Pallas kernels for 28% -> 29%
where the time goes in v10:
time: 109 us; the launch traced here: 108 us
  Pallas kernels  49.8 us (46%)
  blocking collectives  25.6 us (23%)
  starting transfers between devices  21.8 us (20%)
  local copies, waits for them, and re-layouts  5.35 us (5%)
  waiting for transfers between devices  4.31 us (4%)
    pallas_call x4, Pallas kernels, conv_step(): pl.pallas_call(functools.partial(conv_kernel, start, rows, part, tail, re...  31.3 us
    all_to_all x1, blocking collectives, body(): lax.all_to_all(done, ('gy', 'gx'), split_axis=0, concat_axis=0, tiled=True)  25.6 us
    pallas_call x2, Pallas kernels, block_step(): pl.pallas_call(block_kernel, grid=(lanes, piece_y), in_specs=in_specs, ou...  14.2 us
    ppermute x4, starting transfers between devices, shifted(): return lax.ppermute(value, axis, pairs)  12.2 us
    all_to_all x2, starting transfers between devices, body(): lax.all_to_all(sent, ('gy', 'gx'), split_axis=0, concat_axis=0, tiled=True)  9.63 us
    unnamed x40, local copies, waits for them, and re-layouts  5.29 us
    all_to_all x2, waiting for transfers between devices, body(): lax.all_to_all(sent, ('gy', 'gx'), split_axis=0, concat_axis=0, tiled=True)  3.4 us
    pallas_call x1, Pallas kernels, body(): pl.pallas_call(ring_kernel, grid=(1,), in_specs=[*(whole(array) for array...  2.21 us
  transfers between devices with their start and end apart: 6, of which 3 were waited for; matrix products, arithmetic and copies ran while one was open for 0% of the time, Pallas kernels for 29%

profile of v10, /device:TPU:1, one launch (start us, length us, event | category | flops | bytes accessed | tf_op | source)
XLA Modules:
  0.0 108.0 jit_solution(2846875633271457279)
XLA Ops:
  0.6 0.0 copy-start
  0.6 1.9 %copy-done = bf16[48,64,512]{2,1,0:T(8,128)(2,1)S(1)} copy-done((bf16[48,64,512]{2,1,0:T(8,128)(2,1)S(1)}, bf16[48,64,512]{2,1,0:T(8,128)(2,1)}, u32[]{:S(2)}) %copy-start) | copy-done | bytes 3145752
  2.5 1.1 %copy-done.2 = bf16[48,64,128]{2,1,0:T(8,128)(2,1)S(1)} copy-done((bf16[48,64,128]{2,1,0:T(8,128)(2,1)S(1)}, bf16[48,64,128]{2,1,0:T(8,128)(2,1)}, u32[]{:S(2)}) %copy-start.2) | copy-done | bytes 786456
  3.7 1.4 %copy-done.4 = f32[48,64,128]{2,1,0:T(8,128)S(1)} copy-done((f32[48,64,128]{2,1,0:T(8,128)S(1)}, f32[48,64,128]{2,1,0:T(8,128)}, u32[]{:S(2)}) %copy-start.4) | copy-done | bytes 1572888
  5.1 0.6 shard_map.105
  5.7 4.2 %collective-permute-start = (bf16[48,2,768]{2,1,0:T(2,128)(2,1)S(1)}, bf16[48,2,768]{2,1,0:T(2,128)(2,1)S(1)}, u32[]{:S(2)}, u32[]{:S(2)}) collective-permute-start(bf16[48,2,768]{2,1,0:T(2,128)(2,1)S(1)} %get-tuple-element.28), channel_id=1, source_target_pairs={{0,1},{1,2},{2,3},{4,5},{5,6},{6,7},{8,9},{9,10},{10,11},{12,13},{... | collective-permute-start | bytes 442376 | tf_op jit(solution)/shard_map/ppermute | solution.py:549
  9.9 1.3 %collective-permute-start.1 = (bf16[48,2,768]{2,1,0:T(2,128)(2,1)S(1)}, bf16[48,2,768]{2,1,0:T(2,128)(2,1)S(1)}, u32[]{:S(2)}, u32[]{:S(2)}) collective-permute-start(bf16[48,2,768]{2,1,0:T(2,128)(2,1)S(1)} %get-tuple-element.29), channel_id=1, source_target_pairs={{1,0},{2,1},{3,2},{5,4},{6,5},{7,6},{9,8},{10,9},{11,10},{13,12},{... | collective-permute-start | bytes 442376 | tf_op jit(solution)/shard_map/ppermute | solution.py:549
  11.2 5.2 %shard_map.104 = (bf16[48,64,128]{2,1,0:T(8,128)(2,1)S(1)}, f32[48,64,128]{2,1,0:T(8,128)S(1)}) custom-call(bf16[48,64,512]{2,1,0:T(8,128)(2,1)S(1)} %copy-done, bf16[48,64,128]{2,1,0:T(8,128)(2,1)S(1)} %copy-done.2, f32[48,64,128]{2,1,0:T(8,128)S(1)} %copy-done.4, f32[1,512]{1,0:T(1,128)S(1)} %bitcast.21, bf16[3456,512]{1,0:T(8,128)(2,1)S(1)} %bitcast.11), custom_call_target="tpu_custom_call" | custom-call | flops 4529848320 | bytes 6160384 | tf_op jit(solution)/shard_map/pallas_call | solution.py:262
  16.5 4.6 %collective-permute-start.2 = (bf16[2,68,768]{2,1,0:T(8,128)(2,1)S(1)}, bf16[2,68,768]{2,1,0:T(8,128)(2,1)S(1)}, u32[]{:S(2)}, u32[]{:S(2)}) collective-permute-start(bf16[2,68,768]{2,1,0:T(8,128)(2,1)S(1)} %get-tuple-element.35), channel_id=1, source_target_pairs={{0,4},{4,8},{8,12},{12,16},{16,20},{20,24},{24,28},{1,5},{5,9},{9,... | collective-permute-start | bytes 626696 | tf_op jit(solution)/shard_map/ppermute | solution.py:549
  21.2 2.1 %collective-permute-start.3 = (bf16[2,68,768]{2,1,0:T(8,128)(2,1)S(1)}, bf16[2,68,768]{2,1,0:T(8,128)(2,1)S(1)}, u32[]{:S(2)}, u32[]{:S(2)}) collective-permute-start(bf16[2,68,768]{2,1,0:T(8,128)(2,1)S(1)} %get-tuple-element.36), channel_id=1, source_target_pairs={{4,0},{8,4},{12,8},{16,12},{20,16},{24,20},{28,24},{5,1},{9,5},{13... | collective-permute-start | bytes 626696 | tf_op jit(solution)/shard_map/ppermute | solution.py:549
  23.3 4.2 %shard_map.106 = (bf16[48,64,128]{2,1,0:T(8,128)(2,1)S(1)}, f32[48,64,128]{2,1,0:T(8,128)S(1)}) custom-call(bf16[48,64,512]{2,1,0:T(8,128)(2,1)S(1)} %copy-done, bf16[48,64,128]{2,1,0:T(8,128)(2,1)S(1)} %copy-done.2, f32[48,64,128]{2,1,0:T(8,128)S(1)} %copy-done.4, f32[1,512]{1,0:T(1,128)S(1)} %bitcast.22, ...), custom_call_target="tpu_custom_call", output_to_operand_aliasing={{0}: (5, {}), {1}: (6, {})} | custom-call | flops 3623878656 | bytes 5636096 | tf_op jit(solution)/shard_map/pallas_call | solution.py:262
  27.5 0.9 collective-permute-done.3.below.args_11_.args_22_
  28.4 2.2 %shard_map.107 = (f32[4,64,128]{2,1,0:T(8,128)S(1)}, f32[4,64,128]{2,1,0:T(8,128)S(1)}, f32[4,64,128]{2,1,0:T(8,128)S(1)}, f32[4,64,128]{2,1,0:T(8,128)S(1)}, f32[2,64,256]{2,1,0:T(8,128)S(1)}) custom-call(bf16[2,68,768]{2,1,0:T(8,128)(2,1)S(1)} %collective-permute-done.2.above.args_10_.args_21_, ...), custom_call_target="tpu_custom_call" | custom-call | flops 1811939328 | bytes 3538944 | tf_op jit(solution)/shard_map/pallas_call | solution.py:582
  30.7 9.3 %shard_map.108 = (bf16[8,4,4,16,128]{4,3,2,1,0:T(8,128)(2,1)S(1)}, f32[48,64,128]{2,1,0:T(8,128)}) custom-call(bf16[48,64,512]{2,1,0:T(8,128)(2,1)S(1)} %copy-done.1, bf16[48,64,128]{2,1,0:T(8,128)(2,1)S(1)} %get-tuple-element.33.args_1_.args_3_.args_4_.args_5_, f32[48,64,128]{2,1,0:T(8,128)S(1)} %get-tuple-element.34.args_2_.args_6_, ...), custom_call_target="tpu_custom_call" | custom-call | flops 7247757312 | bytes 7733248 | tf_op jit(solution)/shard_map/pallas_call | solution.py:262
  40.1 0.8 copy-done.7
  40.9 6.3 %all-to-all-start.1 = ((bf16[32,4,16,128]{3,2,1,0:T(8,128)(2,1)}), bf16[32,4,16,128]{3,2,1,0:T(8,128)(2,1)S(1)}, u32[]{:S(2)}, u32[]{:S(2)}) async-start(bf16[32,4,16,128]{3,2,1,0:T(8,128)(2,1)} %bitcast.18), calls=%async_computation.1 | async-start | bytes 1048576 | tf_op jit(solution)/shard_map/all_to_all | solution.py:614
  47.2 12.7 %shard_map.109 = (bf16[8,4,2,16,128]{4,3,2,1,0:T(8,128)(2,1)}, f32[48,64,128]{2,1,0:T(8,128)}) custom-call(bf16[48,64,512]{2,1,0:T(8,128)(2,1)} %args_9_.1, bf16[48,64,512]{2,1,0:T(8,128)(2,1)} %args_9_.1, bf16[48,64,512]{2,1,0:T(8,128)(2,1)} %args_9_.1, bf16[48,64,128]{2,1,0:T(8,128)(2,1)} %copy-done.3, ...), custom_call_target="tpu_custom_call", output_to_operand_aliasing={{1}: (23, {})} | custom-call | flops 3623878656 | bytes 5636096 | tf_op jit(solution)/shard_map/pallas_call | solution.py:262
  59.9 2.5 %all-to-all-done.1 = bf16[32,4,16,128]{3,2,1,0:T(8,128)(2,1)S(1)} async-done(((bf16[32,4,16,128]{3,2,1,0:T(8,128)(2,1)}), bf16[32,4,16,128]{3,2,1,0:T(8,128)(2,1)S(1)}, u32[]{:S(2)}, u32[]{:S(2)}) %all-to-all-start.1) | async-done | bytes 524320 | tf_op jit(solution)/shard_map/all_to_all | solution.py:614
  62.5 3.3 %all-to-all-start = ((bf16[32,2,16,128]{3,2,1,0:T(8,128)(2,1)}), bf16[32,2,16,128]{3,2,1,0:T(8,128)(2,1)S(1)}, u32[]{:S(2)}, u32[]{:S(2)}) async-start(bf16[32,2,16,128]{3,2,1,0:T(8,128)(2,1)} %bitcast.25), calls=%async_computation | async-start | bytes 524288 | tf_op jit(solution)/shard_map/all_to_all | solution.py:614
  65.8 9.4 %shard_map.110.rest_0_ = bf16[8,1,4,6,16,128]{5,4,3,2,1,0:T(8,128)(2,1)S(1)} custom-call(bf16[8,1,4,4,16,128]{5,4,3,2,1,0:T(8,128)(2,1)S(1)} %bitcast.17, bf16[128,768]{1,0:T(8,128)(2,1)S(1)} %copy-done.16, bf16[256,128]{1,0:T(8,128)(2,1)S(1)} %copy-done.19, bf16[128,512]{1,0:T(8,128)(2,1)S(1)} %copy-done.17, bf16[512,128]{1,0:T(8,128)(2,1)S(1)} %copy-done.18), custom_call_target="tpu_custom_call" | custom-call | flops 6144000000 | bytes 1848576 | tf_op jit(solution)/shard_map/pallas_call | solution.py:474
  75.3 0.9 all-to-all-done
  76.1 4.8 %shard_map.111 = bf16[8,1,4,6,16,128]{5,4,3,2,1,0:T(8,128)(2,1)S(1)} custom-call(bf16[8,1,4,2,16,128]{5,4,3,2,1,0:T(8,128)(2,1)S(1)} %bitcast.19, bf16[128,768]{1,0:T(8,128)(2,1)S(1)} %copy-done.16, bf16[256,128]{1,0:T(8,128)(2,1)S(1)} %copy-done.19, bf16[128,512]{1,0:T(8,128)(2,1)S(1)} %copy-done.17, ...), custom_call_target="tpu_custom_call", output_to_operand_aliasing={{}: (5, {})} | custom-call | flops 3072000000 | bytes 1324288 | tf_op jit(solution)/shard_map/pallas_call | solution.py:474
  80.9 25.6 %all_to_all.15 = bf16[32,6,16,128]{3,2,1,0:T(8,128)(2,1)S(1)} all-to-all(bf16[32,6,16,128]{3,2,1,0:T(8,128)(2,1)S(1)} %bitcast.16), channel_id=1, replica_groups=mesh['gy'=8,'gx'=4] {'gy','gx'}, dimensions={0} | all-to-all | bytes 1572864 | tf_op jit(solution)/shard_map/all_to_all | solution.py:621
  106.5 1.5 %shard_map.112 = bf16[48,64,128]{2,1,0:T(8,128)(2,1)} custom-call(bf16[8,4,6,16,128]{4,3,2,1,0:T(8,128)(2,1)S(1)} %bitcast.15), custom_call_target="tpu_custom_call" | custom-call | bytes 1572864 | tf_op jit(solution)/shard_map/pallas_call | solution.py:520
  (43 shorter events, 0.2 us)
Async XLA Ops:
  0.6 1.9 %copy-start = (bf16[48,64,512]{2,1,0:T(8,128)(2,1)S(1)}, bf16[48,64,512]{2,1,0:T(8,128)(2,1)}, u32[]{:S(2)}) copy-start(bf16[48,64,512]{2,1,0:T(8,128)(2,1)} %args_9_.1) | copy-start | bytes 9437188
  3.7 1.4 %copy-start.4 = (f32[48,64,128]{2,1,0:T(8,128)S(1)}, f32[48,64,128]{2,1,0:T(8,128)}, u32[]{:S(2)}) copy-start(f32[48,64,128]{2,1,0:T(8,128)} %args_13_.1) | copy-start | bytes 4718596
  5.1 6.1 %copy-start.5 = (bf16[3,3,384,512]{3,2,1,0:T(8,128)(2,1)S(1)}, bf16[3,3,384,512]{3,2,1,0:T(8,128)(2,1)}, u32[]{:S(2)}) copy-start(bf16[3,3,384,512]{3,2,1,0:T(8,128)(2,1)} %param.12) | copy-start | bytes 10616836
  5.1 6.1 %copy-start.15 = (f32[512]{0:T(512)S(1)}, f32[512]{0:T(512)}, u32[]{:S(2)}) copy-start(f32[512]{0:T(512)} %param.13) | copy-start | bytes 6148
  5.7 10.7 %collective-permute-start = (bf16[48,2,768]{2,1,0:T(2,128)(2,1)S(1)}, bf16[48,2,768]{2,1,0:T(2,128)(2,1)S(1)}, u32[]{:S(2)}, u32[]{:S(2)}) collective-permute-start(bf16[48,2,768]{2,1,0:T(2,128)(2,1)S(1)} %get-tuple-element.28), channel_id=1, source_target_pairs={{0,1},{1,2},{2,3},{4,5},{5,6},{6,7},{8,9},{9,10},{10,11},{12,13},{... | collective-permute-start | bytes 442376 | tf_op jit(solution)/shard_map/ppermute | solution.py:549
  9.9 6.5 %collective-permute-start.1 = (bf16[48,2,768]{2,1,0:T(2,128)(2,1)S(1)}, bf16[48,2,768]{2,1,0:T(2,128)(2,1)S(1)}, u32[]{:S(2)}, u32[]{:S(2)}) collective-permute-start(bf16[48,2,768]{2,1,0:T(2,128)(2,1)S(1)} %get-tuple-element.29), channel_id=1, source_target_pairs={{1,0},{2,1},{3,2},{5,4},{6,5},{7,6},{9,8},{10,9},{11,10},{13,12},{... | collective-permute-start | bytes 442376 | tf_op jit(solution)/shard_map/ppermute | solution.py:549
  16.5 11.0 %collective-permute-start.2 = (bf16[2,68,768]{2,1,0:T(8,128)(2,1)S(1)}, bf16[2,68,768]{2,1,0:T(8,128)(2,1)S(1)}, u32[]{:S(2)}, u32[]{:S(2)}) collective-permute-start(bf16[2,68,768]{2,1,0:T(8,128)(2,1)S(1)} %get-tuple-element.35), channel_id=1, source_target_pairs={{0,4},{4,8},{8,12},{12,16},{16,20},{20,24},{24,28},{1,5},{5,9},{9,... | collective-permute-start | bytes 626696 | tf_op jit(solution)/shard_map/ppermute | solution.py:549
  21.2 7.3 %collective-permute-start.3 = (bf16[2,68,768]{2,1,0:T(8,128)(2,1)S(1)}, bf16[2,68,768]{2,1,0:T(8,128)(2,1)S(1)}, u32[]{:S(2)}, u32[]{:S(2)}) collective-permute-start(bf16[2,68,768]{2,1,0:T(8,128)(2,1)S(1)} %get-tuple-element.36), channel_id=1, source_target_pairs={{4,0},{8,4},{12,8},{16,12},{20,16},{24,20},{28,24},{5,1},{9,5},{13... | collective-permute-start | bytes 626696 | tf_op jit(solution)/shard_map/ppermute | solution.py:549
  27.5 3.2 %copy-start.3 = (bf16[48,64,128]{2,1,0:T(8,128)(2,1)}, bf16[48,64,128]{2,1,0:T(8,128)(2,1)S(1)}, u32[]{:S(2)}) copy-start(bf16[48,64,128]{2,1,0:T(8,128)(2,1)S(1)} %get-tuple-element.33.args_1_.args_3_.args_4_.args_5_) | copy-start | bytes 2359300
  27.5 3.2 %copy-start.6 = (f32[48,64,128]{2,1,0:T(8,128)}, f32[48,64,128]{2,1,0:T(8,128)S(1)}, u32[]{:S(2)}) copy-start(f32[48,64,128]{2,1,0:T(8,128)S(1)} %get-tuple-element.34.args_2_.args_6_) | copy-start | bytes 4718596
  27.5 3.2 %copy-start.8 = (bf16[2,68,768]{2,1,0:T(8,128)(2,1)}, bf16[2,68,768]{2,1,0:T(8,128)(2,1)S(1)}, u32[]{:S(2)}) copy-start(bf16[2,68,768]{2,1,0:T(8,128)(2,1)S(1)} %collective-permute-done.2.above.args_10_.args_21_) | copy-start | bytes 626692
  28.4 2.3 %copy-start.9 = (bf16[2,68,768]{2,1,0:T(8,128)(2,1)}, bf16[2,68,768]{2,1,0:T(8,128)(2,1)S(1)}, u32[]{:S(2)}) copy-start(bf16[2,68,768]{2,1,0:T(8,128)(2,1)S(1)} %collective-permute-done.3.below.args_11_.args_22_) | copy-start | bytes 626692
  28.4 2.3 %copy-start.1 = (bf16[48,64,512]{2,1,0:T(8,128)(2,1)S(1)}, bf16[48,64,512]{2,1,0:T(8,128)(2,1)}, u32[]{:S(2)}) copy-start(bf16[48,64,512]{2,1,0:T(8,128)(2,1)} %args_9_.1) | copy-start | bytes 9437188
  30.6 9.4 %copy-start.10 = (f32[4,64,128]{2,1,0:T(8,128)}, f32[4,64,128]{2,1,0:T(8,128)S(1)}, u32[]{:S(2)}) copy-start(f32[4,64,128]{2,1,0:T(8,128)S(1)} %get-tuple-element.41.args_7_.args_18_) | copy-start | bytes 393220
  30.7 9.4 %copy-start.11 = (f32[4,64,128]{2,1,0:T(8,128)}, f32[4,64,128]{2,1,0:T(8,128)S(1)}, u32[]{:S(2)}) copy-start(f32[4,64,128]{2,1,0:T(8,128)S(1)} %get-tuple-element.42.args_8_.args_19_) | copy-start | bytes 393220
  30.7 9.4 %copy-start.12 = (f32[4,64,128]{2,1,0:T(8,128)}, f32[4,64,128]{2,1,0:T(8,128)S(1)}, u32[]{:S(2)}) copy-start(f32[4,64,128]{2,1,0:T(8,128)S(1)} %get-tuple-element.39.args_5_.args_16_) | copy-start | bytes 393220
  30.7 9.4 %copy-start.13 = (f32[4,64,128]{2,1,0:T(8,128)}, f32[4,64,128]{2,1,0:T(8,128)S(1)}, u32[]{:S(2)}) copy-start(f32[4,64,128]{2,1,0:T(8,128)S(1)} %get-tuple-element.40.args_6_.args_17_) | copy-start | bytes 393220
  30.7 9.4 %copy-start.14 = (f32[2,64,256]{2,1,0:T(8,128)}, f32[2,64,256]{2,1,0:T(8,128)S(1)}, u32[]{:S(2)}) copy-start(f32[2,64,256]{2,1,0:T(8,128)S(1)} %get-tuple-element.43.args_9_.args_20_) | copy-start | bytes 393220
  40.9 21.6 %all-to-all-start.1 = ((bf16[32,4,16,128]{3,2,1,0:T(8,128)(2,1)}), bf16[32,4,16,128]{3,2,1,0:T(8,128)(2,1)S(1)}, u32[]{:S(2)}, u32[]{:S(2)}) async-start(bf16[32,4,16,128]{3,2,1,0:T(8,128)(2,1)} %bitcast.18), calls=%async_computation.1 | async-start | bytes 1048576 | tf_op jit(solution)/shard_map/all_to_all | solution.py:614
  47.2 18.6 %copy-start.16 = (bf16[128,768]{1,0:T(8,128)(2,1)S(1)}, bf16[128,768]{1,0:T(8,128)(2,1)}, u32[]{:S(2)}) copy-start(bf16[128,768]{1,0:T(8,128)(2,1)} %w_qkv.3) | copy-start | bytes 589828
  47.2 18.6 %copy-start.17 = (bf16[128,512]{1,0:T(8,128)(2,1)S(1)}, bf16[128,512]{1,0:T(8,128)(2,1)}, u32[]{:S(2)}) copy-start(bf16[128,512]{1,0:T(8,128)(2,1)} %w_up.3) | copy-start | bytes 393220
  47.2 18.6 %copy-start.18 = (bf16[512,128]{1,0:T(8,128)(2,1)S(1)}, bf16[512,128]{1,0:T(8,128)(2,1)}, u32[]{:S(2)}) copy-start(bf16[512,128]{1,0:T(8,128)(2,1)} %w_down.3) | copy-start | bytes 393220
  47.2 18.6 %copy-start.19 = (bf16[256,128]{1,0:T(8,128)(2,1)S(1)}, bf16[256,128]{1,0:T(8,128)(2,1)}, u32[]{:S(2)}) copy-start(bf16[256,128]{1,0:T(8,128)(2,1)} %w_out.3) | copy-start | bytes 196612
  62.5 13.7 %all-to-all-start = ((bf16[32,2,16,128]{3,2,1,0:T(8,128)(2,1)}), bf16[32,2,16,128]{3,2,1,0:T(8,128)(2,1)S(1)}, u32[]{:S(2)}, u32[]{:S(2)}) async-start(bf16[32,2,16,128]{3,2,1,0:T(8,128)(2,1)} %bitcast.25), calls=%async_computation | async-start | bytes 524288 | tf_op jit(solution)/shard_map/all_to_all | solution.py:614
  (2 other events, 1.9 us)

commit v11 on v10

--- a/solution.py
+++ b/solution.py
@@ -407,54 +407,76 @@
         fill(ones, group, group, 0)
         keys_t[...] = w_qkv[:, embed : 2 * embed].astype(F32).T.astype(BF)
 
-    flat[...] = x[...].astype(F32).reshape(flat.shape)
-    groups = flat.shape[0] // group
-    cells = jnp.concatenate([flat[pl.ds(g, group, stride=groups), :] for g in range(groups)], axis=0)
-    normed = layer_norm(cells).astype(BF)
-    queries = jnp.dot(normed, w_qkv[:, :embed], preferred_element_type=F32).astype(BF)
-    values = jnp.dot(normed, w_qkv[:, 2 * embed :], preferred_element_type=F32).astype(BF)
-    keys = lax.dot_general(keys_t[...], normed, (((1,), (1,)), ((), ())), preferred_element_type=F32)
-    side = lax.broadcasted_iota(jnp.int32, (embed, 2 * group), 1) < group
-    raised = [[], []]
-    for pair in range(groups // 2):
-        both = keys[:, pair * 2 * group : (pair + 1) * 2 * group]
-        turned = pltpu.roll(both, group, axis=1)
-        for place, twice in enumerate((jnp.where(side, both, turned), jnp.where(side, turned, both))):
-            twice = twice.astype(BF)
-            start = (2 * pair + place) * group
-            for half in range(2):
-                part = twice[half * tile : (half + 1) * tile]
-                spread = jnp.concatenate([part * own_low[...], part * own_high[...]], axis=1)
-                scores = jnp.dot(
-                    queries[start : start + group, half * tile : (half + 1) * tile], spread, preferred_element_type=F32
+    def work(sub):
+        flat[sub] = x[:, :, sub].astype(F32).reshape(flat.shape[1:])
+        groups = flat.shape[1] // group
+        cells = jnp.concatenate([flat[sub, pl.ds(g, group, stride=groups), :] for g in range(groups)], axis=0)
+        normed = layer_norm(cells).astype(BF)
+        yield
+        queries = jnp.dot(normed, w_qkv[:, :embed], preferred_element_type=F32).astype(BF)
+        values = jnp.dot(normed, w_qkv[:, 2 * embed :], preferred_element_type=F32).astype(BF)
+        keys = lax.dot_general(keys_t[...], normed, (((1,), (1,)), ((), ())), preferred_element_type=F32)
+        yield
+        side = lax.broadcasted_iota(jnp.int32, (embed, 2 * group), 1) < group
+        raised = [[], []]
+        for pair in range(groups // 2):
+            both = keys[:, pair * 2 * group : (pair + 1) * 2 * group]
+            turned = pltpu.roll(both, group, axis=1)
+            for place, twice in enumerate((jnp.where(side, both, turned), jnp.where(side, turned, both))):
+                twice = twice.astype(BF)
+                start = (2 * pair + place) * group
+                for half in range(2):
+                    part = twice[half * tile : (half + 1) * tile]
+                    spread = jnp.concatenate([part * own_low[...], part * own_high[...]], axis=1)
+                    scores = jnp.dot(
+                        queries[start : start + group, half * tile : (half + 1) * tile],
+                        spread,
+                        preferred_element_type=F32,
+                    )
+                    raised[half].append(jnp.minimum(jnp.exp2(scores * (LOG2E * HDIM**-0.5)), BF_MAX).astype(BF))
+            if pair % 2:
+                yield
+        attn = []
+        for half in range(2):
+            part = jnp.concatenate(raised[half], axis=0)
+            total = jnp.dot(part, ones[...], preferred_element_type=F32)
+            guess = pl.reciprocal(total, approx=True)
+            attn.append((part.astype(F32) * (guess * (2.0 - total * guess))).astype(BF))
+        yield
+        heads = []
+        for half in range(2):
+            column = []
+            for g in range(groups):
+                held = values[g * group : (g + 1) * group, half * tile : (half + 1) * tile]
+                spread = jnp.concatenate([held] * (HEADS // 2), axis=0) * own_values[...]
+                column.append(
+                    jnp.dot(attn[half][g * group : (g + 1) * group], spread, preferred_element_type=F32).astype(BF)
                 )
-                raised[half].append(jnp.minimum(jnp.exp2(scores * (LOG2E * HDIM**-0.5)), BF_MAX).astype(BF))
-    heads = []
-    for half in range(2):
-        part = jnp.concatenate(raised[half], axis=0)
-        total = jnp.dot(part, ones[...], preferred_element_type=F32)
-        guess = pl.reciprocal(total, approx=True)
-        attn = (part.astype(F32) * (guess * (2.0 - total * guess))).astype(BF)
-        column = []
+            heads.append(jnp.concatenate(column, axis=0))
+        heads = jnp.concatenate(heads, axis=1)
+        yield
+        attended = jnp.dot(heads, w_out[...], preferred_element_type=F32).astype(BF)
+        mixed = cells + attended.astype(F32)
+        normed_two = layer_norm(mixed).astype(BF)
+        yield
+        up = jnp.dot(normed_two, w_up[...], preferred_element_type=F32)
+        bent = jnp.tanh(up * (0.7978845608 + (0.7978845608 * 0.044715) * (up * up)))
+        half_up = 0.5 * up
+        expanded = (half_up + half_up * bent).astype(BF)
+        yield
+        result = mixed + jnp.dot(expanded, w_down[...], preferred_element_type=F32)
         for g in range(groups):
-            held = values[g * group : (g + 1) * group, half * tile : (half + 1) * tile]
-            spread = jnp.concatenate([held] * (HEADS // 2), axis=0) * own_values[...]
-            column.append(
-                jnp.dot(attn[g * group : (g + 1) * group], spread, preferred_element_type=F32).astype(BF)
-            )
-        heads.append(jnp.concatenate(column, axis=0))
-    heads = jnp.concatenate(heads, axis=1)
-    attended = jnp.dot(heads, w_out[...], preferred_element_type=F32).astype(BF)
-    mixed = cells + attended.astype(F32)
-    normed_two = layer_norm(mixed).astype(BF)
-    up = jnp.dot(normed_two, w_up[...], preferred_element_type=F32)
-    bent = jnp.tanh(up * (0.7978845608 + (0.7978845608 * 0.044715) * (up * up)))
-    half_up = 0.5 * up
-    expanded = (half_up + half_up * bent).astype(BF)
-    result = mixed + jnp.dot(expanded, w_down[...], preferred_element_type=F32)
-    for g in range(groups):
-        back[pl.ds(g, group, stride=groups), :] = result[g * group : (g + 1) * group]
-    out[...] = back[...].reshape(x.shape).astype(BF)
+            back[sub, pl.ds(g, group, stride=groups), :] = result[g * group : (g + 1) * group]
+        out[:, :, sub] = back[sub].reshape(x.shape[:2] + x.shape[3:]).astype(BF)
+
+    waiting = [work(sub) for sub in range(x.shape[2])]
+    running = []
+    while waiting or running:
+        if waiting:
+            running.append(waiting.pop(0))
+        for one in list(running):
+            if next(one, running) is running:
+                running.remove(one)
 
 
 def block_step(moved, carry, first, pieces, devices_y, devices_x, w_qkv, w_out, w_up, w_down):
@@ -462,7 +484,8 @@
     lanes = devices_y // GRID
     view = moved.reshape(GRID, lanes, devices_x, piece_y, piece_cols, width)
     tokens = GRID * devices_x * piece_cols
-    block = (GRID, None, devices_x, None, piece_cols, width)
+    subs = 2 if piece_y % 2 == 0 and first % 2 == 0 else 1
+    block = (GRID, None, devices_x, subs, piece_cols, width)
     operands = [view, w_qkv, w_out, w_up, w_down]
     in_specs = [pl.BlockSpec(block, lambda i, j: (0, i, 0, j, 0, 0)), *(whole(array) for array in operands[1:])]
     aliases = {}
@@ -473,13 +496,13 @@
     total = lanes * piece_y * tokens
     return pl.pallas_call(
         block_kernel,
-        grid=(lanes, piece_y),
+        grid=(lanes, piece_y // subs),
         in_specs=in_specs,
-        out_specs=pl.BlockSpec(block, lambda i, j: (0, i, 0, first + j, 0, 0)),
+        out_specs=pl.BlockSpec(block, lambda i, j: (0, i, 0, first // subs + j, 0, 0)),
         out_shape=jax.ShapeDtypeStruct((GRID, lanes, devices_x, pieces, piece_cols, width), BF),
         scratch_shapes=[
-            pltpu.VMEM((tokens, width), F32),
-            pltpu.VMEM((tokens, width), F32),
+            pltpu.VMEM((subs, tokens, width), F32),
+            pltpu.VMEM((subs, tokens, width), F32),
             pltpu.VMEM((w_out.shape[0], width), BF),
             pltpu.VMEM((HEADS // 2 * HDIM, 2 * GRID * GRID), BF),
             pltpu.VMEM((HEADS // 2 * HDIM, 2 * GRID * GRID), BF),

time: 109 us -> 105 us (0.963)
  Pallas kernels: 49.8 us -> 46.6 us
  blocking collectives: 25.6 us -> 23.4 us
  waiting for transfers between devices: 4.31 us -> 6.48 us
    pallas_call x2, Pallas kernels: 14.2 us -> 11 us  [block_step(): pl.pallas_call(block_kernel, grid=(lanes, piece_y // subs), in_specs=in_s...]
    all_to_all x1, blocking collectives: 25.6 us -> 23.4 us  [body(): lax.all_to_all(done, ('gy', 'gx'), split_axis=0, concat_axis=0, tiled=True)]
    all_to_all x2, waiting for transfers between devices: 3.4 us -> 5.56 us  [body(): lax.all_to_all(sent, ('gy', 'gx'), split_axis=0, concat_axis=0, tiled=True)]
  transfers between devices with their start and end apart: 6 -> 6, of which waited for: 3 -> 3; matrix products, arithmetic and copies ran while one was open for 0% -> 0% of each run, Pallas kernels for 29% -> 28%
where the time goes in v11:
time: 105 us
  Pallas kernels  46.6 us (44%)
  blocking collectives  23.4 us (22%)
  starting transfers between devices  21.8 us (21%)
  waiting for transfers between devices  6.48 us (6%)
  local copies, waits for them, and re-layouts  5.35 us (5%)
    pallas_call x4, Pallas kernels, conv_step(): pl.pallas_call(functools.partial(conv_kernel, start, rows, part, tail, re...  31.3 us
    all_to_all x1, blocking collectives, body(): lax.all_to_all(done, ('gy', 'gx'), split_axis=0, concat_axis=0, tiled=True)  23.4 us
    ppermute x4, starting transfers between devices, shifted(): return lax.ppermute(value, axis, pairs)  12.2 us
    pallas_call x2, Pallas kernels, block_step(): pl.pallas_call(block_kernel, grid=(lanes, piece_y // subs), in_specs=in_s...  11 us
    all_to_all x2, starting transfers between devices, body(): lax.all_to_all(sent, ('gy', 'gx'), split_axis=0, concat_axis=0, tiled=True)  9.63 us
    all_to_all x2, waiting for transfers between devices, body(): lax.all_to_all(sent, ('gy', 'gx'), split_axis=0, concat_axis=0, tiled=True)  5.56 us
    unnamed x40, local copies, waits for them, and re-layouts  5.29 us
    pallas_call x1, Pallas kernels, body(): pl.pallas_call(ring_kernel, grid=(1,), in_specs=[*(whole(array) for array...  2.21 us
  transfers between devices with their start and end apart: 6, of which 3 were waited for; matrix products, arithmetic and copies ran while one was open for 0% of the time, Pallas kernels for 28%

profile of v11, /device:TPU:1, one launch (start us, length us, event | category | flops | bytes accessed | tf_op | source)
XLA Modules:
  0.0 104.8 jit_solution(13986183363450788699)
XLA Ops:
  0.6 0.0 copy-start
  0.6 1.9 %copy-done = bf16[48,64,512]{2,1,0:T(8,128)(2,1)S(1)} copy-done((bf16[48,64,512]{2,1,0:T(8,128)(2,1)S(1)}, bf16[48,64,512]{2,1,0:T(8,128)(2,1)}, u32[]{:S(2)}) %copy-start) | copy-done | bytes 3145752
  2.5 1.1 %copy-done.2 = bf16[48,64,128]{2,1,0:T(8,128)(2,1)S(1)} copy-done((bf16[48,64,128]{2,1,0:T(8,128)(2,1)S(1)}, bf16[48,64,128]{2,1,0:T(8,128)(2,1)}, u32[]{:S(2)}) %copy-start.2) | copy-done | bytes 786456
  3.7 1.4 %copy-done.4 = f32[48,64,128]{2,1,0:T(8,128)S(1)} copy-done((f32[48,64,128]{2,1,0:T(8,128)S(1)}, f32[48,64,128]{2,1,0:T(8,128)}, u32[]{:S(2)}) %copy-start.4) | copy-done | bytes 1572888
  5.1 0.6 shard_map.105
  5.7 4.2 %collective-permute-start = (bf16[48,2,768]{2,1,0:T(2,128)(2,1)S(1)}, bf16[48,2,768]{2,1,0:T(2,128)(2,1)S(1)}, u32[]{:S(2)}, u32[]{:S(2)}) collective-permute-start(bf16[48,2,768]{2,1,0:T(2,128)(2,1)S(1)} %get-tuple-element.28), channel_id=1, source_target_pairs={{0,1},{1,2},{2,3},{4,5},{5,6},{6,7},{8,9},{9,10},{10,11},{12,13},{... | collective-permute-start | bytes 442376 | tf_op jit(solution)/shard_map/ppermute | solution.py:572
  9.9 1.3 %collective-permute-start.1 = (bf16[48,2,768]{2,1,0:T(2,128)(2,1)S(1)}, bf16[48,2,768]{2,1,0:T(2,128)(2,1)S(1)}, u32[]{:S(2)}, u32[]{:S(2)}) collective-permute-start(bf16[48,2,768]{2,1,0:T(2,128)(2,1)S(1)} %get-tuple-element.29), channel_id=1, source_target_pairs={{1,0},{2,1},{3,2},{5,4},{6,5},{7,6},{9,8},{10,9},{11,10},{13,12},{... | collective-permute-start | bytes 442376 | tf_op jit(solution)/shard_map/ppermute | solution.py:572
  11.2 5.2 %shard_map.104 = (bf16[48,64,128]{2,1,0:T(8,128)(2,1)S(1)}, f32[48,64,128]{2,1,0:T(8,128)S(1)}) custom-call(bf16[48,64,512]{2,1,0:T(8,128)(2,1)S(1)} %copy-done, bf16[48,64,128]{2,1,0:T(8,128)(2,1)S(1)} %copy-done.2, f32[48,64,128]{2,1,0:T(8,128)S(1)} %copy-done.4, f32[1,512]{1,0:T(1,128)S(1)} %bitcast.21, bf16[3456,512]{1,0:T(8,128)(2,1)S(1)} %bitcast.11), custom_call_target="tpu_custom_call" | custom-call | flops 4529848320 | bytes 6160384 | tf_op jit(solution)/shard_map/pallas_call | solution.py:262
  16.5 4.6 %collective-permute-start.2 = (bf16[2,68,768]{2,1,0:T(8,128)(2,1)S(1)}, bf16[2,68,768]{2,1,0:T(8,128)(2,1)S(1)}, u32[]{:S(2)}, u32[]{:S(2)}) collective-permute-start(bf16[2,68,768]{2,1,0:T(8,128)(2,1)S(1)} %get-tuple-element.35), channel_id=1, source_target_pairs={{0,4},{4,8},{8,12},{12,16},{16,20},{20,24},{24,28},{1,5},{5,9},{9,... | collective-permute-start | bytes 626696 | tf_op jit(solution)/shard_map/ppermute | solution.py:572
  21.2 2.1 %collective-permute-start.3 = (bf16[2,68,768]{2,1,0:T(8,128)(2,1)S(1)}, bf16[2,68,768]{2,1,0:T(8,128)(2,1)S(1)}, u32[]{:S(2)}, u32[]{:S(2)}) collective-permute-start(bf16[2,68,768]{2,1,0:T(8,128)(2,1)S(1)} %get-tuple-element.36), channel_id=1, source_target_pairs={{4,0},{8,4},{12,8},{16,12},{20,16},{24,20},{28,24},{5,1},{9,5},{13... | collective-permute-start | bytes 626696 | tf_op jit(solution)/shard_map/ppermute | solution.py:572
  23.3 4.2 %shard_map.106 = (bf16[48,64,128]{2,1,0:T(8,128)(2,1)S(1)}, f32[48,64,128]{2,1,0:T(8,128)S(1)}) custom-call(bf16[48,64,512]{2,1,0:T(8,128)(2,1)S(1)} %copy-done, bf16[48,64,128]{2,1,0:T(8,128)(2,1)S(1)} %copy-done.2, f32[48,64,128]{2,1,0:T(8,128)S(1)} %copy-done.4, f32[1,512]{1,0:T(1,128)S(1)} %bitcast.22, ...), custom_call_target="tpu_custom_call", output_to_operand_aliasing={{0}: (5, {}), {1}: (6, {})} | custom-call | flops 3623878656 | bytes 5636096 | tf_op jit(solution)/shard_map/pallas_call | solution.py:262
  27.5 0.9 collective-permute-done.3.below.args_11_.args_22_
  28.4 2.2 %shard_map.107 = (f32[4,64,128]{2,1,0:T(8,128)S(1)}, f32[4,64,128]{2,1,0:T(8,128)S(1)}, f32[4,64,128]{2,1,0:T(8,128)S(1)}, f32[4,64,128]{2,1,0:T(8,128)S(1)}, f32[2,64,256]{2,1,0:T(8,128)S(1)}) custom-call(bf16[2,68,768]{2,1,0:T(8,128)(2,1)S(1)} %collective-permute-done.2.above.args_10_.args_21_, ...), custom_call_target="tpu_custom_call" | custom-call | flops 1811939328 | bytes 3538944 | tf_op jit(solution)/shard_map/pallas_call | solution.py:605
  30.7 9.3 %shard_map.108 = (bf16[8,4,4,16,128]{4,3,2,1,0:T(8,128)(2,1)S(1)}, f32[48,64,128]{2,1,0:T(8,128)}) custom-call(bf16[48,64,512]{2,1,0:T(8,128)(2,1)S(1)} %copy-done.1, bf16[48,64,128]{2,1,0:T(8,128)(2,1)S(1)} %get-tuple-element.33.args_1_.args_3_.args_4_.args_5_, f32[48,64,128]{2,1,0:T(8,128)S(1)} %get-tuple-element.34.args_2_.args_6_, ...), custom_call_target="tpu_custom_call" | custom-call | flops 7247757312 | bytes 7733248 | tf_op jit(solution)/shard_map/pallas_call | solution.py:262
  40.1 0.8 copy-done.7
  40.9 6.3 %all-to-all-start.1 = ((bf16[32,4,16,128]{3,2,1,0:T(8,128)(2,1)}), bf16[32,4,16,128]{3,2,1,0:T(8,128)(2,1)S(1)}, u32[]{:S(2)}, u32[]{:S(2)}) async-start(bf16[32,4,16,128]{3,2,1,0:T(8,128)(2,1)} %bitcast.18), calls=%async_computation.1 | async-start | bytes 1048576 | tf_op jit(solution)/shard_map/all_to_all | solution.py:637
  47.2 12.7 %shard_map.109 = (bf16[8,4,2,16,128]{4,3,2,1,0:T(8,128)(2,1)}, f32[48,64,128]{2,1,0:T(8,128)}) custom-call(bf16[48,64,512]{2,1,0:T(8,128)(2,1)} %args_9_.1, bf16[48,64,512]{2,1,0:T(8,128)(2,1)} %args_9_.1, bf16[48,64,512]{2,1,0:T(8,128)(2,1)} %args_9_.1, bf16[48,64,128]{2,1,0:T(8,128)(2,1)} %copy-done.3, ...), custom_call_target="tpu_custom_call", output_to_operand_aliasing={{1}: (23, {})} | custom-call | flops 3623878656 | bytes 5636096 | tf_op jit(solution)/shard_map/pallas_call | solution.py:262
  59.9 2.5 %all-to-all-done.1 = bf16[32,4,16,128]{3,2,1,0:T(8,128)(2,1)S(1)} async-done(((bf16[32,4,16,128]{3,2,1,0:T(8,128)(2,1)}), bf16[32,4,16,128]{3,2,1,0:T(8,128)(2,1)S(1)}, u32[]{:S(2)}, u32[]{:S(2)}) %all-to-all-start.1) | async-done | bytes 524320 | tf_op jit(solution)/shard_map/all_to_all | solution.py:637
  62.5 3.3 %all-to-all-start = ((bf16[32,2,16,128]{3,2,1,0:T(8,128)(2,1)}), bf16[32,2,16,128]{3,2,1,0:T(8,128)(2,1)S(1)}, u32[]{:S(2)}, u32[]{:S(2)}) async-start(bf16[32,2,16,128]{3,2,1,0:T(8,128)(2,1)} %bitcast.25), calls=%async_computation | async-start | bytes 524288 | tf_op jit(solution)/shard_map/all_to_all | solution.py:637
  65.8 7.2 %shard_map.110.rest_0_ = bf16[8,1,4,6,16,128]{5,4,3,2,1,0:T(8,128)(2,1)S(1)} custom-call(bf16[8,1,4,4,16,128]{5,4,3,2,1,0:T(8,128)(2,1)S(1)} %bitcast.17, bf16[128,768]{1,0:T(8,128)(2,1)S(1)} %copy-done.16, bf16[256,128]{1,0:T(8,128)(2,1)S(1)} %copy-done.19, bf16[128,512]{1,0:T(8,128)(2,1)S(1)} %copy-done.17, bf16[512,128]{1,0:T(8,128)(2,1)S(1)} %copy-done.18), custom_call_target="tpu_custom_call" | custom-call | flops 6144000000 | bytes 1848576 | tf_op jit(solution)/shard_map/pallas_call | solution.py:497
  73.1 3.1 %all-to-all-done = bf16[32,2,16,128]{3,2,1,0:T(8,128)(2,1)S(1)} async-done(((bf16[32,2,16,128]{3,2,1,0:T(8,128)(2,1)}), bf16[32,2,16,128]{3,2,1,0:T(8,128)(2,1)S(1)}, u32[]{:S(2)}, u32[]{:S(2)}) %all-to-all-start) | async-done | bytes 262176 | tf_op jit(solution)/shard_map/all_to_all | solution.py:637
  76.1 3.7 %shard_map.111 = bf16[8,1,4,6,16,128]{5,4,3,2,1,0:T(8,128)(2,1)S(1)} custom-call(bf16[8,1,4,2,16,128]{5,4,3,2,1,0:T(8,128)(2,1)S(1)} %bitcast.19, bf16[128,768]{1,0:T(8,128)(2,1)S(1)} %copy-done.16, bf16[256,128]{1,0:T(8,128)(2,1)S(1)} %copy-done.19, bf16[128,512]{1,0:T(8,128)(2,1)S(1)} %copy-done.17, ...), custom_call_target="tpu_custom_call", output_to_operand_aliasing={{}: (5, {})} | custom-call | flops 3072000000 | bytes 1324288 | tf_op jit(solution)/shard_map/pallas_call | solution.py:497
  79.9 23.4 %all_to_all.15 = bf16[32,6,16,128]{3,2,1,0:T(8,128)(2,1)S(1)} all-to-all(bf16[32,6,16,128]{3,2,1,0:T(8,128)(2,1)S(1)} %bitcast.16), channel_id=1, replica_groups=mesh['gy'=8,'gx'=4] {'gy','gx'}, dimensions={0} | all-to-all | bytes 1572864 | tf_op jit(solution)/shard_map/all_to_all | solution.py:644
  103.3 1.5 %shard_map.112 = bf16[48,64,128]{2,1,0:T(8,128)(2,1)} custom-call(bf16[8,4,6,16,128]{4,3,2,1,0:T(8,128)(2,1)S(1)} %bitcast.15), custom_call_target="tpu_custom_call" | custom-call | bytes 1572864 | tf_op jit(solution)/shard_map/pallas_call | solution.py:543
  (43 shorter events, 0.2 us)
Async XLA Ops:
  0.6 1.9 %copy-start = (bf16[48,64,512]{2,1,0:T(8,128)(2,1)S(1)}, bf16[48,64,512]{2,1,0:T(8,128)(2,1)}, u32[]{:S(2)}) copy-start(bf16[48,64,512]{2,1,0:T(8,128)(2,1)} %args_9_.1) | copy-start | bytes 9437188
  3.7 1.4 %copy-start.4 = (f32[48,64,128]{2,1,0:T(8,128)S(1)}, f32[48,64,128]{2,1,0:T(8,128)}, u32[]{:S(2)}) copy-start(f32[48,64,128]{2,1,0:T(8,128)} %args_13_.1) | copy-start | bytes 4718596
  5.1 6.1 %copy-start.5 = (bf16[3,3,384,512]{3,2,1,0:T(8,128)(2,1)S(1)}, bf16[3,3,384,512]{3,2,1,0:T(8,128)(2,1)}, u32[]{:S(2)}) copy-start(bf16[3,3,384,512]{3,2,1,0:T(8,128)(2,1)} %param.12) | copy-start | bytes 10616836
  5.1 6.1 %copy-start.15 = (f32[512]{0:T(512)S(1)}, f32[512]{0:T(512)}, u32[]{:S(2)}) copy-start(f32[512]{0:T(512)} %param.13) | copy-start | bytes 6148
  5.7 10.7 %collective-permute-start = (bf16[48,2,768]{2,1,0:T(2,128)(2,1)S(1)}, bf16[48,2,768]{2,1,0:T(2,128)(2,1)S(1)}, u32[]{:S(2)}, u32[]{:S(2)}) collective-permute-start(bf16[48,2,768]{2,1,0:T(2,128)(2,1)S(1)} %get-tuple-element.28), channel_id=1, source_target_pairs={{0,1},{1,2},{2,3},{4,5},{5,6},{6,7},{8,9},{9,10},{10,11},{12,13},{... | collective-permute-start | bytes 442376 | tf_op jit(solution)/shard_map/ppermute | solution.py:572
  9.9 6.5 %collective-permute-start.1 = (bf16[48,2,768]{2,1,0:T(2,128)(2,1)S(1)}, bf16[48,2,768]{2,1,0:T(2,128)(2,1)S(1)}, u32[]{:S(2)}, u32[]{:S(2)}) collective-permute-start(bf16[48,2,768]{2,1,0:T(2,128)(2,1)S(1)} %get-tuple-element.29), channel_id=1, source_target_pairs={{1,0},{2,1},{3,2},{5,4},{6,5},{7,6},{9,8},{10,9},{11,10},{13,12},{... | collective-permute-start | bytes 442376 | tf_op jit(solution)/shard_map/ppermute | solution.py:572
  16.5 11.0 %collective-permute-start.2 = (bf16[2,68,768]{2,1,0:T(8,128)(2,1)S(1)}, bf16[2,68,768]{2,1,0:T(8,128)(2,1)S(1)}, u32[]{:S(2)}, u32[]{:S(2)}) collective-permute-start(bf16[2,68,768]{2,1,0:T(8,128)(2,1)S(1)} %get-tuple-element.35), channel_id=1, source_target_pairs={{0,4},{4,8},{8,12},{12,16},{16,20},{20,24},{24,28},{1,5},{5,9},{9,... | collective-permute-start | bytes 626696 | tf_op jit(solution)/shard_map/ppermute | solution.py:572
  21.2 7.3 %collective-permute-start.3 = (bf16[2,68,768]{2,1,0:T(8,128)(2,1)S(1)}, bf16[2,68,768]{2,1,0:T(8,128)(2,1)S(1)}, u32[]{:S(2)}, u32[]{:S(2)}) collective-permute-start(bf16[2,68,768]{2,1,0:T(8,128)(2,1)S(1)} %get-tuple-element.36), channel_id=1, source_target_pairs={{4,0},{8,4},{12,8},{16,12},{20,16},{24,20},{28,24},{5,1},{9,5},{13... | collective-permute-start | bytes 626696 | tf_op jit(solution)/shard_map/ppermute | solution.py:572
  27.5 3.2 %copy-start.3 = (bf16[48,64,128]{2,1,0:T(8,128)(2,1)}, bf16[48,64,128]{2,1,0:T(8,128)(2,1)S(1)}, u32[]{:S(2)}) copy-start(bf16[48,64,128]{2,1,0:T(8,128)(2,1)S(1)} %get-tuple-element.33.args_1_.args_3_.args_4_.args_5_) | copy-start | bytes 2359300
  27.5 3.2 %copy-start.6 = (f32[48,64,128]{2,1,0:T(8,128)}, f32[48,64,128]{2,1,0:T(8,128)S(1)}, u32[]{:S(2)}) copy-start(f32[48,64,128]{2,1,0:T(8,128)S(1)} %get-tuple-element.34.args_2_.args_6_) | copy-start | bytes 4718596
  27.5 3.2 %copy-start.8 = (bf16[2,68,768]{2,1,0:T(8,128)(2,1)}, bf16[2,68,768]{2,1,0:T(8,128)(2,1)S(1)}, u32[]{:S(2)}) copy-start(bf16[2,68,768]{2,1,0:T(8,128)(2,1)S(1)} %collective-permute-done.2.above.args_10_.args_21_) | copy-start | bytes 626692
  28.4 2.3 %copy-start.9 = (bf16[2,68,768]{2,1,0:T(8,128)(2,1)}, bf16[2,68,768]{2,1,0:T(8,128)(2,1)S(1)}, u32[]{:S(2)}) copy-start(bf16[2,68,768]{2,1,0:T(8,128)(2,1)S(1)} %collective-permute-done.3.below.args_11_.args_22_) | copy-start | bytes 626692
  28.4 2.3 %copy-start.1 = (bf16[48,64,512]{2,1,0:T(8,128)(2,1)S(1)}, bf16[48,64,512]{2,1,0:T(8,128)(2,1)}, u32[]{:S(2)}) copy-start(bf16[48,64,512]{2,1,0:T(8,128)(2,1)} %args_9_.1) | copy-start | bytes 9437188
  30.6 9.4 %copy-start.10 = (f32[4,64,128]{2,1,0:T(8,128)}, f32[4,64,128]{2,1,0:T(8,128)S(1)}, u32[]{:S(2)}) copy-start(f32[4,64,128]{2,1,0:T(8,128)S(1)} %get-tuple-element.41.args_7_.args_18_) | copy-start | bytes 393220
  30.7 9.4 %copy-start.11 = (f32[4,64,128]{2,1,0:T(8,128)}, f32[4,64,128]{2,1,0:T(8,128)S(1)}, u32[]{:S(2)}) copy-start(f32[4,64,128]{2,1,0:T(8,128)S(1)} %get-tuple-element.42.args_8_.args_19_) | copy-start | bytes 393220
  30.7 9.4 %copy-start.12 = (f32[4,64,128]{2,1,0:T(8,128)}, f32[4,64,128]{2,1,0:T(8,128)S(1)}, u32[]{:S(2)}) copy-start(f32[4,64,128]{2,1,0:T(8,128)S(1)} %get-tuple-element.39.args_5_.args_16_) | copy-start | bytes 393220
  30.7 9.4 %copy-start.13 = (f32[4,64,128]{2,1,0:T(8,128)}, f32[4,64,128]{2,1,0:T(8,128)S(1)}, u32[]{:S(2)}) copy-start(f32[4,64,128]{2,1,0:T(8,128)S(1)} %get-tuple-element.40.args_6_.args_17_) | copy-start | bytes 393220
  30.7 9.4 %copy-start.14 = (f32[2,64,256]{2,1,0:T(8,128)}, f32[2,64,256]{2,1,0:T(8,128)S(1)}, u32[]{:S(2)}) copy-start(f32[2,64,256]{2,1,0:T(8,128)S(1)} %get-tuple-element.43.args_9_.args_20_) | copy-start | bytes 393220
  40.9 21.6 %all-to-all-start.1 = ((bf16[32,4,16,128]{3,2,1,0:T(8,128)(2,1)}), bf16[32,4,16,128]{3,2,1,0:T(8,128)(2,1)S(1)}, u32[]{:S(2)}, u32[]{:S(2)}) async-start(bf16[32,4,16,128]{3,2,1,0:T(8,128)(2,1)} %bitcast.18), calls=%async_computation.1 | async-start | bytes 1048576 | tf_op jit(solution)/shard_map/all_to_all | solution.py:637
  47.2 18.6 %copy-start.16 = (bf16[128,768]{1,0:T(8,128)(2,1)S(1)}, bf16[128,768]{1,0:T(8,128)(2,1)}, u32[]{:S(2)}) copy-start(bf16[128,768]{1,0:T(8,128)(2,1)} %w_qkv.3) | copy-start | bytes 589828
  47.2 18.6 %copy-start.17 = (bf16[128,512]{1,0:T(8,128)(2,1)S(1)}, bf16[128,512]{1,0:T(8,128)(2,1)}, u32[]{:S(2)}) copy-start(bf16[128,512]{1,0:T(8,128)(2,1)} %w_up.3) | copy-start | bytes 393220
  47.2 18.6 %copy-start.18 = (bf16[512,128]{1,0:T(8,128)(2,1)S(1)}, bf16[512,128]{1,0:T(8,128)(2,1)}, u32[]{:S(2)}) copy-start(bf16[512,128]{1,0:T(8,128)(2,1)} %w_down.3) | copy-start | bytes 393220
  47.2 18.6 %copy-start.19 = (bf16[256,128]{1,0:T(8,128)(2,1)S(1)}, bf16[256,128]{1,0:T(8,128)(2,1)}, u32[]{:S(2)}) copy-start(bf16[256,128]{1,0:T(8,128)(2,1)} %w_out.3) | copy-start | bytes 196612
  62.5 13.7 %all-to-all-start = ((bf16[32,2,16,128]{3,2,1,0:T(8,128)(2,1)}), bf16[32,2,16,128]{3,2,1,0:T(8,128)(2,1)S(1)}, u32[]{:S(2)}, u32[]{:S(2)}) async-start(bf16[32,2,16,128]{3,2,1,0:T(8,128)(2,1)} %bitcast.25), calls=%async_computation | async-start | bytes 524288 | tf_op jit(solution)/shard_map/all_to_all | solution.py:637
  (2 other events, 1.9 us)

commit v12 on v11

--- a/solution.py
+++ b/solution.py
@@ -145,7 +145,7 @@
                 write(row, new_cell, new_hidden)
             leave(first, depth)
 
-        depth = step_rows(0, extent, 12)
+        depth = step_rows(0, extent, 4)
         for pos in range(depth + 2):
             build(pos)
         while loads:
@@ -484,7 +484,7 @@
     lanes = devices_y // GRID
     view = moved.reshape(GRID, lanes, devices_x, piece_y, piece_cols, width)
     tokens = GRID * devices_x * piece_cols
-    subs = 2 if piece_y % 2 == 0 and first % 2 == 0 else 1
+    subs = max(size for size in (1, 2, 4) if piece_y % size == 0 and first % size == 0)
     block = (GRID, None, devices_x, subs, piece_cols, width)
     operands = [view, w_qkv, w_out, w_up, w_down]
     in_specs = [pl.BlockSpec(block, lambda i, j: (0, i, 0, j, 0, 0)), *(whole(array) for array in operands[1:])]

time: 105 us -> 105 us (level)
  transfers between devices with their start and end apart: 6 -> 6, of which waited for: 3 -> 3; matrix products, arithmetic and copies ran while one was open for 0% -> 0% of each run, Pallas kernels for 28% -> 27%
where the time goes in v12:
time: 105 us
  Pallas kernels  45.9 us (44%)
  blocking collectives  23.2 us (22%)
  starting transfers between devices  21.7 us (21%)
  waiting for transfers between devices  7.4 us (7%)
  local copies, waits for them, and re-layouts  5.35 us (5%)
    pallas_call x4, Pallas kernels, conv_step(): pl.pallas_call(functools.partial(conv_kernel, start, rows, part, tail, re...  31.3 us
    all_to_all x1, blocking collectives, body(): lax.all_to_all(done, ('gy', 'gx'), split_axis=0, concat_axis=0, tiled=True)  23.2 us
    ppermute x4, starting transfers between devices, shifted(): return lax.ppermute(value, axis, pairs)  12.1 us
    pallas_call x2, Pallas kernels, block_step(): pl.pallas_call(block_kernel, grid=(lanes, piece_y // subs), in_specs=in_s...  10.2 us
    all_to_all x2, starting transfers between devices, body(): lax.all_to_all(sent, ('gy', 'gx'), split_axis=0, concat_axis=0, tiled=True)  9.55 us
    all_to_all x2, waiting for transfers between devices, body(): lax.all_to_all(sent, ('gy', 'gx'), split_axis=0, concat_axis=0, tiled=True)  6.51 us
    unnamed x40, local copies, waits for them, and re-layouts  5.29 us
    pallas_call x1, Pallas kernels, body(): pl.pallas_call(ring_kernel, grid=(1,), in_specs=[*(whole(array) for array...  2.21 us
  transfers between devices with their start and end apart: 6, of which 3 were waited for; matrix products, arithmetic and copies ran while one was open for 0% of the time, Pallas kernels for 27%

profile of v12, /device:TPU:1, one launch (start us, length us, event | category | flops | bytes accessed | tf_op | source)
XLA Modules:
  0.0 104.5 jit_solution(3137126585552989947)
XLA Ops:
  0.6 0.0 copy-start
  0.6 1.9 %copy-done = bf16[48,64,512]{2,1,0:T(8,128)(2,1)S(1)} copy-done((bf16[48,64,512]{2,1,0:T(8,128)(2,1)S(1)}, bf16[48,64,512]{2,1,0:T(8,128)(2,1)}, u32[]{:S(2)}) %copy-start) | copy-done | bytes 3145752
  2.5 1.1 %copy-done.2 = bf16[48,64,128]{2,1,0:T(8,128)(2,1)S(1)} copy-done((bf16[48,64,128]{2,1,0:T(8,128)(2,1)S(1)}, bf16[48,64,128]{2,1,0:T(8,128)(2,1)}, u32[]{:S(2)}) %copy-start.2) | copy-done | bytes 786456
  3.7 1.4 %copy-done.4 = f32[48,64,128]{2,1,0:T(8,128)S(1)} copy-done((f32[48,64,128]{2,1,0:T(8,128)S(1)}, f32[48,64,128]{2,1,0:T(8,128)}, u32[]{:S(2)}) %copy-start.4) | copy-done | bytes 1572888
  5.1 0.6 shard_map.105
  5.7 4.2 %collective-permute-start = (bf16[48,2,768]{2,1,0:T(2,128)(2,1)S(1)}, bf16[48,2,768]{2,1,0:T(2,128)(2,1)S(1)}, u32[]{:S(2)}, u32[]{:S(2)}) collective-permute-start(bf16[48,2,768]{2,1,0:T(2,128)(2,1)S(1)} %get-tuple-element.28), channel_id=1, source_target_pairs={{0,1},{1,2},{2,3},{4,5},{5,6},{6,7},{8,9},{9,10},{10,11},{12,13},{... | collective-permute-start | bytes 442376 | tf_op jit(solution)/shard_map/ppermute | solution.py:572
  9.9 1.3 %collective-permute-start.1 = (bf16[48,2,768]{2,1,0:T(2,128)(2,1)S(1)}, bf16[48,2,768]{2,1,0:T(2,128)(2,1)S(1)}, u32[]{:S(2)}, u32[]{:S(2)}) collective-permute-start(bf16[48,2,768]{2,1,0:T(2,128)(2,1)S(1)} %get-tuple-element.29), channel_id=1, source_target_pairs={{1,0},{2,1},{3,2},{5,4},{6,5},{7,6},{9,8},{10,9},{11,10},{13,12},{... | collective-permute-start | bytes 442376 | tf_op jit(solution)/shard_map/ppermute | solution.py:572
  11.2 5.2 %shard_map.104 = (bf16[48,64,128]{2,1,0:T(8,128)(2,1)S(1)}, f32[48,64,128]{2,1,0:T(8,128)S(1)}) custom-call(bf16[48,64,512]{2,1,0:T(8,128)(2,1)S(1)} %copy-done, bf16[48,64,128]{2,1,0:T(8,128)(2,1)S(1)} %copy-done.2, f32[48,64,128]{2,1,0:T(8,128)S(1)} %copy-done.4, f32[1,512]{1,0:T(1,128)S(1)} %bitcast.21, bf16[3456,512]{1,0:T(8,128)(2,1)S(1)} %bitcast.11), custom_call_target="tpu_custom_call" | custom-call | flops 4529848320 | bytes 6160384 | tf_op jit(solution)/shard_map/pallas_call | solution.py:262
  16.6 4.5 %collective-permute-start.2 = (bf16[2,68,768]{2,1,0:T(8,128)(2,1)S(1)}, bf16[2,68,768]{2,1,0:T(8,128)(2,1)S(1)}, u32[]{:S(2)}, u32[]{:S(2)}) collective-permute-start(bf16[2,68,768]{2,1,0:T(8,128)(2,1)S(1)} %get-tuple-element.35), channel_id=1, source_target_pairs={{0,4},{4,8},{8,12},{12,16},{16,20},{20,24},{24,28},{1,5},{5,9},{9,... | collective-permute-start | bytes 626696 | tf_op jit(solution)/shard_map/ppermute | solution.py:572
  21.2 2.1 %collective-permute-start.3 = (bf16[2,68,768]{2,1,0:T(8,128)(2,1)S(1)}, bf16[2,68,768]{2,1,0:T(8,128)(2,1)S(1)}, u32[]{:S(2)}, u32[]{:S(2)}) collective-permute-start(bf16[2,68,768]{2,1,0:T(8,128)(2,1)S(1)} %get-tuple-element.36), channel_id=1, source_target_pairs={{4,0},{8,4},{12,8},{16,12},{20,16},{24,20},{28,24},{5,1},{9,5},{13... | collective-permute-start | bytes 626696 | tf_op jit(solution)/shard_map/ppermute | solution.py:572
  23.3 4.2 %shard_map.106 = (bf16[48,64,128]{2,1,0:T(8,128)(2,1)S(1)}, f32[48,64,128]{2,1,0:T(8,128)S(1)}) custom-call(bf16[48,64,512]{2,1,0:T(8,128)(2,1)S(1)} %copy-done, bf16[48,64,128]{2,1,0:T(8,128)(2,1)S(1)} %copy-done.2, f32[48,64,128]{2,1,0:T(8,128)S(1)} %copy-done.4, f32[1,512]{1,0:T(1,128)S(1)} %bitcast.22, ...), custom_call_target="tpu_custom_call", output_to_operand_aliasing={{0}: (5, {}), {1}: (6, {})} | custom-call | flops 3623878656 | bytes 5636096 | tf_op jit(solution)/shard_map/pallas_call | solution.py:262
  27.5 0.9 collective-permute-done.3.below.args_11_.args_22_
  28.4 2.2 %shard_map.107 = (f32[4,64,128]{2,1,0:T(8,128)S(1)}, f32[4,64,128]{2,1,0:T(8,128)S(1)}, f32[4,64,128]{2,1,0:T(8,128)S(1)}, f32[4,64,128]{2,1,0:T(8,128)S(1)}, f32[2,64,256]{2,1,0:T(8,128)S(1)}) custom-call(bf16[2,68,768]{2,1,0:T(8,128)(2,1)S(1)} %collective-permute-done.2.above.args_10_.args_21_, ...), custom_call_target="tpu_custom_call" | custom-call | flops 1811939328 | bytes 3538944 | tf_op jit(solution)/shard_map/pallas_call | solution.py:605
  30.7 9.3 %shard_map.108 = (bf16[8,4,4,16,128]{4,3,2,1,0:T(8,128)(2,1)S(1)}, f32[48,64,128]{2,1,0:T(8,128)}) custom-call(bf16[48,64,512]{2,1,0:T(8,128)(2,1)S(1)} %copy-done.1, bf16[48,64,128]{2,1,0:T(8,128)(2,1)S(1)} %get-tuple-element.33.args_1_.args_3_.args_4_.args_5_, f32[48,64,128]{2,1,0:T(8,128)S(1)} %get-tuple-element.34.args_2_.args_6_, ...), custom_call_target="tpu_custom_call" | custom-call | flops 7247757312 | bytes 7733248 | tf_op jit(solution)/shard_map/pallas_call | solution.py:262
  40.1 0.8 copy-done.7
  40.9 6.4 %all-to-all-start.1 = ((bf16[32,4,16,128]{3,2,1,0:T(8,128)(2,1)}), bf16[32,4,16,128]{3,2,1,0:T(8,128)(2,1)S(1)}, u32[]{:S(2)}, u32[]{:S(2)}) async-start(bf16[32,4,16,128]{3,2,1,0:T(8,128)(2,1)} %bitcast.18), calls=%async_computation.1 | async-start | bytes 1048576 | tf_op jit(solution)/shard_map/all_to_all | solution.py:637
  47.3 12.6 %shard_map.109 = (bf16[8,4,2,16,128]{4,3,2,1,0:T(8,128)(2,1)}, f32[48,64,128]{2,1,0:T(8,128)}) custom-call(bf16[48,64,512]{2,1,0:T(8,128)(2,1)} %args_9_.1, bf16[48,64,512]{2,1,0:T(8,128)(2,1)} %args_9_.1, bf16[48,64,512]{2,1,0:T(8,128)(2,1)} %args_9_.1, bf16[48,64,128]{2,1,0:T(8,128)(2,1)} %copy-done.3, ...), custom_call_target="tpu_custom_call", output_to_operand_aliasing={{1}: (23, {})} | custom-call | flops 3623878656 | bytes 5636096 | tf_op jit(solution)/shard_map/pallas_call | solution.py:262
  59.9 2.7 %all-to-all-done.1 = bf16[32,4,16,128]{3,2,1,0:T(8,128)(2,1)S(1)} async-done(((bf16[32,4,16,128]{3,2,1,0:T(8,128)(2,1)}), bf16[32,4,16,128]{3,2,1,0:T(8,128)(2,1)S(1)}, u32[]{:S(2)}, u32[]{:S(2)}) %all-to-all-start.1) | async-done | bytes 524320 | tf_op jit(solution)/shard_map/all_to_all | solution.py:637
  62.6 3.2 %all-to-all-start = ((bf16[32,2,16,128]{3,2,1,0:T(8,128)(2,1)}), bf16[32,2,16,128]{3,2,1,0:T(8,128)(2,1)S(1)}, u32[]{:S(2)}, u32[]{:S(2)}) async-start(bf16[32,2,16,128]{3,2,1,0:T(8,128)(2,1)} %bitcast.25), calls=%async_computation | async-start | bytes 524288 | tf_op jit(solution)/shard_map/all_to_all | solution.py:637
  65.8 6.5 %shard_map.110.rest_0_ = bf16[8,1,4,6,16,128]{5,4,3,2,1,0:T(8,128)(2,1)S(1)} custom-call(bf16[8,1,4,4,16,128]{5,4,3,2,1,0:T(8,128)(2,1)S(1)} %bitcast.17, bf16[128,768]{1,0:T(8,128)(2,1)S(1)} %copy-done.16, bf16[256,128]{1,0:T(8,128)(2,1)S(1)} %copy-done.19, bf16[128,512]{1,0:T(8,128)(2,1)S(1)} %copy-done.17, bf16[512,128]{1,0:T(8,128)(2,1)S(1)} %copy-done.18), custom_call_target="tpu_custom_call" | custom-call | flops 6144000000 | bytes 1848576 | tf_op jit(solution)/shard_map/pallas_call | solution.py:497
  72.3 3.8 %all-to-all-done = bf16[32,2,16,128]{3,2,1,0:T(8,128)(2,1)S(1)} async-done(((bf16[32,2,16,128]{3,2,1,0:T(8,128)(2,1)}), bf16[32,2,16,128]{3,2,1,0:T(8,128)(2,1)S(1)}, u32[]{:S(2)}, u32[]{:S(2)}) %all-to-all-start) | async-done | bytes 262176 | tf_op jit(solution)/shard_map/all_to_all | solution.py:637
  76.1 3.7 %shard_map.111 = bf16[8,1,4,6,16,128]{5,4,3,2,1,0:T(8,128)(2,1)S(1)} custom-call(bf16[8,1,4,2,16,128]{5,4,3,2,1,0:T(8,128)(2,1)S(1)} %bitcast.19, bf16[128,768]{1,0:T(8,128)(2,1)S(1)} %copy-done.16, bf16[256,128]{1,0:T(8,128)(2,1)S(1)} %copy-done.19, bf16[128,512]{1,0:T(8,128)(2,1)S(1)} %copy-done.17, ...), custom_call_target="tpu_custom_call", output_to_operand_aliasing={{}: (5, {})} | custom-call | flops 3072000000 | bytes 1324288 | tf_op jit(solution)/shard_map/pallas_call | solution.py:497
  79.8 23.2 %all_to_all.15 = bf16[32,6,16,128]{3,2,1,0:T(8,128)(2,1)S(1)} all-to-all(bf16[32,6,16,128]{3,2,1,0:T(8,128)(2,1)S(1)} %bitcast.16), channel_id=1, replica_groups=mesh['gy'=8,'gx'=4] {'gy','gx'}, dimensions={0} | all-to-all | bytes 1572864 | tf_op jit(solution)/shard_map/all_to_all | solution.py:644
  103.0 1.5 %shard_map.112 = bf16[48,64,128]{2,1,0:T(8,128)(2,1)} custom-call(bf16[8,4,6,16,128]{4,3,2,1,0:T(8,128)(2,1)S(1)} %bitcast.15), custom_call_target="tpu_custom_call" | custom-call | bytes 1572864 | tf_op jit(solution)/shard_map/pallas_call | solution.py:543
  (43 shorter events, 0.2 us)
Async XLA Ops:
  0.6 1.9 %copy-start = (bf16[48,64,512]{2,1,0:T(8,128)(2,1)S(1)}, bf16[48,64,512]{2,1,0:T(8,128)(2,1)}, u32[]{:S(2)}) copy-start(bf16[48,64,512]{2,1,0:T(8,128)(2,1)} %args_9_.1) | copy-start | bytes 9437188
  3.7 1.4 %copy-start.4 = (f32[48,64,128]{2,1,0:T(8,128)S(1)}, f32[48,64,128]{2,1,0:T(8,128)}, u32[]{:S(2)}) copy-start(f32[48,64,128]{2,1,0:T(8,128)} %args_13_.1) | copy-start | bytes 4718596
  5.1 6.1 %copy-start.5 = (bf16[3,3,384,512]{3,2,1,0:T(8,128)(2,1)S(1)}, bf16[3,3,384,512]{3,2,1,0:T(8,128)(2,1)}, u32[]{:S(2)}) copy-start(bf16[3,3,384,512]{3,2,1,0:T(8,128)(2,1)} %param.12) | copy-start | bytes 10616836
  5.1 6.1 %copy-start.15 = (f32[512]{0:T(512)S(1)}, f32[512]{0:T(512)}, u32[]{:S(2)}) copy-start(f32[512]{0:T(512)} %param.13) | copy-start | bytes 6148
  5.7 10.8 %collective-permute-start = (bf16[48,2,768]{2,1,0:T(2,128)(2,1)S(1)}, bf16[48,2,768]{2,1,0:T(2,128)(2,1)S(1)}, u32[]{:S(2)}, u32[]{:S(2)}) collective-permute-start(bf16[48,2,768]{2,1,0:T(2,128)(2,1)S(1)} %get-tuple-element.28), channel_id=1, source_target_pairs={{0,1},{1,2},{2,3},{4,5},{5,6},{6,7},{8,9},{9,10},{10,11},{12,13},{... | collective-permute-start | bytes 442376 | tf_op jit(solution)/shard_map/ppermute | solution.py:572
  9.9 6.6 %collective-permute-start.1 = (bf16[48,2,768]{2,1,0:T(2,128)(2,1)S(1)}, bf16[48,2,768]{2,1,0:T(2,128)(2,1)S(1)}, u32[]{:S(2)}, u32[]{:S(2)}) collective-permute-start(bf16[48,2,768]{2,1,0:T(2,128)(2,1)S(1)} %get-tuple-element.29), channel_id=1, source_target_pairs={{1,0},{2,1},{3,2},{5,4},{6,5},{7,6},{9,8},{10,9},{11,10},{13,12},{... | collective-permute-start | bytes 442376 | tf_op jit(solution)/shard_map/ppermute | solution.py:572
  16.6 10.9 %collective-permute-start.2 = (bf16[2,68,768]{2,1,0:T(8,128)(2,1)S(1)}, bf16[2,68,768]{2,1,0:T(8,128)(2,1)S(1)}, u32[]{:S(2)}, u32[]{:S(2)}) collective-permute-start(bf16[2,68,768]{2,1,0:T(8,128)(2,1)S(1)} %get-tuple-element.35), channel_id=1, source_target_pairs={{0,4},{4,8},{8,12},{12,16},{16,20},{20,24},{24,28},{1,5},{5,9},{9,... | collective-permute-start | bytes 626696 | tf_op jit(solution)/shard_map/ppermute | solution.py:572
  21.2 7.3 %collective-permute-start.3 = (bf16[2,68,768]{2,1,0:T(8,128)(2,1)S(1)}, bf16[2,68,768]{2,1,0:T(8,128)(2,1)S(1)}, u32[]{:S(2)}, u32[]{:S(2)}) collective-permute-start(bf16[2,68,768]{2,1,0:T(8,128)(2,1)S(1)} %get-tuple-element.36), channel_id=1, source_target_pairs={{4,0},{8,4},{12,8},{16,12},{20,16},{24,20},{28,24},{5,1},{9,5},{13... | collective-permute-start | bytes 626696 | tf_op jit(solution)/shard_map/ppermute | solution.py:572
  27.5 3.2 %copy-start.3 = (bf16[48,64,128]{2,1,0:T(8,128)(2,1)}, bf16[48,64,128]{2,1,0:T(8,128)(2,1)S(1)}, u32[]{:S(2)}) copy-start(bf16[48,64,128]{2,1,0:T(8,128)(2,1)S(1)} %get-tuple-element.33.args_1_.args_3_.args_4_.args_5_) | copy-start | bytes 2359300
  27.5 3.2 %copy-start.6 = (f32[48,64,128]{2,1,0:T(8,128)}, f32[48,64,128]{2,1,0:T(8,128)S(1)}, u32[]{:S(2)}) copy-start(f32[48,64,128]{2,1,0:T(8,128)S(1)} %get-tuple-element.34.args_2_.args_6_) | copy-start | bytes 4718596
  27.5 3.2 %copy-start.8 = (bf16[2,68,768]{2,1,0:T(8,128)(2,1)}, bf16[2,68,768]{2,1,0:T(8,128)(2,1)S(1)}, u32[]{:S(2)}) copy-start(bf16[2,68,768]{2,1,0:T(8,128)(2,1)S(1)} %collective-permute-done.2.above.args_10_.args_21_) | copy-start | bytes 626692
  28.4 2.3 %copy-start.9 = (bf16[2,68,768]{2,1,0:T(8,128)(2,1)}, bf16[2,68,768]{2,1,0:T(8,128)(2,1)S(1)}, u32[]{:S(2)}) copy-start(bf16[2,68,768]{2,1,0:T(8,128)(2,1)S(1)} %collective-permute-done.3.below.args_11_.args_22_) | copy-start | bytes 626692
  28.4 2.3 %copy-start.1 = (bf16[48,64,512]{2,1,0:T(8,128)(2,1)S(1)}, bf16[48,64,512]{2,1,0:T(8,128)(2,1)}, u32[]{:S(2)}) copy-start(bf16[48,64,512]{2,1,0:T(8,128)(2,1)} %args_9_.1) | copy-start | bytes 9437188
  30.6 9.4 %copy-start.10 = (f32[4,64,128]{2,1,0:T(8,128)}, f32[4,64,128]{2,1,0:T(8,128)S(1)}, u32[]{:S(2)}) copy-start(f32[4,64,128]{2,1,0:T(8,128)S(1)} %get-tuple-element.41.args_7_.args_18_) | copy-start | bytes 393220
  30.7 9.4 %copy-start.11 = (f32[4,64,128]{2,1,0:T(8,128)}, f32[4,64,128]{2,1,0:T(8,128)S(1)}, u32[]{:S(2)}) copy-start(f32[4,64,128]{2,1,0:T(8,128)S(1)} %get-tuple-element.42.args_8_.args_19_) | copy-start | bytes 393220
  30.7 9.4 %copy-start.12 = (f32[4,64,128]{2,1,0:T(8,128)}, f32[4,64,128]{2,1,0:T(8,128)S(1)}, u32[]{:S(2)}) copy-start(f32[4,64,128]{2,1,0:T(8,128)S(1)} %get-tuple-element.39.args_5_.args_16_) | copy-start | bytes 393220
  30.7 9.4 %copy-start.13 = (f32[4,64,128]{2,1,0:T(8,128)}, f32[4,64,128]{2,1,0:T(8,128)S(1)}, u32[]{:S(2)}) copy-start(f32[4,64,128]{2,1,0:T(8,128)S(1)} %get-tuple-element.40.args_6_.args_17_) | copy-start | bytes 393220
  30.7 9.4 %copy-start.14 = (f32[2,64,256]{2,1,0:T(8,128)}, f32[2,64,256]{2,1,0:T(8,128)S(1)}, u32[]{:S(2)}) copy-start(f32[2,64,256]{2,1,0:T(8,128)S(1)} %get-tuple-element.43.args_9_.args_20_) | copy-start | bytes 393220
  40.9 21.7 %all-to-all-start.1 = ((bf16[32,4,16,128]{3,2,1,0:T(8,128)(2,1)}), bf16[32,4,16,128]{3,2,1,0:T(8,128)(2,1)S(1)}, u32[]{:S(2)}, u32[]{:S(2)}) async-start(bf16[32,4,16,128]{3,2,1,0:T(8,128)(2,1)} %bitcast.18), calls=%async_computation.1 | async-start | bytes 1048576 | tf_op jit(solution)/shard_map/all_to_all | solution.py:637
  47.3 18.5 %copy-start.16 = (bf16[128,768]{1,0:T(8,128)(2,1)S(1)}, bf16[128,768]{1,0:T(8,128)(2,1)}, u32[]{:S(2)}) copy-start(bf16[128,768]{1,0:T(8,128)(2,1)} %w_qkv.3) | copy-start | bytes 589828
  47.3 18.5 %copy-start.17 = (bf16[128,512]{1,0:T(8,128)(2,1)S(1)}, bf16[128,512]{1,0:T(8,128)(2,1)}, u32[]{:S(2)}) copy-start(bf16[128,512]{1,0:T(8,128)(2,1)} %w_up.3) | copy-start | bytes 393220
  47.3 18.5 %copy-start.18 = (bf16[512,128]{1,0:T(8,128)(2,1)S(1)}, bf16[512,128]{1,0:T(8,128)(2,1)}, u32[]{:S(2)}) copy-start(bf16[512,128]{1,0:T(8,128)(2,1)} %w_down.3) | copy-start | bytes 393220
  47.3 18.5 %copy-start.19 = (bf16[256,128]{1,0:T(8,128)(2,1)S(1)}, bf16[256,128]{1,0:T(8,128)(2,1)}, u32[]{:S(2)}) copy-start(bf16[256,128]{1,0:T(8,128)(2,1)} %w_out.3) | copy-start | bytes 196612
  62.6 13.5 %all-to-all-start = ((bf16[32,2,16,128]{3,2,1,0:T(8,128)(2,1)}), bf16[32,2,16,128]{3,2,1,0:T(8,128)(2,1)S(1)}, u32[]{:S(2)}, u32[]{:S(2)}) async-start(bf16[32,2,16,128]{3,2,1,0:T(8,128)(2,1)} %bitcast.25), calls=%async_computation | async-start | bytes 524288 | tf_op jit(solution)/shard_map/all_to_all | solution.py:637
  (2 other events, 1.9 us)

commit v13 on v12

--- a/solution.py
+++ b/solution.py
@@ -414,6 +414,7 @@
         normed = layer_norm(cells).astype(BF)
         yield
         queries = jnp.dot(normed, w_qkv[:, :embed], preferred_element_type=F32).astype(BF)
+        yield
         values = jnp.dot(normed, w_qkv[:, 2 * embed :], preferred_element_type=F32).astype(BF)
         keys = lax.dot_general(keys_t[...], normed, (((1,), (1,)), ((), ())), preferred_element_type=F32)
         yield
@@ -434,15 +435,14 @@
                         preferred_element_type=F32,
                     )
                     raised[half].append(jnp.minimum(jnp.exp2(scores * (LOG2E * HDIM**-0.5)), BF_MAX).astype(BF))
-            if pair % 2:
-                yield
+            yield
         attn = []
         for half in range(2):
             part = jnp.concatenate(raised[half], axis=0)
             total = jnp.dot(part, ones[...], preferred_element_type=F32)
             guess = pl.reciprocal(total, approx=True)
             attn.append((part.astype(F32) * (guess * (2.0 - total * guess))).astype(BF))
-        yield
+            yield
         heads = []
         for half in range(2):
             column = []
@@ -453,10 +453,11 @@
                     jnp.dot(attn[half][g * group : (g + 1) * group], spread, preferred_element_type=F32).astype(BF)
                 )
             heads.append(jnp.concatenate(column, axis=0))
+            yield
         heads = jnp.concatenate(heads, axis=1)
-        yield
         attended = jnp.dot(heads, w_out[...], preferred_element_type=F32).astype(BF)
         mixed = cells + attended.astype(F32)
+        yield
         normed_two = layer_norm(mixed).astype(BF)
         yield
         up = jnp.dot(normed_two, w_up[...], preferred_element_type=F32)

time: 105 us -> 105 us (level)
  no operation moved by 1% of the time
where the time goes in v13:
time: 105 us; the launch traced here: 104 us
  Pallas kernels  45.5 us (43%)
  blocking collectives  23.2 us (22%)
  starting transfers between devices  21.7 us (21%)
  waiting for transfers between devices  7.41 us (7%)
  local copies, waits for them, and re-layouts  5.35 us (5%)
    pallas_call x4, Pallas kernels, conv_step(): pl.pallas_call(functools.partial(conv_kernel, start, rows, part, tail, re...  31.3 us
    all_to_all x1, blocking collectives, body(): lax.all_to_all(done, ('gy', 'gx'), split_axis=0, concat_axis=0, tiled=True)  23.2 us
    ppermute x4, starting transfers between devices, shifted(): return lax.ppermute(value, axis, pairs)  12.1 us
    pallas_call x2, Pallas kernels, block_step(): pl.pallas_call(block_kernel, grid=(lanes, piece_y // subs), in_specs=in_s...  9.84 us
    all_to_all x2, starting transfers between devices, body(): lax.all_to_all(sent, ('gy', 'gx'), split_axis=0, concat_axis=0, tiled=True)  9.55 us
    all_to_all x2, waiting for transfers between devices, body(): lax.all_to_all(sent, ('gy', 'gx'), split_axis=0, concat_axis=0, tiled=True)  6.52 us
    unnamed x40, local copies, waits for them, and re-layouts  5.29 us
    pallas_call x1, Pallas kernels, body(): pl.pallas_call(ring_kernel, grid=(1,), in_specs=[*(whole(array) for array...  2.21 us
  transfers between devices with their start and end apart: 6, of which 3 were waited for; matrix products, arithmetic and copies ran while one was open for 0% of the time, Pallas kernels for 27%

profile of v13, /device:TPU:1, one launch (start us, length us, event | category | flops | bytes accessed | tf_op | source)
XLA Modules:
  0.0 104.2 jit_solution(8306297031239918655)
XLA Ops:
  0.6 0.0 copy-start
  0.6 1.9 %copy-done = bf16[48,64,512]{2,1,0:T(8,128)(2,1)S(1)} copy-done((bf16[48,64,512]{2,1,0:T(8,128)(2,1)S(1)}, bf16[48,64,512]{2,1,0:T(8,128)(2,1)}, u32[]{:S(2)}) %copy-start) | copy-done | bytes 3145752
  2.5 1.1 %copy-done.2 = bf16[48,64,128]{2,1,0:T(8,128)(2,1)S(1)} copy-done((bf16[48,64,128]{2,1,0:T(8,128)(2,1)S(1)}, bf16[48,64,128]{2,1,0:T(8,128)(2,1)}, u32[]{:S(2)}) %copy-start.2) | copy-done | bytes 786456
  3.7 1.4 %copy-done.4 = f32[48,64,128]{2,1,0:T(8,128)S(1)} copy-done((f32[48,64,128]{2,1,0:T(8,128)S(1)}, f32[48,64,128]{2,1,0:T(8,128)}, u32[]{:S(2)}) %copy-start.4) | copy-done | bytes 1572888
  5.1 0.6 shard_map.105
  5.7 4.2 %collective-permute-start = (bf16[48,2,768]{2,1,0:T(2,128)(2,1)S(1)}, bf16[48,2,768]{2,1,0:T(2,128)(2,1)S(1)}, u32[]{:S(2)}, u32[]{:S(2)}) collective-permute-start(bf16[48,2,768]{2,1,0:T(2,128)(2,1)S(1)} %get-tuple-element.28), channel_id=1, source_target_pairs={{0,1},{1,2},{2,3},{4,5},{5,6},{6,7},{8,9},{9,10},{10,11},{12,13},{... | collective-permute-start | bytes 442376 | tf_op jit(solution)/shard_map/ppermute | solution.py:573
  9.9 1.3 %collective-permute-start.1 = (bf16[48,2,768]{2,1,0:T(2,128)(2,1)S(1)}, bf16[48,2,768]{2,1,0:T(2,128)(2,1)S(1)}, u32[]{:S(2)}, u32[]{:S(2)}) collective-permute-start(bf16[48,2,768]{2,1,0:T(2,128)(2,1)S(1)} %get-tuple-element.29), channel_id=1, source_target_pairs={{1,0},{2,1},{3,2},{5,4},{6,5},{7,6},{9,8},{10,9},{11,10},{13,12},{... | collective-permute-start | bytes 442376 | tf_op jit(solution)/shard_map/ppermute | solution.py:573
  11.2 5.2 %shard_map.104 = (bf16[48,64,128]{2,1,0:T(8,128)(2,1)S(1)}, f32[48,64,128]{2,1,0:T(8,128)S(1)}) custom-call(bf16[48,64,512]{2,1,0:T(8,128)(2,1)S(1)} %copy-done, bf16[48,64,128]{2,1,0:T(8,128)(2,1)S(1)} %copy-done.2, f32[48,64,128]{2,1,0:T(8,128)S(1)} %copy-done.4, f32[1,512]{1,0:T(1,128)S(1)} %bitcast.21, bf16[3456,512]{1,0:T(8,128)(2,1)S(1)} %bitcast.11), custom_call_target="tpu_custom_call" | custom-call | flops 4529848320 | bytes 6160384 | tf_op jit(solution)/shard_map/pallas_call | solution.py:262
  16.6 4.5 %collective-permute-start.2 = (bf16[2,68,768]{2,1,0:T(8,128)(2,1)S(1)}, bf16[2,68,768]{2,1,0:T(8,128)(2,1)S(1)}, u32[]{:S(2)}, u32[]{:S(2)}) collective-permute-start(bf16[2,68,768]{2,1,0:T(8,128)(2,1)S(1)} %get-tuple-element.35), channel_id=1, source_target_pairs={{0,4},{4,8},{8,12},{12,16},{16,20},{20,24},{24,28},{1,5},{5,9},{9,... | collective-permute-start | bytes 626696 | tf_op jit(solution)/shard_map/ppermute | solution.py:573
  21.2 2.1 %collective-permute-start.3 = (bf16[2,68,768]{2,1,0:T(8,128)(2,1)S(1)}, bf16[2,68,768]{2,1,0:T(8,128)(2,1)S(1)}, u32[]{:S(2)}, u32[]{:S(2)}) collective-permute-start(bf16[2,68,768]{2,1,0:T(8,128)(2,1)S(1)} %get-tuple-element.36), channel_id=1, source_target_pairs={{4,0},{8,4},{12,8},{16,12},{20,16},{24,20},{28,24},{5,1},{9,5},{13... | collective-permute-start | bytes 626696 | tf_op jit(solution)/shard_map/ppermute | solution.py:573
  23.3 4.2 %shard_map.106 = (bf16[48,64,128]{2,1,0:T(8,128)(2,1)S(1)}, f32[48,64,128]{2,1,0:T(8,128)S(1)}) custom-call(bf16[48,64,512]{2,1,0:T(8,128)(2,1)S(1)} %copy-done, bf16[48,64,128]{2,1,0:T(8,128)(2,1)S(1)} %copy-done.2, f32[48,64,128]{2,1,0:T(8,128)S(1)} %copy-done.4, f32[1,512]{1,0:T(1,128)S(1)} %bitcast.22, ...), custom_call_target="tpu_custom_call", output_to_operand_aliasing={{0}: (5, {}), {1}: (6, {})} | custom-call | flops 3623878656 | bytes 5636096 | tf_op jit(solution)/shard_map/pallas_call | solution.py:262
  27.5 0.9 collective-permute-done.3.below.args_11_.args_22_
  28.4 2.2 %shard_map.107 = (f32[4,64,128]{2,1,0:T(8,128)S(1)}, f32[4,64,128]{2,1,0:T(8,128)S(1)}, f32[4,64,128]{2,1,0:T(8,128)S(1)}, f32[4,64,128]{2,1,0:T(8,128)S(1)}, f32[2,64,256]{2,1,0:T(8,128)S(1)}) custom-call(bf16[2,68,768]{2,1,0:T(8,128)(2,1)S(1)} %collective-permute-done.2.above.args_10_.args_21_, ...), custom_call_target="tpu_custom_call" | custom-call | flops 1811939328 | bytes 3538944 | tf_op jit(solution)/shard_map/pallas_call | solution.py:606
  30.7 9.3 %shard_map.108 = (bf16[8,4,4,16,128]{4,3,2,1,0:T(8,128)(2,1)S(1)}, f32[48,64,128]{2,1,0:T(8,128)}) custom-call(bf16[48,64,512]{2,1,0:T(8,128)(2,1)S(1)} %copy-done.1, bf16[48,64,128]{2,1,0:T(8,128)(2,1)S(1)} %get-tuple-element.33.args_1_.args_3_.args_4_.args_5_, f32[48,64,128]{2,1,0:T(8,128)S(1)} %get-tuple-element.34.args_2_.args_6_, ...), custom_call_target="tpu_custom_call" | custom-call | flops 7247757312 | bytes 7733248 | tf_op jit(solution)/shard_map/pallas_call | solution.py:262
  40.1 0.8 copy-done.7
  40.9 6.4 %all-to-all-start.1 = ((bf16[32,4,16,128]{3,2,1,0:T(8,128)(2,1)}), bf16[32,4,16,128]{3,2,1,0:T(8,128)(2,1)S(1)}, u32[]{:S(2)}, u32[]{:S(2)}) async-start(bf16[32,4,16,128]{3,2,1,0:T(8,128)(2,1)} %bitcast.18), calls=%async_computation.1 | async-start | bytes 1048576 | tf_op jit(solution)/shard_map/all_to_all | solution.py:638
  47.3 12.6 %shard_map.109 = (bf16[8,4,2,16,128]{4,3,2,1,0:T(8,128)(2,1)}, f32[48,64,128]{2,1,0:T(8,128)}) custom-call(bf16[48,64,512]{2,1,0:T(8,128)(2,1)} %args_9_.1, bf16[48,64,512]{2,1,0:T(8,128)(2,1)} %args_9_.1, bf16[48,64,512]{2,1,0:T(8,128)(2,1)} %args_9_.1, bf16[48,64,128]{2,1,0:T(8,128)(2,1)} %copy-done.3, ...), custom_call_target="tpu_custom_call", output_to_operand_aliasing={{1}: (23, {})} | custom-call | flops 3623878656 | bytes 5636096 | tf_op jit(solution)/shard_map/pallas_call | solution.py:262
  59.9 2.7 %all-to-all-done.1 = bf16[32,4,16,128]{3,2,1,0:T(8,128)(2,1)S(1)} async-done(((bf16[32,4,16,128]{3,2,1,0:T(8,128)(2,1)}), bf16[32,4,16,128]{3,2,1,0:T(8,128)(2,1)S(1)}, u32[]{:S(2)}, u32[]{:S(2)}) %all-to-all-start.1) | async-done | bytes 524320 | tf_op jit(solution)/shard_map/all_to_all | solution.py:638
  62.6 3.2 %all-to-all-start = ((bf16[32,2,16,128]{3,2,1,0:T(8,128)(2,1)}), bf16[32,2,16,128]{3,2,1,0:T(8,128)(2,1)S(1)}, u32[]{:S(2)}, u32[]{:S(2)}) async-start(bf16[32,2,16,128]{3,2,1,0:T(8,128)(2,1)} %bitcast.25), calls=%async_computation | async-start | bytes 524288 | tf_op jit(solution)/shard_map/all_to_all | solution.py:638
  65.8 6.5 %shard_map.110.rest_0_ = bf16[8,1,4,6,16,128]{5,4,3,2,1,0:T(8,128)(2,1)S(1)} custom-call(bf16[8,1,4,4,16,128]{5,4,3,2,1,0:T(8,128)(2,1)S(1)} %bitcast.17, bf16[128,768]{1,0:T(8,128)(2,1)S(1)} %copy-done.16, bf16[256,128]{1,0:T(8,128)(2,1)S(1)} %copy-done.19, bf16[128,512]{1,0:T(8,128)(2,1)S(1)} %copy-done.17, bf16[512,128]{1,0:T(8,128)(2,1)S(1)} %copy-done.18), custom_call_target="tpu_custom_call" | custom-call | flops 6144000000 | bytes 1848576 | tf_op jit(solution)/shard_map/pallas_call | solution.py:498
  72.3 3.8 %all-to-all-done = bf16[32,2,16,128]{3,2,1,0:T(8,128)(2,1)S(1)} async-done(((bf16[32,2,16,128]{3,2,1,0:T(8,128)(2,1)}), bf16[32,2,16,128]{3,2,1,0:T(8,128)(2,1)S(1)}, u32[]{:S(2)}, u32[]{:S(2)}) %all-to-all-start) | async-done | bytes 262176 | tf_op jit(solution)/shard_map/all_to_all | solution.py:638
  76.1 3.4 %shard_map.111 = bf16[8,1,4,6,16,128]{5,4,3,2,1,0:T(8,128)(2,1)S(1)} custom-call(bf16[8,1,4,2,16,128]{5,4,3,2,1,0:T(8,128)(2,1)S(1)} %bitcast.19, bf16[128,768]{1,0:T(8,128)(2,1)S(1)} %copy-done.16, bf16[256,128]{1,0:T(8,128)(2,1)S(1)} %copy-done.19, bf16[128,512]{1,0:T(8,128)(2,1)S(1)} %copy-done.17, ...), custom_call_target="tpu_custom_call", output_to_operand_aliasing={{}: (5, {})} | custom-call | flops 3072000000 | bytes 1324288 | tf_op jit(solution)/shard_map/pallas_call | solution.py:498
  79.5 23.2 %all_to_all.15 = bf16[32,6,16,128]{3,2,1,0:T(8,128)(2,1)S(1)} all-to-all(bf16[32,6,16,128]{3,2,1,0:T(8,128)(2,1)S(1)} %bitcast.16), channel_id=1, replica_groups=mesh['gy'=8,'gx'=4] {'gy','gx'}, dimensions={0} | all-to-all | bytes 1572864 | tf_op jit(solution)/shard_map/all_to_all | solution.py:645
  102.7 1.5 %shard_map.112 = bf16[48,64,128]{2,1,0:T(8,128)(2,1)} custom-call(bf16[8,4,6,16,128]{4,3,2,1,0:T(8,128)(2,1)S(1)} %bitcast.15), custom_call_target="tpu_custom_call" | custom-call | bytes 1572864 | tf_op jit(solution)/shard_map/pallas_call | solution.py:544
  (43 shorter events, 0.2 us)
Async XLA Ops:
  0.6 1.9 %copy-start = (bf16[48,64,512]{2,1,0:T(8,128)(2,1)S(1)}, bf16[48,64,512]{2,1,0:T(8,128)(2,1)}, u32[]{:S(2)}) copy-start(bf16[48,64,512]{2,1,0:T(8,128)(2,1)} %args_9_.1) | copy-start | bytes 9437188
  3.7 1.4 %copy-start.4 = (f32[48,64,128]{2,1,0:T(8,128)S(1)}, f32[48,64,128]{2,1,0:T(8,128)}, u32[]{:S(2)}) copy-start(f32[48,64,128]{2,1,0:T(8,128)} %args_13_.1) | copy-start | bytes 4718596
  5.1 6.1 %copy-start.5 = (bf16[3,3,384,512]{3,2,1,0:T(8,128)(2,1)S(1)}, bf16[3,3,384,512]{3,2,1,0:T(8,128)(2,1)}, u32[]{:S(2)}) copy-start(bf16[3,3,384,512]{3,2,1,0:T(8,128)(2,1)} %param.12) | copy-start | bytes 10616836
  5.1 6.1 %copy-start.15 = (f32[512]{0:T(512)S(1)}, f32[512]{0:T(512)}, u32[]{:S(2)}) copy-start(f32[512]{0:T(512)} %param.13) | copy-start | bytes 6148
  5.7 10.8 %collective-permute-start = (bf16[48,2,768]{2,1,0:T(2,128)(2,1)S(1)}, bf16[48,2,768]{2,1,0:T(2,128)(2,1)S(1)}, u32[]{:S(2)}, u32[]{:S(2)}) collective-permute-start(bf16[48,2,768]{2,1,0:T(2,128)(2,1)S(1)} %get-tuple-element.28), channel_id=1, source_target_pairs={{0,1},{1,2},{2,3},{4,5},{5,6},{6,7},{8,9},{9,10},{10,11},{12,13},{... | collective-permute-start | bytes 442376 | tf_op jit(solution)/shard_map/ppermute | solution.py:573
  9.9 6.6 %collective-permute-start.1 = (bf16[48,2,768]{2,1,0:T(2,128)(2,1)S(1)}, bf16[48,2,768]{2,1,0:T(2,128)(2,1)S(1)}, u32[]{:S(2)}, u32[]{:S(2)}) collective-permute-start(bf16[48,2,768]{2,1,0:T(2,128)(2,1)S(1)} %get-tuple-element.29), channel_id=1, source_target_pairs={{1,0},{2,1},{3,2},{5,4},{6,5},{7,6},{9,8},{10,9},{11,10},{13,12},{... | collective-permute-start | bytes 442376 | tf_op jit(solution)/shard_map/ppermute | solution.py:573
  16.6 10.9 %collective-permute-start.2 = (bf16[2,68,768]{2,1,0:T(8,128)(2,1)S(1)}, bf16[2,68,768]{2,1,0:T(8,128)(2,1)S(1)}, u32[]{:S(2)}, u32[]{:S(2)}) collective-permute-start(bf16[2,68,768]{2,1,0:T(8,128)(2,1)S(1)} %get-tuple-element.35), channel_id=1, source_target_pairs={{0,4},{4,8},{8,12},{12,16},{16,20},{20,24},{24,28},{1,5},{5,9},{9,... | collective-permute-start | bytes 626696 | tf_op jit(solution)/shard_map/ppermute | solution.py:573
  21.2 7.3 %collective-permute-start.3 = (bf16[2,68,768]{2,1,0:T(8,128)(2,1)S(1)}, bf16[2,68,768]{2,1,0:T(8,128)(2,1)S(1)}, u32[]{:S(2)}, u32[]{:S(2)}) collective-permute-start(bf16[2,68,768]{2,1,0:T(8,128)(2,1)S(1)} %get-tuple-element.36), channel_id=1, source_target_pairs={{4,0},{8,4},{12,8},{16,12},{20,16},{24,20},{28,24},{5,1},{9,5},{13... | collective-permute-start | bytes 626696 | tf_op jit(solution)/shard_map/ppermute | solution.py:573
  27.5 3.2 %copy-start.3 = (bf16[48,64,128]{2,1,0:T(8,128)(2,1)}, bf16[48,64,128]{2,1,0:T(8,128)(2,1)S(1)}, u32[]{:S(2)}) copy-start(bf16[48,64,128]{2,1,0:T(8,128)(2,1)S(1)} %get-tuple-element.33.args_1_.args_3_.args_4_.args_5_) | copy-start | bytes 2359300
  27.5 3.2 %copy-start.6 = (f32[48,64,128]{2,1,0:T(8,128)}, f32[48,64,128]{2,1,0:T(8,128)S(1)}, u32[]{:S(2)}) copy-start(f32[48,64,128]{2,1,0:T(8,128)S(1)} %get-tuple-element.34.args_2_.args_6_) | copy-start | bytes 4718596
  27.5 3.2 %copy-start.8 = (bf16[2,68,768]{2,1,0:T(8,128)(2,1)}, bf16[2,68,768]{2,1,0:T(8,128)(2,1)S(1)}, u32[]{:S(2)}) copy-start(bf16[2,68,768]{2,1,0:T(8,128)(2,1)S(1)} %collective-permute-done.2.above.args_10_.args_21_) | copy-start | bytes 626692
  28.4 2.3 %copy-start.9 = (bf16[2,68,768]{2,1,0:T(8,128)(2,1)}, bf16[2,68,768]{2,1,0:T(8,128)(2,1)S(1)}, u32[]{:S(2)}) copy-start(bf16[2,68,768]{2,1,0:T(8,128)(2,1)S(1)} %collective-permute-done.3.below.args_11_.args_22_) | copy-start | bytes 626692
  28.4 2.3 %copy-start.1 = (bf16[48,64,512]{2,1,0:T(8,128)(2,1)S(1)}, bf16[48,64,512]{2,1,0:T(8,128)(2,1)}, u32[]{:S(2)}) copy-start(bf16[48,64,512]{2,1,0:T(8,128)(2,1)} %args_9_.1) | copy-start | bytes 9437188
  30.6 9.4 %copy-start.10 = (f32[4,64,128]{2,1,0:T(8,128)}, f32[4,64,128]{2,1,0:T(8,128)S(1)}, u32[]{:S(2)}) copy-start(f32[4,64,128]{2,1,0:T(8,128)S(1)} %get-tuple-element.41.args_7_.args_18_) | copy-start | bytes 393220
  30.7 9.4 %copy-start.11 = (f32[4,64,128]{2,1,0:T(8,128)}, f32[4,64,128]{2,1,0:T(8,128)S(1)}, u32[]{:S(2)}) copy-start(f32[4,64,128]{2,1,0:T(8,128)S(1)} %get-tuple-element.42.args_8_.args_19_) | copy-start | bytes 393220
  30.7 9.4 %copy-start.12 = (f32[4,64,128]{2,1,0:T(8,128)}, f32[4,64,128]{2,1,0:T(8,128)S(1)}, u32[]{:S(2)}) copy-start(f32[4,64,128]{2,1,0:T(8,128)S(1)} %get-tuple-element.39.args_5_.args_16_) | copy-start | bytes 393220
  30.7 9.4 %copy-start.13 = (f32[4,64,128]{2,1,0:T(8,128)}, f32[4,64,128]{2,1,0:T(8,128)S(1)}, u32[]{:S(2)}) copy-start(f32[4,64,128]{2,1,0:T(8,128)S(1)} %get-tuple-element.40.args_6_.args_17_) | copy-start | bytes 393220
  30.7 9.4 %copy-start.14 = (f32[2,64,256]{2,1,0:T(8,128)}, f32[2,64,256]{2,1,0:T(8,128)S(1)}, u32[]{:S(2)}) copy-start(f32[2,64,256]{2,1,0:T(8,128)S(1)} %get-tuple-element.43.args_9_.args_20_) | copy-start | bytes 393220
  40.9 21.7 %all-to-all-start.1 = ((bf16[32,4,16,128]{3,2,1,0:T(8,128)(2,1)}), bf16[32,4,16,128]{3,2,1,0:T(8,128)(2,1)S(1)}, u32[]{:S(2)}, u32[]{:S(2)}) async-start(bf16[32,4,16,128]{3,2,1,0:T(8,128)(2,1)} %bitcast.18), calls=%async_computation.1 | async-start | bytes 1048576 | tf_op jit(solution)/shard_map/all_to_all | solution.py:638
  47.3 18.5 %copy-start.16 = (bf16[128,768]{1,0:T(8,128)(2,1)S(1)}, bf16[128,768]{1,0:T(8,128)(2,1)}, u32[]{:S(2)}) copy-start(bf16[128,768]{1,0:T(8,128)(2,1)} %w_qkv.3) | copy-start | bytes 589828
  47.3 18.5 %copy-start.17 = (bf16[128,512]{1,0:T(8,128)(2,1)S(1)}, bf16[128,512]{1,0:T(8,128)(2,1)}, u32[]{:S(2)}) copy-start(bf16[128,512]{1,0:T(8,128)(2,1)} %w_up.3) | copy-start | bytes 393220
  47.3 18.5 %copy-start.18 = (bf16[512,128]{1,0:T(8,128)(2,1)S(1)}, bf16[512,128]{1,0:T(8,128)(2,1)}, u32[]{:S(2)}) copy-start(bf16[512,128]{1,0:T(8,128)(2,1)} %w_down.3) | copy-start | bytes 393220
  47.3 18.5 %copy-start.19 = (bf16[256,128]{1,0:T(8,128)(2,1)S(1)}, bf16[256,128]{1,0:T(8,128)(2,1)}, u32[]{:S(2)}) copy-start(bf16[256,128]{1,0:T(8,128)(2,1)} %w_out.3) | copy-start | bytes 196612
  62.6 13.5 %all-to-all-start = ((bf16[32,2,16,128]{3,2,1,0:T(8,128)(2,1)}), bf16[32,2,16,128]{3,2,1,0:T(8,128)(2,1)S(1)}, u32[]{:S(2)}, u32[]{:S(2)}) async-start(bf16[32,2,16,128]{3,2,1,0:T(8,128)(2,1)} %bitcast.25), calls=%async_computation | async-start | bytes 524288 | tf_op jit(solution)/shard_map/all_to_all | solution.py:638
  (2 other events, 1.9 us)

commit v14 on v13

--- a/solution.py
+++ b/solution.py
@@ -584,7 +584,7 @@
     ahead = rows - max(size for size in range(1, 13) if rows % size == 0 and rows - size > shares[0] * devices_y)
     tile_shapes = (jax.ShapeDtypeStruct((rows, cols, width), BF), jax.ShapeDtypeStruct((rows, cols, width), F32))
     carry = ()
-    half = -(-ahead // 8) * 4
+    half = -(-ahead // 6) * 4
     for start, extent in ((0, half), (half, ahead - half)):
         spec = pl.BlockSpec(memory_space=pltpu.VMEM)
         if carry:

time: 105 us -> 105 us (level)
  no operation moved by 1% of the time
where the time goes in v14:
time: 105 us
  Pallas kernels  45.5 us (43%)
  blocking collectives  23.2 us (22%)
  starting transfers between devices  21.4 us (20%)
  waiting for transfers between devices  8.43 us (8%)
  local copies, waits for them, and re-layouts  5.35 us (5%)
    pallas_call x4, Pallas kernels, conv_step(): pl.pallas_call(functools.partial(conv_kernel, start, rows, part, tail, re...  31.3 us
    all_to_all x1, blocking collectives, body(): lax.all_to_all(done, ('gy', 'gx'), split_axis=0, concat_axis=0, tiled=True)  23.2 us
    ppermute x4, starting transfers between devices, shifted(): return lax.ppermute(value, axis, pairs)  11.5 us
    all_to_all x2, starting transfers between devices, body(): lax.all_to_all(sent, ('gy', 'gx'), split_axis=0, concat_axis=0, tiled=True)  9.87 us
    pallas_call x2, Pallas kernels, block_step(): pl.pallas_call(block_kernel, grid=(lanes, piece_y // subs), in_specs=in_s...  9.83 us
    all_to_all x2, waiting for transfers between devices, body(): lax.all_to_all(sent, ('gy', 'gx'), split_axis=0, concat_axis=0, tiled=True)  6.53 us
    unnamed x40, local copies, waits for them, and re-layouts  5.29 us
    pallas_call x1, Pallas kernels, body(): pl.pallas_call(ring_kernel, grid=(1,), in_specs=[*(whole(array) for array...  2.21 us
  transfers between devices with their start and end apart: 6, of which 3 were waited for; matrix products, arithmetic and copies ran while one was open for 0% of the time, Pallas kernels for 27%

profile of v14, /device:TPU:1, one launch (start us, length us, event | category | flops | bytes accessed | tf_op | source)
XLA Modules:
  0.0 105.0 jit_solution(14427469928115030819)
XLA Ops:
  0.6 0.0 copy-start
  0.6 1.9 %copy-done = bf16[48,64,512]{2,1,0:T(8,128)(2,1)S(1)} copy-done((bf16[48,64,512]{2,1,0:T(8,128)(2,1)S(1)}, bf16[48,64,512]{2,1,0:T(8,128)(2,1)}, u32[]{:S(2)}) %copy-start) | copy-done | bytes 3145752
  2.5 1.1 %copy-done.2 = bf16[48,64,128]{2,1,0:T(8,128)(2,1)S(1)} copy-done((bf16[48,64,128]{2,1,0:T(8,128)(2,1)S(1)}, bf16[48,64,128]{2,1,0:T(8,128)(2,1)}, u32[]{:S(2)}) %copy-start.2) | copy-done | bytes 786456
  3.7 1.4 %copy-done.3 = f32[48,64,128]{2,1,0:T(8,128)S(1)} copy-done((f32[48,64,128]{2,1,0:T(8,128)S(1)}, f32[48,64,128]{2,1,0:T(8,128)}, u32[]{:S(2)}) %copy-start.3) | copy-done | bytes 1572888
  5.1 0.6 shard_map.105
  5.7 4.2 %collective-permute-start = (bf16[48,2,768]{2,1,0:T(2,128)(2,1)S(1)}, bf16[48,2,768]{2,1,0:T(2,128)(2,1)S(1)}, u32[]{:S(2)}, u32[]{:S(2)}) collective-permute-start(bf16[48,2,768]{2,1,0:T(2,128)(2,1)S(1)} %get-tuple-element.28), channel_id=1, source_target_pairs={{0,1},{1,2},{2,3},{4,5},{5,6},{6,7},{8,9},{9,10},{10,11},{12,13},{... | collective-permute-start | bytes 442376 | tf_op jit(solution)/shard_map/ppermute | solution.py:573
  9.9 1.3 %collective-permute-start.1 = (bf16[48,2,768]{2,1,0:T(2,128)(2,1)S(1)}, bf16[48,2,768]{2,1,0:T(2,128)(2,1)S(1)}, u32[]{:S(2)}, u32[]{:S(2)}) collective-permute-start(bf16[48,2,768]{2,1,0:T(2,128)(2,1)S(1)} %get-tuple-element.29), channel_id=1, source_target_pairs={{1,0},{2,1},{3,2},{5,4},{6,5},{7,6},{9,8},{10,9},{11,10},{13,12},{... | collective-permute-start | bytes 442376 | tf_op jit(solution)/shard_map/ppermute | solution.py:573
  11.2 6.3 %shard_map.104 = (bf16[48,64,128]{2,1,0:T(8,128)(2,1)S(1)}, f32[48,64,128]{2,1,0:T(8,128)S(1)}) custom-call(bf16[48,64,512]{2,1,0:T(8,128)(2,1)S(1)} %copy-done, bf16[48,64,128]{2,1,0:T(8,128)(2,1)S(1)} %copy-done.2, f32[48,64,128]{2,1,0:T(8,128)S(1)} %copy-done.3, f32[1,512]{1,0:T(1,128)S(1)} %bitcast.21, bf16[3456,512]{1,0:T(8,128)(2,1)S(1)} %bitcast.11), custom_call_target="tpu_custom_call" | custom-call | flops 5435817984 | bytes 6684672 | tf_op jit(solution)/shard_map/pallas_call | solution.py:262
  17.7 4.0 %collective-permute-start.2 = (bf16[2,68,768]{2,1,0:T(8,128)(2,1)S(1)}, bf16[2,68,768]{2,1,0:T(8,128)(2,1)S(1)}, u32[]{:S(2)}, u32[]{:S(2)}) collective-permute-start(bf16[2,68,768]{2,1,0:T(8,128)(2,1)S(1)} %get-tuple-element.35), channel_id=1, source_target_pairs={{0,4},{4,8},{8,12},{12,16},{16,20},{20,24},{24,28},{1,5},{5,9},{9,... | collective-permute-start | bytes 626696 | tf_op jit(solution)/shard_map/ppermute | solution.py:573
  21.6 2.1 %collective-permute-start.3 = (bf16[2,68,768]{2,1,0:T(8,128)(2,1)S(1)}, bf16[2,68,768]{2,1,0:T(8,128)(2,1)S(1)}, u32[]{:S(2)}, u32[]{:S(2)}) collective-permute-start(bf16[2,68,768]{2,1,0:T(8,128)(2,1)S(1)} %get-tuple-element.36), channel_id=1, source_target_pairs={{4,0},{8,4},{12,8},{16,12},{20,16},{24,20},{28,24},{5,1},{9,5},{13... | collective-permute-start | bytes 626696 | tf_op jit(solution)/shard_map/ppermute | solution.py:573
  23.7 3.2 %shard_map.106 = (bf16[48,64,128]{2,1,0:T(8,128)(2,1)S(1)}, f32[48,64,128]{2,1,0:T(8,128)S(1)}) custom-call(bf16[48,64,512]{2,1,0:T(8,128)(2,1)S(1)} %copy-done, bf16[48,64,128]{2,1,0:T(8,128)(2,1)S(1)} %copy-done.2, f32[48,64,128]{2,1,0:T(8,128)S(1)} %copy-done.3, f32[1,512]{1,0:T(1,128)S(1)} %bitcast.22, ...), custom_call_target="tpu_custom_call", output_to_operand_aliasing={{0}: (5, {}), {1}: (6, {})} | custom-call | flops 2717908992 | bytes 5111808 | tf_op jit(solution)/shard_map/pallas_call | solution.py:262
  27.0 1.9 %collective-permute-done.3.below.args_11_.args_22_ = bf16[2,68,768]{2,1,0:T(8,128)(2,1)S(1)} collective-permute-done((bf16[2,68,768]{2,1,0:T(8,128)(2,1)S(1)}, bf16[2,68,768]{2,1,0:T(8,128)(2,1)S(1)}, u32[]{:S(2)}, u32[]{:S(2)}) %collective-permute-start.3) | collective-permute-done | bytes 208928 | tf_op jit(solution)/shard_map/ppermute | solution.py:573
  28.9 2.2 %shard_map.107 = (f32[4,64,128]{2,1,0:T(8,128)S(1)}, f32[4,64,128]{2,1,0:T(8,128)S(1)}, f32[4,64,128]{2,1,0:T(8,128)S(1)}, f32[4,64,128]{2,1,0:T(8,128)S(1)}, f32[2,64,256]{2,1,0:T(8,128)S(1)}) custom-call(bf16[2,68,768]{2,1,0:T(8,128)(2,1)S(1)} %collective-permute-done.2.above.args_10_.args_21_, ...), custom_call_target="tpu_custom_call" | custom-call | flops 1811939328 | bytes 3538944 | tf_op jit(solution)/shard_map/pallas_call | solution.py:606
  31.2 9.3 %shard_map.108 = (bf16[8,4,4,16,128]{4,3,2,1,0:T(8,128)(2,1)S(1)}, f32[48,64,128]{2,1,0:T(8,128)}) custom-call(bf16[48,64,512]{2,1,0:T(8,128)(2,1)S(1)} %copy-done.1, bf16[48,64,128]{2,1,0:T(8,128)(2,1)S(1)} %get-tuple-element.33.args_1_.args_3_.args_4_.args_5_, f32[48,64,128]{2,1,0:T(8,128)S(1)} %get-tuple-element.34.args_2_.args_6_, ...), custom_call_target="tpu_custom_call" | custom-call | flops 7247757312 | bytes 7733248 | tf_op jit(solution)/shard_map/pallas_call | solution.py:262
  40.6 0.8 copy-done.7
  41.4 6.7 %all-to-all-start.1 = ((bf16[32,4,16,128]{3,2,1,0:T(8,128)(2,1)}), bf16[32,4,16,128]{3,2,1,0:T(8,128)(2,1)S(1)}, u32[]{:S(2)}, u32[]{:S(2)}) async-start(bf16[32,4,16,128]{3,2,1,0:T(8,128)(2,1)} %bitcast.18), calls=%async_computation.1 | async-start | bytes 1048576 | tf_op jit(solution)/shard_map/all_to_all | solution.py:638
  48.1 12.5 %shard_map.109 = (bf16[8,4,2,16,128]{4,3,2,1,0:T(8,128)(2,1)}, f32[48,64,128]{2,1,0:T(8,128)}) custom-call(bf16[48,64,512]{2,1,0:T(8,128)(2,1)} %args_9_.1, bf16[48,64,512]{2,1,0:T(8,128)(2,1)} %args_9_.1, bf16[48,64,512]{2,1,0:T(8,128)(2,1)} %args_9_.1, bf16[48,64,128]{2,1,0:T(8,128)(2,1)} %copy-done.5, ...), custom_call_target="tpu_custom_call", output_to_operand_aliasing={{1}: (23, {})} | custom-call | flops 3623878656 | bytes 5636096 | tf_op jit(solution)/shard_map/pallas_call | solution.py:262
  60.7 2.7 %all-to-all-done.1 = bf16[32,4,16,128]{3,2,1,0:T(8,128)(2,1)S(1)} async-done(((bf16[32,4,16,128]{3,2,1,0:T(8,128)(2,1)}), bf16[32,4,16,128]{3,2,1,0:T(8,128)(2,1)S(1)}, u32[]{:S(2)}, u32[]{:S(2)}) %all-to-all-start.1) | async-done | bytes 524320 | tf_op jit(solution)/shard_map/all_to_all | solution.py:638
  63.4 3.2 %all-to-all-start = ((bf16[32,2,16,128]{3,2,1,0:T(8,128)(2,1)}), bf16[32,2,16,128]{3,2,1,0:T(8,128)(2,1)S(1)}, u32[]{:S(2)}, u32[]{:S(2)}) async-start(bf16[32,2,16,128]{3,2,1,0:T(8,128)(2,1)} %bitcast.25), calls=%async_computation | async-start | bytes 524288 | tf_op jit(solution)/shard_map/all_to_all | solution.py:638
  66.6 6.5 %shard_map.110.rest_0_ = bf16[8,1,4,6,16,128]{5,4,3,2,1,0:T(8,128)(2,1)S(1)} custom-call(bf16[8,1,4,4,16,128]{5,4,3,2,1,0:T(8,128)(2,1)S(1)} %bitcast.17, bf16[128,768]{1,0:T(8,128)(2,1)S(1)} %copy-done.16, bf16[256,128]{1,0:T(8,128)(2,1)S(1)} %copy-done.19, bf16[128,512]{1,0:T(8,128)(2,1)S(1)} %copy-done.17, bf16[512,128]{1,0:T(8,128)(2,1)S(1)} %copy-done.18), custom_call_target="tpu_custom_call" | custom-call | flops 6144000000 | bytes 1848576 | tf_op jit(solution)/shard_map/pallas_call | solution.py:498
  73.0 3.8 %all-to-all-done = bf16[32,2,16,128]{3,2,1,0:T(8,128)(2,1)S(1)} async-done(((bf16[32,2,16,128]{3,2,1,0:T(8,128)(2,1)}), bf16[32,2,16,128]{3,2,1,0:T(8,128)(2,1)S(1)}, u32[]{:S(2)}, u32[]{:S(2)}) %all-to-all-start) | async-done | bytes 262176 | tf_op jit(solution)/shard_map/all_to_all | solution.py:638
  76.9 3.4 %shard_map.111 = bf16[8,1,4,6,16,128]{5,4,3,2,1,0:T(8,128)(2,1)S(1)} custom-call(bf16[8,1,4,2,16,128]{5,4,3,2,1,0:T(8,128)(2,1)S(1)} %bitcast.19, bf16[128,768]{1,0:T(8,128)(2,1)S(1)} %copy-done.16, bf16[256,128]{1,0:T(8,128)(2,1)S(1)} %copy-done.19, bf16[128,512]{1,0:T(8,128)(2,1)S(1)} %copy-done.17, ...), custom_call_target="tpu_custom_call", output_to_operand_aliasing={{}: (5, {})} | custom-call | flops 3072000000 | bytes 1324288 | tf_op jit(solution)/shard_map/pallas_call | solution.py:498
  80.3 23.2 %all_to_all.15 = bf16[32,6,16,128]{3,2,1,0:T(8,128)(2,1)S(1)} all-to-all(bf16[32,6,16,128]{3,2,1,0:T(8,128)(2,1)S(1)} %bitcast.16), channel_id=1, replica_groups=mesh['gy'=8,'gx'=4] {'gy','gx'}, dimensions={0} | all-to-all | bytes 1572864 | tf_op jit(solution)/shard_map/all_to_all | solution.py:645
  103.5 1.5 %shard_map.112 = bf16[48,64,128]{2,1,0:T(8,128)(2,1)} custom-call(bf16[8,4,6,16,128]{4,3,2,1,0:T(8,128)(2,1)S(1)} %bitcast.15), custom_call_target="tpu_custom_call" | custom-call | bytes 1572864 | tf_op jit(solution)/shard_map/pallas_call | solution.py:544
  (43 shorter events, 0.2 us)
Async XLA Ops:
  0.6 1.9 %copy-start = (bf16[48,64,512]{2,1,0:T(8,128)(2,1)S(1)}, bf16[48,64,512]{2,1,0:T(8,128)(2,1)}, u32[]{:S(2)}) copy-start(bf16[48,64,512]{2,1,0:T(8,128)(2,1)} %args_9_.1) | copy-start | bytes 9437188
  3.7 1.4 %copy-start.3 = (f32[48,64,128]{2,1,0:T(8,128)S(1)}, f32[48,64,128]{2,1,0:T(8,128)}, u32[]{:S(2)}) copy-start(f32[48,64,128]{2,1,0:T(8,128)} %args_13_.1) | copy-start | bytes 4718596
  5.1 6.1 %copy-start.4 = (bf16[3,3,384,512]{3,2,1,0:T(8,128)(2,1)S(1)}, bf16[3,3,384,512]{3,2,1,0:T(8,128)(2,1)}, u32[]{:S(2)}) copy-start(bf16[3,3,384,512]{3,2,1,0:T(8,128)(2,1)} %param.12) | copy-start | bytes 10616836
  5.1 6.1 %copy-start.15 = (f32[512]{0:T(512)S(1)}, f32[512]{0:T(512)}, u32[]{:S(2)}) copy-start(f32[512]{0:T(512)} %param.13) | copy-start | bytes 6148
  5.7 11.8 %collective-permute-start = (bf16[48,2,768]{2,1,0:T(2,128)(2,1)S(1)}, bf16[48,2,768]{2,1,0:T(2,128)(2,1)S(1)}, u32[]{:S(2)}, u32[]{:S(2)}) collective-permute-start(bf16[48,2,768]{2,1,0:T(2,128)(2,1)S(1)} %get-tuple-element.28), channel_id=1, source_target_pairs={{0,1},{1,2},{2,3},{4,5},{5,6},{6,7},{8,9},{9,10},{10,11},{12,13},{... | collective-permute-start | bytes 442376 | tf_op jit(solution)/shard_map/ppermute | solution.py:573
  9.9 7.6 %collective-permute-start.1 = (bf16[48,2,768]{2,1,0:T(2,128)(2,1)S(1)}, bf16[48,2,768]{2,1,0:T(2,128)(2,1)S(1)}, u32[]{:S(2)}, u32[]{:S(2)}) collective-permute-start(bf16[48,2,768]{2,1,0:T(2,128)(2,1)S(1)} %get-tuple-element.29), channel_id=1, source_target_pairs={{1,0},{2,1},{3,2},{5,4},{6,5},{7,6},{9,8},{10,9},{11,10},{13,12},{... | collective-permute-start | bytes 442376 | tf_op jit(solution)/shard_map/ppermute | solution.py:573
  17.7 9.3 %collective-permute-start.2 = (bf16[2,68,768]{2,1,0:T(8,128)(2,1)S(1)}, bf16[2,68,768]{2,1,0:T(8,128)(2,1)S(1)}, u32[]{:S(2)}, u32[]{:S(2)}) collective-permute-start(bf16[2,68,768]{2,1,0:T(8,128)(2,1)S(1)} %get-tuple-element.35), channel_id=1, source_target_pairs={{0,4},{4,8},{8,12},{12,16},{16,20},{20,24},{24,28},{1,5},{5,9},{9,... | collective-permute-start | bytes 626696 | tf_op jit(solution)/shard_map/ppermute | solution.py:573
  21.6 7.3 %collective-permute-start.3 = (bf16[2,68,768]{2,1,0:T(8,128)(2,1)S(1)}, bf16[2,68,768]{2,1,0:T(8,128)(2,1)S(1)}, u32[]{:S(2)}, u32[]{:S(2)}) collective-permute-start(bf16[2,68,768]{2,1,0:T(8,128)(2,1)S(1)} %get-tuple-element.36), channel_id=1, source_target_pairs={{4,0},{8,4},{12,8},{16,12},{20,16},{24,20},{28,24},{5,1},{9,5},{13... | collective-permute-start | bytes 626696 | tf_op jit(solution)/shard_map/ppermute | solution.py:573
  27.0 4.2 %copy-start.5 = (bf16[48,64,128]{2,1,0:T(8,128)(2,1)}, bf16[48,64,128]{2,1,0:T(8,128)(2,1)S(1)}, u32[]{:S(2)}) copy-start(bf16[48,64,128]{2,1,0:T(8,128)(2,1)S(1)} %get-tuple-element.33.args_1_.args_3_.args_4_.args_5_) | copy-start | bytes 2359300
  27.0 4.2 %copy-start.6 = (f32[48,64,128]{2,1,0:T(8,128)}, f32[48,64,128]{2,1,0:T(8,128)S(1)}, u32[]{:S(2)}) copy-start(f32[48,64,128]{2,1,0:T(8,128)S(1)} %get-tuple-element.34.args_2_.args_6_) | copy-start | bytes 4718596
  27.0 4.2 %copy-start.8 = (bf16[2,68,768]{2,1,0:T(8,128)(2,1)}, bf16[2,68,768]{2,1,0:T(8,128)(2,1)S(1)}, u32[]{:S(2)}) copy-start(bf16[2,68,768]{2,1,0:T(8,128)(2,1)S(1)} %collective-permute-done.2.above.args_10_.args_21_) | copy-start | bytes 626692
  28.9 2.3 %copy-start.9 = (bf16[2,68,768]{2,1,0:T(8,128)(2,1)}, bf16[2,68,768]{2,1,0:T(8,128)(2,1)S(1)}, u32[]{:S(2)}) copy-start(bf16[2,68,768]{2,1,0:T(8,128)(2,1)S(1)} %collective-permute-done.3.below.args_11_.args_22_) | copy-start | bytes 626692
  28.9 2.3 %copy-start.1 = (bf16[48,64,512]{2,1,0:T(8,128)(2,1)S(1)}, bf16[48,64,512]{2,1,0:T(8,128)(2,1)}, u32[]{:S(2)}) copy-start(bf16[48,64,512]{2,1,0:T(8,128)(2,1)} %args_9_.1) | copy-start | bytes 9437188
  31.1 9.4 %copy-start.10 = (f32[4,64,128]{2,1,0:T(8,128)}, f32[4,64,128]{2,1,0:T(8,128)S(1)}, u32[]{:S(2)}) copy-start(f32[4,64,128]{2,1,0:T(8,128)S(1)} %get-tuple-element.41.args_7_.args_18_) | copy-start | bytes 393220
  31.1 9.4 %copy-start.11 = (f32[4,64,128]{2,1,0:T(8,128)}, f32[4,64,128]{2,1,0:T(8,128)S(1)}, u32[]{:S(2)}) copy-start(f32[4,64,128]{2,1,0:T(8,128)S(1)} %get-tuple-element.42.args_8_.args_19_) | copy-start | bytes 393220
  31.1 9.4 %copy-start.12 = (f32[4,64,128]{2,1,0:T(8,128)}, f32[4,64,128]{2,1,0:T(8,128)S(1)}, u32[]{:S(2)}) copy-start(f32[4,64,128]{2,1,0:T(8,128)S(1)} %get-tuple-element.39.args_5_.args_16_) | copy-start | bytes 393220
  31.1 9.4 %copy-start.13 = (f32[4,64,128]{2,1,0:T(8,128)}, f32[4,64,128]{2,1,0:T(8,128)S(1)}, u32[]{:S(2)}) copy-start(f32[4,64,128]{2,1,0:T(8,128)S(1)} %get-tuple-element.40.args_6_.args_17_) | copy-start | bytes 393220
  31.1 9.4 %copy-start.14 = (f32[2,64,256]{2,1,0:T(8,128)}, f32[2,64,256]{2,1,0:T(8,128)S(1)}, u32[]{:S(2)}) copy-start(f32[2,64,256]{2,1,0:T(8,128)S(1)} %get-tuple-element.43.args_9_.args_20_) | copy-start | bytes 393220
  41.4 22.0 %all-to-all-start.1 = ((bf16[32,4,16,128]{3,2,1,0:T(8,128)(2,1)}), bf16[32,4,16,128]{3,2,1,0:T(8,128)(2,1)S(1)}, u32[]{:S(2)}, u32[]{:S(2)}) async-start(bf16[32,4,16,128]{3,2,1,0:T(8,128)(2,1)} %bitcast.18), calls=%async_computation.1 | async-start | bytes 1048576 | tf_op jit(solution)/shard_map/all_to_all | solution.py:638
  48.1 18.5 %copy-start.16 = (bf16[128,768]{1,0:T(8,128)(2,1)S(1)}, bf16[128,768]{1,0:T(8,128)(2,1)}, u32[]{:S(2)}) copy-start(bf16[128,768]{1,0:T(8,128)(2,1)} %w_qkv.3) | copy-start | bytes 589828
  48.1 18.5 %copy-start.17 = (bf16[128,512]{1,0:T(8,128)(2,1)S(1)}, bf16[128,512]{1,0:T(8,128)(2,1)}, u32[]{:S(2)}) copy-start(bf16[128,512]{1,0:T(8,128)(2,1)} %w_up.3) | copy-start | bytes 393220
  48.1 18.5 %copy-start.18 = (bf16[512,128]{1,0:T(8,128)(2,1)S(1)}, bf16[512,128]{1,0:T(8,128)(2,1)}, u32[]{:S(2)}) copy-start(bf16[512,128]{1,0:T(8,128)(2,1)} %w_down.3) | copy-start | bytes 393220
  48.1 18.5 %copy-start.19 = (bf16[256,128]{1,0:T(8,128)(2,1)S(1)}, bf16[256,128]{1,0:T(8,128)(2,1)}, u32[]{:S(2)}) copy-start(bf16[256,128]{1,0:T(8,128)(2,1)} %w_out.3) | copy-start | bytes 196612
  63.4 13.5 %all-to-all-start = ((bf16[32,2,16,128]{3,2,1,0:T(8,128)(2,1)}), bf16[32,2,16,128]{3,2,1,0:T(8,128)(2,1)S(1)}, u32[]{:S(2)}, u32[]{:S(2)}) async-start(bf16[32,2,16,128]{3,2,1,0:T(8,128)(2,1)} %bitcast.25), calls=%async_computation | async-start | bytes 524288 | tf_op jit(solution)/shard_map/all_to_all | solution.py:638
  (2 other events, 1.9 us)

commit v15 on v13

--- a/solution.py
+++ b/solution.py
@@ -518,23 +518,24 @@
     )(*operands)
 
 
-def unpack_kernel(shares, local_m, piece_x, src, out):
+def unpack_kernel(shares, local_m, piece_x, unit, src, out, lines_out, sem):
     owners_y, owners_x = src.shape[:2]
-    unit = out.shape[0]
     lines, first = [], 0
     for share in shares:
         lines += [(owner_y, first + piece) for owner_y in range(owners_y) for piece in range(share)]
         first += share
+    leaving = []
     for step in range(len(lines) // unit):
-
-        @pl.when(pl.program_id(0) == step)
-        def _():
-            for row, (owner_y, piece) in enumerate(lines[step * unit : (step + 1) * unit]):
-                wide = src[owner_y, :, piece].astype(F32)
-                parts = [
-                    wide[owner, m * piece_x : (m + 1) * piece_x] for m in range(local_m) for owner in range(owners_x)
-                ]
-                out[row] = jnp.concatenate(parts, axis=0).astype(BF)
+        for row in range(step * unit, (step + 1) * unit):
+            owner_y, piece = lines[row]
+            wide = src[owner_y, :, piece].astype(F32)
+            parts = [wide[owner, m * piece_x : (m + 1) * piece_x] for m in range(local_m) for owner in range(owners_x)]
+            lines_out[row] = jnp.concatenate(parts, axis=0).astype(BF)
+        run = pl.ds(step * unit, unit)
+        leaving.append(pltpu.make_async_copy(lines_out.at[run], out.at[run], sem.at[step]))
+        leaving[-1].start()
+    for copy in leaving:
+        copy.wait()
 
 
 def unpack_step(landed, shares, cols, local_m, piece_x):
@@ -542,11 +543,11 @@
     rows = owners_y * pieces
     unit = 16 if rows % 16 == 0 else rows
     return pl.pallas_call(
-        functools.partial(unpack_kernel, shares, local_m, piece_x),
-        grid=(rows // unit,),
+        functools.partial(unpack_kernel, shares, local_m, piece_x, unit),
         in_specs=[pl.BlockSpec(memory_space=pltpu.VMEM)],
-        out_specs=pl.BlockSpec((unit, cols, width), lambda step: (step, 0, 0)),
+        out_specs=pl.BlockSpec(memory_space=pl.ANY),
         out_shape=jax.ShapeDtypeStruct((rows, cols, width), BF),
+        scratch_shapes=[pltpu.VMEM((rows, cols, width), BF), pltpu.SemaphoreType.DMA((rows // unit,))],
         compiler_params=pltpu.CompilerParams(vmem_limit_bytes=VMEM_LIMIT),
         cost_estimate=pl.CostEstimate(flops=0, bytes_accessed=rows * cols * width * 4, transcendentals=0),
     )(landed)

time: 105 us -> 104 us (level)
  no operation moved by 1% of the time
where the time goes in v15:
time: 104 us
  Pallas kernels  44.9 us (43%)
  blocking collectives  23.2 us (22%)
  starting transfers between devices  21.7 us (21%)
  waiting for transfers between devices  7.41 us (7%)
  local copies, waits for them, and re-layouts  5.35 us (5%)
  between operations  1.22 us (1%)
    pallas_call x4, Pallas kernels, conv_step(): pl.pallas_call(functools.partial(conv_kernel, start, rows, part, tail, re...  31.3 us
    all_to_all x1, blocking collectives, body(): lax.all_to_all(done, ('gy', 'gx'), split_axis=0, concat_axis=0, tiled=True)  23.2 us
    ppermute x4, starting transfers between devices, shifted(): return lax.ppermute(value, axis, pairs)  12.1 us
    pallas_call x2, Pallas kernels, block_step(): pl.pallas_call(block_kernel, grid=(lanes, piece_y // subs), in_specs=in_s...  9.84 us
    all_to_all x2, starting transfers between devices, body(): lax.all_to_all(sent, ('gy', 'gx'), split_axis=0, concat_axis=0, tiled=True)  9.55 us
    all_to_all x2, waiting for transfers between devices, body(): lax.all_to_all(sent, ('gy', 'gx'), split_axis=0, concat_axis=0, tiled=True)  6.52 us
    unnamed x40, local copies, waits for them, and re-layouts  5.29 us
    pallas_call x1, Pallas kernels, body(): pl.pallas_call(ring_kernel, grid=(1,), in_specs=[*(whole(array) for array...  2.21 us
  transfers between devices with their start and end apart: 6, of which 3 were waited for; matrix products, arithmetic and copies ran while one was open for 0% of the time, Pallas kernels for 27%

profile of v15, /device:TPU:1, one launch (start us, length us, event | category | flops | bytes accessed | tf_op | source)
XLA Modules:
  0.0 103.8 jit_solution(14887776618485425599)
XLA Ops:
  0.6 1.9 %copy-done = bf16[48,64,512]{2,1,0:T(8,128)(2,1)S(1)} copy-done((bf16[48,64,512]{2,1,0:T(8,128)(2,1)S(1)}, bf16[48,64,512]{2,1,0:T(8,128)(2,1)}, u32[]{:S(2)}) %copy-start) | copy-done | bytes 3145752
  2.5 1.1 %copy-done.2 = bf16[48,64,128]{2,1,0:T(8,128)(2,1)S(1)} copy-done((bf16[48,64,128]{2,1,0:T(8,128)(2,1)S(1)}, bf16[48,64,128]{2,1,0:T(8,128)(2,1)}, u32[]{:S(2)}) %copy-start.2) | copy-done | bytes 786456
  3.7 1.4 %copy-done.4 = f32[48,64,128]{2,1,0:T(8,128)S(1)} copy-done((f32[48,64,128]{2,1,0:T(8,128)S(1)}, f32[48,64,128]{2,1,0:T(8,128)}, u32[]{:S(2)}) %copy-start.4) | copy-done | bytes 1572888
  5.1 0.6 shard_map.105
  5.7 4.2 %collective-permute-start = (bf16[48,2,768]{2,1,0:T(2,128)(2,1)S(1)}, bf16[48,2,768]{2,1,0:T(2,128)(2,1)S(1)}, u32[]{:S(2)}, u32[]{:S(2)}) collective-permute-start(bf16[48,2,768]{2,1,0:T(2,128)(2,1)S(1)} %get-tuple-element.28), channel_id=1, source_target_pairs={{0,1},{1,2},{2,3},{4,5},{5,6},{6,7},{8,9},{9,10},{10,11},{12,13},{... | collective-permute-start | bytes 442376 | tf_op jit(solution)/shard_map/ppermute | solution.py:574
  9.9 1.3 %collective-permute-start.1 = (bf16[48,2,768]{2,1,0:T(2,128)(2,1)S(1)}, bf16[48,2,768]{2,1,0:T(2,128)(2,1)S(1)}, u32[]{:S(2)}, u32[]{:S(2)}) collective-permute-start(bf16[48,2,768]{2,1,0:T(2,128)(2,1)S(1)} %get-tuple-element.29), channel_id=1, source_target_pairs={{1,0},{2,1},{3,2},{5,4},{6,5},{7,6},{9,8},{10,9},{11,10},{13,12},{... | collective-permute-start | bytes 442376 | tf_op jit(solution)/shard_map/ppermute | solution.py:574
  11.2 5.2 %shard_map.104 = (bf16[48,64,128]{2,1,0:T(8,128)(2,1)S(1)}, f32[48,64,128]{2,1,0:T(8,128)S(1)}) custom-call(bf16[48,64,512]{2,1,0:T(8,128)(2,1)S(1)} %copy-done, bf16[48,64,128]{2,1,0:T(8,128)(2,1)S(1)} %copy-done.2, f32[48,64,128]{2,1,0:T(8,128)S(1)} %copy-done.4, f32[1,512]{1,0:T(1,128)S(1)} %bitcast.21, bf16[3456,512]{1,0:T(8,128)(2,1)S(1)} %bitcast.11), custom_call_target="tpu_custom_call" | custom-call | flops 4529848320 | bytes 6160384 | tf_op jit(solution)/shard_map/pallas_call | solution.py:262
  16.6 4.5 %collective-permute-start.2 = (bf16[2,68,768]{2,1,0:T(8,128)(2,1)S(1)}, bf16[2,68,768]{2,1,0:T(8,128)(2,1)S(1)}, u32[]{:S(2)}, u32[]{:S(2)}) collective-permute-start(bf16[2,68,768]{2,1,0:T(8,128)(2,1)S(1)} %get-tuple-element.35), channel_id=1, source_target_pairs={{0,4},{4,8},{8,12},{12,16},{16,20},{20,24},{24,28},{1,5},{5,9},{9,... | collective-permute-start | bytes 626696 | tf_op jit(solution)/shard_map/ppermute | solution.py:574
  21.2 2.1 %collective-permute-start.3 = (bf16[2,68,768]{2,1,0:T(8,128)(2,1)S(1)}, bf16[2,68,768]{2,1,0:T(8,128)(2,1)S(1)}, u32[]{:S(2)}, u32[]{:S(2)}) collective-permute-start(bf16[2,68,768]{2,1,0:T(8,128)(2,1)S(1)} %get-tuple-element.36), channel_id=1, source_target_pairs={{4,0},{8,4},{12,8},{16,12},{20,16},{24,20},{28,24},{5,1},{9,5},{13... | collective-permute-start | bytes 626696 | tf_op jit(solution)/shard_map/ppermute | solution.py:574
  23.3 4.2 %shard_map.106 = (bf16[48,64,128]{2,1,0:T(8,128)(2,1)S(1)}, f32[48,64,128]{2,1,0:T(8,128)S(1)}) custom-call(bf16[48,64,512]{2,1,0:T(8,128)(2,1)S(1)} %copy-done, bf16[48,64,128]{2,1,0:T(8,128)(2,1)S(1)} %copy-done.2, f32[48,64,128]{2,1,0:T(8,128)S(1)} %copy-done.4, f32[1,512]{1,0:T(1,128)S(1)} %bitcast.22, ...), custom_call_target="tpu_custom_call", output_to_operand_aliasing={{0}: (5, {}), {1}: (6, {})} | custom-call | flops 3623878656 | bytes 5636096 | tf_op jit(solution)/shard_map/pallas_call | solution.py:262
  27.5 0.0 copy-start.3
  27.5 0.9 collective-permute-done.3.below.args_11_.args_22_
  28.4 2.2 %shard_map.107 = (f32[4,64,128]{2,1,0:T(8,128)S(1)}, f32[4,64,128]{2,1,0:T(8,128)S(1)}, f32[4,64,128]{2,1,0:T(8,128)S(1)}, f32[4,64,128]{2,1,0:T(8,128)S(1)}, f32[2,64,256]{2,1,0:T(8,128)S(1)}) custom-call(bf16[2,68,768]{2,1,0:T(8,128)(2,1)S(1)} %collective-permute-done.2.above.args_10_.args_21_, ...), custom_call_target="tpu_custom_call" | custom-call | flops 1811939328 | bytes 3538944 | tf_op jit(solution)/shard_map/pallas_call | solution.py:607
  30.7 9.3 %shard_map.108 = (bf16[8,4,4,16,128]{4,3,2,1,0:T(8,128)(2,1)S(1)}, f32[48,64,128]{2,1,0:T(8,128)}) custom-call(bf16[48,64,512]{2,1,0:T(8,128)(2,1)S(1)} %copy-done.1, bf16[48,64,128]{2,1,0:T(8,128)(2,1)S(1)} %get-tuple-element.33.args_1_.args_3_.args_4_.args_5_, f32[48,64,128]{2,1,0:T(8,128)S(1)} %get-tuple-element.34.args_2_.args_6_, ...), custom_call_target="tpu_custom_call" | custom-call | flops 7247757312 | bytes 7733248 | tf_op jit(solution)/shard_map/pallas_call | solution.py:262
  40.1 0.8 copy-done.7
  40.9 6.4 %all-to-all-start.1 = ((bf16[32,4,16,128]{3,2,1,0:T(8,128)(2,1)}), bf16[32,4,16,128]{3,2,1,0:T(8,128)(2,1)S(1)}, u32[]{:S(2)}, u32[]{:S(2)}) async-start(bf16[32,4,16,128]{3,2,1,0:T(8,128)(2,1)} %bitcast.18), calls=%async_computation.1 | async-start | bytes 1048576 | tf_op jit(solution)/shard_map/all_to_all | solution.py:639
  47.3 12.6 %shard_map.109 = (bf16[8,4,2,16,128]{4,3,2,1,0:T(8,128)(2,1)}, f32[48,64,128]{2,1,0:T(8,128)}) custom-call(bf16[48,64,512]{2,1,0:T(8,128)(2,1)} %args_9_.1, bf16[48,64,512]{2,1,0:T(8,128)(2,1)} %args_9_.1, bf16[48,64,512]{2,1,0:T(8,128)(2,1)} %args_9_.1, bf16[48,64,128]{2,1,0:T(8,128)(2,1)} %copy-done.3, ...), custom_call_target="tpu_custom_call", output_to_operand_aliasing={{1}: (23, {})} | custom-call | flops 3623878656 | bytes 5636096 | tf_op jit(solution)/shard_map/pallas_call | solution.py:262
  59.9 2.7 %all-to-all-done.1 = bf16[32,4,16,128]{3,2,1,0:T(8,128)(2,1)S(1)} async-done(((bf16[32,4,16,128]{3,2,1,0:T(8,128)(2,1)}), bf16[32,4,16,128]{3,2,1,0:T(8,128)(2,1)S(1)}, u32[]{:S(2)}, u32[]{:S(2)}) %all-to-all-start.1) | async-done | bytes 524320 | tf_op jit(solution)/shard_map/all_to_all | solution.py:639
  62.6 3.2 %all-to-all-start = ((bf16[32,2,16,128]{3,2,1,0:T(8,128)(2,1)}), bf16[32,2,16,128]{3,2,1,0:T(8,128)(2,1)S(1)}, u32[]{:S(2)}, u32[]{:S(2)}) async-start(bf16[32,2,16,128]{3,2,1,0:T(8,128)(2,1)} %bitcast.25), calls=%async_computation | async-start | bytes 524288 | tf_op jit(solution)/shard_map/all_to_all | solution.py:639
  65.8 6.5 %shard_map.110.rest_0_ = bf16[8,1,4,6,16,128]{5,4,3,2,1,0:T(8,128)(2,1)S(1)} custom-call(bf16[8,1,4,4,16,128]{5,4,3,2,1,0:T(8,128)(2,1)S(1)} %bitcast.17, bf16[128,768]{1,0:T(8,128)(2,1)S(1)} %copy-done.16, bf16[256,128]{1,0:T(8,128)(2,1)S(1)} %copy-done.19, bf16[128,512]{1,0:T(8,128)(2,1)S(1)} %copy-done.17, bf16[512,128]{1,0:T(8,128)(2,1)S(1)} %copy-done.18), custom_call_target="tpu_custom_call" | custom-call | flops 6144000000 | bytes 1848576 | tf_op jit(solution)/shard_map/pallas_call | solution.py:498
  72.3 3.8 %all-to-all-done = bf16[32,2,16,128]{3,2,1,0:T(8,128)(2,1)S(1)} async-done(((bf16[32,2,16,128]{3,2,1,0:T(8,128)(2,1)}), bf16[32,2,16,128]{3,2,1,0:T(8,128)(2,1)S(1)}, u32[]{:S(2)}, u32[]{:S(2)}) %all-to-all-start) | async-done | bytes 262176 | tf_op jit(solution)/shard_map/all_to_all | solution.py:639
  76.1 3.4 %shard_map.111 = bf16[8,1,4,6,16,128]{5,4,3,2,1,0:T(8,128)(2,1)S(1)} custom-call(bf16[8,1,4,2,16,128]{5,4,3,2,1,0:T(8,128)(2,1)S(1)} %bitcast.19, bf16[128,768]{1,0:T(8,128)(2,1)S(1)} %copy-done.16, bf16[256,128]{1,0:T(8,128)(2,1)S(1)} %copy-done.19, bf16[128,512]{1,0:T(8,128)(2,1)S(1)} %copy-done.17, ...), custom_call_target="tpu_custom_call", output_to_operand_aliasing={{}: (5, {})} | custom-call | flops 3072000000 | bytes 1324288 | tf_op jit(solution)/shard_map/pallas_call | solution.py:498
  79.5 23.2 %all_to_all.15 = bf16[32,6,16,128]{3,2,1,0:T(8,128)(2,1)S(1)} all-to-all(bf16[32,6,16,128]{3,2,1,0:T(8,128)(2,1)S(1)} %bitcast.16), channel_id=1, replica_groups=mesh['gy'=8,'gx'=4] {'gy','gx'}, dimensions={0} | all-to-all | bytes 1572864 | tf_op jit(solution)/shard_map/all_to_all | solution.py:646
  102.7 0.9 shard_map.112
  (43 shorter events, 0.2 us)
Async XLA Ops:
  0.6 1.9 %copy-start = (bf16[48,64,512]{2,1,0:T(8,128)(2,1)S(1)}, bf16[48,64,512]{2,1,0:T(8,128)(2,1)}, u32[]{:S(2)}) copy-start(bf16[48,64,512]{2,1,0:T(8,128)(2,1)} %args_9_.1) | copy-start | bytes 9437188
  3.7 1.4 %copy-start.4 = (f32[48,64,128]{2,1,0:T(8,128)S(1)}, f32[48,64,128]{2,1,0:T(8,128)}, u32[]{:S(2)}) copy-start(f32[48,64,128]{2,1,0:T(8,128)} %args_13_.1) | copy-start | bytes 4718596
  5.1 6.1 %copy-start.5 = (bf16[3,3,384,512]{3,2,1,0:T(8,128)(2,1)S(1)}, bf16[3,3,384,512]{3,2,1,0:T(8,128)(2,1)}, u32[]{:S(2)}) copy-start(bf16[3,3,384,512]{3,2,1,0:T(8,128)(2,1)} %param.12) | copy-start | bytes 10616836
  5.1 6.1 %copy-start.15 = (f32[512]{0:T(512)S(1)}, f32[512]{0:T(512)}, u32[]{:S(2)}) copy-start(f32[512]{0:T(512)} %param.13) | copy-start | bytes 6148
  5.7 10.8 %collective-permute-start = (bf16[48,2,768]{2,1,0:T(2,128)(2,1)S(1)}, bf16[48,2,768]{2,1,0:T(2,128)(2,1)S(1)}, u32[]{:S(2)}, u32[]{:S(2)}) collective-permute-start(bf16[48,2,768]{2,1,0:T(2,128)(2,1)S(1)} %get-tuple-element.28), channel_id=1, source_target_pairs={{0,1},{1,2},{2,3},{4,5},{5,6},{6,7},{8,9},{9,10},{10,11},{12,13},{... | collective-permute-start | bytes 442376 | tf_op jit(solution)/shard_map/ppermute | solution.py:574
  9.9 6.6 %collective-permute-start.1 = (bf16[48,2,768]{2,1,0:T(2,128)(2,1)S(1)}, bf16[48,2,768]{2,1,0:T(2,128)(2,1)S(1)}, u32[]{:S(2)}, u32[]{:S(2)}) collective-permute-start(bf16[48,2,768]{2,1,0:T(2,128)(2,1)S(1)} %get-tuple-element.29), channel_id=1, source_target_pairs={{1,0},{2,1},{3,2},{5,4},{6,5},{7,6},{9,8},{10,9},{11,10},{13,12},{... | collective-permute-start | bytes 442376 | tf_op jit(solution)/shard_map/ppermute | solution.py:574
  16.6 10.9 %collective-permute-start.2 = (bf16[2,68,768]{2,1,0:T(8,128)(2,1)S(1)}, bf16[2,68,768]{2,1,0:T(8,128)(2,1)S(1)}, u32[]{:S(2)}, u32[]{:S(2)}) collective-permute-start(bf16[2,68,768]{2,1,0:T(8,128)(2,1)S(1)} %get-tuple-element.35), channel_id=1, source_target_pairs={{0,4},{4,8},{8,12},{12,16},{16,20},{20,24},{24,28},{1,5},{5,9},{9,... | collective-permute-start | bytes 626696 | tf_op jit(solution)/shard_map/ppermute | solution.py:574
  21.2 7.3 %collective-permute-start.3 = (bf16[2,68,768]{2,1,0:T(8,128)(2,1)S(1)}, bf16[2,68,768]{2,1,0:T(8,128)(2,1)S(1)}, u32[]{:S(2)}, u32[]{:S(2)}) collective-permute-start(bf16[2,68,768]{2,1,0:T(8,128)(2,1)S(1)} %get-tuple-element.36), channel_id=1, source_target_pairs={{4,0},{8,4},{12,8},{16,12},{20,16},{24,20},{28,24},{5,1},{9,5},{13... | collective-permute-start | bytes 626696 | tf_op jit(solution)/shard_map/ppermute | solution.py:574
  27.5 3.2 %copy-start.3 = (bf16[48,64,128]{2,1,0:T(8,128)(2,1)}, bf16[48,64,128]{2,1,0:T(8,128)(2,1)S(1)}, u32[]{:S(2)}) copy-start(bf16[48,64,128]{2,1,0:T(8,128)(2,1)S(1)} %get-tuple-element.33.args_1_.args_3_.args_4_.args_5_) | copy-start | bytes 2359300
  27.5 3.2 %copy-start.6 = (f32[48,64,128]{2,1,0:T(8,128)}, f32[48,64,128]{2,1,0:T(8,128)S(1)}, u32[]{:S(2)}) copy-start(f32[48,64,128]{2,1,0:T(8,128)S(1)} %get-tuple-element.34.args_2_.args_6_) | copy-start | bytes 4718596
  27.5 3.2 %copy-start.8 = (bf16[2,68,768]{2,1,0:T(8,128)(2,1)}, bf16[2,68,768]{2,1,0:T(8,128)(2,1)S(1)}, u32[]{:S(2)}) copy-start(bf16[2,68,768]{2,1,0:T(8,128)(2,1)S(1)} %collective-permute-done.2.above.args_10_.args_21_) | copy-start | bytes 626692
  28.4 2.3 %copy-start.9 = (bf16[2,68,768]{2,1,0:T(8,128)(2,1)}, bf16[2,68,768]{2,1,0:T(8,128)(2,1)S(1)}, u32[]{:S(2)}) copy-start(bf16[2,68,768]{2,1,0:T(8,128)(2,1)S(1)} %collective-permute-done.3.below.args_11_.args_22_) | copy-start | bytes 626692
  28.4 2.3 %copy-start.1 = (bf16[48,64,512]{2,1,0:T(8,128)(2,1)S(1)}, bf16[48,64,512]{2,1,0:T(8,128)(2,1)}, u32[]{:S(2)}) copy-start(bf16[48,64,512]{2,1,0:T(8,128)(2,1)} %args_9_.1) | copy-start | bytes 9437188
  30.6 9.4 %copy-start.10 = (f32[4,64,128]{2,1,0:T(8,128)}, f32[4,64,128]{2,1,0:T(8,128)S(1)}, u32[]{:S(2)}) copy-start(f32[4,64,128]{2,1,0:T(8,128)S(1)} %get-tuple-element.41.args_7_.args_18_) | copy-start | bytes 393220
  30.7 9.4 %copy-start.11 = (f32[4,64,128]{2,1,0:T(8,128)}, f32[4,64,128]{2,1,0:T(8,128)S(1)}, u32[]{:S(2)}) copy-start(f32[4,64,128]{2,1,0:T(8,128)S(1)} %get-tuple-element.42.args_8_.args_19_) | copy-start | bytes 393220
  30.7 9.4 %copy-start.12 = (f32[4,64,128]{2,1,0:T(8,128)}, f32[4,64,128]{2,1,0:T(8,128)S(1)}, u32[]{:S(2)}) copy-start(f32[4,64,128]{2,1,0:T(8,128)S(1)} %get-tuple-element.39.args_5_.args_16_) | copy-start | bytes 393220
  30.7 9.4 %copy-start.13 = (f32[4,64,128]{2,1,0:T(8,128)}, f32[4,64,128]{2,1,0:T(8,128)S(1)}, u32[]{:S(2)}) copy-start(f32[4,64,128]{2,1,0:T(8,128)S(1)} %get-tuple-element.40.args_6_.args_17_) | copy-start | bytes 393220
  30.7 9.4 %copy-start.14 = (f32[2,64,256]{2,1,0:T(8,128)}, f32[2,64,256]{2,1,0:T(8,128)S(1)}, u32[]{:S(2)}) copy-start(f32[2,64,256]{2,1,0:T(8,128)S(1)} %get-tuple-element.43.args_9_.args_20_) | copy-start | bytes 393220
  40.9 21.7 %all-to-all-start.1 = ((bf16[32,4,16,128]{3,2,1,0:T(8,128)(2,1)}), bf16[32,4,16,128]{3,2,1,0:T(8,128)(2,1)S(1)}, u32[]{:S(2)}, u32[]{:S(2)}) async-start(bf16[32,4,16,128]{3,2,1,0:T(8,128)(2,1)} %bitcast.18), calls=%async_computation.1 | async-start | bytes 1048576 | tf_op jit(solution)/shard_map/all_to_all | solution.py:639
  47.3 18.5 %copy-start.16 = (bf16[128,768]{1,0:T(8,128)(2,1)S(1)}, bf16[128,768]{1,0:T(8,128)(2,1)}, u32[]{:S(2)}) copy-start(bf16[128,768]{1,0:T(8,128)(2,1)} %w_qkv.3) | copy-start | bytes 589828
  47.3 18.5 %copy-start.17 = (bf16[128,512]{1,0:T(8,128)(2,1)S(1)}, bf16[128,512]{1,0:T(8,128)(2,1)}, u32[]{:S(2)}) copy-start(bf16[128,512]{1,0:T(8,128)(2,1)} %w_up.3) | copy-start | bytes 393220
  47.3 18.5 %copy-start.18 = (bf16[512,128]{1,0:T(8,128)(2,1)S(1)}, bf16[512,128]{1,0:T(8,128)(2,1)}, u32[]{:S(2)}) copy-start(bf16[512,128]{1,0:T(8,128)(2,1)} %w_down.3) | copy-start | bytes 393220
  47.3 18.5 %copy-start.19 = (bf16[256,128]{1,0:T(8,128)(2,1)S(1)}, bf16[256,128]{1,0:T(8,128)(2,1)}, u32[]{:S(2)}) copy-start(bf16[256,128]{1,0:T(8,128)(2,1)} %w_out.3) | copy-start | bytes 196612
  62.6 13.5 %all-to-all-start = ((bf16[32,2,16,128]{3,2,1,0:T(8,128)(2,1)}), bf16[32,2,16,128]{3,2,1,0:T(8,128)(2,1)S(1)}, u32[]{:S(2)}, u32[]{:S(2)}) async-start(bf16[32,2,16,128]{3,2,1,0:T(8,128)(2,1)} %bitcast.25), calls=%async_computation | async-start | bytes 524288 | tf_op jit(solution)/shard_map/all_to_all | solution.py:639
  (2 other events, 1.9 us)
